TPU v7x, 32 devices: a whole 2x2x4 slice. The times are simulated.
32 devices in a mesh: point: 4 (over z), dom: 8 (over y, x, core).
Axes of the slice: x: 2, y: 2, z: 4, core: 2. Of those that a mesh axis runs over, the one named last changes fastest.
Arguments:
- sources: float32 [16, 16, 1024], P(None, 'dom'), may hold values from -17 to 17
- potential: float32 [16, 1024], P('dom'), may hold values from 0 to 2
- iter_counts: int32 [4], P('point'), may hold values from 1 to 6, as said below
Outputs:
- gram_b: float32 [2, 64, 64], replicated
- gram_a: float32 [2, 64, 64], replicated
Inputs may be any that keep to these rules, and one draw needn't show every extreme that they name: `iter_counts`: iterations of each quadrature point; some point takes 6 in every draw.
All inputs are finite; a program needn't handle non-finite values.
Results may differ from a plain program's by a relative error of at most 0.00018.
Values sent between devices are 32-bit elements; how exact they have to be, the bound alone decides.
No kernel may reach another device: no remote copies, remote signals or barrier semaphores. Data moves between devices by JAX's collectives and lax.ppermute only.
A program may use at most 64 MiB of HBM per device.

v0:
```python
import math

import jax
import jax.numpy as jnp
from jax import lax
from jax.sharding import PartitionSpec as P

MOMENTS = 4
ITERS = 6
GX = 32


COEF_NEAR = 4.0 / 3.0
COEF_FAR = -1.0 / 12.0
GAMMA = 2.0
RADIUS = 1.5


def padded_2(block, sides, width):
    for axis, dim in sides:
        count = lax.axis_size(axis)
        forward = [(i, i + 1) for i in range(count - 1)]
        forward.append((count - 1, 0))
        backward = [(target, source) for source, target in forward]
        low = lax.ppermute(
            lax.slice_in_dim(block, block.shape[dim] - width, None, axis=dim), axis, forward
        )
        high = lax.ppermute(lax.slice_in_dim(block, 0, width, axis=dim), axis, backward)
        block = jnp.concatenate([low, block, high], axis=dim)
    return block


def plane_terms(values, side):
    lead = values.shape[:-1]
    planes = values.reshape(lead + (side, side))
    summed = COEF_NEAR * (
        jnp.roll(planes, 1, -2)
        + jnp.roll(planes, -1, -2)
        + jnp.roll(planes, 1, -1)
        + jnp.roll(planes, -1, -1)
    )
    summed = summed + COEF_FAR * (
        jnp.roll(planes, 2, -2)
        + jnp.roll(planes, -2, -2)
        + jnp.roll(planes, 2, -1)
        + jnp.roll(planes, -2, -1)
    )
    return summed.reshape(values.shape)


def complex_mul(first, second):
    return jnp.stack(
        [first[0] * second[0] - first[1] * second[1], first[0] * second[1] + first[1] * second[0]]
    )


def complex_div(first, second):
    denom = second[0] * second[0] + second[1] * second[1]
    return jnp.stack(
        [
            (first[0] * second[0] + first[1] * second[1]) / denom,
            (first[1] * second[0] - first[0] * second[1]) / denom,
        ]
    )


def bilinear(first, second):
    real_part = jnp.sum(first[0] * second[0] - first[1] * second[1], axis=(1, 2))
    imag_part = jnp.sum(first[0] * second[1] + first[1] * second[0], axis=(1, 2))
    return jnp.stack([real_part, imag_part])


def scaled(coeffs, values):
    return complex_mul(coeffs[:, :, None, None], values)


def shifted(values, potential, shift_re, shift_im):
    padded = padded_2(values, (("dom", 2),), 2)
    depth = values.shape[2]
    lap = -7.5 * values + plane_terms(values, GX)
    lap = lap + COEF_NEAR * (padded[:, :, 3 : 3 + depth] + padded[:, :, 1 : 1 + depth])
    lap = lap + COEF_FAR * (padded[:, :, 4 : 4 + depth] + padded[:, :, 0:depth])
    applied = -0.5 * lap + potential * values
    return jnp.stack(
        [
            shift_re * values[0] - shift_im * values[1] - applied[0],
            shift_re * values[1] + shift_im * values[0] - applied[1],
        ]
    )


def residual_sum(values):
    return lax.psum(bilinear(values, values), "dom")


def moment_terms(solution, residual, sources, angle_now, shift_re, shift_im):
    applied = jnp.stack(
        [
            shift_re * solution[0] - shift_im * solution[1] - sources[0] + residual[0],
            shift_re * solution[1] + shift_im * solution[0] - sources[1] + residual[1],
        ]
    )
    angles = (jnp.arange(MOMENTS).astype(jnp.float32) + 1.0) * angle_now
    coeffs = 0.25 * jnp.stack([jnp.cos(angles), jnp.sin(angles)])
    s_terms = complex_mul(coeffs[:, :, None, None, None], solution[:, None])
    h_terms = complex_mul(coeffs[:, :, None, None, None], applied[:, None])
    width = MOMENTS * solution.shape[1]
    return (s_terms.reshape(2, width, -1), h_terms.reshape(2, width, -1))


def gram_of(left, right):
    width = left.shape[1]
    joined = lax.dot_general(
        left.reshape(2 * width, -1),
        right.reshape(2 * width, -1),
        (((1,), (1,)), ((), ())),
        precision=lax.Precision.HIGHEST,
        preferred_element_type=jnp.float32,
    )
    blocks = joined.reshape(2, width, 2, width)
    return jnp.stack([blocks[0, :, 0] + blocks[1, :, 1], blocks[0, :, 1] - blocks[1, :, 0]])


def on_device(sources, potential, iter_counts):
    complex_src = jnp.stack([sources, jnp.zeros_like(sources)])
    angle_now = (
        2.0 * math.pi * (lax.axis_index("point").astype(jnp.float32) + 0.5) / lax.axis_size("point")
    )
    shift_re = GAMMA + RADIUS * jnp.cos(angle_now)
    shift_im = RADIUS * jnp.sin(angle_now)
    limit = iter_counts[0]
    solution = jnp.zeros_like(complex_src)

    def one_turn(turn_idx, state):
        solution, residual, search, norm_now = state
        product = shifted(search, potential, shift_re, shift_im)
        curve = lax.psum(bilinear(search, product), "dom")
        step_size = complex_div(norm_now, curve)
        new_residual = residual - scaled(step_size, product)
        norm_next = residual_sum(new_residual)
        fresh = (
            solution + scaled(step_size, search),
            new_residual,
            new_residual + scaled(complex_div(norm_next, norm_now), search),
            norm_next,
        )
        keep_mask = turn_idx < limit
        return jax.tree.map(lambda newer, older: jnp.where(keep_mask, newer, older), fresh, state)

    start = (solution, complex_src, complex_src, residual_sum(complex_src))
    solution, residual, search, norm_now = lax.fori_loop(0, ITERS, one_turn, start)
    s_terms, h_terms = moment_terms(solution, residual, complex_src, angle_now, shift_re, shift_im)
    cells = sources.shape[1] * sources.shape[2] * lax.axis_size("dom")
    s_total, h_total = lax.psum((s_terms, h_terms), "point")
    gram_b, gram_a = lax.psum((gram_of(s_total, s_total), gram_of(s_total, h_total)), "dom")
    return (gram_b / cells, gram_a / cells)


def solution(mesh):
    placed = (P(None, "dom", None), P("dom", None), P("point"))
    return jax.shard_map(
        on_device, mesh=mesh, in_specs=placed, out_specs=(P(), P()), check_vma=False
    )
```

profile of v0, /device:TPU:0, one launch (start us, length us, event | category | flops | bytes accessed | tf_op | source)
XLA Modules:
  0.0 389.6 jit_solution(443842755520658986)
XLA Ops:
  7.4 1.2 multiply_reduce_fusion.2
  8.6 15.1 %psum.57 = f32[2,16]{1,0:T(2,128)S(1)} all-reduce(f32[2,16]{1,0:T(2,128)S(1)} %pad_maximum_fusion.8), channel_id=1, replica_groups=mesh['point'=4,'dom'=8] {'dom'}, use_global_device_ids=true, to_apply=%region_2.0 | all-reduce | flops 32 | bytes 256 | tf_op jit(solution)/shard_map/psum | solution.py:93
  23.8 0.7 copy-done.3
  24.5 204.8 %while.20 = (s32[]{:T(128)}, f32[2,16,2,1024]{3,1,2,0:T(8,128)S(1)}, f32[2,16,2,1024]{3,1,2,0:T(8,128)S(1)}, f32[2,16,2,1024]{3,1,2,0:T(8,128)S(1)}, f32[2,16]{1...) while((s32[]{:T(128)}, ...), condition=%wide.region_10.11_spmd.clone, body=%wide.region_3.10_spmd.clone.sunk | while | flops 4227524 | bytes 16788452 | solution.py:151
  24.5 2.6 collective-permute-start.1
  29.6 1.7 fusion.66
  31.3 0.5 reshape.485
  32.8 13.1 %psum.66 = f32[2,16]{1,0:T(2,128)S(1)} all-reduce(f32[2,16]{1,0:T(2,128)S(1)} %pad_maximum_fusion.11), channel_id=1, replica_groups=mesh['point'=4,'dom'=8] {'dom'}, use_global_device_ids=true, to_apply=%region_6.6 | all-reduce | flops 32 | bytes 256 | tf_op jit(solution)/shard_map/while/body/eval_jaxpr/psum | solution.py:137
  46.4 11.8 %psum.67 = f32[2,16]{1,0:T(2,128)S(1)} all-reduce(f32[2,16]{1,0:T(2,128)S(1)} %pad_maximum_fusion.12), channel_id=1, replica_groups=mesh['point'=4,'dom'=8] {'dom'}, use_global_device_ids=true, to_apply=%region_9.9 | all-reduce | flops 32 | bytes 256 | tf_op jit(solution)/shard_map/while/body/eval_jaxpr/psum | solution.py:93
  58.6 2.6 collective-permute-start.1
  63.7 1.7 fusion.66
  65.4 0.5 reshape.485
  66.6 0.7 collective-permute-done
  67.6 12.5 %psum.66 = f32[2,16]{1,0:T(2,128)S(1)} all-reduce(f32[2,16]{1,0:T(2,128)S(1)} %pad_maximum_fusion.11), channel_id=1, replica_groups=mesh['point'=4,'dom'=8] {'dom'}, use_global_device_ids=true, to_apply=%region_6.6 | all-reduce | flops 32 | bytes 256 | tf_op jit(solution)/shard_map/while/body/eval_jaxpr/psum | solution.py:137
  80.6 11.8 %psum.67 = f32[2,16]{1,0:T(2,128)S(1)} all-reduce(f32[2,16]{1,0:T(2,128)S(1)} %pad_maximum_fusion.12), channel_id=1, replica_groups=mesh['point'=4,'dom'=8] {'dom'}, use_global_device_ids=true, to_apply=%region_9.9 | all-reduce | flops 32 | bytes 256 | tf_op jit(solution)/shard_map/while/body/eval_jaxpr/psum | solution.py:93
  92.8 2.6 collective-permute-start.1
  97.9 1.7 fusion.66
  99.6 0.5 reshape.485
  100.7 0.7 collective-permute-done
  101.8 12.4 %psum.66 = f32[2,16]{1,0:T(2,128)S(1)} all-reduce(f32[2,16]{1,0:T(2,128)S(1)} %pad_maximum_fusion.11), channel_id=1, replica_groups=mesh['point'=4,'dom'=8] {'dom'}, use_global_device_ids=true, to_apply=%region_6.6 | all-reduce | flops 32 | bytes 256 | tf_op jit(solution)/shard_map/while/body/eval_jaxpr/psum | solution.py:137
  114.7 11.8 %psum.67 = f32[2,16]{1,0:T(2,128)S(1)} all-reduce(f32[2,16]{1,0:T(2,128)S(1)} %pad_maximum_fusion.12), channel_id=1, replica_groups=mesh['point'=4,'dom'=8] {'dom'}, use_global_device_ids=true, to_apply=%region_9.9 | all-reduce | flops 32 | bytes 256 | tf_op jit(solution)/shard_map/while/body/eval_jaxpr/psum | solution.py:93
  126.9 2.6 collective-permute-start.1
  132.0 1.7 fusion.66
  134.9 0.8 collective-permute-done
  136.0 12.4 %psum.66 = f32[2,16]{1,0:T(2,128)S(1)} all-reduce(f32[2,16]{1,0:T(2,128)S(1)} %pad_maximum_fusion.11), channel_id=1, replica_groups=mesh['point'=4,'dom'=8] {'dom'}, use_global_device_ids=true, to_apply=%region_6.6 | all-reduce | flops 32 | bytes 256 | tf_op jit(solution)/shard_map/while/body/eval_jaxpr/psum | solution.py:137
  148.9 11.8 %psum.67 = f32[2,16]{1,0:T(2,128)S(1)} all-reduce(f32[2,16]{1,0:T(2,128)S(1)} %pad_maximum_fusion.12), channel_id=1, replica_groups=mesh['point'=4,'dom'=8] {'dom'}, use_global_device_ids=true, to_apply=%region_9.9 | all-reduce | flops 32 | bytes 256 | tf_op jit(solution)/shard_map/while/body/eval_jaxpr/psum | solution.py:93
  161.1 2.6 collective-permute-start.1
  166.2 1.7 fusion.66
  167.9 0.5 reshape.485
  169.0 0.9 collective-permute-done
  170.3 12.2 %psum.66 = f32[2,16]{1,0:T(2,128)S(1)} all-reduce(f32[2,16]{1,0:T(2,128)S(1)} %pad_maximum_fusion.11), channel_id=1, replica_groups=mesh['point'=4,'dom'=8] {'dom'}, use_global_device_ids=true, to_apply=%region_6.6 | all-reduce | flops 32 | bytes 256 | tf_op jit(solution)/shard_map/while/body/eval_jaxpr/psum | solution.py:137
  183.0 11.8 %psum.67 = f32[2,16]{1,0:T(2,128)S(1)} all-reduce(f32[2,16]{1,0:T(2,128)S(1)} %pad_maximum_fusion.12), channel_id=1, replica_groups=mesh['point'=4,'dom'=8] {'dom'}, use_global_device_ids=true, to_apply=%region_9.9 | all-reduce | flops 32 | bytes 256 | tf_op jit(solution)/shard_map/while/body/eval_jaxpr/psum | solution.py:93
  195.2 2.6 collective-permute-start.1
  200.3 1.7 fusion.66
  202.0 0.5 reshape.485
  203.2 1.0 collective-permute-done
  204.5 12.1 %psum.66 = f32[2,16]{1,0:T(2,128)S(1)} all-reduce(f32[2,16]{1,0:T(2,128)S(1)} %pad_maximum_fusion.11), channel_id=1, replica_groups=mesh['point'=4,'dom'=8] {'dom'}, use_global_device_ids=true, to_apply=%region_6.6 | all-reduce | flops 32 | bytes 256 | tf_op jit(solution)/shard_map/while/body/eval_jaxpr/psum | solution.py:137
  217.1 11.8 %psum.67 = f32[2,16]{1,0:T(2,128)S(1)} all-reduce(f32[2,16]{1,0:T(2,128)S(1)} %pad_maximum_fusion.12), channel_id=1, replica_groups=mesh['point'=4,'dom'=8] {'dom'}, use_global_device_ids=true, to_apply=%region_9.9 | all-reduce | flops 32 | bytes 256 | tf_op jit(solution)/shard_map/while/body/eval_jaxpr/psum | solution.py:93
  233.1 1.1 pad_maximum_fusion.5
  234.1 1.1 pad_maximum_fusion.4
  235.5 86.7 %all-reduce.8.cloned.1.call-done = (f32[2,64,2048]{2,1,0:T(8,128)}, f32[2,64,2048]{2,1,0:T(8,128)}) async-done(((f32[2,64,2048]{2,1,0:T(8,128)}, f32[2,64,2048]{2,1,0:T(8,128)}), (f32[2,64,2048]{2,1,0:T(8,128)}, f32[2,64,2048]{2,1,0:T(8,128)})) %all-reduce.8.cloned.1.call-update) | async-done | bytes 2097168 | tf_op jit(solution)/shard_map/psum | solution.py:154
  322.1 3.3 fusion.27
  325.5 1.6 fusion.24
  327.2 0.6 pad_maximum_fusion.7
  327.8 0.6 pad_maximum_fusion.6
  328.5 52.2 %all-reduce.6.cloned.1.call-done = (f32[2,64,64]{2,1,0:T(8,128)}, f32[2,64,64]{2,1,0:T(8,128)}) async-done(((f32[2,64,64]{2,1,0:T(8,128)}, f32[2,64,64]{2,1,0:T(8,128)}), (f32[2,64,64]{2,1,0:T(8,128)}, f32[2,64,64]{2,1,0:T(8,128)})) %all-reduce.6.cloned.1.call-update) | async-done | bytes 65552 | tf_op jit(solution)/shard_map/psum | solution.py:155
  380.6 1.5 broadcast_multiply_fusion
  382.1 0.6 broadcast_multiply_fusion.1
  (194 shorter events, 26.0 us)
Async XLA Ops:
  7.2 1.4 copy-start.1
  7.2 314.9 %all-reduce.8.cloned.1.call-start = ((), (), s32[]{:S(2)}) async-start(), calls=%async_computation.1 | async-start | bytes 4194304 | tf_op jit(solution)/shard_map/psum | solution.py:154
  23.8 0.7 copy-start.3
  24.5 8.0 %collective-permute-start = (f32[2,16,2,1024]{3,1,2,0:T(8,128)S(1)}, f32[2,16,2,1024]{3,1,2,0:T(8,128)S(1)}, u32[]{:S(2)}, u32[]{:S(2)}) collective-permute-start(f32[2,16,2,1024]{3,1,2,0:T(8,128)S(1)} %get-tuple-element.398), channel_id=1, source_target_pairs={{0,1},{1,2},{2,3},{3,4},{4,5},{5,6},{6,7},{7,0},{8,9},{9,10},{10,1... | collective-permute-start | bytes 786440 | tf_op jit(solution)/shard_map/while/body/eval_jaxpr/ppermute | solution.py:25
  24.5 8.0 %collective-permute-start.1 = (f32[2,16,2,1024]{3,1,2,0:T(8,128)S(1)}, f32[2,16,2,1024]{3,1,2,0:T(8,128)S(1)}, u32[]{:S(2)}, u32[]{:S(2)}) collective-permute-start(f32[2,16,2,1024]{3,1,2,0:T(8,128)S(1)} %get-tuple-element.398), channel_id=1, source_target_pairs={{1,0},{2,1},{3,2},{4,3},{5,4},{6,5},{7,6},{0,7},{9,8},{10,9},{11,1... | collective-permute-start | bytes 786440 | tf_op jit(solution)/shard_map/while/body/eval_jaxpr/ppermute | solution.py:28
  58.6 8.7 %collective-permute-start = (f32[2,16,2,1024]{3,1,2,0:T(8,128)S(1)}, f32[2,16,2,1024]{3,1,2,0:T(8,128)S(1)}, u32[]{:S(2)}, u32[]{:S(2)}) collective-permute-start(f32[2,16,2,1024]{3,1,2,0:T(8,128)S(1)} %get-tuple-element.398), channel_id=1, source_target_pairs={{0,1},{1,2},{2,3},{3,4},{4,5},{5,6},{6,7},{7,0},{8,9},{9,10},{10,1... | collective-permute-start | bytes 786440 | tf_op jit(solution)/shard_map/while/body/eval_jaxpr/ppermute | solution.py:25
  58.6 8.7 %collective-permute-start.1 = (f32[2,16,2,1024]{3,1,2,0:T(8,128)S(1)}, f32[2,16,2,1024]{3,1,2,0:T(8,128)S(1)}, u32[]{:S(2)}, u32[]{:S(2)}) collective-permute-start(f32[2,16,2,1024]{3,1,2,0:T(8,128)S(1)} %get-tuple-element.398), channel_id=1, source_target_pairs={{1,0},{2,1},{3,2},{4,3},{5,4},{6,5},{7,6},{0,7},{9,8},{10,9},{11,1... | collective-permute-start | bytes 786440 | tf_op jit(solution)/shard_map/while/body/eval_jaxpr/ppermute | solution.py:28
  92.7 8.8 %collective-permute-start = (f32[2,16,2,1024]{3,1,2,0:T(8,128)S(1)}, f32[2,16,2,1024]{3,1,2,0:T(8,128)S(1)}, u32[]{:S(2)}, u32[]{:S(2)}) collective-permute-start(f32[2,16,2,1024]{3,1,2,0:T(8,128)S(1)} %get-tuple-element.398), channel_id=1, source_target_pairs={{0,1},{1,2},{2,3},{3,4},{4,5},{5,6},{6,7},{7,0},{8,9},{9,10},{10,1... | collective-permute-start | bytes 786440 | tf_op jit(solution)/shard_map/while/body/eval_jaxpr/ppermute | solution.py:25
  92.8 8.7 %collective-permute-start.1 = (f32[2,16,2,1024]{3,1,2,0:T(8,128)S(1)}, f32[2,16,2,1024]{3,1,2,0:T(8,128)S(1)}, u32[]{:S(2)}, u32[]{:S(2)}) collective-permute-start(f32[2,16,2,1024]{3,1,2,0:T(8,128)S(1)} %get-tuple-element.398), channel_id=1, source_target_pairs={{1,0},{2,1},{3,2},{4,3},{5,4},{6,5},{7,6},{0,7},{9,8},{10,9},{11,1... | collective-permute-start | bytes 786440 | tf_op jit(solution)/shard_map/while/body/eval_jaxpr/ppermute | solution.py:28
  126.9 8.8 %collective-permute-start = (f32[2,16,2,1024]{3,1,2,0:T(8,128)S(1)}, f32[2,16,2,1024]{3,1,2,0:T(8,128)S(1)}, u32[]{:S(2)}, u32[]{:S(2)}) collective-permute-start(f32[2,16,2,1024]{3,1,2,0:T(8,128)S(1)} %get-tuple-element.398), channel_id=1, source_target_pairs={{0,1},{1,2},{2,3},{3,4},{4,5},{5,6},{6,7},{7,0},{8,9},{9,10},{10,1... | collective-permute-start | bytes 786440 | tf_op jit(solution)/shard_map/while/body/eval_jaxpr/ppermute | solution.py:25
  126.9 8.8 %collective-permute-start.1 = (f32[2,16,2,1024]{3,1,2,0:T(8,128)S(1)}, f32[2,16,2,1024]{3,1,2,0:T(8,128)S(1)}, u32[]{:S(2)}, u32[]{:S(2)}) collective-permute-start(f32[2,16,2,1024]{3,1,2,0:T(8,128)S(1)} %get-tuple-element.398), channel_id=1, source_target_pairs={{1,0},{2,1},{3,2},{4,3},{5,4},{6,5},{7,6},{0,7},{9,8},{10,9},{11,1... | collective-permute-start | bytes 786440 | tf_op jit(solution)/shard_map/while/body/eval_jaxpr/ppermute | solution.py:28
  161.0 8.9 %collective-permute-start = (f32[2,16,2,1024]{3,1,2,0:T(8,128)S(1)}, f32[2,16,2,1024]{3,1,2,0:T(8,128)S(1)}, u32[]{:S(2)}, u32[]{:S(2)}) collective-permute-start(f32[2,16,2,1024]{3,1,2,0:T(8,128)S(1)} %get-tuple-element.398), channel_id=1, source_target_pairs={{0,1},{1,2},{2,3},{3,4},{4,5},{5,6},{6,7},{7,0},{8,9},{9,10},{10,1... | collective-permute-start | bytes 786440 | tf_op jit(solution)/shard_map/while/body/eval_jaxpr/ppermute | solution.py:25
  161.1 8.9 %collective-permute-start.1 = (f32[2,16,2,1024]{3,1,2,0:T(8,128)S(1)}, f32[2,16,2,1024]{3,1,2,0:T(8,128)S(1)}, u32[]{:S(2)}, u32[]{:S(2)}) collective-permute-start(f32[2,16,2,1024]{3,1,2,0:T(8,128)S(1)} %get-tuple-element.398), channel_id=1, source_target_pairs={{1,0},{2,1},{3,2},{4,3},{5,4},{6,5},{7,6},{0,7},{9,8},{10,9},{11,1... | collective-permute-start | bytes 786440 | tf_op jit(solution)/shard_map/while/body/eval_jaxpr/ppermute | solution.py:28
  195.2 9.1 %collective-permute-start = (f32[2,16,2,1024]{3,1,2,0:T(8,128)S(1)}, f32[2,16,2,1024]{3,1,2,0:T(8,128)S(1)}, u32[]{:S(2)}, u32[]{:S(2)}) collective-permute-start(f32[2,16,2,1024]{3,1,2,0:T(8,128)S(1)} %get-tuple-element.398), channel_id=1, source_target_pairs={{0,1},{1,2},{2,3},{3,4},{4,5},{5,6},{6,7},{7,0},{8,9},{9,10},{10,1... | collective-permute-start | bytes 786440 | tf_op jit(solution)/shard_map/while/body/eval_jaxpr/ppermute | solution.py:25
  195.2 9.0 %collective-permute-start.1 = (f32[2,16,2,1024]{3,1,2,0:T(8,128)S(1)}, f32[2,16,2,1024]{3,1,2,0:T(8,128)S(1)}, u32[]{:S(2)}, u32[]{:S(2)}) collective-permute-start(f32[2,16,2,1024]{3,1,2,0:T(8,128)S(1)} %get-tuple-element.398), channel_id=1, source_target_pairs={{1,0},{2,1},{3,2},{4,3},{5,4},{6,5},{7,6},{0,7},{9,8},{10,9},{11,1... | collective-permute-start | bytes 786440 | tf_op jit(solution)/shard_map/while/body/eval_jaxpr/ppermute | solution.py:28
  235.2 145.4 %all-reduce.6.cloned.1.call-start = ((), (), s32[]{:S(2)}) async-start(), calls=%async_computation | async-start | bytes 262144 | tf_op jit(solution)/shard_map/psum | solution.py:155
  322.1 3.3 copy-start
  322.1 3.3 copy-start.2
  380.6 1.5 copy-start.4
Sparse Core Ops, SparseCore 0:
  235.3 86.7 all-reduce.7
  328.6 51.9 all-reduce.5
where the time goes:
time: 390 us
  blocking collectives  161 us (41%)
  waiting for transfers between devices  143 us (37%)
  other arithmetic  24.1 us (6%)
  local copies, waits for them, and re-layouts  21.3 us (5%)
  starting transfers between devices  16.4 us (4%)
  between operations  14.4 us (4%)
  matrix products  4.96 us (1%)
  loops' own time  4.79 us (1%)
    psum x1, waiting for transfers between devices, on_device(): s_total, h_total = lax.psum((s_terms, h_terms), 'point')  86.7 us
    psum x7, blocking collectives, residual_sum(): return lax.psum(bilinear(values, values), 'dom')  85.9 us
    psum x6, blocking collectives, one_turn(): curve = lax.psum(bilinear(search, product), 'dom')  74.7 us
    psum x1, waiting for transfers between devices, on_device(): lax.psum((gram_of(s_total, s_total), gram_of(s_total, h_total)), 'dom')  52.2 us
    ppermute x6, starting transfers between devices, padded_2(): lax.ppermute(lax.slice_in_dim(block, 0, width, axis=dim), axis, backward)  15.8 us
    add x6, other arithmetic, plane_terms(): summed + COEF_FAR * (jnp.roll(planes, 2, -2) + jnp.roll(planes, -2, -2) +...  10.2 us
  transfers between devices with their start and end apart: 14, of which 7 were waited for; matrix products, arithmetic and copies ran while one was open for 7% of the time, Pallas kernels for 0%

commit v1 on v0

--- a/solution.py
+++ b/solution.py
@@ -1,8 +1,12 @@
+import functools
 import math
 
 import jax
 import jax.numpy as jnp
+import numpy as np
 from jax import lax
+from jax.experimental import pallas as pl
+from jax.experimental.pallas import tpu as pltpu
 from jax.sharding import PartitionSpec as P
 
 MOMENTS = 4
@@ -121,7 +125,7 @@
     return jnp.stack([blocks[0, :, 0] + blocks[1, :, 1], blocks[0, :, 1] - blocks[1, :, 0]])
 
 
-def on_device(sources, potential, iter_counts):
+def split_grid(sources, potential, iter_counts):
     complex_src = jnp.stack([sources, jnp.zeros_like(sources)])
     angle_now = (
         2.0 * math.pi * (lax.axis_index("point").astype(jnp.float32) + 0.5) / lax.axis_size("point")
@@ -156,6 +160,323 @@
     return (gram_b / cells, gram_a / cells)
 
 
+Y_IN, X_IN = 2, 4
+Y_OUT, X_OUT = GX // Y_IN, GX // X_IN
+ROWS = Y_IN * X_IN
+LANES = Y_OUT * X_OUT
+SUB = 8
+BASIS = ITERS + 1
+
+
+def to_blocked(values):
+    split = values.reshape(values.shape[:-1] + (Y_OUT, Y_IN, X_OUT, X_IN))
+    lead = values.ndim - 1
+    order = tuple(range(lead)) + (lead + 1, lead + 3, lead, lead + 2)
+    return split.transpose(order).reshape(values.shape[:-1] + (ROWS, LANES))
+
+
+def packed_block(sources, potential):
+    count = sources.shape[0]
+    rows = to_blocked(sources).transpose(1, 2, 0, 3).reshape(-1, LANES)
+    levels = to_blocked(potential).reshape(-1, LANES)
+    return jnp.concatenate([rows, levels], axis=0)
+
+
+def lane_sum(values):
+    return jnp.broadcast_to(jnp.sum(values, axis=1, keepdims=True), values.shape)
+
+
+def ratio(top, bottom):
+    return jnp.where(bottom > 0.0, top / jnp.where(bottom > 0.0, bottom, 1.0), 0.0)
+
+
+def x_next(values, wrap_mask):
+    return jnp.where(wrap_mask, pltpu.roll(values, X_OUT - 1, 1), pltpu.roll(values, LANES - 1, 1))
+
+
+def x_prev(values, wrap_mask):
+    return jnp.where(wrap_mask, pltpu.roll(values, LANES - X_OUT + 1, 1), pltpu.roll(values, 1, 1))
+
+
+def plane_of(basis, plane, row):
+    return [basis[plane, pl.ds(row, SUB), pl.ds(m * LANES, LANES)] for m in range(ROWS)]
+
+
+def apply_plane(basis, diagonal, plane, planes, row, last_x, first_x):
+    here = plane_of(basis, plane, row)
+    above = plane_of(basis, lax.rem(plane + 1, planes), row)
+    below = plane_of(basis, lax.rem(plane + planes - 1, planes), row)
+    above_2 = plane_of(basis, lax.rem(plane + 2, planes), row)
+    below_2 = plane_of(basis, lax.rem(plane + planes - 2, planes), row)
+    y_up = [pltpu.roll(value, LANES - X_OUT, 1) for value in here]
+    y_down = [pltpu.roll(value, X_OUT, 1) for value in here]
+    out = []
+    for yi in range(Y_IN):
+        line = here[yi * X_IN : (yi + 1) * X_IN]
+        before = [x_prev(line[X_IN - 2], first_x), x_prev(line[X_IN - 1], first_x)]
+        after = [x_next(line[0], last_x), x_next(line[1], last_x)]
+        wide = before + line + after
+        for xi in range(X_IN):
+            m = yi * X_IN + xi
+            other = (1 - yi) * X_IN + xi
+            y_next = here[other] if yi == 0 else y_up[other]
+            y_prev = here[other] if yi == 1 else y_down[other]
+            near = (wide[xi + 1] + wide[xi + 3]) + (y_next + y_prev) + (above[m] + below[m])
+            far = (wide[xi] + wide[xi + 4]) + (y_up[m] + y_down[m]) + (above_2[m] + below_2[m])
+            level = diagonal[plane, pl.ds(m, 1), :]
+            out.append(level * here[m] - (0.5 * COEF_NEAR) * near - (0.5 * COEF_FAR) * far)
+    return here, out
+
+
+def cmul(first, second):
+    return (
+        first[0] * second[0] - first[1] * second[1],
+        first[0] * second[1] + first[1] * second[0],
+    )
+
+
+def weights_of(alphas, norms, limits, coeffs, shape):
+    points = len(limits)
+    count = shape[0]
+    half = MOMENTS * count
+    lane = lax.broadcasted_iota(jnp.int32, shape, 1)
+    source = lax.broadcasted_iota(jnp.int32, shape, 0)
+    own = lax.rem(lane, count) == source
+    left_half = lane < half
+    betas = [ratio(norms[i + 1], norms[i]) for i in range(ITERS - 1)]
+    sums = [[jnp.zeros(shape, jnp.float32)] * 2 for _ in range(BASIS)]
+    zero = jnp.zeros(shape, jnp.float32)
+    one = jnp.ones(shape, jnp.float32)
+    for point in range(points):
+        angle = 2.0 * math.pi * (point + 0.5) / points
+        shift = (GAMMA + RADIUS * math.cos(angle), RADIUS * math.sin(angle))
+        limit = limits[point]
+        product = (one, zero)
+        products = [product]
+        links = []
+        pivot = (shift[0] - alphas[0], zero + shift[1])
+        for i in range(ITERS):
+            size = pivot[0] * pivot[0] + pivot[1] * pivot[1]
+            inverse = (pivot[0] / size, -pivot[1] / size)
+            product = cmul(product, inverse)
+            products.append(product)
+            if i < ITERS - 1:
+                link = (betas[i] * inverse[0], betas[i] * inverse[1])
+                links.append(link)
+                pivot = (shift[0] - alphas[i + 1] - link[0], shift[1] - link[1])
+        solved = [None] * ITERS
+        for i in reversed(range(ITERS)):
+            value = products[i + 1]
+            if i < ITERS - 1:
+                step = cmul(links[i], solved[i + 1])
+                value = (value[0] + step[0], value[1] + step[1])
+            used = i < limit
+            solved[i] = (jnp.where(used, value[0], 0.0), jnp.where(used, value[1], 0.0))
+        applied = []
+        for i in range(BASIS):
+            left = limit == i
+            rest = (
+                jnp.where(left, products[i][0], 0.0),
+                jnp.where(left, products[i][1], 0.0),
+            )
+            if i < ITERS:
+                turned = (
+                    shift[0] * solved[i][0] - shift[1] * solved[i][1],
+                    shift[0] * solved[i][1] + shift[1] * solved[i][0],
+                )
+                rest = (rest[0] + turned[0], rest[1] + turned[1])
+            if i == 0:
+                rest = (rest[0] - 1.0, rest[1])
+            applied.append(rest)
+        tail = applied[ITERS]
+        for back, factor in ((1, alphas[ITERS - 1]), (2, betas[ITERS - 2])):
+            part = applied[ITERS - back]
+            applied[ITERS - back] = (part[0] - factor * tail[0], part[1] - factor * tail[1])
+        moment = (coeffs[2 * point : 2 * point + 1, :], coeffs[2 * point + 1 : 2 * point + 2, :])
+        for i in range(BASIS):
+            left = solved[i] if i < ITERS else (zero, zero)
+            both = (
+                jnp.where(left_half, left[0], applied[i][0]),
+                jnp.where(left_half, left[1], applied[i][1]),
+            )
+            term = cmul(moment, both)
+            sums[i] = [sums[i][0] + term[0], sums[i][1] + term[1]]
+    return [[jnp.where(own, part, 0.0) for part in pair] for pair in sums]
+
+
+def exact_dot(first, second, dims):
+    return lax.dot_general(
+        first,
+        second,
+        (dims, ((), ())),
+        precision=lax.Precision.HIGHEST,
+        preferred_element_type=jnp.float32,
+    )
+
+
+def solve_kernel(parts, count, planes, points, meta, coeffs, *refs):
+    blocks = refs[:parts]
+    out_b, out_a, basis, diagonal, gram = refs[parts:]
+    depth = planes // parts
+    groups = count // SUB
+    lane = lax.broadcasted_iota(jnp.int32, (SUB, LANES), 1)
+    last_x = lax.rem(lane, X_OUT) == X_OUT - 1
+    first_x = lax.rem(lane, X_OUT) == 0
+
+    for turn in range(parts):
+        slab = jnp.bitwise_xor(meta[0], turn) * depth
+        for deep in range(depth):
+            for m in range(ROWS):
+                start = (deep * ROWS + m) * count
+                basis[slab + deep, 0:count, m * LANES : (m + 1) * LANES] = blocks[turn][
+                    start : start + count, :
+                ]
+            start = depth * ROWS * count + deep * ROWS
+            diagonal[slab + deep] = blocks[turn][start : start + ROWS, :] + 3.75
+
+    blank = jnp.zeros((SUB, LANES), jnp.float32)
+    alphas, norms = [], []
+    for i in range(ITERS):
+
+        def apply_turn(plane, sums, i=i):
+            new_sums = []
+            for group in range(groups):
+                row = i * count + group * SUB
+                here, out = apply_plane(basis, diagonal, plane, planes, row, last_x, first_x)
+                curve, norm = sums[group]
+                for m in range(ROWS):
+                    basis[plane, pl.ds(row + count, SUB), pl.ds(m * LANES, LANES)] = out[m]
+                    curve = curve + here[m] * out[m]
+                    if i == 0:
+                        norm = norm + here[m] * here[m]
+                new_sums.append((curve, norm))
+            return tuple(new_sums)
+
+        sums = lax.fori_loop(0, planes, apply_turn, ((blank, blank),) * groups)
+        if i == 0:
+            norms.append([lane_sum(norm) for _, norm in sums])
+        alphas.append([ratio(lane_sum(sums[g][0]), norms[i][g]) for g in range(groups)])
+        if i == ITERS - 1:
+            break
+        betas = [ratio(norms[i][g], norms[i - 1][g]) for g in range(groups)] if i else None
+
+        def step_turn(plane, sums, i=i, betas=betas):
+            new_sums = []
+            for group in range(groups):
+                row = i * count + group * SUB
+                norm = sums[group]
+                for m in range(ROWS):
+                    lanes = pl.ds(m * LANES, LANES)
+                    value = basis[plane, pl.ds(row + count, SUB), lanes]
+                    value = value - alphas[i][group] * basis[plane, pl.ds(row, SUB), lanes]
+                    if i:
+                        value = value - betas[group] * basis[plane, pl.ds(row - count, SUB), lanes]
+                    basis[plane, pl.ds(row + count, SUB), lanes] = value
+                    norm = norm + value * value
+                new_sums.append(norm)
+            return tuple(new_sums)
+
+        sums = lax.fori_loop(0, planes, step_turn, (blank,) * groups)
+        norms.append([lane_sum(norm) for norm in sums])
+
+    size = BASIS * count
+    gram[...] = jnp.zeros_like(gram)
+
+    def gram_turn(plane, carry):
+        values = basis[plane]
+        high = values.astype(jnp.bfloat16)
+        low = (values - high.astype(jnp.float32)).astype(jnp.bfloat16)
+        gram[...] += lax.dot_general(
+            high,
+            jnp.concatenate([high, low], axis=0),
+            (((1,), (1,)), ((), ())),
+            preferred_element_type=jnp.float32,
+        )
+        return carry
+
+    lax.fori_loop(0, planes, gram_turn, 0)
+    cross = gram[:, size:]
+    pairs = gram[:, :size] + cross + cross.T
+
+    shape = (count, LANES)
+    limits = [meta[2 + jnp.bitwise_xor(meta[1], point)] for point in range(points)]
+    alphas = [jnp.concatenate(value, axis=0) for value in alphas]
+    norms = [jnp.concatenate(value, axis=0) for value in norms]
+    weights = weights_of(alphas, norms, limits, coeffs, shape)
+    real = jnp.concatenate([pair[0] for pair in weights], axis=0)
+    imag = jnp.concatenate([pair[1] for pair in weights], axis=0)
+    right = exact_dot(pairs, jnp.concatenate([real, imag], axis=1), ((1,), (0,)))
+    half = MOMENTS * count
+    left = jnp.concatenate([real[:, :half], imag[:, :half]], axis=1)
+    joined = exact_dot(left.T, right, ((1,), (0,)))
+    scale = 1.0 / (planes * ROWS * LANES)
+    width = 2 * half
+    real = (joined[:half, :width] + joined[half:, width:]) * scale
+    imag = (joined[:half, width:] - joined[half:, :width]) * scale
+    out_b[0] = real[:, :half]
+    out_b[1] = imag[:, :half]
+    out_a[0] = real[:, half:]
+    out_a[1] = imag[:, half:]
+
+
+def swapped(values, axis, size, mask):
+    return lax.ppermute(values, axis, [(i ^ mask, i) for i in range(size)])
+
+
+def whole_grid(sources, potential, iter_counts, *, parts, points):
+    count, depth, _ = sources.shape
+    planes = parts * depth
+    block = packed_block(sources, potential)
+    even = [block] + [swapped(block, "dom", parts, mask) for mask in range(2, parts, 2)]
+    odd = [swapped(value, "dom", parts, 1) for value in even]
+    blocks = [value for pair in zip(even, odd) for value in pair]
+    limits = [iter_counts] + [
+        swapped(iter_counts, "point", points, mask) for mask in range(1, points)
+    ]
+    place = jnp.stack([lax.axis_index("dom"), lax.axis_index("point")]).astype(jnp.int32)
+    meta = jnp.concatenate([place] + limits)
+    angles = 2.0 * math.pi * (np.arange(points)[:, None] + 0.5) / points
+    turns = np.tile(np.repeat(np.arange(MOMENTS) + 1.0, count), 2)[None, :] * angles
+    coeffs = 0.25 * np.stack([np.cos(turns), np.sin(turns)], axis=1).reshape(2 * points, -1)
+    vmem = pl.BlockSpec(memory_space=pltpu.VMEM)
+    smem = pl.BlockSpec(memory_space=pltpu.SMEM)
+    size = BASIS * count
+    width = MOMENTS * count
+    out = jax.ShapeDtypeStruct((2, width, width), jnp.float32)
+    return pl.pallas_call(
+        functools.partial(solve_kernel, parts, count, planes, points),
+        out_shape=(out, out),
+        in_specs=[smem, vmem] + [vmem] * parts,
+        out_specs=(vmem, vmem),
+        scratch_shapes=[
+            pltpu.VMEM((planes, size, ROWS * LANES), jnp.float32),
+            pltpu.VMEM((planes, ROWS, LANES), jnp.float32),
+            pltpu.VMEM((size, 2 * size), jnp.float32),
+        ],
+        compiler_params=pltpu.CompilerParams(vmem_limit_bytes=40 * 2**20),
+    )(meta, jnp.asarray(coeffs, jnp.float32), *blocks)
+
+
+def power_of_two(value):
+    return value > 0 and value & (value - 1) == 0
+
+
+def on_device(sources, potential, iter_counts):
+    parts, points = lax.axis_size("dom"), lax.axis_size("point")
+    count, depth, cells = sources.shape
+    held = BASIS * count * parts * depth * cells * 4
+    fits = (
+        held <= 16 * 2**20
+        and power_of_two(parts)
+        and power_of_two(points)
+        and 2 * MOMENTS * count == LANES
+        and cells == GX * GX == ROWS * LANES
+    )
+    if not fits:
+        return split_grid(sources, potential, iter_counts)
+    return whole_grid(sources, potential, iter_counts, parts=parts, points=points)
+
+
 def solution(mesh):
     placed = (P(None, "dom", None), P("dom", None), P("point"))
     return jax.shard_map(

time: 390 us -> 54.4 us (0.14)
  blocking collectives: 161 us -> 0 us
  waiting for transfers between devices: 143 us -> 12 us
  other arithmetic: 24.1 us -> 0.01 us
  Pallas kernels: 0 us -> 23.1 us
  local copies, waits for them, and re-layouts: 21.3 us -> 4.8 us
  between operations: 14.4 us -> 1.4 us
  matrix products: 4.96 us -> 0 us
  loops' own time: 4.79 us -> 0 us
    psum x13 -> x0, blocking collectives: 161 us -> none  [the longest x7 85.9 us: residual_sum(): return lax.psum(bilinear(values, values), 'dom')]
    psum x2 -> x0, waiting for transfers between devices: 139 us -> none  [the longest x1 86.7 us: on_device(): s_total, h_total = lax.psum((s_terms, h_terms), 'point')]
    pallas_call x0 -> x1, Pallas kernels: none -> 23.1 us  [whole_grid(): pl.pallas_call(functools.partial(solve_kernel, parts, count, planes, poin...]
    slice x48 -> x0, local copies, waits for them, and re-layouts: 12.4 us -> none  [the longest x12 4.49 us: plane_terms(): jnp.roll(planes, -1, -1)]
    add x21 -> x0, other arithmetic: 11.5 us -> none  [the longest x6 10.2 us: plane_terms(): summed + COEF_FAR * (jnp.roll(planes, 2, -2) + jnp.roll(planes, -2, -2) +...]
    ppermute x12 -> x10, waiting for transfers between devices: 4.2 us -> 12 us  [swapped(): return lax.ppermute(values, axis, [(i ^ mask, i) for i in range(size)])]
    dot_general x2 -> x0, matrix products: 4.96 us -> none  [gram_of(): lax.dot_general(left.reshape(2 * width, -1), right.reshape(2 * width, -1)...]
    another operation x1 -> x0, loops' own time: 4.79 us -> none  [on_device(): lax.fori_loop(0, ITERS, one_turn, start)]
  transfers between devices with their start and end apart: 14 -> 10, of which waited for: 7 -> 5; matrix products, arithmetic and copies ran while one was open for 7% -> 4% of each run, Pallas kernels for 0% -> 0%
where the time goes in v1:
time: 54.4 us; the launch traced here: 54.1 us
  Pallas kernels  23.1 us (42%)
  starting transfers between devices  12.8 us (24%)
  waiting for transfers between devices  12 us (22%)
  local copies, waits for them, and re-layouts  4.8 us (9%)
  between operations  1.4 us (3%)
    pallas_call x1, Pallas kernels, whole_grid(): pl.pallas_call(functools.partial(solve_kernel, parts, count, planes, poin...  23.1 us
    ppermute x10, starting transfers between devices, swapped(): return lax.ppermute(values, axis, [(i ^ mask, i) for i in range(size)])  12.8 us
    ppermute x10, waiting for transfers between devices, swapped(): return lax.ppermute(values, axis, [(i ^ mask, i) for i in range(size)])  12 us
    concatenate x1, local copies, waits for them, and re-layouts, whole_grid(): meta = jnp.concatenate([place] + limits)  1.9 us
    unnamed x5, local copies, waits for them, and re-layouts  1.65 us
  transfers between devices with their start and end apart: 10, of which 5 were waited for; matrix products, arithmetic and copies ran while one was open for 4% of the time, Pallas kernels for 0%

profile of v1, /device:TPU:0, one launch (start us, length us, event | category | flops | bytes accessed | tf_op | source)
XLA Modules:
  0.0 54.1 jit_solution(13992641301563142224)
XLA Ops:
  0.6 1.2 %copy.8 = f32[16,2,1024]{0,2,1:T(8,128)S(1)} copy(f32[16,2,1024]{2,1,0:T(2,128)} %param.4) | data formatting | bytes 262144 | tf_op args[0]
  1.9 0.1 copy.9
  2.0 0.0 copy-start.1
  2.0 0.3 copy.10
  2.3 0.4 copy-done.1
  2.7 0.3 reshape.19
  3.0 0.5 copy.11
  3.4 0.1 reshape_reshape.3
  3.6 3.0 %collective-permute-start.4 = (f32[272,128]{1,0:T(8,128)S(1)}, f32[272,128]{1,0:T(8,128)S(1)}, u32[]{:S(2)}, u32[]{:S(2)}) collective-permute-start(f32[272,128]{1,0:T(8,128)S(1)} %pad_maximum_fusion.refs_0_), channel_id=1, source_target_pairs={{2,0},{3,1},{0,2},{1,3},{6,4},{7,5},{4,6},{5,7},{10,8},{11,9},{8,1... | collective-permute-start | bytes 417800 | tf_op jit(solution)/shard_map/ppermute | solution.py:423
  6.6 1.5 %collective-permute-start.6 = (f32[272,128]{1,0:T(8,128)S(1)}, f32[272,128]{1,0:T(8,128)S(1)}, u32[]{:S(2)}, u32[]{:S(2)}) collective-permute-start(f32[272,128]{1,0:T(8,128)S(1)} %pad_maximum_fusion.refs_0_), channel_id=1, source_target_pairs={{4,0},{5,1},{6,2},{7,3},{0,4},{1,5},{2,6},{3,7},{12,8},{13,9},{14,... | collective-permute-start | bytes 417800 | tf_op jit(solution)/shard_map/ppermute | solution.py:423
  8.1 0.0 collective-permute-start.8
  8.1 0.0 collective-permute-start.3
  8.1 2.5 %collective-permute-done.4.refs_2_ = f32[272,128]{1,0:T(8,128)S(1)} collective-permute-done((f32[272,128]{1,0:T(8,128)S(1)}, f32[272,128]{1,0:T(8,128)S(1)}, u32[]{:S(2)}, u32[]{:S(2)}) %collective-permute-start.4) | collective-permute-done | bytes 139296 | tf_op jit(solution)/shard_map/ppermute | solution.py:423
  10.7 0.0 collective-permute-start.5
  10.7 4.0 %collective-permute-done.6.refs_4_ = f32[272,128]{1,0:T(8,128)S(1)} collective-permute-done((f32[272,128]{1,0:T(8,128)S(1)}, f32[272,128]{1,0:T(8,128)S(1)}, u32[]{:S(2)}, u32[]{:S(2)}) %collective-permute-start.6) | collective-permute-done | bytes 139296 | tf_op jit(solution)/shard_map/ppermute | solution.py:423
  14.7 0.0 collective-permute-start.7
  14.7 0.0 collective-permute-done.8.refs_6_
  14.7 0.5 collective-permute-start.9
  15.2 1.6 %collective-permute-start = (s32[1]{0:T(128)}, s32[1]{0:T(128)}, u32[]{:S(2)}, u32[]{:S(2)}) collective-permute-start(s32[1]{0:T(128)} %param.6), channel_id=1, source_target_pairs={{8,0},{0,8},{24,16},{16,24},{9,1},{1,9},{25,17},{17,25},{10,2},{2,... | collective-permute-start | bytes 20 | tf_op jit(solution)/shard_map/ppermute | solution.py:423
  17.5 0.0 copy-start
  17.5 1.4 %collective-permute-done = s32[1]{0:T(128)} collective-permute-done((s32[1]{0:T(128)}, s32[1]{0:T(128)}, u32[]{:S(2)}, u32[]{:S(2)}) %collective-permute-start) | collective-permute-done | bytes 36 | tf_op jit(solution)/shard_map/ppermute | solution.py:423
  18.9 2.6 %collective-permute-start.1 = (s32[1]{0:T(128)}, s32[1]{0:T(128)}, u32[]{:S(2)}, u32[]{:S(2)}) collective-permute-start(s32[1]{0:T(128)} %param.6), channel_id=1, source_target_pairs={{16,0},{24,8},{0,16},{8,24},{17,1},{25,9},{1,17},{9,25},{18,2},{26... | collective-permute-start | bytes 20 | tf_op jit(solution)/shard_map/ppermute | solution.py:423
  21.4 2.1 %collective-permute-done.1 = s32[1]{0:T(128)} collective-permute-done((s32[1]{0:T(128)}, s32[1]{0:T(128)}, u32[]{:S(2)}, u32[]{:S(2)}) %collective-permute-start.1) | collective-permute-done | bytes 36 | tf_op jit(solution)/shard_map/ppermute | solution.py:423
  23.5 3.6 %collective-permute-start.2 = (s32[1]{0:T(128)}, s32[1]{0:T(128)}, u32[]{:S(2)}, u32[]{:S(2)}) collective-permute-start(s32[1]{0:T(128)} %param.6), channel_id=1, source_target_pairs={{24,0},{16,8},{8,16},{0,24},{25,1},{17,9},{9,17},{1,25},{26,2},{18... | collective-permute-start | bytes 20 | tf_op jit(solution)/shard_map/ppermute | solution.py:423
  27.1 2.0 %collective-permute-done.2 = s32[1]{0:T(128)} collective-permute-done((s32[1]{0:T(128)}, s32[1]{0:T(128)}, u32[]{:S(2)}, u32[]{:S(2)}) %collective-permute-start.2) | collective-permute-done | bytes 36 | tf_op jit(solution)/shard_map/ppermute | solution.py:423
  29.1 1.9 %concatenate.6.meta = s32[6]{0:T(128)S(1)} concatenate(s32[1]{0:T(128)} %bitcast, s32[1]{0:T(128)} %bitcast.1, s32[1]{0:T(128)S(6)} %copy.12, s32[1]{0:T(128)} %collective-permute-done, s32[1]{0:T(128)} %collective-permute-done.1, s32[1]{0:T(128)} %collective-permute-done.2), dimensions={0} | concatenate | bytes 48 | tf_op jit(solution)/shard_map/concatenate | solution.py:437
  31.0 0.0 collective-permute-done.3.refs_1_
  31.0 0.0 collective-permute-done.5.refs_3_
  31.0 0.0 collective-permute-done.7.refs_5_
  31.0 0.0 collective-permute-done.9.refs_7_
  31.0 0.0 copy-done
  31.0 23.1 %shard_map.59 = (f32[2,64,64]{2,1,0:T(8,128)}, f32[2,64,64]{2,1,0:T(8,128)}) custom-call(s32[6]{0:T(128)S(1)} %concatenate.6.meta, f32[8,128]{1,0:T(8,128)S(1)} %copy-done, f32[272,128]{1,0:T(8,128)S(1)} %pad_maximum_fusion.refs_0_, f32[272,128]{1,0:T(8,128)S(1)} %collective-permute-done.3.refs_1_, f32[272,128]{1,0:T(8,128)S(1)} %collective-permute-done.4.refs_2_, ...), custom_call_target="tpu_custom_call" | custom-call | tf_op jit(solution)/shard_map/pallas_call | solution.py:446
  (1 shorter events, 0.0 us)
Async XLA Ops:
  2.0 0.7 %copy-start.1 = (f32[2,1024]{1,0:T(2,128)S(1)}, f32[2,1024]{1,0:T(2,128)}, u32[]{:S(2)}) copy-start(f32[2,1024]{1,0:T(2,128)} %param.5) | copy-start | bytes 24580
  3.6 7.1 %collective-permute-start.4 = (f32[272,128]{1,0:T(8,128)S(1)}, f32[272,128]{1,0:T(8,128)S(1)}, u32[]{:S(2)}, u32[]{:S(2)}) collective-permute-start(f32[272,128]{1,0:T(8,128)S(1)} %pad_maximum_fusion.refs_0_), channel_id=1, source_target_pairs={{2,0},{3,1},{0,2},{1,3},{6,4},{7,5},{4,6},{5,7},{10,8},{11,9},{8,1... | collective-permute-start | bytes 417800 | tf_op jit(solution)/shard_map/ppermute | solution.py:423
  6.6 8.1 %collective-permute-start.6 = (f32[272,128]{1,0:T(8,128)S(1)}, f32[272,128]{1,0:T(8,128)S(1)}, u32[]{:S(2)}, u32[]{:S(2)}) collective-permute-start(f32[272,128]{1,0:T(8,128)S(1)} %pad_maximum_fusion.refs_0_), channel_id=1, source_target_pairs={{4,0},{5,1},{6,2},{7,3},{0,4},{1,5},{2,6},{3,7},{12,8},{13,9},{14,... | collective-permute-start | bytes 417800 | tf_op jit(solution)/shard_map/ppermute | solution.py:423
  8.1 6.6 %collective-permute-start.8 = (f32[272,128]{1,0:T(8,128)S(1)}, f32[272,128]{1,0:T(8,128)S(1)}, u32[]{:S(2)}, u32[]{:S(2)}) collective-permute-start(f32[272,128]{1,0:T(8,128)S(1)} %pad_maximum_fusion.refs_0_), channel_id=1, source_target_pairs={{6,0},{7,1},{4,2},{5,3},{2,4},{3,5},{0,6},{1,7},{14,8},{15,9},{12,... | collective-permute-start | bytes 417800 | tf_op jit(solution)/shard_map/ppermute | solution.py:423
  8.1 22.9 %collective-permute-start.3 = (f32[272,128]{1,0:T(8,128)S(1)}, f32[272,128]{1,0:T(8,128)S(1)}, u32[]{:S(2)}, u32[]{:S(2)}) collective-permute-start(f32[272,128]{1,0:T(8,128)S(1)} %pad_maximum_fusion.refs_0_), channel_id=1, source_target_pairs={{1,0},{0,1},{3,2},{2,3},{5,4},{4,5},{7,6},{6,7},{9,8},{8,9},{11,10... | collective-permute-start | bytes 417800 | tf_op jit(solution)/shard_map/ppermute | solution.py:423
  10.7 20.3 %collective-permute-start.5 = (f32[272,128]{1,0:T(8,128)S(1)}, f32[272,128]{1,0:T(8,128)S(1)}, u32[]{:S(2)}, u32[]{:S(2)}) collective-permute-start(f32[272,128]{1,0:T(8,128)S(1)} %collective-permute-done.4.refs_2_), channel_id=1, source_target_pairs={{1,0},{0,1},{3,2},{2,3},{5,4},{4,5},{7,6},{6,7},{9,8},{8,9},{11,10... | collective-permute-start | bytes 417800 | tf_op jit(solution)/shard_map/ppermute | solution.py:423
  14.7 16.3 %collective-permute-start.7 = (f32[272,128]{1,0:T(8,128)S(1)}, f32[272,128]{1,0:T(8,128)S(1)}, u32[]{:S(2)}, u32[]{:S(2)}) collective-permute-start(f32[272,128]{1,0:T(8,128)S(1)} %collective-permute-done.6.refs_4_), channel_id=1, source_target_pairs={{1,0},{0,1},{3,2},{2,3},{5,4},{4,5},{7,6},{6,7},{9,8},{8,9},{11,10... | collective-permute-start | bytes 417800 | tf_op jit(solution)/shard_map/ppermute | solution.py:423
  14.7 16.3 %collective-permute-start.9 = (f32[272,128]{1,0:T(8,128)S(1)}, f32[272,128]{1,0:T(8,128)S(1)}, u32[]{:S(2)}, u32[]{:S(2)}) collective-permute-start(f32[272,128]{1,0:T(8,128)S(1)} %collective-permute-done.8.refs_6_), channel_id=1, source_target_pairs={{1,0},{0,1},{3,2},{2,3},{5,4},{4,5},{7,6},{6,7},{9,8},{8,9},{11,10... | collective-permute-start | bytes 417800 | tf_op jit(solution)/shard_map/ppermute | solution.py:423
  15.2 3.6 %collective-permute-start = (s32[1]{0:T(128)}, s32[1]{0:T(128)}, u32[]{:S(2)}, u32[]{:S(2)}) collective-permute-start(s32[1]{0:T(128)} %param.6), channel_id=1, source_target_pairs={{8,0},{0,8},{24,16},{16,24},{9,1},{1,9},{25,17},{17,25},{10,2},{2,... | collective-permute-start | bytes 20 | tf_op jit(solution)/shard_map/ppermute | solution.py:423
  17.5 13.5 %copy-start = (f32[8,128]{1,0:T(8,128)S(1)}, f32[8,128]{1,0:T(8,128)}, u32[]{:S(2)}) copy-start(f32[8,128]{1,0:T(8,128)} %constant.10.clone.coeffs) | copy-start | bytes 12292
  18.9 4.7 %collective-permute-start.1 = (s32[1]{0:T(128)}, s32[1]{0:T(128)}, u32[]{:S(2)}, u32[]{:S(2)}) collective-permute-start(s32[1]{0:T(128)} %param.6), channel_id=1, source_target_pairs={{16,0},{24,8},{0,16},{8,24},{17,1},{25,9},{1,17},{9,25},{18,2},{26... | collective-permute-start | bytes 20 | tf_op jit(solution)/shard_map/ppermute | solution.py:423
  23.5 5.6 %collective-permute-start.2 = (s32[1]{0:T(128)}, s32[1]{0:T(128)}, u32[]{:S(2)}, u32[]{:S(2)}) collective-permute-start(s32[1]{0:T(128)} %param.6), channel_id=1, source_target_pairs={{24,0},{16,8},{8,16},{0,24},{25,1},{17,9},{9,17},{1,25},{26,2},{18... | collective-permute-start | bytes 20 | tf_op jit(solution)/shard_map/ppermute | solution.py:423

commit v2 on v1

--- a/solution.py
+++ b/solution.py
@@ -168,18 +168,69 @@
 BASIS = ITERS + 1
 
 
-def to_blocked(values):
-    split = values.reshape(values.shape[:-1] + (Y_OUT, Y_IN, X_OUT, X_IN))
-    lead = values.ndim - 1
-    order = tuple(range(lead)) + (lead + 1, lead + 3, lead, lead + 2)
-    return split.transpose(order).reshape(values.shape[:-1] + (ROWS, LANES))
-
-
-def packed_block(sources, potential):
-    count = sources.shape[0]
-    rows = to_blocked(sources).transpose(1, 2, 0, 3).reshape(-1, LANES)
-    levels = to_blocked(potential).reshape(-1, LANES)
-    return jnp.concatenate([rows, levels], axis=0)
+def pack_kernel(depth, groups, counts, rows, levels, *refs):
+    outs = refs
+    columns = rows.shape[0] // (SUB * groups * depth)
+    source = lax.broadcasted_iota(jnp.int32, (LANES, LANES), 0)
+    target = lax.broadcasted_iota(jnp.int32, (LANES, LANES), 1)
+    inner = target // (LANES // ROWS)
+    outer = target % (LANES // ROWS)
+    cell = (outer // X_OUT * Y_IN + inner // X_IN) * GX + outer % X_OUT * X_IN + inner % X_IN
+    swap = jnp.where(source == cell, 1.0, 0.0).astype(jnp.float32)
+    parts = []
+    for deep in range(depth):
+        for group in range(groups):
+            for column in range(columns):
+                start = (group * SUB * columns + column) * depth + deep
+                parts.append(rows[pl.ds(start, SUB, stride=columns * depth), :])
+        parts.append(levels[pl.ds(deep, columns, stride=depth), :])
+    mixed = exact_dot(jnp.concatenate(parts, axis=0), swap, ((1,), (0,)))
+    block = LANES // ROWS
+    lane_block = lax.broadcasted_iota(jnp.int32, (SUB, LANES), 1) // block
+    row = lax.broadcasted_iota(jnp.int32, (SUB, LANES), 0)
+    for deep in range(depth):
+        base = deep * (groups + 1) * columns * SUB - deep * (columns - 1) * SUB
+        for group in range(groups):
+            pieces = [
+                mixed[base + (group * columns + column) * SUB :][:SUB] for column in range(columns)
+            ]
+            for m in range(ROWS):
+                value = pieces[m]
+                for column in range(columns):
+                    if column != m:
+                        moved = pltpu.roll(pieces[column], (column - m) * block % LANES, 1)
+                        value = jnp.where(lane_block == column, moved, value)
+                start = (deep * ROWS + m) * SUB
+                outs[group][start : start + SUB, :] = value
+        piece = mixed[base + groups * columns * SUB :][:SUB]
+        value = piece
+        for far in range(1, columns):
+            moved = pltpu.roll(pltpu.roll(piece, far * block, 1), columns - far, 0)
+            value = jnp.where(lane_block == (row + far) % columns, moved, value)
+        start = depth * ROWS * SUB + deep * ROWS
+        outs[0][start : start + ROWS, :] = value
+    count = jnp.full((SUB, LANES), counts[0].astype(jnp.float32))
+    for out in outs:
+        out[out.shape[0] - SUB :, :] = count
+
+
+def packed_blocks(sources, potential, iter_counts):
+    count, depth, cells = sources.shape
+    columns = cells // LANES
+    rows = sources.reshape(count, depth, columns, LANES).transpose(0, 2, 1, 3)
+    levels = potential.reshape(depth, columns, LANES).transpose(1, 0, 2)
+    vmem = pl.BlockSpec(memory_space=pltpu.VMEM)
+    smem = pl.BlockSpec(memory_space=pltpu.SMEM)
+    groups = count // SUB
+    size = depth * ROWS * SUB + SUB
+    sizes = [size + depth * ROWS] + [size] * (groups - 1)
+    return pl.pallas_call(
+        functools.partial(pack_kernel, depth, groups),
+        out_shape=[jax.ShapeDtypeStruct((rows_out, LANES), jnp.float32) for rows_out in sizes],
+        in_specs=[smem, vmem, vmem],
+        out_specs=[vmem] * groups,
+        name="pack",
+    )(iter_counts, rows.reshape(-1, LANES), levels.reshape(-1, LANES))
 
 
 def lane_sum(values):
@@ -235,13 +286,14 @@
     )
 
 
-def weights_of(alphas, norms, limits, coeffs, shape):
+def weights_of(alphas, norms, limits, coeffs, group, groups):
     points = len(limits)
-    count = shape[0]
+    shape = (SUB, LANES)
+    count = groups * SUB
     half = MOMENTS * count
     lane = lax.broadcasted_iota(jnp.int32, shape, 1)
     source = lax.broadcasted_iota(jnp.int32, shape, 0)
-    own = lax.rem(lane, count) == source
+    own = lax.rem(lane, count) == source + group * SUB
     left_half = lane < half
     betas = [ratio(norms[i + 1], norms[i]) for i in range(ITERS - 1)]
     sums = [[jnp.zeros(shape, jnp.float32)] * 2 for _ in range(BASIS)]
@@ -270,7 +322,7 @@
             if i < ITERS - 1:
                 step = cmul(links[i], solved[i + 1])
                 value = (value[0] + step[0], value[1] + step[1])
-            used = i < limit
+            used = limit > i
             solved[i] = (jnp.where(used, value[0], 0.0), jnp.where(used, value[1], 0.0))
         applied = []
         for i in range(BASIS):
@@ -314,76 +366,82 @@
     )
 
 
-def solve_kernel(parts, count, planes, points, meta, coeffs, *refs):
-    blocks = refs[:parts]
-    out_b, out_a, basis, diagonal, gram = refs[parts:]
+def krylov(blocks, basis, diagonal, fill_diagonal):
+    parts, planes = len(blocks), basis.shape[0]
     depth = planes // parts
-    groups = count // SUB
     lane = lax.broadcasted_iota(jnp.int32, (SUB, LANES), 1)
     last_x = lax.rem(lane, X_OUT) == X_OUT - 1
     first_x = lax.rem(lane, X_OUT) == 0
-
+    here = lax.axis_index("dom")
     for turn in range(parts):
-        slab = jnp.bitwise_xor(meta[0], turn) * depth
+        slab = jnp.bitwise_xor(here, turn) * depth
         for deep in range(depth):
             for m in range(ROWS):
-                start = (deep * ROWS + m) * count
-                basis[slab + deep, 0:count, m * LANES : (m + 1) * LANES] = blocks[turn][
-                    start : start + count, :
+                start = (deep * ROWS + m) * SUB
+                basis[slab + deep, 0:SUB, m * LANES : (m + 1) * LANES] = blocks[turn][
+                    start : start + SUB, :
                 ]
-            start = depth * ROWS * count + deep * ROWS
-            diagonal[slab + deep] = blocks[turn][start : start + ROWS, :] + 3.75
+            if fill_diagonal:
+                start = depth * ROWS * SUB + deep * ROWS
+                diagonal[slab + deep] = blocks[turn][start : start + ROWS, :] + 3.75
 
     blank = jnp.zeros((SUB, LANES), jnp.float32)
     alphas, norms = [], []
     for i in range(ITERS):
-
-        def apply_turn(plane, sums, i=i):
-            new_sums = []
-            for group in range(groups):
-                row = i * count + group * SUB
-                here, out = apply_plane(basis, diagonal, plane, planes, row, last_x, first_x)
-                curve, norm = sums[group]
-                for m in range(ROWS):
-                    basis[plane, pl.ds(row + count, SUB), pl.ds(m * LANES, LANES)] = out[m]
-                    curve = curve + here[m] * out[m]
-                    if i == 0:
-                        norm = norm + here[m] * here[m]
-                new_sums.append((curve, norm))
-            return tuple(new_sums)
-
-        sums = lax.fori_loop(0, planes, apply_turn, ((blank, blank),) * groups)
+        row = i * SUB
+
+        def apply_turn(plane, sums, i=i, row=row):
+            curve, norm = sums
+            here, out = apply_plane(basis, diagonal, plane, planes, row, last_x, first_x)
+            for m in range(ROWS):
+                basis[plane, pl.ds(row + SUB, SUB), pl.ds(m * LANES, LANES)] = out[m]
+                curve = curve + here[m] * out[m]
+                if i == 0:
+                    norm = norm + here[m] * here[m]
+            return curve, norm
+
+        curve, norm = lax.fori_loop(0, planes, apply_turn, (blank, blank), unroll=2)
         if i == 0:
-            norms.append([lane_sum(norm) for _, norm in sums])
-        alphas.append([ratio(lane_sum(sums[g][0]), norms[i][g]) for g in range(groups)])
+            norms.append(lane_sum(norm))
+        alphas.append(ratio(lane_sum(curve), norms[i]))
         if i == ITERS - 1:
             break
-        betas = [ratio(norms[i][g], norms[i - 1][g]) for g in range(groups)] if i else None
-
-        def step_turn(plane, sums, i=i, betas=betas):
-            new_sums = []
-            for group in range(groups):
-                row = i * count + group * SUB
-                norm = sums[group]
-                for m in range(ROWS):
-                    lanes = pl.ds(m * LANES, LANES)
-                    value = basis[plane, pl.ds(row + count, SUB), lanes]
-                    value = value - alphas[i][group] * basis[plane, pl.ds(row, SUB), lanes]
-                    if i:
-                        value = value - betas[group] * basis[plane, pl.ds(row - count, SUB), lanes]
-                    basis[plane, pl.ds(row + count, SUB), lanes] = value
-                    norm = norm + value * value
-                new_sums.append(norm)
-            return tuple(new_sums)
-
-        sums = lax.fori_loop(0, planes, step_turn, (blank,) * groups)
-        norms.append([lane_sum(norm) for norm in sums])
-
-    size = BASIS * count
+        beta = ratio(norms[i], norms[i - 1]) if i else None
+
+        def step_turn(plane, norm, i=i, row=row, alpha=alphas[i], beta=beta):
+            for m in range(ROWS):
+                lanes = pl.ds(m * LANES, LANES)
+                value = basis[plane, pl.ds(row + SUB, SUB), lanes]
+                value = value - alpha * basis[plane, pl.ds(row, SUB), lanes]
+                if i:
+                    value = value - beta * basis[plane, pl.ds(row - SUB, SUB), lanes]
+                basis[plane, pl.ds(row + SUB, SUB), lanes] = value
+                norm = norm + value * value
+            return norm
+
+        norms.append(lane_sum(lax.fori_loop(0, planes, step_turn, blank, unroll=4)))
+    return alphas, norms
+
+
+def first_kernel(*refs):
+    blocks, (basis, diagonal, scalars) = refs[:-3], refs[-3:]
+    alphas, norms = krylov(blocks, basis, diagonal, True)
+    for i, value in enumerate(alphas + norms):
+        scalars[i] = value
+
+
+def second_kernel(groups, points, masks, counts, coeffs, *refs):
+    first = refs[: 3 * (groups - 1)]
+    out_b, out_a, basis, gram, limits = refs[-5:]
+    tails, blocks = refs[len(first) : len(first) + points - 1], refs[len(first) + points - 1 : -5]
+    planes = basis.shape[0]
+    alphas, norms = krylov(blocks, basis, first[1], False)
+    bases = [first[3 * g] for g in range(groups - 1)] + [basis]
+    size = BASIS * SUB * groups
     gram[...] = jnp.zeros_like(gram)
 
     def gram_turn(plane, carry):
-        values = basis[plane]
+        values = jnp.concatenate([part[plane] for part in bases], axis=0)
         high = values.astype(jnp.bfloat16)
         low = (values - high.astype(jnp.float32)).astype(jnp.bfloat16)
         gram[...] += lax.dot_general(
@@ -398,15 +456,24 @@
     cross = gram[:, size:]
     pairs = gram[:, :size] + cross + cross.T
 
-    shape = (count, LANES)
-    limits = [meta[2 + jnp.bitwise_xor(meta[1], point)] for point in range(points)]
-    alphas = [jnp.concatenate(value, axis=0) for value in alphas]
-    norms = [jnp.concatenate(value, axis=0) for value in norms]
-    weights = weights_of(alphas, norms, limits, coeffs, shape)
-    real = jnp.concatenate([pair[0] for pair in weights], axis=0)
-    imag = jnp.concatenate([pair[1] for pair in weights], axis=0)
+    here = lax.axis_index("point")
+    limits[here] = jnp.full((SUB, LANES), counts[0].astype(jnp.float32))
+    for mask, tail in zip(masks, tails):
+        limits[jnp.bitwise_xor(here, mask)] = tail[tail.shape[0] - SUB :, :]
+    reals, imags = [], []
+    for group in range(groups):
+        if group < groups - 1:
+            scalars = first[3 * group + 2]
+            alpha = [scalars[i] for i in range(ITERS)]
+            norm = [scalars[ITERS + i] for i in range(ITERS)]
+        else:
+            alpha, norm = alphas, norms
+        weights = weights_of(alpha, norm, [limits[j] for j in range(points)], coeffs, group, groups)
+        reals += [pair[0] for pair in weights]
+        imags += [pair[1] for pair in weights]
+    real, imag = jnp.concatenate(reals, axis=0), jnp.concatenate(imags, axis=0)
     right = exact_dot(pairs, jnp.concatenate([real, imag], axis=1), ((1,), (0,)))
-    half = MOMENTS * count
+    half = MOMENTS * SUB * groups
     left = jnp.concatenate([real[:, :half], imag[:, :half]], axis=1)
     joined = exact_dot(left.T, right, ((1,), (0,)))
     scale = 1.0 / (planes * ROWS * LANES)
@@ -419,46 +486,72 @@
     out_a[1] = imag[:, half:]
 
 
-def swapped(values, axis, size, mask):
-    return lax.ppermute(values, axis, [(i ^ mask, i) for i in range(size)])
+def exchanged(values, mask, other, parts, points):
+    pairs = [
+        ((point ^ other) * parts + (part ^ mask), point * parts + part)
+        for point in range(points)
+        for part in range(parts)
+    ]
+    return lax.ppermute(values, ("point", "dom"), pairs)
 
 
 def whole_grid(sources, potential, iter_counts, *, parts, points):
     count, depth, _ = sources.shape
     planes = parts * depth
-    block = packed_block(sources, potential)
-    even = [block] + [swapped(block, "dom", parts, mask) for mask in range(2, parts, 2)]
-    odd = [swapped(value, "dom", parts, 1) for value in even]
-    blocks = [value for pair in zip(even, odd) for value in pair]
-    limits = [iter_counts] + [
-        swapped(iter_counts, "point", points, mask) for mask in range(1, points)
-    ]
-    place = jnp.stack([lax.axis_index("dom"), lax.axis_index("point")]).astype(jnp.int32)
-    meta = jnp.concatenate([place] + limits)
+    groups = count // SUB
+    packed = packed_blocks(sources, potential, iter_counts)
+    crossing = {(0, 2): 1, (0, 4): 2, (1, 6): 3}
+    masks, tails, arrived = [], [], []
+    for group in range(groups):
+        even = [packed[group]]
+        for mask in range(2, parts, 2):
+            other = crossing.get((group, mask), 0)
+            even.append(exchanged(packed[group], mask, other, parts, points))
+            if other:
+                masks.append(other)
+                tails.append(even[-1])
+        odd = [exchanged(value, 1, 0, parts, points) for value in even]
+        arrived.append([value for pair in zip(even, odd) for value in pair])
     angles = 2.0 * math.pi * (np.arange(points)[:, None] + 0.5) / points
     turns = np.tile(np.repeat(np.arange(MOMENTS) + 1.0, count), 2)[None, :] * angles
     coeffs = 0.25 * np.stack([np.cos(turns), np.sin(turns)], axis=1).reshape(2 * points, -1)
     vmem = pl.BlockSpec(memory_space=pltpu.VMEM)
     smem = pl.BlockSpec(memory_space=pltpu.SMEM)
+    cells = planes * ROWS * LANES
+    cost = pl.CostEstimate(
+        flops=ITERS * SUB * cells * 30, bytes_accessed=16 * 2**20, transcendentals=0
+    )
+    basis_shape = (planes, BASIS * SUB, ROWS * LANES)
+    first = pl.pallas_call(
+        first_kernel,
+        out_shape=(
+            jax.ShapeDtypeStruct(basis_shape, jnp.float32),
+            jax.ShapeDtypeStruct((planes, ROWS, LANES), jnp.float32),
+            jax.ShapeDtypeStruct((2 * ITERS, SUB, LANES), jnp.float32),
+        ),
+        in_specs=[vmem] * parts,
+        out_specs=(vmem,) * 3,
+        compiler_params=pltpu.CompilerParams(vmem_limit_bytes=16 * 2**20),
+        cost_estimate=cost,
+        name="first_group",
+    )(*arrived[0])
     size = BASIS * count
     width = MOMENTS * count
     out = jax.ShapeDtypeStruct((2, width, width), jnp.float32)
     return pl.pallas_call(
-        functools.partial(solve_kernel, parts, count, planes, points),
+        functools.partial(second_kernel, groups, points, masks),
         out_shape=(out, out),
-        in_specs=[smem, vmem] + [vmem] * parts,
+        in_specs=[smem, vmem] + [vmem] * (3 + len(tails) + parts),
         out_specs=(vmem, vmem),
         scratch_shapes=[
-            pltpu.VMEM((planes, size, ROWS * LANES), jnp.float32),
-            pltpu.VMEM((planes, ROWS, LANES), jnp.float32),
+            pltpu.VMEM(basis_shape, jnp.float32),
             pltpu.VMEM((size, 2 * size), jnp.float32),
+            pltpu.VMEM((points, SUB, LANES), jnp.float32),
         ],
-        compiler_params=pltpu.CompilerParams(vmem_limit_bytes=40 * 2**20),
-    )(meta, jnp.asarray(coeffs, jnp.float32), *blocks)
-
-
-def power_of_two(value):
-    return value > 0 and value & (value - 1) == 0
+        compiler_params=pltpu.CompilerParams(vmem_limit_bytes=24 * 2**20),
+        cost_estimate=cost,
+        name="second_group",
+    )(iter_counts, jnp.asarray(coeffs, jnp.float32), *first, *tails, *arrived[1])
 
 
 def on_device(sources, potential, iter_counts):
@@ -467,8 +560,9 @@
     held = BASIS * count * parts * depth * cells * 4
     fits = (
         held <= 16 * 2**20
-        and power_of_two(parts)
-        and power_of_two(points)
+        and parts == 8
+        and points == 4
+        and count == 2 * SUB
         and 2 * MOMENTS * count == LANES
         and cells == GX * GX == ROWS * LANES
     )

time: 54.4 us -> 52.3 us (0.961)
  waiting for transfers between devices: 12 us -> 7.85 us
  Pallas kernels: 23.1 us -> 25.7 us
  local copies, waits for them, and re-layouts: 4.8 us -> 2.45 us
  starting transfers between devices: 12.8 us -> 14.7 us
    ppermute x10 -> x14, waiting for transfers between devices: 12 us -> 7.85 us  [exchanged(): return lax.ppermute(values, ('point', 'dom'), pairs)]
    pallas_call x1 -> x3, Pallas kernels: 23.1 us -> 25.7 us  [the longest x1 15 us: whole_grid(): pl.pallas_call(functools.partial(second_kernel, groups, points, masks), o...]
    concatenate x1 -> x0, local copies, waits for them, and re-layouts: 1.9 us -> none  [whole_grid(): meta = jnp.concatenate([place] + limits)]
    ppermute x10 -> x14, starting transfers between devices: 12.8 us -> 14.7 us  [exchanged(): return lax.ppermute(values, ('point', 'dom'), pairs)]
    transpose x3 -> x0, local copies, waits for them, and re-layouts: 0.88 us -> none  [the longest x2 0.58 us: to_blocked(): return split.transpose(order).reshape(values.shape[:-1] + (ROWS, LANES))]
    unnamed x5 -> x6, local copies, waits for them, and re-layouts: 1.65 us -> 2.45 us
  transfers between devices with their start and end apart: 10 -> 14, of which waited for: 5 -> 2; matrix products, arithmetic and copies ran while one was open for 4% -> 0% of each run, Pallas kernels for 0% -> 17%
where the time goes in v2:
time: 52.3 us; the launch traced here: 52 us
  Pallas kernels  25.7 us (49%)
  starting transfers between devices  14.7 us (28%)
  waiting for transfers between devices  7.85 us (15%)
  local copies, waits for them, and re-layouts  2.45 us (5%)
  between operations  1.32 us (3%)
    pallas_call x1, Pallas kernels, whole_grid(): pl.pallas_call(functools.partial(second_kernel, groups, points, masks), o...  15 us
    ppermute x14, starting transfers between devices, exchanged(): return lax.ppermute(values, ('point', 'dom'), pairs)  14.7 us
    pallas_call x1, Pallas kernels, whole_grid(): pl.pallas_call(first_kernel, out_shape=(jax.ShapeDtypeStruct(basis_shape,...  8.58 us
    ppermute x14, waiting for transfers between devices, exchanged(): return lax.ppermute(values, ('point', 'dom'), pairs)  7.85 us
    unnamed x6, local copies, waits for them, and re-layouts  2.45 us
    pallas_call x1, Pallas kernels, packed_blocks(): pl.pallas_call(functools.partial(pack_kernel, depth, groups), out_shape=[...  2.13 us
  transfers between devices with their start and end apart: 14, of which 2 were waited for; matrix products, arithmetic and copies ran while one was open for 0% of the time, Pallas kernels for 17%

profile of v2, /device:TPU:0, one launch (start us, length us, event | category | flops | bytes accessed | tf_op | source)
XLA Modules:
  0.0 52.0 jit_solution(16729720677648119942)
XLA Ops:
  1.3 2.1 %pack.1 = (f32[152,128]{1,0:T(8,128)}, f32[136,128]{1,0:T(8,128)}) custom-call(s32[1]{0:T(128)S(6)} %copy.8.counts, f32[256,128]{1,0:T(8,128)} %bitcast.10, f32[16,128]{1,0:T(8,128)} %bitcast.11), custom_call_target="tpu_custom_call" | custom-call | tf_op jit(solution)/shard_map/pack/pallas_call | solution.py:227
  3.4 4.0 %collective-permute-start.1 = (f32[152,128]{1,0:T(8,128)}, f32[152,128]{1,0:T(8,128)S(1)}, u32[]{:S(2)}, u32[]{:S(2)}) collective-permute-start(f32[152,128]{1,0:T(8,128)} %get-tuple-element.7.refs_0_), channel_id=1, source_target_pairs={{10,0},{11,1},{8,2},{9,3},{14,4},{15,5},{12,6},{13,7},{2,8},{3,9},... | collective-permute-start | bytes 233480 | tf_op jit(solution)/shard_map/ppermute | solution.py:495
  7.4 3.5 %collective-permute-start.3 = (f32[152,128]{1,0:T(8,128)}, f32[152,128]{1,0:T(8,128)S(1)}, u32[]{:S(2)}, u32[]{:S(2)}) collective-permute-start(f32[152,128]{1,0:T(8,128)} %get-tuple-element.7.refs_0_), channel_id=1, source_target_pairs={{20,0},{21,1},{22,2},{23,3},{16,4},{17,5},{18,6},{19,7},{28,8},{29... | collective-permute-start | bytes 233480 | tf_op jit(solution)/shard_map/ppermute | solution.py:495
  10.9 0.5 %collective-permute-start.9 = (f32[136,128]{1,0:T(8,128)}, f32[136,128]{1,0:T(8,128)S(1)}, u32[]{:S(2)}, u32[]{:S(2)}) collective-permute-start(f32[136,128]{1,0:T(8,128)} %get-tuple-element.11.refs_6_), channel_id=1, source_target_pairs={{2,0},{3,1},{0,2},{1,3},{6,4},{7,5},{4,6},{5,7},{10,8},{11,9},{8,1... | collective-permute-start | bytes 208904 | tf_op jit(solution)/shard_map/ppermute | solution.py:495
  11.4 0.5 collective-permute-start.11
  12.0 2.4 %collective-permute-start.5 = (f32[152,128]{1,0:T(8,128)}, f32[152,128]{1,0:T(8,128)S(1)}, u32[]{:S(2)}, u32[]{:S(2)}) collective-permute-start(f32[152,128]{1,0:T(8,128)} %get-tuple-element.7.refs_0_), channel_id=1, source_target_pairs={{6,0},{7,1},{4,2},{5,3},{2,4},{3,5},{0,6},{1,7},{14,8},{15,9},{12,... | collective-permute-start | bytes 233480 | tf_op jit(solution)/shard_map/ppermute | solution.py:495
  14.4 1.6 %collective-permute-done.9.refs_8_ = f32[136,128]{1,0:T(8,128)S(1)} collective-permute-done((f32[136,128]{1,0:T(8,128)}, f32[136,128]{1,0:T(8,128)S(1)}, u32[]{:S(2)}, u32[]{:S(2)}) %collective-permute-start.9) | collective-permute-done | bytes 69664 | tf_op jit(solution)/shard_map/ppermute | solution.py:495
  16.0 0.0 collective-permute-start
  16.0 0.0 collective-permute-done.1.refs_2_.refs_3_
  16.0 0.5 collective-permute-start.2
  16.5 0.0 collective-permute-done.3.refs_4_
  16.5 0.1 collective-permute-start.4
  16.6 0.0 collective-permute-done.11.refs_10_
  16.6 2.1 %collective-permute-start.7 = (f32[136,128]{1,0:T(8,128)}, f32[136,128]{1,0:T(8,128)S(1)}, u32[]{:S(2)}, u32[]{:S(2)}) collective-permute-start(f32[136,128]{1,0:T(8,128)} %get-tuple-element.11.refs_6_), channel_id=1, source_target_pairs={{30,0},{31,1},{28,2},{29,3},{26,4},{27,5},{24,6},{25,7},{22,8},{23... | collective-permute-start | bytes 208904 | tf_op jit(solution)/shard_map/ppermute | solution.py:495
  18.7 0.0 collective-permute-done.5.refs_6_
  18.7 0.0 collective-permute-start.6
  18.7 6.2 %collective-permute-done.7.refs_5_.refs_12_ = f32[136,128]{1,0:T(8,128)S(1)} collective-permute-done((f32[136,128]{1,0:T(8,128)}, f32[136,128]{1,0:T(8,128)S(1)}, u32[]{:S(2)}, u32[]{:S(2)}) %collective-permute-start.7) | collective-permute-done | bytes 69664 | tf_op jit(solution)/shard_map/ppermute | solution.py:495
  24.9 0.0 collective-permute-start.8
  24.9 0.0 collective-permute-done.refs_1_
  24.9 0.5 collective-permute-start.10
  25.4 0.0 collective-permute-done.2.refs_3_
  25.4 0.1 collective-permute-start.12
  25.5 0.0 collective-permute-done.4.refs_5_
  25.5 0.4 collective-permute-start.13
  26.0 0.0 collective-permute-done.6.refs_7_
  26.0 0.0 copy-start
  26.0 0.9 %copy-done = f32[152,128]{1,0:T(8,128)S(1)} copy-done((f32[152,128]{1,0:T(8,128)S(1)}, f32[152,128]{1,0:T(8,128)}, u32[]{:S(2)}) %copy-start) | copy-done | bytes 77848
  26.9 8.6 %first_group.1 = (f32[16,56,1024]{2,1,0:T(8,128)S(1)}, f32[16,8,128]{2,1,0:T(8,128)S(1)}, f32[12,8,128]{2,1,0:T(8,128)S(1)}) custom-call(f32[152,128]{1,0:T(8,128)S(1)} %copy-done, f32[152,128]{1,0:T(8,128)S(1)} %collective-permute-done.refs_1_, f32[152,128]{1,0:T(8,128)S(1)} %collective-permute-done.1.refs_2_.refs_3_, ...), custom_call_target="tpu_custom_call" | custom-call | flops 23592960 | bytes 16777216 | tf_op jit(solution)/shard_map/first_group/pallas_call | solution.py:525
  35.4 0.0 collective-permute-done.8.refs_7_
  35.4 0.0 collective-permute-done.10.refs_9_
  35.4 0.0 collective-permute-done.12.refs_11_
  35.5 0.0 collective-permute-done.13.refs_13_
  35.5 0.0 copy-start.1
  35.5 0.9 %copy-done.1 = f32[136,128]{1,0:T(8,128)S(1)} copy-done((f32[136,128]{1,0:T(8,128)S(1)}, f32[136,128]{1,0:T(8,128)}, u32[]{:S(2)}) %copy-start.1) | copy-done | bytes 69656
  36.3 0.0 copy-start.2
  36.4 0.7 %copy-done.2 = f32[8,128]{1,0:T(8,128)S(1)} copy-done((f32[8,128]{1,0:T(8,128)S(1)}, f32[8,128]{1,0:T(8,128)}, u32[]{:S(2)}) %copy-start.2) | copy-done | bytes 4120
  37.0 15.0 %second_group.1 = (f32[2,64,64]{2,1,0:T(8,128)}, f32[2,64,64]{2,1,0:T(8,128)}) custom-call(s32[1]{0:T(128)S(6)} %copy.8.counts, f32[8,128]{1,0:T(8,128)S(1)} %copy-done.2, f32[16,56,1024]{2,1,0:T(8,128)S(1)} %get-tuple-element.8.refs_0_, f32[16,8,128]{2,1,0:T(8,128)S(1)} %get-tuple-element.9.refs_1_, f32[12,8,128]{2,1,0:T(8,128)S(1)} %get-tuple-element.10.refs_2_, ...), custom_call_target="tpu_custom_call" | custom-call | flops 23592960 | bytes 16777216 | tf_op jit(solution)/shard_map/second_group/pallas_call | solution.py:541
Async XLA Ops:
  3.4 12.6 %collective-permute-start.1 = (f32[152,128]{1,0:T(8,128)}, f32[152,128]{1,0:T(8,128)S(1)}, u32[]{:S(2)}, u32[]{:S(2)}) collective-permute-start(f32[152,128]{1,0:T(8,128)} %get-tuple-element.7.refs_0_), channel_id=1, source_target_pairs={{10,0},{11,1},{8,2},{9,3},{14,4},{15,5},{12,6},{13,7},{2,8},{3,9},... | collective-permute-start | bytes 233480 | tf_op jit(solution)/shard_map/ppermute | solution.py:495
  7.4 9.2 %collective-permute-start.3 = (f32[152,128]{1,0:T(8,128)}, f32[152,128]{1,0:T(8,128)S(1)}, u32[]{:S(2)}, u32[]{:S(2)}) collective-permute-start(f32[152,128]{1,0:T(8,128)} %get-tuple-element.7.refs_0_), channel_id=1, source_target_pairs={{20,0},{21,1},{22,2},{23,3},{16,4},{17,5},{18,6},{19,7},{28,8},{29... | collective-permute-start | bytes 233480 | tf_op jit(solution)/shard_map/ppermute | solution.py:495
  10.9 5.1 %collective-permute-start.9 = (f32[136,128]{1,0:T(8,128)}, f32[136,128]{1,0:T(8,128)S(1)}, u32[]{:S(2)}, u32[]{:S(2)}) collective-permute-start(f32[136,128]{1,0:T(8,128)} %get-tuple-element.11.refs_6_), channel_id=1, source_target_pairs={{2,0},{3,1},{0,2},{1,3},{6,4},{7,5},{4,6},{5,7},{10,8},{11,9},{8,1... | collective-permute-start | bytes 208904 | tf_op jit(solution)/shard_map/ppermute | solution.py:495
  11.4 5.2 %collective-permute-start.11 = (f32[136,128]{1,0:T(8,128)}, f32[136,128]{1,0:T(8,128)S(1)}, u32[]{:S(2)}, u32[]{:S(2)}) collective-permute-start(f32[136,128]{1,0:T(8,128)} %get-tuple-element.11.refs_6_), channel_id=1, source_target_pairs={{4,0},{5,1},{6,2},{7,3},{0,4},{1,5},{2,6},{3,7},{12,8},{13,9},{14,... | collective-permute-start | bytes 208904 | tf_op jit(solution)/shard_map/ppermute | solution.py:495
  12.0 6.8 %collective-permute-start.5 = (f32[152,128]{1,0:T(8,128)}, f32[152,128]{1,0:T(8,128)S(1)}, u32[]{:S(2)}, u32[]{:S(2)}) collective-permute-start(f32[152,128]{1,0:T(8,128)} %get-tuple-element.7.refs_0_), channel_id=1, source_target_pairs={{6,0},{7,1},{4,2},{5,3},{2,4},{3,5},{0,6},{1,7},{14,8},{15,9},{12,... | collective-permute-start | bytes 233480 | tf_op jit(solution)/shard_map/ppermute | solution.py:495
  16.0 8.9 %collective-permute-start = (f32[152,128]{1,0:T(8,128)}, f32[152,128]{1,0:T(8,128)S(1)}, u32[]{:S(2)}, u32[]{:S(2)}) collective-permute-start(f32[152,128]{1,0:T(8,128)} %get-tuple-element.7.refs_0_), channel_id=1, source_target_pairs={{1,0},{0,1},{3,2},{2,3},{5,4},{4,5},{7,6},{6,7},{9,8},{8,9},{11,10... | collective-permute-start | bytes 233480 | tf_op jit(solution)/shard_map/ppermute | solution.py:495
  16.0 9.4 %collective-permute-start.2 = (f32[152,128]{1,0:T(8,128)S(1)}, f32[152,128]{1,0:T(8,128)S(1)}, u32[]{:S(2)}, u32[]{:S(2)}) collective-permute-start(f32[152,128]{1,0:T(8,128)S(1)} %collective-permute-done.1.refs_2_.refs_3_), channel_id=1, source_target_pairs={{1,0},{0,1},{3,2},{2,3},{5,4},{4,5},{7,6},{6,7},{9,8},{8,9},{11,10... | collective-permute-start | bytes 233480 | tf_op jit(solution)/shard_map/ppermute | solution.py:495
  16.5 9.0 %collective-permute-start.4 = (f32[152,128]{1,0:T(8,128)S(1)}, f32[152,128]{1,0:T(8,128)S(1)}, u32[]{:S(2)}, u32[]{:S(2)}) collective-permute-start(f32[152,128]{1,0:T(8,128)S(1)} %collective-permute-done.3.refs_4_), channel_id=1, source_target_pairs={{1,0},{0,1},{3,2},{2,3},{5,4},{4,5},{7,6},{6,7},{9,8},{8,9},{11,10... | collective-permute-start | bytes 233480 | tf_op jit(solution)/shard_map/ppermute | solution.py:495
  16.6 8.3 %collective-permute-start.7 = (f32[136,128]{1,0:T(8,128)}, f32[136,128]{1,0:T(8,128)S(1)}, u32[]{:S(2)}, u32[]{:S(2)}) collective-permute-start(f32[136,128]{1,0:T(8,128)} %get-tuple-element.11.refs_6_), channel_id=1, source_target_pairs={{30,0},{31,1},{28,2},{29,3},{26,4},{27,5},{24,6},{25,7},{22,8},{23... | collective-permute-start | bytes 208904 | tf_op jit(solution)/shard_map/ppermute | solution.py:495
  18.7 7.2 %collective-permute-start.6 = (f32[152,128]{1,0:T(8,128)S(1)}, f32[152,128]{1,0:T(8,128)S(1)}, u32[]{:S(2)}, u32[]{:S(2)}) collective-permute-start(f32[152,128]{1,0:T(8,128)S(1)} %collective-permute-done.5.refs_6_), channel_id=1, source_target_pairs={{1,0},{0,1},{3,2},{2,3},{5,4},{4,5},{7,6},{6,7},{9,8},{8,9},{11,10... | collective-permute-start | bytes 233480 | tf_op jit(solution)/shard_map/ppermute | solution.py:495
  24.9 10.5 %collective-permute-start.8 = (f32[136,128]{1,0:T(8,128)}, f32[136,128]{1,0:T(8,128)S(1)}, u32[]{:S(2)}, u32[]{:S(2)}) collective-permute-start(f32[136,128]{1,0:T(8,128)} %get-tuple-element.11.refs_6_), channel_id=1, source_target_pairs={{1,0},{0,1},{3,2},{2,3},{5,4},{4,5},{7,6},{6,7},{9,8},{8,9},{11,10... | collective-permute-start | bytes 208904 | tf_op jit(solution)/shard_map/ppermute | solution.py:495
  24.9 10.5 %collective-permute-start.10 = (f32[136,128]{1,0:T(8,128)S(1)}, f32[136,128]{1,0:T(8,128)S(1)}, u32[]{:S(2)}, u32[]{:S(2)}) collective-permute-start(f32[136,128]{1,0:T(8,128)S(1)} %collective-permute-done.9.refs_8_), channel_id=1, source_target_pairs={{1,0},{0,1},{3,2},{2,3},{5,4},{4,5},{7,6},{6,7},{9,8},{8,9},{11,10... | collective-permute-start | bytes 208904 | tf_op jit(solution)/shard_map/ppermute | solution.py:495
  25.4 10.0 %collective-permute-start.12 = (f32[136,128]{1,0:T(8,128)S(1)}, f32[136,128]{1,0:T(8,128)S(1)}, u32[]{:S(2)}, u32[]{:S(2)}) collective-permute-start(f32[136,128]{1,0:T(8,128)S(1)} %collective-permute-done.11.refs_10_), channel_id=1, source_target_pairs={{1,0},{0,1},{3,2},{2,3},{5,4},{4,5},{7,6},{6,7},{9,8},{8,9},{11,10... | collective-permute-start | bytes 208904 | tf_op jit(solution)/shard_map/ppermute | solution.py:495
  25.5 9.9 %collective-permute-start.13 = (f32[136,128]{1,0:T(8,128)S(1)}, f32[136,128]{1,0:T(8,128)S(1)}, u32[]{:S(2)}, u32[]{:S(2)}) collective-permute-start(f32[136,128]{1,0:T(8,128)S(1)} %collective-permute-done.7.refs_5_.refs_12_), channel_id=1, source_target_pairs={{1,0},{0,1},{3,2},{2,3},{5,4},{4,5},{7,6},{6,7},{9,8},{8,9},{11,10... | collective-permute-start | bytes 208904 | tf_op jit(solution)/shard_map/ppermute | solution.py:495
  26.0 0.9 %copy-start = (f32[152,128]{1,0:T(8,128)S(1)}, f32[152,128]{1,0:T(8,128)}, u32[]{:S(2)}) copy-start(f32[152,128]{1,0:T(8,128)} %get-tuple-element.7.refs_0_) | copy-start | bytes 233476
  35.5 0.9 %copy-start.1 = (f32[136,128]{1,0:T(8,128)S(1)}, f32[136,128]{1,0:T(8,128)}, u32[]{:S(2)}) copy-start(f32[136,128]{1,0:T(8,128)} %get-tuple-element.11.refs_6_) | copy-start | bytes 208900
  36.3 0.7 %copy-start.2 = (f32[8,128]{1,0:T(8,128)S(1)}, f32[8,128]{1,0:T(8,128)}, u32[]{:S(2)}) copy-start(f32[8,128]{1,0:T(8,128)} %constant.2.clone.coeffs) | copy-start | bytes 12292

commit v3 on v1

--- a/solution.py
+++ b/solution.py
@@ -3,7 +3,6 @@
 
 import jax
 import jax.numpy as jnp
-import numpy as np
 from jax import lax
 from jax.experimental import pallas as pl
 from jax.experimental.pallas import tpu as pltpu
@@ -166,20 +165,68 @@
 LANES = Y_OUT * X_OUT
 SUB = 8
 BASIS = ITERS + 1
-
-
-def to_blocked(values):
-    split = values.reshape(values.shape[:-1] + (Y_OUT, Y_IN, X_OUT, X_IN))
-    lead = values.ndim - 1
-    order = tuple(range(lead)) + (lead + 1, lead + 3, lead, lead + 2)
-    return split.transpose(order).reshape(values.shape[:-1] + (ROWS, LANES))
-
-
-def packed_block(sources, potential):
-    count = sources.shape[0]
-    rows = to_blocked(sources).transpose(1, 2, 0, 3).reshape(-1, LANES)
-    levels = to_blocked(potential).reshape(-1, LANES)
-    return jnp.concatenate([rows, levels], axis=0)
+H_SCALE = 2.0 / COEF_NEAR
+FAR_SCALED = 0.5 * H_SCALE * COEF_FAR
+
+
+def pack_kernel(depth, groups, counts, rows, levels, out):
+    columns = rows.shape[0] // (SUB * groups * depth)
+    source = lax.broadcasted_iota(jnp.int32, (LANES, LANES), 0)
+    target = lax.broadcasted_iota(jnp.int32, (LANES, LANES), 1)
+    inner = target // (LANES // ROWS)
+    outer = target % (LANES // ROWS)
+    cell = (outer // X_OUT * Y_IN + inner // X_IN) * GX + outer % X_OUT * X_IN + inner % X_IN
+    swap = jnp.where(source == cell, 1.0, 0.0).astype(jnp.float32)
+    parts = []
+    for deep in range(depth):
+        for group in range(groups):
+            for column in range(columns):
+                start = (group * SUB * columns + column) * depth + deep
+                parts.append(rows[pl.ds(start, SUB, stride=columns * depth), :])
+        parts.append(levels[pl.ds(deep, columns, stride=depth), :])
+    mixed = exact_dot(jnp.concatenate(parts, axis=0), swap, ((1,), (0,)))
+    block = LANES // ROWS
+    lane_block = lax.broadcasted_iota(jnp.int32, (SUB, LANES), 1) // block
+    row = lax.broadcasted_iota(jnp.int32, (SUB, LANES), 0)
+    for deep in range(depth):
+        base = deep * (groups + 1) * columns * SUB - deep * (columns - 1) * SUB
+        for group in range(groups):
+            pieces = [
+                mixed[base + (group * columns + column) * SUB :][:SUB] for column in range(columns)
+            ]
+            for m in range(ROWS):
+                value = pieces[m]
+                for column in range(columns):
+                    if column != m:
+                        moved = pltpu.roll(pieces[column], (column - m) * block % LANES, 1)
+                        value = jnp.where(lane_block == column, moved, value)
+                start = ((deep * ROWS + m) * groups + group) * SUB
+                out[start : start + SUB, :] = value
+        piece = mixed[base + groups * columns * SUB :][:SUB]
+        value = piece
+        for far in range(1, columns):
+            moved = pltpu.roll(pltpu.roll(piece, far * block, 1), columns - far, 0)
+            value = jnp.where(lane_block == (row + far) % columns, moved, value)
+        start = depth * ROWS * SUB * groups + deep * ROWS
+        out[start : start + ROWS, :] = value
+    out[out.shape[0] - SUB :, :] = jnp.full((SUB, LANES), counts[0].astype(jnp.float32))
+
+
+def packed_block(sources, potential, iter_counts):
+    count, depth, cells = sources.shape
+    columns = cells // LANES
+    rows = sources.reshape(count, depth, columns, LANES).transpose(0, 2, 1, 3)
+    levels = potential.reshape(depth, columns, LANES).transpose(1, 0, 2)
+    vmem = pl.BlockSpec(memory_space=pltpu.VMEM)
+    smem = pl.BlockSpec(memory_space=pltpu.SMEM)
+    size = depth * ROWS * (count + 1) + SUB
+    return pl.pallas_call(
+        functools.partial(pack_kernel, depth, count // SUB),
+        out_shape=jax.ShapeDtypeStruct((size, LANES), jnp.float32),
+        in_specs=[smem, vmem, vmem],
+        out_specs=vmem,
+        name="pack",
+    )(iter_counts, rows.reshape(-1, LANES), levels.reshape(-1, LANES))
 
 
 def lane_sum(values):
@@ -198,16 +245,15 @@
     return jnp.where(wrap_mask, pltpu.roll(values, LANES - X_OUT + 1, 1), pltpu.roll(values, 1, 1))
 
 
-def plane_of(basis, plane, row):
-    return [basis[plane, pl.ds(row, SUB), pl.ds(m * LANES, LANES)] for m in range(ROWS)]
-
-
-def apply_plane(basis, diagonal, plane, planes, row, last_x, first_x):
-    here = plane_of(basis, plane, row)
-    above = plane_of(basis, lax.rem(plane + 1, planes), row)
-    below = plane_of(basis, lax.rem(plane + planes - 1, planes), row)
-    above_2 = plane_of(basis, lax.rem(plane + 2, planes), row)
-    below_2 = plane_of(basis, lax.rem(plane + planes - 2, planes), row)
+def apply_plane(vector, diagonal, plane, planes, group, last_x, first_x):
+    rows = pl.ds(group * SUB, SUB)
+
+    def plane_at(index):
+        return [vector[index, rows, pl.ds(m * LANES, LANES)] for m in range(ROWS)]
+
+    here = plane_at(plane)
+    above, below = (plane_at(lax.rem(plane + far, planes)) for far in (1, planes - 1))
+    above_2, below_2 = (plane_at(lax.rem(plane + far, planes)) for far in (2, planes - 2))
     y_up = [pltpu.roll(value, LANES - X_OUT, 1) for value in here]
     y_down = [pltpu.roll(value, X_OUT, 1) for value in here]
     out = []
@@ -224,7 +270,7 @@
             near = (wide[xi + 1] + wide[xi + 3]) + (y_next + y_prev) + (above[m] + below[m])
             far = (wide[xi] + wide[xi + 4]) + (y_up[m] + y_down[m]) + (above_2[m] + below_2[m])
             level = diagonal[plane, pl.ds(m, 1), :]
-            out.append(level * here[m] - (0.5 * COEF_NEAR) * near - (0.5 * COEF_FAR) * far)
+            out.append(level * here[m] - near - FAR_SCALED * far)
     return here, out
 
 
@@ -235,9 +281,22 @@
     )
 
 
-def weights_of(alphas, norms, limits, coeffs, shape):
+def moment_coeffs(point, points, count):
+    lane = lax.broadcasted_iota(jnp.int32, (1, LANES), 1)
+    moment = lax.rem(lane, MOMENTS * count) // count
+    angle = 2.0 * math.pi * (point + 0.5) / points
+    parts = []
+    for func in (math.cos, math.sin):
+        value = jnp.full((1, LANES), 0.25 * func(angle), jnp.float32)
+        for k in range(1, MOMENTS):
+            value = jnp.where(moment == k, 0.25 * func((k + 1) * angle), value)
+        parts.append(value)
+    return parts
+
+
+def weights_of(alphas, norms, limits, count):
     points = len(limits)
-    count = shape[0]
+    shape = (count, LANES)
     half = MOMENTS * count
     lane = lax.broadcasted_iota(jnp.int32, shape, 1)
     source = lax.broadcasted_iota(jnp.int32, shape, 0)
@@ -250,27 +309,28 @@
     for point in range(points):
         angle = 2.0 * math.pi * (point + 0.5) / points
         shift = (GAMMA + RADIUS * math.cos(angle), RADIUS * math.sin(angle))
+        scaled_shift = (H_SCALE * shift[0], H_SCALE * shift[1])
         limit = limits[point]
         product = (one, zero)
         products = [product]
         links = []
-        pivot = (shift[0] - alphas[0], zero + shift[1])
+        pivot = (scaled_shift[0] - alphas[0], zero + scaled_shift[1])
         for i in range(ITERS):
-            size = pivot[0] * pivot[0] + pivot[1] * pivot[1]
-            inverse = (pivot[0] / size, -pivot[1] / size)
+            size = 1.0 / (pivot[0] * pivot[0] + pivot[1] * pivot[1])
+            inverse = (pivot[0] * size, -pivot[1] * size)
             product = cmul(product, inverse)
             products.append(product)
             if i < ITERS - 1:
                 link = (betas[i] * inverse[0], betas[i] * inverse[1])
                 links.append(link)
-                pivot = (shift[0] - alphas[i + 1] - link[0], shift[1] - link[1])
+                pivot = (scaled_shift[0] - alphas[i + 1] - link[0], scaled_shift[1] - link[1])
         solved = [None] * ITERS
         for i in reversed(range(ITERS)):
-            value = products[i + 1]
+            value = (H_SCALE * products[i + 1][0], H_SCALE * products[i + 1][1])
             if i < ITERS - 1:
                 step = cmul(links[i], solved[i + 1])
                 value = (value[0] + step[0], value[1] + step[1])
-            used = i < limit
+            used = limit > i
             solved[i] = (jnp.where(used, value[0], 0.0), jnp.where(used, value[1], 0.0))
         applied = []
         for i in range(BASIS):
@@ -292,7 +352,7 @@
         for back, factor in ((1, alphas[ITERS - 1]), (2, betas[ITERS - 2])):
             part = applied[ITERS - back]
             applied[ITERS - back] = (part[0] - factor * tail[0], part[1] - factor * tail[1])
-        moment = (coeffs[2 * point : 2 * point + 1, :], coeffs[2 * point + 1 : 2 * point + 2, :])
+        moment = moment_coeffs(point, points, count)
         for i in range(BASIS):
             left = solved[i] if i < ITERS else (zero, zero)
             both = (
@@ -314,41 +374,47 @@
     )
 
 
-def solve_kernel(parts, count, planes, points, meta, coeffs, *refs):
+def solve_kernel(parts, points, count, *refs):
     blocks = refs[:parts]
-    out_b, out_a, basis, diagonal, gram = refs[parts:]
+    out_b, out_a = refs[parts : parts + 2]
+    vectors = refs[parts + 2 : parts + 2 + BASIS]
+    applied, diagonal, gram, limits = refs[parts + 2 + BASIS :]
+    planes = diagonal.shape[0]
     depth = planes // parts
     groups = count // SUB
     lane = lax.broadcasted_iota(jnp.int32, (SUB, LANES), 1)
     last_x = lax.rem(lane, X_OUT) == X_OUT - 1
     first_x = lax.rem(lane, X_OUT) == 0
+    here = lax.axis_index("dom")
+    point_here = lax.axis_index("point")
+    core = jnp.bitwise_and(here, 1)
 
     for turn in range(parts):
-        slab = jnp.bitwise_xor(meta[0], turn) * depth
+        slab = jnp.bitwise_xor(here, turn) * depth
         for deep in range(depth):
             for m in range(ROWS):
                 start = (deep * ROWS + m) * count
-                basis[slab + deep, 0:count, m * LANES : (m + 1) * LANES] = blocks[turn][
-                    start : start + count, :
-                ]
+                lanes = pl.ds(m * LANES, LANES)
+                vectors[0][slab + deep, :, lanes] = blocks[turn][start : start + count, :]
             start = depth * ROWS * count + deep * ROWS
-            diagonal[slab + deep] = blocks[turn][start : start + ROWS, :] + 3.75
+            diagonal[slab + deep] = H_SCALE * (blocks[turn][start : start + ROWS, :] + 3.75)
 
     blank = jnp.zeros((SUB, LANES), jnp.float32)
     alphas, norms = [], []
     for i in range(ITERS):
-
-        def apply_turn(plane, sums, i=i):
+        source, target = vectors[i], applied if i < ITERS - 1 else vectors[ITERS]
+
+        def apply_turn(plane, sums, i=i, source=source, target=target):
             new_sums = []
             for group in range(groups):
-                row = i * count + group * SUB
-                here, out = apply_plane(basis, diagonal, plane, planes, row, last_x, first_x)
+                rows = pl.ds(group * SUB, SUB)
                 curve, norm = sums[group]
+                value, out = apply_plane(source, diagonal, plane, planes, group, last_x, first_x)
                 for m in range(ROWS):
-                    basis[plane, pl.ds(row + count, SUB), pl.ds(m * LANES, LANES)] = out[m]
-                    curve = curve + here[m] * out[m]
+                    target[plane, rows, pl.ds(m * LANES, LANES)] = out[m]
+                    curve = curve + value[m] * out[m]
                     if i == 0:
-                        norm = norm + here[m] * here[m]
+                        norm = norm + value[m] * value[m]
                 new_sums.append((curve, norm))
             return tuple(new_sums)
 
@@ -360,30 +426,30 @@
             break
         betas = [ratio(norms[i][g], norms[i - 1][g]) for g in range(groups)] if i else None
 
-        def step_turn(plane, sums, i=i, betas=betas):
+        def step_turn(plane, sums, i=i, alpha=alphas[i], betas=betas):
             new_sums = []
             for group in range(groups):
-                row = i * count + group * SUB
+                rows = pl.ds(group * SUB, SUB)
                 norm = sums[group]
                 for m in range(ROWS):
                     lanes = pl.ds(m * LANES, LANES)
-                    value = basis[plane, pl.ds(row + count, SUB), lanes]
-                    value = value - alphas[i][group] * basis[plane, pl.ds(row, SUB), lanes]
+                    value = applied[plane, rows, lanes]
+                    value = value - alpha[group] * vectors[i][plane, rows, lanes]
                     if i:
-                        value = value - betas[group] * basis[plane, pl.ds(row - count, SUB), lanes]
-                    basis[plane, pl.ds(row + count, SUB), lanes] = value
+                        value = value - betas[group] * vectors[i - 1][plane, rows, lanes]
+                    vectors[i + 1][plane, rows, lanes] = value
                     norm = norm + value * value
                 new_sums.append(norm)
             return tuple(new_sums)
 
-        sums = lax.fori_loop(0, planes, step_turn, (blank,) * groups)
+        sums = lax.fori_loop(0, planes, step_turn, (blank,) * groups, unroll=2)
         norms.append([lane_sum(norm) for norm in sums])
 
     size = BASIS * count
     gram[...] = jnp.zeros_like(gram)
 
     def gram_turn(plane, carry):
-        values = basis[plane]
+        values = jnp.concatenate([vector[plane] for vector in vectors], axis=0)
         high = values.astype(jnp.bfloat16)
         low = (values - high.astype(jnp.float32)).astype(jnp.bfloat16)
         gram[...] += lax.dot_general(
@@ -398,11 +464,15 @@
     cross = gram[:, size:]
     pairs = gram[:, :size] + cross + cross.T
 
-    shape = (count, LANES)
-    limits = [meta[2 + jnp.bitwise_xor(meta[1], point)] for point in range(points)]
+    tails = [block[block.shape[0] - SUB :, :] for block in blocks]
+    limits[point_here] = tails[0]
+    limits[jnp.bitwise_xor(point_here, 1 + core)] = tails[2]
+    limits[jnp.bitwise_xor(point_here, 2 - core)] = tails[3]
+    limits[jnp.bitwise_xor(point_here, 3)] = jnp.where(core == 0, tails[4], tails[5])
+    bounds = [jnp.concatenate([limits[j]] * groups, axis=0) for j in range(points)]
     alphas = [jnp.concatenate(value, axis=0) for value in alphas]
     norms = [jnp.concatenate(value, axis=0) for value in norms]
-    weights = weights_of(alphas, norms, limits, coeffs, shape)
+    weights = weights_of(alphas, norms, bounds, count)
     real = jnp.concatenate([pair[0] for pair in weights], axis=0)
     imag = jnp.concatenate([pair[1] for pair in weights], axis=0)
     right = exact_dot(pairs, jnp.concatenate([real, imag], axis=1), ((1,), (0,)))
@@ -419,46 +489,44 @@
     out_a[1] = imag[:, half:]
 
 
-def swapped(values, axis, size, mask):
-    return lax.ppermute(values, axis, [(i ^ mask, i) for i in range(size)])
+CROSSING = {2: (1, 2), 4: (3, 0), 6: (0, 0)}
+
+
+def exchanged(values, mask, parts, points):
+    pairs = []
+    for point in range(points):
+        for part in range(parts):
+            other = CROSSING[mask][part % 2] if mask in CROSSING else 0
+            pairs.append(((point ^ other) * parts + (part ^ mask), point * parts + part))
+    return lax.ppermute(values, ("point", "dom"), pairs)
 
 
 def whole_grid(sources, potential, iter_counts, *, parts, points):
     count, depth, _ = sources.shape
     planes = parts * depth
-    block = packed_block(sources, potential)
-    even = [block] + [swapped(block, "dom", parts, mask) for mask in range(2, parts, 2)]
-    odd = [swapped(value, "dom", parts, 1) for value in even]
+    block = packed_block(sources, potential, iter_counts)
+    even = [block] + [exchanged(block, mask, parts, points) for mask in range(2, parts, 2)]
+    odd = [exchanged(value, 1, parts, points) for value in even]
     blocks = [value for pair in zip(even, odd) for value in pair]
-    limits = [iter_counts] + [
-        swapped(iter_counts, "point", points, mask) for mask in range(1, points)
-    ]
-    place = jnp.stack([lax.axis_index("dom"), lax.axis_index("point")]).astype(jnp.int32)
-    meta = jnp.concatenate([place] + limits)
-    angles = 2.0 * math.pi * (np.arange(points)[:, None] + 0.5) / points
-    turns = np.tile(np.repeat(np.arange(MOMENTS) + 1.0, count), 2)[None, :] * angles
-    coeffs = 0.25 * np.stack([np.cos(turns), np.sin(turns)], axis=1).reshape(2 * points, -1)
     vmem = pl.BlockSpec(memory_space=pltpu.VMEM)
-    smem = pl.BlockSpec(memory_space=pltpu.SMEM)
     size = BASIS * count
     width = MOMENTS * count
     out = jax.ShapeDtypeStruct((2, width, width), jnp.float32)
+    vector = pltpu.VMEM((planes, count, ROWS * LANES), jnp.float32)
     return pl.pallas_call(
-        functools.partial(solve_kernel, parts, count, planes, points),
+        functools.partial(solve_kernel, parts, points, count),
         out_shape=(out, out),
-        in_specs=[smem, vmem] + [vmem] * parts,
+        in_specs=[vmem] * parts,
         out_specs=(vmem, vmem),
-        scratch_shapes=[
-            pltpu.VMEM((planes, size, ROWS * LANES), jnp.float32),
+        scratch_shapes=[vector] * (BASIS + 1)
+        + [
             pltpu.VMEM((planes, ROWS, LANES), jnp.float32),
             pltpu.VMEM((size, 2 * size), jnp.float32),
+            pltpu.VMEM((points, SUB, LANES), jnp.float32),
         ],
-        compiler_params=pltpu.CompilerParams(vmem_limit_bytes=40 * 2**20),
-    )(meta, jnp.asarray(coeffs, jnp.float32), *blocks)
-
-
-def power_of_two(value):
-    return value > 0 and value & (value - 1) == 0
+        compiler_params=pltpu.CompilerParams(vmem_limit_bytes=32 * 2**20),
+        name="solve",
+    )(*blocks)
 
 
 def on_device(sources, potential, iter_counts):
@@ -467,8 +535,9 @@
     held = BASIS * count * parts * depth * cells * 4
     fits = (
         held <= 16 * 2**20
-        and power_of_two(parts)
-        and power_of_two(points)
+        and parts == 8
+        and points == 4
+        and count == 2 * SUB
         and 2 * MOMENTS * count == LANES
         and cells == GX * GX == ROWS * LANES
     )

time: 54.4 us -> 42.6 us (0.78)
  starting transfers between devices: 12.8 us -> 7.45 us
  local copies, waits for them, and re-layouts: 4.8 us -> 0.91 us
  waiting for transfers between devices: 12 us -> 8.52 us
  Pallas kernels: 23.1 us -> 24.2 us
    ppermute x10 -> x7, starting transfers between devices: 12.8 us -> 7.45 us  [exchanged(): return lax.ppermute(values, ('point', 'dom'), pairs)]
    ppermute x10 -> x7, waiting for transfers between devices: 12 us -> 8.52 us  [exchanged(): return lax.ppermute(values, ('point', 'dom'), pairs)]
    concatenate x1 -> x0, local copies, waits for them, and re-layouts: 1.9 us -> none  [whole_grid(): meta = jnp.concatenate([place] + limits)]
    pallas_call x1 -> x2, Pallas kernels: 23.1 us -> 24.2 us  [the longest x1 22.1 us: whole_grid(): pl.pallas_call(functools.partial(solve_kernel, parts, points, count), out...]
    transpose x3 -> x0, local copies, waits for them, and re-layouts: 0.88 us -> none  [the longest x2 0.58 us: to_blocked(): return split.transpose(order).reshape(values.shape[:-1] + (ROWS, LANES))]
    unnamed x5 -> x2, local copies, waits for them, and re-layouts: 1.65 us -> 0.91 us
  transfers between devices with their start and end apart: 10 -> 7, of which waited for: 5 -> 4; matrix products, arithmetic and copies ran while one was open for 4% -> 0% of each run, Pallas kernels for 0% -> 0%
where the time goes in v3:
time: 42.6 us; the launch traced here: 42.4 us
  Pallas kernels  24.2 us (57%)
  waiting for transfers between devices  8.52 us (20%)
  starting transfers between devices  7.45 us (17%)
  between operations  1.3 us (3%)
  local copies, waits for them, and re-layouts  0.91 us (2%)
    pallas_call x1, Pallas kernels, whole_grid(): pl.pallas_call(functools.partial(solve_kernel, parts, points, count), out...  22.1 us
    ppermute x7, waiting for transfers between devices, exchanged(): return lax.ppermute(values, ('point', 'dom'), pairs)  8.52 us
    ppermute x7, starting transfers between devices, exchanged(): return lax.ppermute(values, ('point', 'dom'), pairs)  7.45 us
    pallas_call x1, Pallas kernels, packed_block(): pl.pallas_call(functools.partial(pack_kernel, depth, count // SUB), out_s...  2.12 us
    unnamed x2, local copies, waits for them, and re-layouts  0.91 us
  transfers between devices with their start and end apart: 7, of which 4 were waited for; matrix products, arithmetic and copies ran while one was open for 0% of the time, Pallas kernels for 0%

profile of v3, /device:TPU:0, one launch (start us, length us, event | category | flops | bytes accessed | tf_op | source)
XLA Modules:
  0.0 42.4 jit_solution(11926996821495491290)
XLA Ops:
  1.3 2.1 %pack.1.refs_0_ = f32[280,128]{1,0:T(8,128)} custom-call(s32[1]{0:T(128)S(6)} %copy.7.counts, f32[256,128]{1,0:T(8,128)} %bitcast.10, f32[16,128]{1,0:T(8,128)} %bitcast.11), custom_call_target="tpu_custom_call" | custom-call | tf_op jit(solution)/shard_map/pack/pallas_call | solution.py:223
  3.4 3.9 %collective-permute-start.5 = (f32[280,128]{1,0:T(8,128)}, f32[280,128]{1,0:T(8,128)S(1)}, u32[]{:S(2)}, u32[]{:S(2)}) collective-permute-start(f32[280,128]{1,0:T(8,128)} %pack.1.refs_0_), channel_id=1, source_target_pairs={{6,0},{7,1},{4,2},{5,3},{2,4},{3,5},{0,6},{1,7},{14,8},{15,9},{12,... | collective-permute-start | bytes 430088 | tf_op jit(solution)/shard_map/ppermute | solution.py:501
  7.3 3.5 %collective-permute-start.3 = (f32[280,128]{1,0:T(8,128)}, f32[280,128]{1,0:T(8,128)S(1)}, u32[]{:S(2)}, u32[]{:S(2)}) collective-permute-start(f32[280,128]{1,0:T(8,128)} %pack.1.refs_0_), channel_id=1, source_target_pairs={{28,0},{5,1},{30,2},{7,3},{24,4},{1,5},{26,6},{3,7},{20,8},{13,9},... | collective-permute-start | bytes 430088 | tf_op jit(solution)/shard_map/ppermute | solution.py:501
  10.8 0.0 collective-permute-start.1
  10.8 0.0 collective-permute-start
  10.8 0.9 %collective-permute-done.5.refs_6_ = f32[280,128]{1,0:T(8,128)S(1)} collective-permute-done((f32[280,128]{1,0:T(8,128)}, f32[280,128]{1,0:T(8,128)S(1)}, u32[]{:S(2)}, u32[]{:S(2)}) %collective-permute-start.5) | collective-permute-done | bytes 143392 | tf_op jit(solution)/shard_map/ppermute | solution.py:501
  11.8 0.0 collective-permute-start.6
  11.8 4.1 %collective-permute-done.3.refs_4_ = f32[280,128]{1,0:T(8,128)S(1)} collective-permute-done((f32[280,128]{1,0:T(8,128)}, f32[280,128]{1,0:T(8,128)S(1)}, u32[]{:S(2)}, u32[]{:S(2)}) %collective-permute-start.3) | collective-permute-done | bytes 143392 | tf_op jit(solution)/shard_map/ppermute | solution.py:501
  15.9 0.0 collective-permute-start.4
  15.9 2.1 %collective-permute-done.1.refs_2_ = f32[280,128]{1,0:T(8,128)S(1)} collective-permute-done((f32[280,128]{1,0:T(8,128)}, f32[280,128]{1,0:T(8,128)S(1)}, u32[]{:S(2)}, u32[]{:S(2)}) %collective-permute-start.1) | collective-permute-done | bytes 143392 | tf_op jit(solution)/shard_map/ppermute | solution.py:501
  18.0 0.0 collective-permute-start.2
  18.0 0.0 collective-permute-done.refs_1_
  18.0 0.0 collective-permute-done.6.refs_7_
  18.0 0.0 collective-permute-done.4.refs_5_
  18.0 1.3 %collective-permute-done.2.refs_3_ = f32[280,128]{1,0:T(8,128)S(1)} collective-permute-done((f32[280,128]{1,0:T(8,128)S(1)}, f32[280,128]{1,0:T(8,128)S(1)}, u32[]{:S(2)}, u32[]{:S(2)}) %collective-permute-start.2) | collective-permute-done | bytes 143392 | tf_op jit(solution)/shard_map/ppermute | solution.py:501
  19.4 0.0 copy-start
  19.4 0.9 %copy-done = f32[280,128]{1,0:T(8,128)S(1)} copy-done((f32[280,128]{1,0:T(8,128)S(1)}, f32[280,128]{1,0:T(8,128)}, u32[]{:S(2)}) %copy-start) | copy-done | bytes 143384
  20.3 22.1 %solve.1 = (f32[2,64,64]{2,1,0:T(8,128)}, f32[2,64,64]{2,1,0:T(8,128)}) custom-call(f32[280,128]{1,0:T(8,128)S(1)} %copy-done, f32[280,128]{1,0:T(8,128)S(1)} %collective-permute-done.refs_1_, f32[280,128]{1,0:T(8,128)S(1)} %collective-permute-done.1.refs_2_, f32[280,128]{1,0:T(8,128)S(1)} %collective-permute-done.2.refs_3_, ...), custom_call_target="tpu_custom_call" | custom-call | tf_op jit(solution)/shard_map/solve/pallas_call | solution.py:516
Async XLA Ops:
  3.4 8.4 %collective-permute-start.5 = (f32[280,128]{1,0:T(8,128)}, f32[280,128]{1,0:T(8,128)S(1)}, u32[]{:S(2)}, u32[]{:S(2)}) collective-permute-start(f32[280,128]{1,0:T(8,128)} %pack.1.refs_0_), channel_id=1, source_target_pairs={{6,0},{7,1},{4,2},{5,3},{2,4},{3,5},{0,6},{1,7},{14,8},{15,9},{12,... | collective-permute-start | bytes 430088 | tf_op jit(solution)/shard_map/ppermute | solution.py:501
  7.3 8.6 %collective-permute-start.3 = (f32[280,128]{1,0:T(8,128)}, f32[280,128]{1,0:T(8,128)S(1)}, u32[]{:S(2)}, u32[]{:S(2)}) collective-permute-start(f32[280,128]{1,0:T(8,128)} %pack.1.refs_0_), channel_id=1, source_target_pairs={{28,0},{5,1},{30,2},{7,3},{24,4},{1,5},{26,6},{3,7},{20,8},{13,9},... | collective-permute-start | bytes 430088 | tf_op jit(solution)/shard_map/ppermute | solution.py:501
  10.8 7.2 %collective-permute-start.1 = (f32[280,128]{1,0:T(8,128)}, f32[280,128]{1,0:T(8,128)S(1)}, u32[]{:S(2)}, u32[]{:S(2)}) collective-permute-start(f32[280,128]{1,0:T(8,128)} %pack.1.refs_0_), channel_id=1, source_target_pairs={{10,0},{19,1},{8,2},{17,3},{14,4},{23,5},{12,6},{21,7},{2,8},{27,9... | collective-permute-start | bytes 430088 | tf_op jit(solution)/shard_map/ppermute | solution.py:501
  10.8 7.2 %collective-permute-start = (f32[280,128]{1,0:T(8,128)}, f32[280,128]{1,0:T(8,128)S(1)}, u32[]{:S(2)}, u32[]{:S(2)}) collective-permute-start(f32[280,128]{1,0:T(8,128)} %pack.1.refs_0_), channel_id=1, source_target_pairs={{1,0},{0,1},{3,2},{2,3},{5,4},{4,5},{7,6},{6,7},{9,8},{8,9},{11,10... | collective-permute-start | bytes 430088 | tf_op jit(solution)/shard_map/ppermute | solution.py:501
  11.8 6.2 %collective-permute-start.6 = (f32[280,128]{1,0:T(8,128)S(1)}, f32[280,128]{1,0:T(8,128)S(1)}, u32[]{:S(2)}, u32[]{:S(2)}) collective-permute-start(f32[280,128]{1,0:T(8,128)S(1)} %collective-permute-done.5.refs_6_), channel_id=1, source_target_pairs={{1,0},{0,1},{3,2},{2,3},{5,4},{4,5},{7,6},{6,7},{9,8},{8,9},{11,10... | collective-permute-start | bytes 430088 | tf_op jit(solution)/shard_map/ppermute | solution.py:501
  15.9 2.1 %collective-permute-start.4 = (f32[280,128]{1,0:T(8,128)S(1)}, f32[280,128]{1,0:T(8,128)S(1)}, u32[]{:S(2)}, u32[]{:S(2)}) collective-permute-start(f32[280,128]{1,0:T(8,128)S(1)} %collective-permute-done.3.refs_4_), channel_id=1, source_target_pairs={{1,0},{0,1},{3,2},{2,3},{5,4},{4,5},{7,6},{6,7},{9,8},{8,9},{11,10... | collective-permute-start | bytes 430088 | tf_op jit(solution)/shard_map/ppermute | solution.py:501
  18.0 1.4 %collective-permute-start.2 = (f32[280,128]{1,0:T(8,128)S(1)}, f32[280,128]{1,0:T(8,128)S(1)}, u32[]{:S(2)}, u32[]{:S(2)}) collective-permute-start(f32[280,128]{1,0:T(8,128)S(1)} %collective-permute-done.1.refs_2_), channel_id=1, source_target_pairs={{1,0},{0,1},{3,2},{2,3},{5,4},{4,5},{7,6},{6,7},{9,8},{8,9},{11,10... | collective-permute-start | bytes 430088 | tf_op jit(solution)/shard_map/ppermute | solution.py:501
  19.4 0.9 %copy-start = (f32[280,128]{1,0:T(8,128)S(1)}, f32[280,128]{1,0:T(8,128)}, u32[]{:S(2)}) copy-start(f32[280,128]{1,0:T(8,128)} %pack.1.refs_0_) | copy-start | bytes 430084

commit v4 on v3

--- a/solution.py
+++ b/solution.py
@@ -225,6 +225,7 @@
         out_shape=jax.ShapeDtypeStruct((size, LANES), jnp.float32),
         in_specs=[smem, vmem, vmem],
         out_specs=vmem,
+        compiler_params=pltpu.CompilerParams(vmem_limit_bytes=4 * 2**20),
         name="pack",
     )(iter_counts, rows.reshape(-1, LANES), levels.reshape(-1, LANES))
 
@@ -418,7 +419,7 @@
                 new_sums.append((curve, norm))
             return tuple(new_sums)
 
-        sums = lax.fori_loop(0, planes, apply_turn, ((blank, blank),) * groups)
+        sums = lax.fori_loop(0, planes, apply_turn, ((blank, blank),) * groups, unroll=4)
         if i == 0:
             norms.append([lane_sum(norm) for _, norm in sums])
         alphas.append([ratio(lane_sum(sums[g][0]), norms[i][g]) for g in range(groups)])
@@ -442,7 +443,7 @@
                 new_sums.append(norm)
             return tuple(new_sums)
 
-        sums = lax.fori_loop(0, planes, step_turn, (blank,) * groups, unroll=2)
+        sums = lax.fori_loop(0, planes, step_turn, (blank,) * groups, unroll=4)
         norms.append([lane_sum(norm) for norm in sums])
 
     size = BASIS * count
@@ -460,7 +461,7 @@
         )
         return carry
 
-    lax.fori_loop(0, planes, gram_turn, 0)
+    lax.fori_loop(0, planes, gram_turn, 0, unroll=4)
     cross = gram[:, size:]
     pairs = gram[:, :size] + cross + cross.T
 

time: 42.6 us -> 34.4 us (0.81)
  Pallas kernels: 24.2 us -> 15.5 us
  local copies, waits for them, and re-layouts: 0.91 us -> 1.59 us
    pallas_call x1, Pallas kernels: 22.1 us -> 15 us  [whole_grid(): pl.pallas_call(functools.partial(solve_kernel, parts, points, count), out...]
    pallas_call x1, Pallas kernels: 2.12 us -> 0.55 us  [packed_block(): pl.pallas_call(functools.partial(pack_kernel, depth, count // SUB), out_s...]
    unnamed x2 -> x4, local copies, waits for them, and re-layouts: 0.91 us -> 1.59 us
where the time goes in v4:
time: 34.4 us; the launch traced here: 34.2 us
  Pallas kernels  15.5 us (45%)
  waiting for transfers between devices  8.3 us (24%)
  starting transfers between devices  7.52 us (22%)
  local copies, waits for them, and re-layouts  1.59 us (5%)
  between operations  1.31 us (4%)
    pallas_call x1, Pallas kernels, whole_grid(): pl.pallas_call(functools.partial(solve_kernel, parts, points, count), out...  15 us
    ppermute x7, waiting for transfers between devices, exchanged(): return lax.ppermute(values, ('point', 'dom'), pairs)  8.3 us
    ppermute x7, starting transfers between devices, exchanged(): return lax.ppermute(values, ('point', 'dom'), pairs)  7.52 us
    unnamed x4, local copies, waits for them, and re-layouts  1.59 us
  transfers between devices with their start and end apart: 7, of which 4 were waited for; matrix products, arithmetic and copies ran while one was open for 0% of the time, Pallas kernels for 0%

profile of v4, /device:TPU:0, one launch (start us, length us, event | category | flops | bytes accessed | tf_op | source)
XLA Modules:
  0.0 34.2 jit_solution(8477389288904183208)
XLA Ops:
  1.3 0.0 copy-start
  1.3 0.9 %copy-done = f32[16,2,1024]{2,1,0:T(2,128)S(1)} copy-done((f32[16,2,1024]{2,1,0:T(2,128)S(1)}, f32[16,2,1024]{2,1,0:T(2,128)}, u32[]{:S(2)}) %copy-start) | copy-done | bytes 131096
  2.2 0.0 copy-start.1
  2.2 0.7 %copy-done.1 = f32[2,1024]{1,0:T(2,128)S(1)} copy-done((f32[2,1024]{1,0:T(2,128)S(1)}, f32[2,1024]{1,0:T(2,128)}, u32[]{:S(2)}) %copy-start.1) | copy-done | bytes 8216
  2.9 0.6 %pack.1.refs_0_ = f32[280,128]{1,0:T(8,128)S(1)} custom-call(s32[1]{0:T(128)S(6)} %copy.7.counts, f32[256,128]{1,0:T(8,128)S(1)} %bitcast.10, f32[16,128]{1,0:T(8,128)S(1)} %bitcast.11), custom_call_target="tpu_custom_call" | custom-call | tf_op jit(solution)/shard_map/pack/pallas_call | solution.py:223
  3.4 4.0 %collective-permute-start.5 = (f32[280,128]{1,0:T(8,128)S(1)}, f32[280,128]{1,0:T(8,128)S(1)}, u32[]{:S(2)}, u32[]{:S(2)}) collective-permute-start(f32[280,128]{1,0:T(8,128)S(1)} %pack.1.refs_0_), channel_id=1, source_target_pairs={{6,0},{7,1},{4,2},{5,3},{2,4},{3,5},{0,6},{1,7},{14,8},{15,9},{12,... | collective-permute-start | bytes 430088 | tf_op jit(solution)/shard_map/ppermute | solution.py:502
  7.4 3.5 %collective-permute-start.3 = (f32[280,128]{1,0:T(8,128)S(1)}, f32[280,128]{1,0:T(8,128)S(1)}, u32[]{:S(2)}, u32[]{:S(2)}) collective-permute-start(f32[280,128]{1,0:T(8,128)S(1)} %pack.1.refs_0_), channel_id=1, source_target_pairs={{28,0},{5,1},{30,2},{7,3},{24,4},{1,5},{26,6},{3,7},{20,8},{13,9},... | collective-permute-start | bytes 430088 | tf_op jit(solution)/shard_map/ppermute | solution.py:502
  10.9 0.0 collective-permute-start.1
  10.9 0.0 collective-permute-start
  10.9 0.7 %collective-permute-done.5.refs_6_ = f32[280,128]{1,0:T(8,128)S(1)} collective-permute-done((f32[280,128]{1,0:T(8,128)S(1)}, f32[280,128]{1,0:T(8,128)S(1)}, u32[]{:S(2)}, u32[]{:S(2)}) %collective-permute-start.5) | collective-permute-done | bytes 143392 | tf_op jit(solution)/shard_map/ppermute | solution.py:502
  11.6 0.0 collective-permute-start.6
  11.6 4.2 %collective-permute-done.3.refs_4_ = f32[280,128]{1,0:T(8,128)S(1)} collective-permute-done((f32[280,128]{1,0:T(8,128)S(1)}, f32[280,128]{1,0:T(8,128)S(1)}, u32[]{:S(2)}, u32[]{:S(2)}) %collective-permute-start.3) | collective-permute-done | bytes 143392 | tf_op jit(solution)/shard_map/ppermute | solution.py:502
  15.8 0.0 collective-permute-start.4
  15.8 2.1 %collective-permute-done.1.refs_2_ = f32[280,128]{1,0:T(8,128)S(1)} collective-permute-done((f32[280,128]{1,0:T(8,128)S(1)}, f32[280,128]{1,0:T(8,128)S(1)}, u32[]{:S(2)}, u32[]{:S(2)}) %collective-permute-start.1) | collective-permute-done | bytes 143392 | tf_op jit(solution)/shard_map/ppermute | solution.py:502
  17.9 0.0 collective-permute-start.2
  17.9 0.0 collective-permute-done.refs_1_
  17.9 0.0 collective-permute-done.6.refs_7_
  17.9 0.0 collective-permute-done.4.refs_5_
  17.9 1.3 %collective-permute-done.2.refs_3_ = f32[280,128]{1,0:T(8,128)S(1)} collective-permute-done((f32[280,128]{1,0:T(8,128)S(1)}, f32[280,128]{1,0:T(8,128)S(1)}, u32[]{:S(2)}, u32[]{:S(2)}) %collective-permute-start.2) | collective-permute-done | bytes 143392 | tf_op jit(solution)/shard_map/ppermute | solution.py:502
  19.3 15.0 %solve.1 = (f32[2,64,64]{2,1,0:T(8,128)}, f32[2,64,64]{2,1,0:T(8,128)}) custom-call(f32[280,128]{1,0:T(8,128)S(1)} %pack.1.refs_0_, f32[280,128]{1,0:T(8,128)S(1)} %collective-permute-done.refs_1_, f32[280,128]{1,0:T(8,128)S(1)} %collective-permute-done.1.refs_2_, f32[280,128]{1,0:T(8,128)S(1)} %collective-permute-done.2.refs_3_, ...), custom_call_target="tpu_custom_call" | custom-call | tf_op jit(solution)/shard_map/solve/pallas_call | solution.py:517
Async XLA Ops:
  1.3 0.9 %copy-start = (f32[16,2,1024]{2,1,0:T(2,128)S(1)}, f32[16,2,1024]{2,1,0:T(2,128)}, u32[]{:S(2)}) copy-start(f32[16,2,1024]{2,1,0:T(2,128)} %param.3) | copy-start | bytes 393220
  2.2 0.7 %copy-start.1 = (f32[2,1024]{1,0:T(2,128)S(1)}, f32[2,1024]{1,0:T(2,128)}, u32[]{:S(2)}) copy-start(f32[2,1024]{1,0:T(2,128)} %param.4) | copy-start | bytes 24580
  3.4 8.2 %collective-permute-start.5 = (f32[280,128]{1,0:T(8,128)S(1)}, f32[280,128]{1,0:T(8,128)S(1)}, u32[]{:S(2)}, u32[]{:S(2)}) collective-permute-start(f32[280,128]{1,0:T(8,128)S(1)} %pack.1.refs_0_), channel_id=1, source_target_pairs={{6,0},{7,1},{4,2},{5,3},{2,4},{3,5},{0,6},{1,7},{14,8},{15,9},{12,... | collective-permute-start | bytes 430088 | tf_op jit(solution)/shard_map/ppermute | solution.py:502
  7.4 8.4 %collective-permute-start.3 = (f32[280,128]{1,0:T(8,128)S(1)}, f32[280,128]{1,0:T(8,128)S(1)}, u32[]{:S(2)}, u32[]{:S(2)}) collective-permute-start(f32[280,128]{1,0:T(8,128)S(1)} %pack.1.refs_0_), channel_id=1, source_target_pairs={{28,0},{5,1},{30,2},{7,3},{24,4},{1,5},{26,6},{3,7},{20,8},{13,9},... | collective-permute-start | bytes 430088 | tf_op jit(solution)/shard_map/ppermute | solution.py:502
  10.9 7.0 %collective-permute-start.1 = (f32[280,128]{1,0:T(8,128)S(1)}, f32[280,128]{1,0:T(8,128)S(1)}, u32[]{:S(2)}, u32[]{:S(2)}) collective-permute-start(f32[280,128]{1,0:T(8,128)S(1)} %pack.1.refs_0_), channel_id=1, source_target_pairs={{10,0},{19,1},{8,2},{17,3},{14,4},{23,5},{12,6},{21,7},{2,8},{27,9... | collective-permute-start | bytes 430088 | tf_op jit(solution)/shard_map/ppermute | solution.py:502
  10.9 7.0 %collective-permute-start = (f32[280,128]{1,0:T(8,128)S(1)}, f32[280,128]{1,0:T(8,128)S(1)}, u32[]{:S(2)}, u32[]{:S(2)}) collective-permute-start(f32[280,128]{1,0:T(8,128)S(1)} %pack.1.refs_0_), channel_id=1, source_target_pairs={{1,0},{0,1},{3,2},{2,3},{5,4},{4,5},{7,6},{6,7},{9,8},{8,9},{11,10... | collective-permute-start | bytes 430088 | tf_op jit(solution)/shard_map/ppermute | solution.py:502
  11.6 6.3 %collective-permute-start.6 = (f32[280,128]{1,0:T(8,128)S(1)}, f32[280,128]{1,0:T(8,128)S(1)}, u32[]{:S(2)}, u32[]{:S(2)}) collective-permute-start(f32[280,128]{1,0:T(8,128)S(1)} %collective-permute-done.5.refs_6_), channel_id=1, source_target_pairs={{1,0},{0,1},{3,2},{2,3},{5,4},{4,5},{7,6},{6,7},{9,8},{8,9},{11,10... | collective-permute-start | bytes 430088 | tf_op jit(solution)/shard_map/ppermute | solution.py:502
  15.8 2.1 %collective-permute-start.4 = (f32[280,128]{1,0:T(8,128)S(1)}, f32[280,128]{1,0:T(8,128)S(1)}, u32[]{:S(2)}, u32[]{:S(2)}) collective-permute-start(f32[280,128]{1,0:T(8,128)S(1)} %collective-permute-done.3.refs_4_), channel_id=1, source_target_pairs={{1,0},{0,1},{3,2},{2,3},{5,4},{4,5},{7,6},{6,7},{9,8},{8,9},{11,10... | collective-permute-start | bytes 430088 | tf_op jit(solution)/shard_map/ppermute | solution.py:502
  17.9 1.4 %collective-permute-start.2 = (f32[280,128]{1,0:T(8,128)S(1)}, f32[280,128]{1,0:T(8,128)S(1)}, u32[]{:S(2)}, u32[]{:S(2)}) collective-permute-start(f32[280,128]{1,0:T(8,128)S(1)} %collective-permute-done.1.refs_2_), channel_id=1, source_target_pairs={{1,0},{0,1},{3,2},{2,3},{5,4},{4,5},{7,6},{6,7},{9,8},{8,9},{11,10... | collective-permute-start | bytes 430088 | tf_op jit(solution)/shard_map/ppermute | solution.py:502

commit v5 on v4

--- a/solution.py
+++ b/solution.py
@@ -165,6 +165,7 @@
 LANES = Y_OUT * X_OUT
 SUB = 8
 BASIS = ITERS + 1
+CORES = 2
 H_SCALE = 2.0 / COEF_NEAR
 FAR_SCALED = 0.5 * H_SCALE * COEF_FAR
 
@@ -201,18 +202,21 @@
                         moved = pltpu.roll(pieces[column], (column - m) * block % LANES, 1)
                         value = jnp.where(lane_block == column, moved, value)
                 start = ((deep * ROWS + m) * groups + group) * SUB
-                out[start : start + SUB, :] = value
+                out[0, start : start + SUB, :] = value
         piece = mixed[base + groups * columns * SUB :][:SUB]
         value = piece
         for far in range(1, columns):
             moved = pltpu.roll(pltpu.roll(piece, far * block, 1), columns - far, 0)
             value = jnp.where(lane_block == (row + far) % columns, moved, value)
         start = depth * ROWS * SUB * groups + deep * ROWS
-        out[start : start + ROWS, :] = value
-    out[out.shape[0] - SUB :, :] = jnp.full((SUB, LANES), counts[0].astype(jnp.float32))
-
-
-def packed_block(sources, potential, iter_counts):
+        out[0, start : start + ROWS, :] = value
+    size = out.shape[1]
+    out[0, size - SUB :, :] = jnp.full((SUB, LANES), counts[0].astype(jnp.float32))
+    for copy in range(1, out.shape[0]):
+        out[copy] = out[0]
+
+
+def packed_block(sources, potential, iter_counts, copies):
     count, depth, cells = sources.shape
     columns = cells // LANES
     rows = sources.reshape(count, depth, columns, LANES).transpose(0, 2, 1, 3)
@@ -222,7 +226,7 @@
     size = depth * ROWS * (count + 1) + SUB
     return pl.pallas_call(
         functools.partial(pack_kernel, depth, count // SUB),
-        out_shape=jax.ShapeDtypeStruct((size, LANES), jnp.float32),
+        out_shape=jax.ShapeDtypeStruct((copies, size, LANES), jnp.float32),
         in_specs=[smem, vmem, vmem],
         out_specs=vmem,
         compiler_params=pltpu.CompilerParams(vmem_limit_bytes=4 * 2**20),
@@ -375,11 +379,9 @@
     )
 
 
-def solve_kernel(parts, points, count, *refs):
-    blocks = refs[:parts]
-    out_b, out_a = refs[parts : parts + 2]
-    vectors = refs[parts + 2 : parts + 2 + BASIS]
-    applied, diagonal, gram, limits = refs[parts + 2 + BASIS :]
+def solve_kernel(parts, points, count, mine, other, out_b, out_a, *refs):
+    vectors = refs[:BASIS]
+    applied, diagonal, gram, limits = refs[BASIS:]
     planes = diagonal.shape[0]
     depth = planes // parts
     groups = count // SUB
@@ -387,18 +389,20 @@
     last_x = lax.rem(lane, X_OUT) == X_OUT - 1
     first_x = lax.rem(lane, X_OUT) == 0
     here = lax.axis_index("dom")
-    point_here = lax.axis_index("point")
-    core = jnp.bitwise_and(here, 1)
-
-    for turn in range(parts):
-        slab = jnp.bitwise_xor(here, turn) * depth
-        for deep in range(depth):
-            for m in range(ROWS):
-                start = (deep * ROWS + m) * count
-                lanes = pl.ds(m * LANES, LANES)
-                vectors[0][slab + deep, :, lanes] = blocks[turn][start : start + count, :]
-            start = depth * ROWS * count + deep * ROWS
-            diagonal[slab + deep] = H_SCALE * (blocks[turn][start : start + ROWS, :] + 3.75)
+    core = jnp.bitwise_and(here, CORES - 1)
+    origin = jnp.bitwise_xor(lax.axis_index("point"), here // CORES)
+
+    for chip in range(parts // CORES):
+        for block, side in ((mine, core), (other, 1 - core)):
+            slab = (chip * CORES + side) * depth
+            for deep in range(depth):
+                for m in range(ROWS):
+                    start = (deep * ROWS + m) * count
+                    lanes = pl.ds(m * LANES, LANES)
+                    vectors[0][slab + deep, :, lanes] = block[chip, start : start + count, :]
+                start = depth * ROWS * count + deep * ROWS
+                levels = block[chip, start : start + ROWS, :]
+                diagonal[slab + deep] = H_SCALE * (levels + 3.75)
 
     blank = jnp.zeros((SUB, LANES), jnp.float32)
     alphas, norms = [], []
@@ -465,11 +469,11 @@
     cross = gram[:, size:]
     pairs = gram[:, :size] + cross + cross.T
 
-    tails = [block[block.shape[0] - SUB :, :] for block in blocks]
-    limits[point_here] = tails[0]
-    limits[jnp.bitwise_xor(point_here, 1 + core)] = tails[2]
-    limits[jnp.bitwise_xor(point_here, 2 - core)] = tails[3]
-    limits[jnp.bitwise_xor(point_here, 3)] = jnp.where(core == 0, tails[4], tails[5])
+    tail = mine.shape[1] - SUB
+    for chip in range(parts // CORES):
+        limits[jnp.bitwise_xor(origin, chip)] = jnp.where(
+            core == 0, mine[chip, tail:, :], other[chip, tail:, :]
+        )
     bounds = [jnp.concatenate([limits[j]] * groups, axis=0) for j in range(points)]
     alphas = [jnp.concatenate(value, axis=0) for value in alphas]
     norms = [jnp.concatenate(value, axis=0) for value in norms]
@@ -490,25 +494,29 @@
     out_a[1] = imag[:, half:]
 
 
-CROSSING = {2: (1, 2), 4: (3, 0), 6: (0, 0)}
-
-
-def exchanged(values, mask, parts, points):
-    pairs = []
-    for point in range(points):
-        for part in range(parts):
-            other = CROSSING[mask][part % 2] if mask in CROSSING else 0
-            pairs.append(((point ^ other) * parts + (part ^ mask), point * parts + part))
-    return lax.ppermute(values, ("point", "dom"), pairs)
+def chip_groups(parts, points):
+    groups = []
+    for core in range(CORES):
+        for base in range(points):
+            groups.append(
+                [
+                    ((base ^ chip) if core == 0 else base) * parts + chip * CORES + core
+                    for chip in range(parts // CORES)
+                ]
+            )
+    return groups
 
 
 def whole_grid(sources, potential, iter_counts, *, parts, points):
     count, depth, _ = sources.shape
     planes = parts * depth
-    block = packed_block(sources, potential, iter_counts)
-    even = [block] + [exchanged(block, mask, parts, points) for mask in range(2, parts, 2)]
-    odd = [exchanged(value, 1, parts, points) for value in even]
-    blocks = [value for pair in zip(even, odd) for value in pair]
+    chips = parts // CORES
+    copies = packed_block(sources, potential, iter_counts, chips)
+    near = lax.all_to_all(
+        copies, ("point", "dom"), 0, 0, axis_index_groups=chip_groups(parts, points), tiled=True
+    )
+    swap = [(part ^ 1, part) for part in range(parts)]
+    blocks = [near, lax.ppermute(near, "dom", swap)]
     vmem = pl.BlockSpec(memory_space=pltpu.VMEM)
     size = BASIS * count
     width = MOMENTS * count
@@ -517,7 +525,7 @@
     return pl.pallas_call(
         functools.partial(solve_kernel, parts, points, count),
         out_shape=(out, out),
-        in_specs=[vmem] * parts,
+        in_specs=[vmem] * CORES,
         out_specs=(vmem, vmem),
         scratch_shapes=[vector] * (BASIS + 1)
         + [

time: 34.4 us -> 40.4 us (1.17)
  blocking collectives: 0 us -> 19.7 us
  starting transfers between devices: 7.52 us -> 0.01 us
  waiting for transfers between devices: 8.3 us -> 1.98 us
    all_to_all x0 -> x1, blocking collectives: none -> 19.7 us  [whole_grid(): lax.all_to_all(copies, ('point', 'dom'), 0, 0, axis_index_groups=chip_gro...]
    ppermute x7 -> x1, starting transfers between devices: 7.52 us -> 0.01 us  [whole_grid(): blocks = [near, lax.ppermute(near, 'dom', swap)]]
    ppermute x7 -> x1, waiting for transfers between devices: 8.3 us -> 1.98 us  [whole_grid(): blocks = [near, lax.ppermute(near, 'dom', swap)]]
  transfers between devices with their start and end apart: 7 -> 1, of which waited for: 4 -> 1; matrix products, arithmetic and copies ran while one was open for 0% -> 0% of each run, Pallas kernels for 0% -> 0%
where the time goes in v5:
time: 40.4 us; the launch traced here: 40.1 us
  blocking collectives  19.7 us (49%)
  Pallas kernels  15.5 us (38%)
  waiting for transfers between devices  1.98 us (5%)
  local copies, waits for them, and re-layouts  1.59 us (4%)
  between operations  1.3 us (3%)
    all_to_all x1, blocking collectives, whole_grid(): lax.all_to_all(copies, ('point', 'dom'), 0, 0, axis_index_groups=chip_gro...  19.7 us
    pallas_call x1, Pallas kernels, whole_grid(): pl.pallas_call(functools.partial(solve_kernel, parts, points, count), out...  15 us
    ppermute x1, waiting for transfers between devices, whole_grid(): blocks = [near, lax.ppermute(near, 'dom', swap)]  1.98 us
    unnamed x4, local copies, waits for them, and re-layouts  1.59 us
  transfers between devices with their start and end apart: 1, of which 1 were waited for; matrix products, arithmetic and copies ran while one was open for 0% of the time, Pallas kernels for 0%

profile of v5, /device:TPU:0, one launch (start us, length us, event | category | flops | bytes accessed | tf_op | source)
XLA Modules:
  0.0 40.1 jit_solution(9800216845775168620)
XLA Ops:
  1.3 0.0 copy-start
  1.3 0.9 %copy-done = f32[16,2,1024]{2,1,0:T(2,128)S(1)} copy-done((f32[16,2,1024]{2,1,0:T(2,128)S(1)}, f32[16,2,1024]{2,1,0:T(2,128)}, u32[]{:S(2)}) %copy-start) | copy-done | bytes 131096
  2.2 0.0 copy-start.1
  2.2 0.7 %copy-done.1 = f32[2,1024]{1,0:T(2,128)S(1)} copy-done((f32[2,1024]{1,0:T(2,128)S(1)}, f32[2,1024]{1,0:T(2,128)}, u32[]{:S(2)}) %copy-start.1) | copy-done | bytes 8216
  2.9 0.6 %pack.1 = f32[4,280,128]{2,1,0:T(8,128)S(1)} custom-call(s32[1]{0:T(128)S(6)} %copy.7.counts, f32[256,128]{1,0:T(8,128)S(1)} %bitcast.10, f32[16,128]{1,0:T(8,128)S(1)} %bitcast.11), custom_call_target="tpu_custom_call" | custom-call | tf_op jit(solution)/shard_map/pack/pallas_call | solution.py:227
  3.4 19.7 %all_to_all.5.mine = f32[4,280,128]{2,1,0:T(8,128)S(1)} all-to-all(f32[4,280,128]{2,1,0:T(8,128)S(1)} %pack.1), channel_id=1, replica_groups={{0,10,20,30},{8,2,28,22},{16,26,4,14},{24,18,12,6},{1,3,5,7},{9,11,13,1..., dimensions={0} | all-to-all | bytes 1146880 | tf_op jit(solution)/shard_map/all_to_all | solution.py:515
  23.2 0.0 collective-permute-start
  23.2 2.0 %collective-permute-done.other = f32[4,280,128]{2,1,0:T(8,128)S(1)} collective-permute-done((f32[4,280,128]{2,1,0:T(8,128)S(1)}, f32[4,280,128]{2,1,0:T(8,128)S(1)}, u32[]{:S(2)}, u32[]{:S(2)}) %collective-permute-start) | collective-permute-done | bytes 573472 | tf_op jit(solution)/shard_map/ppermute | solution.py:519
  25.1 15.0 %solve.1 = (f32[2,64,64]{2,1,0:T(8,128)}, f32[2,64,64]{2,1,0:T(8,128)}) custom-call(f32[4,280,128]{2,1,0:T(8,128)S(1)} %all_to_all.5.mine, f32[4,280,128]{2,1,0:T(8,128)S(1)} %collective-permute-done.other), custom_call_target="tpu_custom_call" | custom-call | tf_op jit(solution)/shard_map/solve/pallas_call | solution.py:525
Async XLA Ops:
  1.3 0.9 %copy-start = (f32[16,2,1024]{2,1,0:T(2,128)S(1)}, f32[16,2,1024]{2,1,0:T(2,128)}, u32[]{:S(2)}) copy-start(f32[16,2,1024]{2,1,0:T(2,128)} %param.3) | copy-start | bytes 393220
  2.2 0.7 %copy-start.1 = (f32[2,1024]{1,0:T(2,128)S(1)}, f32[2,1024]{1,0:T(2,128)}, u32[]{:S(2)}) copy-start(f32[2,1024]{1,0:T(2,128)} %param.4) | copy-start | bytes 24580
  23.2 2.0 %collective-permute-start = (f32[4,280,128]{2,1,0:T(8,128)S(1)}, f32[4,280,128]{2,1,0:T(8,128)S(1)}, u32[]{:S(2)}, u32[]{:S(2)}) collective-permute-start(f32[4,280,128]{2,1,0:T(8,128)S(1)} %all_to_all.5.mine), channel_id=1, source_target_pairs={{1,0},{0,1},{3,2},{2,3},{5,4},{4,5},{7,6},{6,7},{9,8},{8,9},{11,10... | collective-permute-start | bytes 1720328 | tf_op jit(solution)/shard_map/ppermute | solution.py:519

commit v6 on v5

--- a/solution.py
+++ b/solution.py
@@ -166,11 +166,12 @@
 SUB = 8
 BASIS = ITERS + 1
 CORES = 2
+TOGETHER = 4
 H_SCALE = 2.0 / COEF_NEAR
 FAR_SCALED = 0.5 * H_SCALE * COEF_FAR
 
 
-def pack_kernel(depth, groups, counts, rows, levels, out):
+def pack_kernel(depth, groups, counts, rows, levels, out, count_tile):
     columns = rows.shape[0] // (SUB * groups * depth)
     source = lax.broadcasted_iota(jnp.int32, (LANES, LANES), 0)
     target = lax.broadcasted_iota(jnp.int32, (LANES, LANES), 1)
@@ -210,8 +211,7 @@
             value = jnp.where(lane_block == (row + far) % columns, moved, value)
         start = depth * ROWS * SUB * groups + deep * ROWS
         out[0, start : start + ROWS, :] = value
-    size = out.shape[1]
-    out[0, size - SUB :, :] = jnp.full((SUB, LANES), counts[0].astype(jnp.float32))
+    count_tile[...] = jnp.full((SUB, LANES), counts[0].astype(jnp.float32))
     for copy in range(1, out.shape[0]):
         out[copy] = out[0]
 
@@ -223,12 +223,15 @@
     levels = potential.reshape(depth, columns, LANES).transpose(1, 0, 2)
     vmem = pl.BlockSpec(memory_space=pltpu.VMEM)
     smem = pl.BlockSpec(memory_space=pltpu.SMEM)
-    size = depth * ROWS * (count + 1) + SUB
+    size = depth * ROWS * (count + 1)
     return pl.pallas_call(
         functools.partial(pack_kernel, depth, count // SUB),
-        out_shape=jax.ShapeDtypeStruct((copies, size, LANES), jnp.float32),
+        out_shape=(
+            jax.ShapeDtypeStruct((copies, size, LANES), jnp.float32),
+            jax.ShapeDtypeStruct((SUB, LANES), jnp.float32),
+        ),
         in_specs=[smem, vmem, vmem],
-        out_specs=vmem,
+        out_specs=(vmem, vmem),
         compiler_params=pltpu.CompilerParams(vmem_limit_bytes=4 * 2**20),
         name="pack",
     )(iter_counts, rows.reshape(-1, LANES), levels.reshape(-1, LANES))
@@ -250,33 +253,35 @@
     return jnp.where(wrap_mask, pltpu.roll(values, LANES - X_OUT + 1, 1), pltpu.roll(values, 1, 1))
 
 
-def apply_plane(vector, diagonal, plane, planes, group, last_x, first_x):
+def apply_planes(vector, diagonal, first, count, group, last_x, first_x):
+    planes = vector.shape[0]
     rows = pl.ds(group * SUB, SUB)
-
-    def plane_at(index):
-        return [vector[index, rows, pl.ds(m * LANES, LANES)] for m in range(ROWS)]
-
-    here = plane_at(plane)
-    above, below = (plane_at(lax.rem(plane + far, planes)) for far in (1, planes - 1))
-    above_2, below_2 = (plane_at(lax.rem(plane + far, planes)) for far in (2, planes - 2))
-    y_up = [pltpu.roll(value, LANES - X_OUT, 1) for value in here]
-    y_down = [pltpu.roll(value, X_OUT, 1) for value in here]
-    out = []
-    for yi in range(Y_IN):
-        line = here[yi * X_IN : (yi + 1) * X_IN]
-        before = [x_prev(line[X_IN - 2], first_x), x_prev(line[X_IN - 1], first_x)]
-        after = [x_next(line[0], last_x), x_next(line[1], last_x)]
-        wide = before + line + after
-        for xi in range(X_IN):
-            m = yi * X_IN + xi
-            other = (1 - yi) * X_IN + xi
-            y_next = here[other] if yi == 0 else y_up[other]
-            y_prev = here[other] if yi == 1 else y_down[other]
-            near = (wide[xi + 1] + wide[xi + 3]) + (y_next + y_prev) + (above[m] + below[m])
-            far = (wide[xi] + wide[xi + 4]) + (y_up[m] + y_down[m]) + (above_2[m] + below_2[m])
-            level = diagonal[plane, pl.ds(m, 1), :]
-            out.append(level * here[m] - near - FAR_SCALED * far)
-    return here, out
+    held = {}
+    for far in range(-2, count + 2):
+        index = jnp.bitwise_and(first + (far + planes), planes - 1)
+        held[far] = [vector[index, rows, pl.ds(m * LANES, LANES)] for m in range(ROWS)]
+    for plane in range(count):
+        here, above, below = held[plane], held[plane + 1], held[plane - 1]
+        above_2, below_2 = held[plane + 2], held[plane - 2]
+        y_up = [pltpu.roll(value, LANES - X_OUT, 1) for value in here]
+        y_down = [pltpu.roll(value, X_OUT, 1) for value in here]
+        out = []
+        for yi in range(Y_IN):
+            line = here[yi * X_IN : (yi + 1) * X_IN]
+            before = [x_prev(line[X_IN - 2], first_x), x_prev(line[X_IN - 1], first_x)]
+            after = [x_next(line[0], last_x), x_next(line[1], last_x)]
+            wide = before + line + after
+            for xi in range(X_IN):
+                m = yi * X_IN + xi
+                other = (1 - yi) * X_IN + xi
+                y_next = here[other] if yi == 0 else y_up[other]
+                y_prev = here[other] if yi == 1 else y_down[other]
+                near = (wide[xi + 1] + wide[xi + 3]) + (y_next + y_prev) + (above[m] + below[m])
+                far = (wide[xi] + wide[xi + 4]) + (y_up[m] + y_down[m])
+                far = far + (above_2[m] + below_2[m])
+                level = diagonal[first + plane, pl.ds(m, 1), :]
+                out.append(level * here[m] - near - FAR_SCALED * far)
+        yield here, out
 
 
 def cmul(first, second):
@@ -379,18 +384,15 @@
     )
 
 
-def solve_kernel(parts, points, count, mine, other, out_b, out_a, *refs):
-    vectors = refs[:BASIS]
-    applied, diagonal, gram, limits = refs[BASIS:]
+def krylov_kernel(parts, count, mine, other, *refs):
+    vectors, (scalars, applied, diagonal) = refs[:BASIS], refs[BASIS:]
     planes = diagonal.shape[0]
     depth = planes // parts
     groups = count // SUB
     lane = lax.broadcasted_iota(jnp.int32, (SUB, LANES), 1)
     last_x = lax.rem(lane, X_OUT) == X_OUT - 1
     first_x = lax.rem(lane, X_OUT) == 0
-    here = lax.axis_index("dom")
-    core = jnp.bitwise_and(here, CORES - 1)
-    origin = jnp.bitwise_xor(lax.axis_index("point"), here // CORES)
+    core = jnp.bitwise_and(lax.axis_index("dom"), CORES - 1)
 
     for chip in range(parts // CORES):
         for block, side in ((mine, core), (other, 1 - core)):
@@ -409,21 +411,23 @@
     for i in range(ITERS):
         source, target = vectors[i], applied if i < ITERS - 1 else vectors[ITERS]
 
-        def apply_turn(plane, sums, i=i, source=source, target=target):
+        def apply_turn(turn, sums, i=i, source=source, target=target):
+            first = turn * TOGETHER
             new_sums = []
             for group in range(groups):
                 rows = pl.ds(group * SUB, SUB)
                 curve, norm = sums[group]
-                value, out = apply_plane(source, diagonal, plane, planes, group, last_x, first_x)
-                for m in range(ROWS):
-                    target[plane, rows, pl.ds(m * LANES, LANES)] = out[m]
-                    curve = curve + value[m] * out[m]
-                    if i == 0:
-                        norm = norm + value[m] * value[m]
+                done = apply_planes(source, diagonal, first, TOGETHER, group, last_x, first_x)
+                for plane, (value, out) in enumerate(done):
+                    for m in range(ROWS):
+                        target[first + plane, rows, pl.ds(m * LANES, LANES)] = out[m]
+                        curve = curve + value[m] * out[m]
+                        if i == 0:
+                            norm = norm + value[m] * value[m]
                 new_sums.append((curve, norm))
             return tuple(new_sums)
 
-        sums = lax.fori_loop(0, planes, apply_turn, ((blank, blank),) * groups, unroll=4)
+        sums = lax.fori_loop(0, planes // TOGETHER, apply_turn, ((blank, blank),) * groups)
         if i == 0:
             norms.append([lane_sum(norm) for _, norm in sums])
         alphas.append([ratio(lane_sum(sums[g][0]), norms[i][g]) for g in range(groups)])
@@ -447,9 +451,17 @@
                 new_sums.append(norm)
             return tuple(new_sums)
 
-        sums = lax.fori_loop(0, planes, step_turn, (blank,) * groups, unroll=4)
+        sums = lax.fori_loop(0, planes, step_turn, (blank,) * groups, unroll=TOGETHER)
         norms.append([lane_sum(norm) for norm in sums])
-
+    for i, value in enumerate(alphas + norms):
+        scalars[i] = jnp.concatenate(value, axis=0)
+
+
+def gram_kernel(points, scalars, *refs):
+    tiles, vectors = refs[:points], refs[points : points + BASIS]
+    out_b, out_a, gram, limits = refs[points + BASIS :]
+    planes, count, _ = vectors[0].shape
+    groups = count // SUB
     size = BASIS * count
     gram[...] = jnp.zeros_like(gram)
 
@@ -465,18 +477,16 @@
         )
         return carry
 
-    lax.fori_loop(0, planes, gram_turn, 0, unroll=4)
+    lax.fori_loop(0, planes, gram_turn, 0, unroll=TOGETHER)
     cross = gram[:, size:]
     pairs = gram[:, :size] + cross + cross.T
 
-    tail = mine.shape[1] - SUB
-    for chip in range(parts // CORES):
-        limits[jnp.bitwise_xor(origin, chip)] = jnp.where(
-            core == 0, mine[chip, tail:, :], other[chip, tail:, :]
-        )
+    here = lax.axis_index("point")
+    for far, tile in enumerate(tiles):
+        limits[jnp.bitwise_xor(here, far)] = tile[...]
     bounds = [jnp.concatenate([limits[j]] * groups, axis=0) for j in range(points)]
-    alphas = [jnp.concatenate(value, axis=0) for value in alphas]
-    norms = [jnp.concatenate(value, axis=0) for value in norms]
+    alphas = [scalars[i] for i in range(ITERS)]
+    norms = [scalars[ITERS + i] for i in range(ITERS)]
     weights = weights_of(alphas, norms, bounds, count)
     real = jnp.concatenate([pair[0] for pair in weights], axis=0)
     imag = jnp.concatenate([pair[1] for pair in weights], axis=0)
@@ -494,48 +504,52 @@
     out_a[1] = imag[:, half:]
 
 
-def chip_groups(parts, points):
-    groups = []
-    for core in range(CORES):
-        for base in range(points):
-            groups.append(
-                [
-                    ((base ^ chip) if core == 0 else base) * parts + chip * CORES + core
-                    for chip in range(parts // CORES)
-                ]
-            )
-    return groups
-
-
 def whole_grid(sources, potential, iter_counts, *, parts, points):
     count, depth, _ = sources.shape
     planes = parts * depth
     chips = parts // CORES
-    copies = packed_block(sources, potential, iter_counts, chips)
-    near = lax.all_to_all(
-        copies, ("point", "dom"), 0, 0, axis_index_groups=chip_groups(parts, points), tiled=True
-    )
-    swap = [(part ^ 1, part) for part in range(parts)]
-    blocks = [near, lax.ppermute(near, "dom", swap)]
+    copies, tile = packed_block(sources, potential, iter_counts, chips)
+    same_core = [list(range(core, parts, CORES)) for core in range(CORES)]
+    mine = lax.all_to_all(copies, "dom", 0, 0, axis_index_groups=same_core, tiled=True)
+    other = lax.ppermute(mine, "dom", [(part ^ 1, part) for part in range(parts)])
+    tiles = [tile] + [
+        lax.ppermute(tile, "point", [(point ^ far, point) for point in range(points)])
+        for far in range(1, points)
+    ]
     vmem = pl.BlockSpec(memory_space=pltpu.VMEM)
+    vector = (planes, count, ROWS * LANES)
+    cells = planes * ROWS * LANES
+    *vectors, scalars = pl.pallas_call(
+        functools.partial(krylov_kernel, parts, count),
+        out_shape=[jax.ShapeDtypeStruct(vector, jnp.float32)] * BASIS
+        + [jax.ShapeDtypeStruct((2 * ITERS, count, LANES), jnp.float32)],
+        in_specs=[vmem] * CORES,
+        out_specs=[vmem] * (BASIS + 1),
+        scratch_shapes=[
+            pltpu.VMEM(vector, jnp.float32),
+            pltpu.VMEM((planes, ROWS, LANES), jnp.float32),
+        ],
+        compiler_params=pltpu.CompilerParams(vmem_limit_bytes=16 * 2**20),
+        cost_estimate=pl.CostEstimate(
+            flops=ITERS * count * cells * 30, bytes_accessed=32 * 2**20, transcendentals=0
+        ),
+        name="krylov",
+    )(mine, other)
     size = BASIS * count
     width = MOMENTS * count
     out = jax.ShapeDtypeStruct((2, width, width), jnp.float32)
-    vector = pltpu.VMEM((planes, count, ROWS * LANES), jnp.float32)
     return pl.pallas_call(
-        functools.partial(solve_kernel, parts, points, count),
+        functools.partial(gram_kernel, points),
         out_shape=(out, out),
-        in_specs=[vmem] * CORES,
+        in_specs=[vmem] * (1 + points + BASIS),
         out_specs=(vmem, vmem),
-        scratch_shapes=[vector] * (BASIS + 1)
-        + [
-            pltpu.VMEM((planes, ROWS, LANES), jnp.float32),
+        scratch_shapes=[
             pltpu.VMEM((size, 2 * size), jnp.float32),
             pltpu.VMEM((points, SUB, LANES), jnp.float32),
         ],
-        compiler_params=pltpu.CompilerParams(vmem_limit_bytes=32 * 2**20),
-        name="solve",
-    )(*blocks)
+        compiler_params=pltpu.CompilerParams(vmem_limit_bytes=16 * 2**20),
+        name="gram",
+    )(scalars, *tiles, *vectors)
 
 
 def on_device(sources, potential, iter_counts):
@@ -548,6 +562,7 @@
         and points == 4
         and count == 2 * SUB
         and 2 * MOMENTS * count == LANES
+        and parts * depth == 16
         and cells == GX * GX == ROWS * LANES
     )
     if not fits:

time: 40.4 us -> 37.2 us (0.921)
  blocking collectives: 19.7 us -> 14.1 us
  starting transfers between devices: 0.01 us -> 4.39 us
  waiting for transfers between devices: 1.98 us -> 0.01 us
    all_to_all x1, blocking collectives: 19.7 us -> 14.1 us  [whole_grid(): lax.all_to_all(copies, 'dom', 0, 0, axis_index_groups=same_core, tiled=True)]
    ppermute x1 -> x4, starting transfers between devices: 0.01 us -> 4.39 us  [the longest x3 4.39 us: whole_grid(): lax.ppermute(tile, 'point', [(point ^ far, point) for point in range(poin...]
    ppermute x1 -> x4, waiting for transfers between devices: 1.98 us -> 0.01 us  [the longest x3 0.01 us: whole_grid(): lax.ppermute(tile, 'point', [(point ^ far, point) for point in range(poin...]
    pallas_call x1 -> x2, Pallas kernels: 15 us -> 15 us  [the longest x1 10.3 us: whole_grid(): pl.pallas_call(functools.partial(krylov_kernel, parts, count), out_shape=...]
  transfers between devices with their start and end apart: 1 -> 4, of which waited for: 1 -> 0; matrix products, arithmetic and copies ran while one was open for 0% -> 0% of each run, Pallas kernels for 0% -> 28%
where the time goes in v6:
time: 37.2 us; the launch traced here: 37 us
  Pallas kernels  15.6 us (42%)
  blocking collectives  14.1 us (38%)
  starting transfers between devices  4.39 us (12%)
  local copies, waits for them, and re-layouts  1.59 us (4%)
  between operations  1.31 us (4%)
    all_to_all x1, blocking collectives, whole_grid(): lax.all_to_all(copies, 'dom', 0, 0, axis_index_groups=same_core, tiled=True)  14.1 us
    pallas_call x1, Pallas kernels, whole_grid(): pl.pallas_call(functools.partial(krylov_kernel, parts, count), out_shape=...  10.3 us
    pallas_call x1, Pallas kernels, whole_grid(): pl.pallas_call(functools.partial(gram_kernel, points), out_shape=(out, ou...  4.75 us
    ppermute x3, starting transfers between devices, whole_grid(): lax.ppermute(tile, 'point', [(point ^ far, point) for point in range(poin...  4.39 us
    unnamed x4, local copies, waits for them, and re-layouts  1.59 us
  transfers between devices with their start and end apart: 4, of which 0 were waited for; matrix products, arithmetic and copies ran while one was open for 0% of the time, Pallas kernels for 28%

profile of v6, /device:TPU:0, one launch (start us, length us, event | category | flops | bytes accessed | tf_op | source)
XLA Modules:
  0.0 37.0 jit_solution(13357580650378548539)
XLA Ops:
  1.3 0.0 copy-start
  1.3 0.9 %copy-done = f32[16,2,1024]{2,1,0:T(2,128)S(1)} copy-done((f32[16,2,1024]{2,1,0:T(2,128)S(1)}, f32[16,2,1024]{2,1,0:T(2,128)}, u32[]{:S(2)}) %copy-start) | copy-done | bytes 131096
  2.2 0.0 copy-start.1
  2.2 0.7 %copy-done.1 = f32[2,1024]{1,0:T(2,128)S(1)} copy-done((f32[2,1024]{1,0:T(2,128)S(1)}, f32[2,1024]{1,0:T(2,128)}, u32[]{:S(2)}) %copy-start.1) | copy-done | bytes 8216
  2.9 0.6 %pack.1 = (f32[4,272,128]{2,1,0:T(8,128)S(1)}, f32[8,128]{1,0:T(8,128)S(1)}) custom-call(s32[1]{0:T(128)S(6)} %copy.7.counts, f32[256,128]{1,0:T(8,128)S(1)} %bitcast.10, f32[16,128]{1,0:T(8,128)S(1)} %bitcast.11), custom_call_target="tpu_custom_call" | custom-call | tf_op jit(solution)/shard_map/pack/pallas_call | solution.py:227
  3.4 14.1 %all_to_all.5.mine = f32[4,272,128]{2,1,0:T(8,128)S(1)} all-to-all(f32[4,272,128]{2,1,0:T(8,128)S(1)} %get-tuple-element.12), channel_id=1, replica_groups={{0,2,4,6},{1,3,5,7},{8,10,12,14},{9,11,13,15},{16,18,20,22},{17,19,21,2..., dimensions={0} | all-to-all | bytes 1114112 | tf_op jit(solution)/shard_map/all_to_all | solution.py:513
  17.5 0.0 collective-permute-start
  17.5 1.6 %collective-permute-start.1 = (f32[8,128]{1,0:T(8,128)S(1)}, f32[8,128]{1,0:T(8,128)S(1)}, u32[]{:S(2)}, u32[]{:S(2)}) collective-permute-start(f32[8,128]{1,0:T(8,128)S(1)} %get-tuple-element.14.refs_0_), channel_id=1, source_target_pairs={{8,0},{0,8},{24,16},{16,24},{9,1},{1,9},{25,17},{17,25},{10,2},{2,... | collective-permute-start | bytes 12296 | tf_op jit(solution)/shard_map/ppermute | solution.py:516
  19.1 2.6 %collective-permute-start.2 = (f32[8,128]{1,0:T(8,128)S(1)}, f32[8,128]{1,0:T(8,128)S(1)}, u32[]{:S(2)}, u32[]{:S(2)}) collective-permute-start(f32[8,128]{1,0:T(8,128)S(1)} %get-tuple-element.14.refs_0_), channel_id=1, source_target_pairs={{16,0},{24,8},{0,16},{8,24},{17,1},{25,9},{1,17},{9,25},{18,2},{26... | collective-permute-start | bytes 12296 | tf_op jit(solution)/shard_map/ppermute | solution.py:516
  21.7 0.2 collective-permute-start.3
  21.9 0.0 collective-permute-done.other
  21.9 10.3 %krylov.1 = (f32[16,16,1024]{2,1,0:T(8,128)S(1)}, f32[16,16,1024]{2,1,0:T(8,128)S(1)}, f32[16,16,1024]{2,1,0:T(8,128)S(1)}, f32[16,16,1024]{2,1,0:T(8,128)S(1)},...) custom-call(f32[4,272,128]{2,1,0:T(8,128)S(1)} %all_to_all.5.mine, ...), custom_call_target="tpu_custom_call" | custom-call | flops 47185920 | bytes 33554432 | tf_op jit(solution)/shard_map/krylov/pallas_call | solution.py:522
  32.2 0.0 collective-permute-done.1.refs_1_
  32.2 0.0 collective-permute-done.2.refs_2_
  32.2 0.0 collective-permute-done.3.refs_3_
  32.2 4.8 %gram.1 = (f32[2,64,64]{2,1,0:T(8,128)}, f32[2,64,64]{2,1,0:T(8,128)}) custom-call(f32[12,16,128]{2,1,0:T(8,128)S(1)} %get-tuple-element.13.scalars, f32[8,128]{1,0:T(8,128)S(1)} %get-tuple-element.14.refs_0_, f32[8,128]{1,0:T(8,128)S(1)} %collective-permute-done.1.refs_1_, f32[8,128]{1,0:T(8,128)S(1)} %collective-permute-done.2.refs_2_, ...), custom_call_target="tpu_custom_call" | custom-call | tf_op jit(solution)/shard_map/gram/pallas_call | solution.py:541
Async XLA Ops:
  1.3 0.9 %copy-start = (f32[16,2,1024]{2,1,0:T(2,128)S(1)}, f32[16,2,1024]{2,1,0:T(2,128)}, u32[]{:S(2)}) copy-start(f32[16,2,1024]{2,1,0:T(2,128)} %param.3) | copy-start | bytes 393220
  2.2 0.7 %copy-start.1 = (f32[2,1024]{1,0:T(2,128)S(1)}, f32[2,1024]{1,0:T(2,128)}, u32[]{:S(2)}) copy-start(f32[2,1024]{1,0:T(2,128)} %param.4) | copy-start | bytes 24580
  17.5 4.4 %collective-permute-start = (f32[4,272,128]{2,1,0:T(8,128)S(1)}, f32[4,272,128]{2,1,0:T(8,128)S(1)}, u32[]{:S(2)}, u32[]{:S(2)}) collective-permute-start(f32[4,272,128]{2,1,0:T(8,128)S(1)} %all_to_all.5.mine), channel_id=1, source_target_pairs={{1,0},{0,1},{3,2},{2,3},{5,4},{4,5},{7,6},{6,7},{9,8},{8,9},{11,10... | collective-permute-start | bytes 1671176 | tf_op jit(solution)/shard_map/ppermute | solution.py:514
  17.5 14.7 %collective-permute-start.1 = (f32[8,128]{1,0:T(8,128)S(1)}, f32[8,128]{1,0:T(8,128)S(1)}, u32[]{:S(2)}, u32[]{:S(2)}) collective-permute-start(f32[8,128]{1,0:T(8,128)S(1)} %get-tuple-element.14.refs_0_), channel_id=1, source_target_pairs={{8,0},{0,8},{24,16},{16,24},{9,1},{1,9},{25,17},{17,25},{10,2},{2,... | collective-permute-start | bytes 12296 | tf_op jit(solution)/shard_map/ppermute | solution.py:516
  19.1 13.1 %collective-permute-start.2 = (f32[8,128]{1,0:T(8,128)S(1)}, f32[8,128]{1,0:T(8,128)S(1)}, u32[]{:S(2)}, u32[]{:S(2)}) collective-permute-start(f32[8,128]{1,0:T(8,128)S(1)} %get-tuple-element.14.refs_0_), channel_id=1, source_target_pairs={{16,0},{24,8},{0,16},{8,24},{17,1},{25,9},{1,17},{9,25},{18,2},{26... | collective-permute-start | bytes 12296 | tf_op jit(solution)/shard_map/ppermute | solution.py:516
  21.7 10.5 %collective-permute-start.3 = (f32[8,128]{1,0:T(8,128)S(1)}, f32[8,128]{1,0:T(8,128)S(1)}, u32[]{:S(2)}, u32[]{:S(2)}) collective-permute-start(f32[8,128]{1,0:T(8,128)S(1)} %get-tuple-element.14.refs_0_), channel_id=1, source_target_pairs={{24,0},{16,8},{8,16},{0,24},{25,1},{17,9},{9,17},{1,25},{26,2},{18... | collective-permute-start | bytes 12296 | tf_op jit(solution)/shard_map/ppermute | solution.py:516

commit v7 on v6

--- a/solution.py
+++ b/solution.py
@@ -171,8 +171,9 @@
 FAR_SCALED = 0.5 * H_SCALE * COEF_FAR
 
 
-def pack_kernel(depth, groups, counts, rows, levels, out, count_tile):
-    columns = rows.shape[0] // (SUB * groups * depth)
+def pack_kernel(depth, groups, rows, out):
+    columns = rows.shape[0] // (SUB * groups * depth + depth)
+    first_level = columns * SUB * groups * depth
     source = lax.broadcasted_iota(jnp.int32, (LANES, LANES), 0)
     target = lax.broadcasted_iota(jnp.int32, (LANES, LANES), 1)
     inner = target // (LANES // ROWS)
@@ -185,7 +186,7 @@
             for column in range(columns):
                 start = (group * SUB * columns + column) * depth + deep
                 parts.append(rows[pl.ds(start, SUB, stride=columns * depth), :])
-        parts.append(levels[pl.ds(deep, columns, stride=depth), :])
+        parts.append(rows[pl.ds(first_level + deep, columns, stride=depth), :])
     mixed = exact_dot(jnp.concatenate(parts, axis=0), swap, ((1,), (0,)))
     block = LANES // ROWS
     lane_block = lax.broadcasted_iota(jnp.int32, (SUB, LANES), 1) // block
@@ -203,38 +204,31 @@
                         moved = pltpu.roll(pieces[column], (column - m) * block % LANES, 1)
                         value = jnp.where(lane_block == column, moved, value)
                 start = ((deep * ROWS + m) * groups + group) * SUB
-                out[0, start : start + SUB, :] = value
+                out[start : start + SUB, :] = value
         piece = mixed[base + groups * columns * SUB :][:SUB]
         value = piece
         for far in range(1, columns):
             moved = pltpu.roll(pltpu.roll(piece, far * block, 1), columns - far, 0)
             value = jnp.where(lane_block == (row + far) % columns, moved, value)
         start = depth * ROWS * SUB * groups + deep * ROWS
-        out[0, start : start + ROWS, :] = value
-    count_tile[...] = jnp.full((SUB, LANES), counts[0].astype(jnp.float32))
-    for copy in range(1, out.shape[0]):
-        out[copy] = out[0]
-
-
-def packed_block(sources, potential, iter_counts, copies):
+        out[start : start + ROWS, :] = value
+
+
+def packed_block(sources, potential):
     count, depth, cells = sources.shape
     columns = cells // LANES
-    rows = sources.reshape(count, depth, columns, LANES).transpose(0, 2, 1, 3)
-    levels = potential.reshape(depth, columns, LANES).transpose(1, 0, 2)
+    rows = sources.reshape(count, depth, columns, LANES).transpose(0, 2, 1, 3).reshape(-1, LANES)
+    levels = potential.reshape(depth, columns, LANES).transpose(1, 0, 2).reshape(-1, LANES)
     vmem = pl.BlockSpec(memory_space=pltpu.VMEM)
-    smem = pl.BlockSpec(memory_space=pltpu.SMEM)
     size = depth * ROWS * (count + 1)
     return pl.pallas_call(
         functools.partial(pack_kernel, depth, count // SUB),
-        out_shape=(
-            jax.ShapeDtypeStruct((copies, size, LANES), jnp.float32),
-            jax.ShapeDtypeStruct((SUB, LANES), jnp.float32),
-        ),
-        in_specs=[smem, vmem, vmem],
-        out_specs=(vmem, vmem),
+        out_shape=jax.ShapeDtypeStruct((size, LANES), jnp.float32),
+        in_specs=[vmem],
+        out_specs=vmem,
         compiler_params=pltpu.CompilerParams(vmem_limit_bytes=4 * 2**20),
         name="pack",
-    )(iter_counts, rows.reshape(-1, LANES), levels.reshape(-1, LANES))
+    )(jnp.concatenate([rows, levels], axis=0))
 
 
 def lane_sum(values):
@@ -384,27 +378,26 @@
     )
 
 
-def krylov_kernel(parts, count, mine, other, *refs):
-    vectors, (scalars, applied, diagonal) = refs[:BASIS], refs[BASIS:]
+def krylov_kernel(parts, count, *refs):
+    blocks, vectors = refs[:parts], refs[parts : parts + BASIS]
+    scalars, applied, diagonal = refs[parts + BASIS :]
     planes = diagonal.shape[0]
     depth = planes // parts
     groups = count // SUB
     lane = lax.broadcasted_iota(jnp.int32, (SUB, LANES), 1)
     last_x = lax.rem(lane, X_OUT) == X_OUT - 1
     first_x = lax.rem(lane, X_OUT) == 0
-    core = jnp.bitwise_and(lax.axis_index("dom"), CORES - 1)
-
-    for chip in range(parts // CORES):
-        for block, side in ((mine, core), (other, 1 - core)):
-            slab = (chip * CORES + side) * depth
-            for deep in range(depth):
-                for m in range(ROWS):
-                    start = (deep * ROWS + m) * count
-                    lanes = pl.ds(m * LANES, LANES)
-                    vectors[0][slab + deep, :, lanes] = block[chip, start : start + count, :]
-                start = depth * ROWS * count + deep * ROWS
-                levels = block[chip, start : start + ROWS, :]
-                diagonal[slab + deep] = H_SCALE * (levels + 3.75)
+    here = lax.axis_index("dom")
+    for turn in range(parts):
+        slab = jnp.bitwise_xor(here, turn) * depth
+        for deep in range(depth):
+            for m in range(ROWS):
+                start = (deep * ROWS + m) * count
+                lanes = pl.ds(m * LANES, LANES)
+                vectors[0][slab + deep, :, lanes] = blocks[turn][start : start + count, :]
+            start = depth * ROWS * count + deep * ROWS
+            levels = blocks[turn][start : start + ROWS, :]
+            diagonal[slab + deep] = H_SCALE * (levels + 3.75)
 
     blank = jnp.zeros((SUB, LANES), jnp.float32)
     alphas, norms = [], []
@@ -457,9 +450,8 @@
         scalars[i] = jnp.concatenate(value, axis=0)
 
 
-def gram_kernel(points, scalars, *refs):
-    tiles, vectors = refs[:points], refs[points : points + BASIS]
-    out_b, out_a, gram, limits = refs[points + BASIS :]
+def gram_kernel(points, limits, scalars, *refs):
+    vectors, (out_b, out_a, gram) = refs[:BASIS], refs[BASIS:]
     planes, count, _ = vectors[0].shape
     groups = count // SUB
     size = BASIS * count
@@ -481,9 +473,6 @@
     cross = gram[:, size:]
     pairs = gram[:, :size] + cross + cross.T
 
-    here = lax.axis_index("point")
-    for far, tile in enumerate(tiles):
-        limits[jnp.bitwise_xor(here, far)] = tile[...]
     bounds = [jnp.concatenate([limits[j]] * groups, axis=0) for j in range(points)]
     alphas = [scalars[i] for i in range(ITERS)]
     norms = [scalars[ITERS + i] for i in range(ITERS)]
@@ -504,18 +493,19 @@
     out_a[1] = imag[:, half:]
 
 
+def swapped(values, parts, mask):
+    return lax.ppermute(values, "dom", [(part ^ mask, part) for part in range(parts)])
+
+
 def whole_grid(sources, potential, iter_counts, *, parts, points):
     count, depth, _ = sources.shape
     planes = parts * depth
-    chips = parts // CORES
-    copies, tile = packed_block(sources, potential, iter_counts, chips)
-    same_core = [list(range(core, parts, CORES)) for core in range(CORES)]
-    mine = lax.all_to_all(copies, "dom", 0, 0, axis_index_groups=same_core, tiled=True)
-    other = lax.ppermute(mine, "dom", [(part ^ 1, part) for part in range(parts)])
-    tiles = [tile] + [
-        lax.ppermute(tile, "point", [(point ^ far, point) for point in range(points)])
-        for far in range(1, points)
-    ]
+    tile = jnp.broadcast_to(iter_counts.astype(jnp.float32), (SUB, LANES))
+    limits = lax.all_gather(lax.optimization_barrier(tile), "point")
+    block = packed_block(sources, potential)
+    even = [block] + [swapped(block, parts, mask) for mask in range(CORES, parts, CORES)]
+    odd = [swapped(value, parts, 1) for value in even]
+    blocks = [value for pair in zip(even, odd) for value in pair]
     vmem = pl.BlockSpec(memory_space=pltpu.VMEM)
     vector = (planes, count, ROWS * LANES)
     cells = planes * ROWS * LANES
@@ -523,7 +513,7 @@
         functools.partial(krylov_kernel, parts, count),
         out_shape=[jax.ShapeDtypeStruct(vector, jnp.float32)] * BASIS
         + [jax.ShapeDtypeStruct((2 * ITERS, count, LANES), jnp.float32)],
-        in_specs=[vmem] * CORES,
+        in_specs=[vmem] * parts,
         out_specs=[vmem] * (BASIS + 1),
         scratch_shapes=[
             pltpu.VMEM(vector, jnp.float32),
@@ -534,22 +524,19 @@
             flops=ITERS * count * cells * 30, bytes_accessed=32 * 2**20, transcendentals=0
         ),
         name="krylov",
-    )(mine, other)
+    )(*blocks)
     size = BASIS * count
     width = MOMENTS * count
     out = jax.ShapeDtypeStruct((2, width, width), jnp.float32)
     return pl.pallas_call(
         functools.partial(gram_kernel, points),
         out_shape=(out, out),
-        in_specs=[vmem] * (1 + points + BASIS),
+        in_specs=[vmem] * (2 + BASIS),
         out_specs=(vmem, vmem),
-        scratch_shapes=[
-            pltpu.VMEM((size, 2 * size), jnp.float32),
-            pltpu.VMEM((points, SUB, LANES), jnp.float32),
-        ],
+        scratch_shapes=[pltpu.VMEM((size, 2 * size), jnp.float32)],
         compiler_params=pltpu.CompilerParams(vmem_limit_bytes=16 * 2**20),
         name="gram",
-    )(scalars, *tiles, *vectors)
+    )(limits, scalars, *vectors)
 
 
 def on_device(sources, potential, iter_counts):

time: 37.2 us -> 43.1 us (1.16)
  waiting for transfers between devices: 0.01 us -> 6.58 us
  local copies, waits for them, and re-layouts: 1.59 us -> 0.01 us
  other arithmetic: 0 us -> 0.93 us
  blocking collectives: 14.1 us -> 13.4 us
  starting transfers between devices: 4.39 us -> 5.06 us
    all_to_all x1 -> x0, blocking collectives: 14.1 us -> none  [whole_grid(): lax.all_to_all(copies, 'dom', 0, 0, axis_index_groups=same_core, tiled=True)]
    all_gather x0 -> x1, blocking collectives: none -> 13.4 us  [whole_grid(): limits = lax.all_gather(lax.optimization_barrier(tile), 'point')]
    ppermute x4 -> x7, waiting for transfers between devices: 0.01 us -> 6.58 us  [swapped(): lax.ppermute(values, 'dom', [(part ^ mask, part) for part in range(parts)])]
    unnamed x4 -> x0, local copies, waits for them, and re-layouts: 1.59 us -> none
    concatenate x0 -> x1, other arithmetic: none -> 0.93 us  [packed_block(): jnp.concatenate([rows, levels], axis=0)]
    ppermute x4 -> x7, starting transfers between devices: 4.39 us -> 5.06 us  [swapped(): lax.ppermute(values, 'dom', [(part ^ mask, part) for part in range(parts)])]
  transfers between devices with their start and end apart: 4 -> 7, of which waited for: 0 -> 2; matrix products, arithmetic and copies ran while one was open for 0% -> 0% of each run, Pallas kernels for 28% -> 0%
where the time goes in v7:
time: 43.1 us; the launch traced here: 42.8 us
  Pallas kernels  15.6 us (36%)
  blocking collectives  13.4 us (31%)
  waiting for transfers between devices  6.58 us (15%)
  starting transfers between devices  5.06 us (12%)
  between operations  1.32 us (3%)
  other arithmetic  0.93 us (2%)
    all_gather x1, blocking collectives, whole_grid(): limits = lax.all_gather(lax.optimization_barrier(tile), 'point')  13.4 us
    pallas_call x1, Pallas kernels, whole_grid(): pl.pallas_call(functools.partial(krylov_kernel, parts, count), out_shape=...  10.3 us
    ppermute x7, waiting for transfers between devices, swapped(): lax.ppermute(values, 'dom', [(part ^ mask, part) for part in range(parts)])  6.58 us
    ppermute x7, starting transfers between devices, swapped(): lax.ppermute(values, 'dom', [(part ^ mask, part) for part in range(parts)])  5.06 us
    pallas_call x1, Pallas kernels, whole_grid(): pl.pallas_call(functools.partial(gram_kernel, points), out_shape=(out, ou...  4.75 us
    concatenate x1, other arithmetic, packed_block(): jnp.concatenate([rows, levels], axis=0)  0.93 us
  transfers between devices with their start and end apart: 7, of which 2 were waited for; matrix products, arithmetic and copies ran while one was open for 0% of the time, Pallas kernels for 0%

profile of v7, /device:TPU:0, one launch (start us, length us, event | category | flops | bytes accessed | tf_op | source)
XLA Modules:
  0.0 42.8 jit_solution(18264904866567302288)
XLA Ops:
  0.6 0.9 %pad_maximum_fusion.rows = f32[272,128]{1,0:T(8,128)S(1)} fusion(f32[16,128]{1,0:T(8,128)} %bitcast.14, f32[256,128]{1,0:T(8,128)} %bitcast.13), kind=kLoop, calls=%fused_computation | loop fusion | flops 34816 | bytes 278528 | tf_op jit(solution)/shard_map/concatenate | solution.py:231
  1.6 0.6 %pack.1.refs_0_ = f32[272,128]{1,0:T(8,128)S(1)} custom-call(f32[272,128]{1,0:T(8,128)S(1)} %pad_maximum_fusion.rows), custom_call_target="tpu_custom_call" | custom-call | tf_op jit(solution)/shard_map/pack/pallas_call | solution.py:224
  2.1 3.0 %collective-permute-start.1 = (f32[272,128]{1,0:T(8,128)S(1)}, f32[272,128]{1,0:T(8,128)S(1)}, u32[]{:S(2)}, u32[]{:S(2)}) collective-permute-start(f32[272,128]{1,0:T(8,128)S(1)} %pack.1.refs_0_), channel_id=1, source_target_pairs={{2,0},{3,1},{0,2},{1,3},{6,4},{7,5},{4,6},{5,7},{10,8},{11,9},{8,1... | collective-permute-start | bytes 417800 | tf_op jit(solution)/shard_map/ppermute | solution.py:497
  5.1 1.5 %collective-permute-start.3 = (f32[272,128]{1,0:T(8,128)S(1)}, f32[272,128]{1,0:T(8,128)S(1)}, u32[]{:S(2)}, u32[]{:S(2)}) collective-permute-start(f32[272,128]{1,0:T(8,128)S(1)} %pack.1.refs_0_), channel_id=1, source_target_pairs={{4,0},{5,1},{6,2},{7,3},{0,4},{1,5},{2,6},{3,7},{12,8},{13,9},{14,... | collective-permute-start | bytes 417800 | tf_op jit(solution)/shard_map/ppermute | solution.py:497
  6.7 0.0 collective-permute-start.5
  6.7 0.0 collective-permute-start
  6.7 2.5 %collective-permute-done.1.refs_2_ = f32[272,128]{1,0:T(8,128)S(1)} collective-permute-done((f32[272,128]{1,0:T(8,128)S(1)}, f32[272,128]{1,0:T(8,128)S(1)}, u32[]{:S(2)}, u32[]{:S(2)}) %collective-permute-start.1) | collective-permute-done | bytes 139296 | tf_op jit(solution)/shard_map/ppermute | solution.py:497
  9.2 0.0 collective-permute-start.2
  9.2 4.0 %collective-permute-done.3.refs_4_ = f32[272,128]{1,0:T(8,128)S(1)} collective-permute-done((f32[272,128]{1,0:T(8,128)S(1)}, f32[272,128]{1,0:T(8,128)S(1)}, u32[]{:S(2)}, u32[]{:S(2)}) %collective-permute-start.3) | collective-permute-done | bytes 139296 | tf_op jit(solution)/shard_map/ppermute | solution.py:497
  13.2 0.0 collective-permute-start.4
  13.2 0.0 collective-permute-done.5.refs_6_
  13.3 0.5 %collective-permute-start.6 = (f32[272,128]{1,0:T(8,128)S(1)}, f32[272,128]{1,0:T(8,128)S(1)}, u32[]{:S(2)}, u32[]{:S(2)}) collective-permute-start(f32[272,128]{1,0:T(8,128)S(1)} %collective-permute-done.5.refs_6_), channel_id=1, source_target_pairs={{1,0},{0,1},{3,2},{2,3},{5,4},{4,5},{7,6},{6,7},{9,8},{8,9},{11,10... | collective-permute-start | bytes 417800 | tf_op jit(solution)/shard_map/ppermute | solution.py:497
  14.4 13.4 %all-gather = f32[32,128]{1,0:T(8,128)S(1)} all-gather(f32[8,128]{1,0:T(8,128)S(1)} %broadcast_in_dim.2), channel_id=2, replica_groups=mesh['point'=4,'dom'=8] {'point'}, dimensions={0}, use_global_device_ids=true | all-gather | bytes 20480 | tf_op jit(solution)/shard_map/all_gather | solution.py:504
  27.8 0.0 collective-permute-done.refs_1_
  27.8 0.0 collective-permute-done.2.refs_3_
  27.8 0.0 collective-permute-done.4.refs_5_
  27.8 0.0 collective-permute-done.6.refs_7_
  27.8 10.3 %krylov.1 = (f32[16,16,1024]{2,1,0:T(8,128)S(1)}, f32[16,16,1024]{2,1,0:T(8,128)S(1)}, f32[16,16,1024]{2,1,0:T(8,128)S(1)}, f32[16,16,1024]{2,1,0:T(8,128)S(1)},...) custom-call(f32[272,128]{1,0:T(8,128)S(1)} %pack.1.refs_0_, ...), custom_call_target="tpu_custom_call" | custom-call | flops 47185920 | bytes 33554432 | tf_op jit(solution)/shard_map/krylov/pallas_call | solution.py:512
  38.1 4.7 %gram.1 = (f32[2,64,64]{2,1,0:T(8,128)}, f32[2,64,64]{2,1,0:T(8,128)}) custom-call(f32[4,8,128]{2,1,0:T(8,128)S(1)} %bitcast.12, f32[12,16,128]{2,1,0:T(8,128)S(1)} %get-tuple-element.10.scalars, f32[16,16,1024]{2,1,0:T(8,128)S(1)} %get-tuple-element.11.refs_0_, f32[16,16,1024]{2,1,0:T(8,128)S(1)} %get-tuple-element.12.refs_1_, ...), custom_call_target="tpu_custom_call" | custom-call | tf_op jit(solution)/shard_map/gram/pallas_call | solution.py:531
  (1 shorter events, 0.0 us)
Async XLA Ops:
  2.1 7.1 %collective-permute-start.1 = (f32[272,128]{1,0:T(8,128)S(1)}, f32[272,128]{1,0:T(8,128)S(1)}, u32[]{:S(2)}, u32[]{:S(2)}) collective-permute-start(f32[272,128]{1,0:T(8,128)S(1)} %pack.1.refs_0_), channel_id=1, source_target_pairs={{2,0},{3,1},{0,2},{1,3},{6,4},{7,5},{4,6},{5,7},{10,8},{11,9},{8,1... | collective-permute-start | bytes 417800 | tf_op jit(solution)/shard_map/ppermute | solution.py:497
  5.1 8.1 %collective-permute-start.3 = (f32[272,128]{1,0:T(8,128)S(1)}, f32[272,128]{1,0:T(8,128)S(1)}, u32[]{:S(2)}, u32[]{:S(2)}) collective-permute-start(f32[272,128]{1,0:T(8,128)S(1)} %pack.1.refs_0_), channel_id=1, source_target_pairs={{4,0},{5,1},{6,2},{7,3},{0,4},{1,5},{2,6},{3,7},{12,8},{13,9},{14,... | collective-permute-start | bytes 417800 | tf_op jit(solution)/shard_map/ppermute | solution.py:497
  6.7 6.6 %collective-permute-start.5 = (f32[272,128]{1,0:T(8,128)S(1)}, f32[272,128]{1,0:T(8,128)S(1)}, u32[]{:S(2)}, u32[]{:S(2)}) collective-permute-start(f32[272,128]{1,0:T(8,128)S(1)} %pack.1.refs_0_), channel_id=1, source_target_pairs={{6,0},{7,1},{4,2},{5,3},{2,4},{3,5},{0,6},{1,7},{14,8},{15,9},{12,... | collective-permute-start | bytes 417800 | tf_op jit(solution)/shard_map/ppermute | solution.py:497
  6.7 21.1 %collective-permute-start = (f32[272,128]{1,0:T(8,128)S(1)}, f32[272,128]{1,0:T(8,128)S(1)}, u32[]{:S(2)}, u32[]{:S(2)}) collective-permute-start(f32[272,128]{1,0:T(8,128)S(1)} %pack.1.refs_0_), channel_id=1, source_target_pairs={{1,0},{0,1},{3,2},{2,3},{5,4},{4,5},{7,6},{6,7},{9,8},{8,9},{11,10... | collective-permute-start | bytes 417800 | tf_op jit(solution)/shard_map/ppermute | solution.py:497
  9.2 18.6 %collective-permute-start.2 = (f32[272,128]{1,0:T(8,128)S(1)}, f32[272,128]{1,0:T(8,128)S(1)}, u32[]{:S(2)}, u32[]{:S(2)}) collective-permute-start(f32[272,128]{1,0:T(8,128)S(1)} %collective-permute-done.1.refs_2_), channel_id=1, source_target_pairs={{1,0},{0,1},{3,2},{2,3},{5,4},{4,5},{7,6},{6,7},{9,8},{8,9},{11,10... | collective-permute-start | bytes 417800 | tf_op jit(solution)/shard_map/ppermute | solution.py:497
  13.2 14.5 %collective-permute-start.4 = (f32[272,128]{1,0:T(8,128)S(1)}, f32[272,128]{1,0:T(8,128)S(1)}, u32[]{:S(2)}, u32[]{:S(2)}) collective-permute-start(f32[272,128]{1,0:T(8,128)S(1)} %collective-permute-done.3.refs_4_), channel_id=1, source_target_pairs={{1,0},{0,1},{3,2},{2,3},{5,4},{4,5},{7,6},{6,7},{9,8},{8,9},{11,10... | collective-permute-start | bytes 417800 | tf_op jit(solution)/shard_map/ppermute | solution.py:497
  13.3 14.5 %collective-permute-start.6 = (f32[272,128]{1,0:T(8,128)S(1)}, f32[272,128]{1,0:T(8,128)S(1)}, u32[]{:S(2)}, u32[]{:S(2)}) collective-permute-start(f32[272,128]{1,0:T(8,128)S(1)} %collective-permute-done.5.refs_6_), channel_id=1, source_target_pairs={{1,0},{0,1},{3,2},{2,3},{5,4},{4,5},{7,6},{6,7},{9,8},{8,9},{11,10... | collective-permute-start | bytes 417800 | tf_op jit(solution)/shard_map/ppermute | solution.py:497

commit v8 on v7

--- a/solution.py
+++ b/solution.py
@@ -171,7 +171,7 @@
 FAR_SCALED = 0.5 * H_SCALE * COEF_FAR
 
 
-def pack_kernel(depth, groups, rows, out):
+def pack_kernel(depth, groups, counts, rows, out, tile):
     columns = rows.shape[0] // (SUB * groups * depth + depth)
     first_level = columns * SUB * groups * depth
     source = lax.broadcasted_iota(jnp.int32, (LANES, LANES), 0)
@@ -212,9 +212,10 @@
             value = jnp.where(lane_block == (row + far) % columns, moved, value)
         start = depth * ROWS * SUB * groups + deep * ROWS
         out[start : start + ROWS, :] = value
-
-
-def packed_block(sources, potential):
+    tile[...] = jnp.broadcast_to(counts[...].astype(jnp.float32), (SUB, LANES))
+
+
+def packed_block(sources, potential, iter_counts):
     count, depth, cells = sources.shape
     columns = cells // LANES
     rows = sources.reshape(count, depth, columns, LANES).transpose(0, 2, 1, 3).reshape(-1, LANES)
@@ -223,12 +224,15 @@
     size = depth * ROWS * (count + 1)
     return pl.pallas_call(
         functools.partial(pack_kernel, depth, count // SUB),
-        out_shape=jax.ShapeDtypeStruct((size, LANES), jnp.float32),
-        in_specs=[vmem],
-        out_specs=vmem,
+        out_shape=(
+            jax.ShapeDtypeStruct((size, LANES), jnp.float32),
+            jax.ShapeDtypeStruct((SUB, LANES), jnp.float32),
+        ),
+        in_specs=[vmem, vmem],
+        out_specs=(vmem, vmem),
         compiler_params=pltpu.CompilerParams(vmem_limit_bytes=4 * 2**20),
         name="pack",
-    )(jnp.concatenate([rows, levels], axis=0))
+    )(iter_counts.reshape(1, 1), jnp.concatenate([rows, levels], axis=0))
 
 
 def lane_sum(values):
@@ -273,7 +277,7 @@
                 near = (wide[xi + 1] + wide[xi + 3]) + (y_next + y_prev) + (above[m] + below[m])
                 far = (wide[xi] + wide[xi + 4]) + (y_up[m] + y_down[m])
                 far = far + (above_2[m] + below_2[m])
-                level = diagonal[first + plane, pl.ds(m, 1), :]
+                level = diagonal[first + plane, :, pl.ds(m * LANES, LANES)]
                 out.append(level * here[m] - near - FAR_SCALED * far)
         yield here, out
 
@@ -396,8 +400,10 @@
                 lanes = pl.ds(m * LANES, LANES)
                 vectors[0][slab + deep, :, lanes] = blocks[turn][start : start + count, :]
             start = depth * ROWS * count + deep * ROWS
-            levels = blocks[turn][start : start + ROWS, :]
-            diagonal[slab + deep] = H_SCALE * (levels + 3.75)
+            levels = H_SCALE * (blocks[turn][start : start + ROWS, :] + 3.75)
+            for m in range(ROWS):
+                level = jnp.broadcast_to(levels[m : m + 1, :], (SUB, LANES))
+                diagonal[slab + deep, :, m * LANES : (m + 1) * LANES] = level
 
     blank = jnp.zeros((SUB, LANES), jnp.float32)
     alphas, norms = [], []
@@ -450,8 +456,9 @@
         scalars[i] = jnp.concatenate(value, axis=0)
 
 
-def gram_kernel(points, limits, scalars, *refs):
-    vectors, (out_b, out_a, gram) = refs[:BASIS], refs[BASIS:]
+def gram_kernel(points, scalars, *refs):
+    tiles, vectors = refs[:points], refs[points : points + BASIS]
+    out_b, out_a, gram, limits = refs[points + BASIS :]
     planes, count, _ = vectors[0].shape
     groups = count // SUB
     size = BASIS * count
@@ -473,6 +480,9 @@
     cross = gram[:, size:]
     pairs = gram[:, :size] + cross + cross.T
 
+    here = lax.axis_index("point")
+    for far, tile in enumerate(tiles):
+        limits[jnp.bitwise_xor(here, far)] = tile[...]
     bounds = [jnp.concatenate([limits[j]] * groups, axis=0) for j in range(points)]
     alphas = [scalars[i] for i in range(ITERS)]
     norms = [scalars[ITERS + i] for i in range(ITERS)]
@@ -493,18 +503,18 @@
     out_a[1] = imag[:, half:]
 
 
-def swapped(values, parts, mask):
-    return lax.ppermute(values, "dom", [(part ^ mask, part) for part in range(parts)])
+def swapped(values, axis, size, mask):
+    return lax.ppermute(values, axis, [(index ^ mask, index) for index in range(size)])
 
 
 def whole_grid(sources, potential, iter_counts, *, parts, points):
     count, depth, _ = sources.shape
     planes = parts * depth
-    tile = jnp.broadcast_to(iter_counts.astype(jnp.float32), (SUB, LANES))
-    limits = lax.all_gather(lax.optimization_barrier(tile), "point")
-    block = packed_block(sources, potential)
-    even = [block] + [swapped(block, parts, mask) for mask in range(CORES, parts, CORES)]
-    odd = [swapped(value, parts, 1) for value in even]
+    block, tile = packed_block(sources, potential, iter_counts)
+    even = [block] + [swapped(block, "dom", parts, mask) for mask in range(CORES, parts, CORES)]
+    tiles = [swapped(tile, "point", points, far) for far in range(1, points)]
+    even[2], *tiles = lax.optimization_barrier((even[2], *tiles))
+    odd = [swapped(value, "dom", parts, 1) for value in even]
     blocks = [value for pair in zip(even, odd) for value in pair]
     vmem = pl.BlockSpec(memory_space=pltpu.VMEM)
     vector = (planes, count, ROWS * LANES)
@@ -517,7 +527,7 @@
         out_specs=[vmem] * (BASIS + 1),
         scratch_shapes=[
             pltpu.VMEM(vector, jnp.float32),
-            pltpu.VMEM((planes, ROWS, LANES), jnp.float32),
+            pltpu.VMEM((planes, SUB, ROWS * LANES), jnp.float32),
         ],
         compiler_params=pltpu.CompilerParams(vmem_limit_bytes=16 * 2**20),
         cost_estimate=pl.CostEstimate(
@@ -531,12 +541,15 @@
     return pl.pallas_call(
         functools.partial(gram_kernel, points),
         out_shape=(out, out),
-        in_specs=[vmem] * (2 + BASIS),
+        in_specs=[vmem] * (1 + points + BASIS),
         out_specs=(vmem, vmem),
-        scratch_shapes=[pltpu.VMEM((size, 2 * size), jnp.float32)],
+        scratch_shapes=[
+            pltpu.VMEM((size, 2 * size), jnp.float32),
+            pltpu.VMEM((points, SUB, LANES), jnp.float32),
+        ],
         compiler_params=pltpu.CompilerParams(vmem_limit_bytes=16 * 2**20),
         name="gram",
-    )(limits, scalars, *vectors)
+    )(scalars, tile, *tiles, *vectors)
 
 
 def on_device(sources, potential, iter_counts):

time: 43.1 us -> 33.7 us (0.78)
  blocking collectives: 13.4 us -> 0 us
  starting transfers between devices: 5.06 us -> 9.19 us
    all_gather x1 -> x0, blocking collectives: 13.4 us -> none  [whole_grid(): limits = lax.all_gather(lax.optimization_barrier(tile), 'point')]
    ppermute x7 -> x10, starting transfers between devices: 5.06 us -> 9.19 us  [swapped(): lax.ppermute(values, axis, [(index ^ mask, index) for index in range(size)])]
    ppermute x7 -> x10, waiting for transfers between devices: 6.58 us -> 6.48 us  [swapped(): lax.ppermute(values, axis, [(index ^ mask, index) for index in range(size)])]
  transfers between devices with their start and end apart: 7 -> 10, of which waited for: 2 -> 6; matrix products, arithmetic and copies ran while one was open for 0% -> 0% of each run, Pallas kernels for 0% -> 0%
where the time goes in v8:
time: 33.7 us; the launch traced here: 33.5 us
  Pallas kernels  15.6 us (46%)
  starting transfers between devices  9.19 us (27%)
  waiting for transfers between devices  6.48 us (19%)
  between operations  1.3 us (4%)
  other arithmetic  0.93 us (3%)
    pallas_call x1, Pallas kernels, whole_grid(): pl.pallas_call(functools.partial(krylov_kernel, parts, count), out_shape=...  10.3 us
    ppermute x10, starting transfers between devices, swapped(): lax.ppermute(values, axis, [(index ^ mask, index) for index in range(size)])  9.19 us
    ppermute x10, waiting for transfers between devices, swapped(): lax.ppermute(values, axis, [(index ^ mask, index) for index in range(size)])  6.48 us
    pallas_call x1, Pallas kernels, whole_grid(): pl.pallas_call(functools.partial(gram_kernel, points), out_shape=(out, ou...  4.75 us
    concatenate x1, other arithmetic, packed_block(): jnp.concatenate([rows, levels], axis=0)  0.93 us
  transfers between devices with their start and end apart: 10, of which 6 were waited for; matrix products, arithmetic and copies ran while one was open for 0% of the time, Pallas kernels for 0%

profile of v8, /device:TPU:0, one launch (start us, length us, event | category | flops | bytes accessed | tf_op | source)
XLA Modules:
  0.0 33.5 jit_solution(15764203324039952476)
XLA Ops:
  1.3 0.9 %pad_maximum_fusion.rows = f32[272,128]{1,0:T(8,128)S(1)} fusion(f32[16,128]{1,0:T(8,128)} %bitcast.13, f32[256,128]{1,0:T(8,128)} %bitcast.12), kind=kLoop, calls=%fused_computation | loop fusion | flops 34816 | bytes 278528 | tf_op jit(solution)/shard_map/concatenate | solution.py:235
  2.2 0.6 %pack.1 = (f32[272,128]{1,0:T(8,128)S(1)}, f32[8,128]{1,0:T(8,128)S(1)}) custom-call(s32[1,1]{1,0:T(1,128)} %bitcast.11.counts, f32[272,128]{1,0:T(8,128)S(1)} %pad_maximum_fusion.rows), custom_call_target="tpu_custom_call" | custom-call | tf_op jit(solution)/shard_map/pack/pallas_call | solution.py:225
  2.8 3.0 %collective-permute-start.3 = (f32[272,128]{1,0:T(8,128)S(1)}, f32[272,128]{1,0:T(8,128)S(1)}, u32[]{:S(2)}, u32[]{:S(2)}) collective-permute-start(f32[272,128]{1,0:T(8,128)S(1)} %get-tuple-element.16.refs_0_), channel_id=1, source_target_pairs={{4,0},{5,1},{6,2},{7,3},{0,4},{1,5},{2,6},{3,7},{12,8},{13,9},{14,... | collective-permute-start | bytes 417800 | tf_op jit(solution)/shard_map/ppermute | solution.py:507
  5.8 1.4 %collective-permute-start.8 = (f32[272,128]{1,0:T(8,128)S(1)}, f32[272,128]{1,0:T(8,128)S(1)}, u32[]{:S(2)}, u32[]{:S(2)}) collective-permute-start(f32[272,128]{1,0:T(8,128)S(1)} %get-tuple-element.16.refs_0_), channel_id=1, source_target_pairs={{6,0},{7,1},{4,2},{5,3},{2,4},{3,5},{0,6},{1,7},{14,8},{15,9},{12,... | collective-permute-start | bytes 417800 | tf_op jit(solution)/shard_map/ppermute | solution.py:507
  7.2 0.1 collective-permute-start.1
  7.3 4.0 %collective-permute-start.6 = (f32[8,128]{1,0:T(8,128)S(1)}, f32[8,128]{1,0:T(8,128)S(1)}, u32[]{:S(2)}, u32[]{:S(2)}) collective-permute-start(f32[8,128]{1,0:T(8,128)S(1)} %get-tuple-element.17.refs_0_), channel_id=1, source_target_pairs={{24,0},{16,8},{8,16},{0,24},{25,1},{17,9},{9,17},{1,25},{26,2},{18... | collective-permute-start | bytes 12296 | tf_op jit(solution)/shard_map/ppermute | solution.py:507
  11.4 0.0 collective-permute-start.5
  11.4 1.6 %collective-permute-done.6.refs_3_ = f32[8,128]{1,0:T(8,128)S(1)} collective-permute-done((f32[8,128]{1,0:T(8,128)S(1)}, f32[8,128]{1,0:T(8,128)S(1)}, u32[]{:S(2)}, u32[]{:S(2)}) %collective-permute-start.6) | collective-permute-done | bytes 4128 | tf_op jit(solution)/shard_map/ppermute | solution.py:507
  13.0 0.0 collective-permute-start.4
  13.0 2.9 %collective-permute-done.5.refs_2_ = f32[8,128]{1,0:T(8,128)S(1)} collective-permute-done((f32[8,128]{1,0:T(8,128)S(1)}, f32[8,128]{1,0:T(8,128)S(1)}, u32[]{:S(2)}, u32[]{:S(2)}) %collective-permute-start.5) | collective-permute-done | bytes 4128 | tf_op jit(solution)/shard_map/ppermute | solution.py:507
  15.9 0.0 collective-permute-start
  15.9 0.7 %collective-permute-done.4.refs_1_ = f32[8,128]{1,0:T(8,128)S(1)} collective-permute-done((f32[8,128]{1,0:T(8,128)S(1)}, f32[8,128]{1,0:T(8,128)S(1)}, u32[]{:S(2)}, u32[]{:S(2)}) %collective-permute-start.4) | collective-permute-done | bytes 4128 | tf_op jit(solution)/shard_map/ppermute | solution.py:507
  16.6 0.0 collective-permute-done.3.refs_4_
  16.6 0.0 collective-permute-start.7
  16.6 0.0 collective-permute-done.8.refs_6_
  16.6 0.5 %collective-permute-start.9 = (f32[272,128]{1,0:T(8,128)S(1)}, f32[272,128]{1,0:T(8,128)S(1)}, u32[]{:S(2)}, u32[]{:S(2)}) collective-permute-start(f32[272,128]{1,0:T(8,128)S(1)} %collective-permute-done.8.refs_6_), channel_id=1, source_target_pairs={{1,0},{0,1},{3,2},{2,3},{5,4},{4,5},{7,6},{6,7},{9,8},{8,9},{11,10... | collective-permute-start | bytes 417800 | tf_op jit(solution)/shard_map/ppermute | solution.py:507
  17.1 0.0 collective-permute-done.1.refs_2_
  17.1 0.1 collective-permute-start.2
  17.2 0.1 collective-permute-done.refs_1_
  17.2 0.9 %collective-permute-done.9.refs_7_ = f32[272,128]{1,0:T(8,128)S(1)} collective-permute-done((f32[272,128]{1,0:T(8,128)S(1)}, f32[272,128]{1,0:T(8,128)S(1)}, u32[]{:S(2)}, u32[]{:S(2)}) %collective-permute-start.9) | collective-permute-done | bytes 139296 | tf_op jit(solution)/shard_map/ppermute | solution.py:507
  18.1 0.0 collective-permute-done.7.refs_5_
  18.1 0.3 collective-permute-done.2.refs_3_
  18.5 10.3 %krylov.1 = (f32[16,16,1024]{2,1,0:T(8,128)S(1)}, f32[16,16,1024]{2,1,0:T(8,128)S(1)}, f32[16,16,1024]{2,1,0:T(8,128)S(1)}, f32[16,16,1024]{2,1,0:T(8,128)S(1)},...) custom-call(f32[272,128]{1,0:T(8,128)S(1)} %get-tuple-element.16.ref, ...), custom_call_target="tpu_custom_call" | custom-call | flops 47185920 | bytes 33554432 | tf_op jit(solution)/shard_map/krylov/pallas_call | solution.py:522
  28.8 4.8 %gram.1 = (f32[2,64,64]{2,1,0:T(8,128)}, f32[2,64,64]{2,1,0:T(8,128)}) custom-call(f32[12,16,128]{2,1,0:T(8,128)S(1)} %get-tuple-element.19.scalars, f32[8,128]{1,0:T(8,128)S(1)} %get-tuple-element.17.refs_0_, f32[8,128]{1,0:T(8,128)S(1)} %collective-permute-done.4.refs_1_, f32[8,128]{1,0:T(8,128)S(1)} %collective-permute-done.5.refs_2_, ...), custom_call_target="tpu_custom_call" | custom-call | tf_op jit(solution)/shard_map/gram/pallas_call | solution.py:541
Async XLA Ops:
  2.8 13.8 %collective-permute-start.3 = (f32[272,128]{1,0:T(8,128)S(1)}, f32[272,128]{1,0:T(8,128)S(1)}, u32[]{:S(2)}, u32[]{:S(2)}) collective-permute-start(f32[272,128]{1,0:T(8,128)S(1)} %get-tuple-element.16.refs_0_), channel_id=1, source_target_pairs={{4,0},{5,1},{6,2},{7,3},{0,4},{1,5},{2,6},{3,7},{12,8},{13,9},{14,... | collective-permute-start | bytes 417800 | tf_op jit(solution)/shard_map/ppermute | solution.py:507
  5.8 10.8 %collective-permute-start.8 = (f32[272,128]{1,0:T(8,128)S(1)}, f32[272,128]{1,0:T(8,128)S(1)}, u32[]{:S(2)}, u32[]{:S(2)}) collective-permute-start(f32[272,128]{1,0:T(8,128)S(1)} %get-tuple-element.16.refs_0_), channel_id=1, source_target_pairs={{6,0},{7,1},{4,2},{5,3},{2,4},{3,5},{0,6},{1,7},{14,8},{15,9},{12,... | collective-permute-start | bytes 417800 | tf_op jit(solution)/shard_map/ppermute | solution.py:507
  7.2 9.9 %collective-permute-start.1 = (f32[272,128]{1,0:T(8,128)S(1)}, f32[272,128]{1,0:T(8,128)S(1)}, u32[]{:S(2)}, u32[]{:S(2)}) collective-permute-start(f32[272,128]{1,0:T(8,128)S(1)} %get-tuple-element.16.refs_0_), channel_id=1, source_target_pairs={{2,0},{3,1},{0,2},{1,3},{6,4},{7,5},{4,6},{5,7},{10,8},{11,9},{8,1... | collective-permute-start | bytes 417800 | tf_op jit(solution)/shard_map/ppermute | solution.py:507
  7.3 5.6 %collective-permute-start.6 = (f32[8,128]{1,0:T(8,128)S(1)}, f32[8,128]{1,0:T(8,128)S(1)}, u32[]{:S(2)}, u32[]{:S(2)}) collective-permute-start(f32[8,128]{1,0:T(8,128)S(1)} %get-tuple-element.17.refs_0_), channel_id=1, source_target_pairs={{24,0},{16,8},{8,16},{0,24},{25,1},{17,9},{9,17},{1,25},{26,2},{18... | collective-permute-start | bytes 12296 | tf_op jit(solution)/shard_map/ppermute | solution.py:507
  11.4 4.5 %collective-permute-start.5 = (f32[8,128]{1,0:T(8,128)S(1)}, f32[8,128]{1,0:T(8,128)S(1)}, u32[]{:S(2)}, u32[]{:S(2)}) collective-permute-start(f32[8,128]{1,0:T(8,128)S(1)} %get-tuple-element.17.refs_0_), channel_id=1, source_target_pairs={{16,0},{24,8},{0,16},{8,24},{17,1},{25,9},{1,17},{9,25},{18,2},{26... | collective-permute-start | bytes 12296 | tf_op jit(solution)/shard_map/ppermute | solution.py:507
  13.0 3.6 %collective-permute-start.4 = (f32[8,128]{1,0:T(8,128)S(1)}, f32[8,128]{1,0:T(8,128)S(1)}, u32[]{:S(2)}, u32[]{:S(2)}) collective-permute-start(f32[8,128]{1,0:T(8,128)S(1)} %get-tuple-element.17.refs_0_), channel_id=1, source_target_pairs={{8,0},{0,8},{24,16},{16,24},{9,1},{1,9},{25,17},{17,25},{10,2},{2,... | collective-permute-start | bytes 12296 | tf_op jit(solution)/shard_map/ppermute | solution.py:507
  15.9 1.4 %collective-permute-start = (f32[272,128]{1,0:T(8,128)S(1)}, f32[272,128]{1,0:T(8,128)S(1)}, u32[]{:S(2)}, u32[]{:S(2)}) collective-permute-start(f32[272,128]{1,0:T(8,128)S(1)} %get-tuple-element.16.refs_0_), channel_id=1, source_target_pairs={{1,0},{0,1},{3,2},{2,3},{5,4},{4,5},{7,6},{6,7},{9,8},{8,9},{11,10... | collective-permute-start | bytes 417800 | tf_op jit(solution)/shard_map/ppermute | solution.py:507
  16.6 1.6 %collective-permute-start.7 = (f32[272,128]{1,0:T(8,128)S(1)}, f32[272,128]{1,0:T(8,128)S(1)}, u32[]{:S(2)}, u32[]{:S(2)}) collective-permute-start(f32[272,128]{1,0:T(8,128)S(1)} %collective-permute-done.3.refs_4_), channel_id=1, source_target_pairs={{1,0},{0,1},{3,2},{2,3},{5,4},{4,5},{7,6},{6,7},{9,8},{8,9},{11,10... | collective-permute-start | bytes 417800 | tf_op jit(solution)/shard_map/ppermute | solution.py:507
  16.6 1.6 %collective-permute-start.9 = (f32[272,128]{1,0:T(8,128)S(1)}, f32[272,128]{1,0:T(8,128)S(1)}, u32[]{:S(2)}, u32[]{:S(2)}) collective-permute-start(f32[272,128]{1,0:T(8,128)S(1)} %collective-permute-done.8.refs_6_), channel_id=1, source_target_pairs={{1,0},{0,1},{3,2},{2,3},{5,4},{4,5},{7,6},{6,7},{9,8},{8,9},{11,10... | collective-permute-start | bytes 417800 | tf_op jit(solution)/shard_map/ppermute | solution.py:507
  17.1 1.4 %collective-permute-start.2 = (f32[272,128]{1,0:T(8,128)S(1)}, f32[272,128]{1,0:T(8,128)S(1)}, u32[]{:S(2)}, u32[]{:S(2)}) collective-permute-start(f32[272,128]{1,0:T(8,128)S(1)} %collective-permute-done.1.refs_2_), channel_id=1, source_target_pairs={{1,0},{0,1},{3,2},{2,3},{5,4},{4,5},{7,6},{6,7},{9,8},{8,9},{11,10... | collective-permute-start | bytes 417800 | tf_op jit(solution)/shard_map/ppermute | solution.py:507

commit v9 on v8

--- a/solution.py
+++ b/solution.py
@@ -243,15 +243,11 @@
     return jnp.where(bottom > 0.0, top / jnp.where(bottom > 0.0, bottom, 1.0), 0.0)
 
 
-def x_next(values, wrap_mask):
-    return jnp.where(wrap_mask, pltpu.roll(values, X_OUT - 1, 1), pltpu.roll(values, LANES - 1, 1))
-
-
-def x_prev(values, wrap_mask):
-    return jnp.where(wrap_mask, pltpu.roll(values, LANES - X_OUT + 1, 1), pltpu.roll(values, 1, 1))
-
-
-def apply_planes(vector, diagonal, first, count, group, last_x, first_x):
+def lane_moved(values, lanes):
+    return jnp.take_along_axis(values, lanes, axis=1)
+
+
+def apply_planes(vector, diagonal, first, count, group, x_after, x_before):
     planes = vector.shape[0]
     rows = pl.ds(group * SUB, SUB)
     held = {}
@@ -266,8 +262,8 @@
         out = []
         for yi in range(Y_IN):
             line = here[yi * X_IN : (yi + 1) * X_IN]
-            before = [x_prev(line[X_IN - 2], first_x), x_prev(line[X_IN - 1], first_x)]
-            after = [x_next(line[0], last_x), x_next(line[1], last_x)]
+            before = [lane_moved(value, x_before) for value in line[X_IN - 2 :]]
+            after = [lane_moved(value, x_after) for value in line[:2]]
             wide = before + line + after
             for xi in range(X_IN):
                 m = yi * X_IN + xi
@@ -389,8 +385,9 @@
     depth = planes // parts
     groups = count // SUB
     lane = lax.broadcasted_iota(jnp.int32, (SUB, LANES), 1)
-    last_x = lax.rem(lane, X_OUT) == X_OUT - 1
-    first_x = lax.rem(lane, X_OUT) == 0
+    x_out = jnp.bitwise_and(lane, X_OUT - 1)
+    x_after = lane - x_out + jnp.bitwise_and(x_out + 1, X_OUT - 1)
+    x_before = lane - x_out + jnp.bitwise_and(x_out + X_OUT - 1, X_OUT - 1)
     here = lax.axis_index("dom")
     for turn in range(parts):
         slab = jnp.bitwise_xor(here, turn) * depth
@@ -416,7 +413,7 @@
             for group in range(groups):
                 rows = pl.ds(group * SUB, SUB)
                 curve, norm = sums[group]
-                done = apply_planes(source, diagonal, first, TOGETHER, group, last_x, first_x)
+                done = apply_planes(source, diagonal, first, TOGETHER, group, x_after, x_before)
                 for plane, (value, out) in enumerate(done):
                     for m in range(ROWS):
                         target[first + plane, rows, pl.ds(m * LANES, LANES)] = out[m]
@@ -469,16 +466,16 @@
         high = values.astype(jnp.bfloat16)
         low = (values - high.astype(jnp.float32)).astype(jnp.bfloat16)
         gram[...] += lax.dot_general(
+            jnp.concatenate([high, low], axis=0),
             high,
-            jnp.concatenate([high, low], axis=0),
             (((1,), (1,)), ((), ())),
             preferred_element_type=jnp.float32,
         )
         return carry
 
     lax.fori_loop(0, planes, gram_turn, 0, unroll=TOGETHER)
-    cross = gram[:, size:]
-    pairs = gram[:, :size] + cross + cross.T
+    cross = gram[size:, :]
+    pairs = gram[:size, :] + cross + cross.T
 
     here = lax.axis_index("point")
     for far, tile in enumerate(tiles):
@@ -513,7 +510,6 @@
     block, tile = packed_block(sources, potential, iter_counts)
     even = [block] + [swapped(block, "dom", parts, mask) for mask in range(CORES, parts, CORES)]
     tiles = [swapped(tile, "point", points, far) for far in range(1, points)]
-    even[2], *tiles = lax.optimization_barrier((even[2], *tiles))
     odd = [swapped(value, "dom", parts, 1) for value in even]
     blocks = [value for pair in zip(even, odd) for value in pair]
     vmem = pl.BlockSpec(memory_space=pltpu.VMEM)
@@ -530,9 +526,6 @@
             pltpu.VMEM((planes, SUB, ROWS * LANES), jnp.float32),
         ],
         compiler_params=pltpu.CompilerParams(vmem_limit_bytes=16 * 2**20),
-        cost_estimate=pl.CostEstimate(
-            flops=ITERS * count * cells * 30, bytes_accessed=32 * 2**20, transcendentals=0
-        ),
         name="krylov",
     )(*blocks)
     size = BASIS * count
@@ -544,7 +537,7 @@
         in_specs=[vmem] * (1 + points + BASIS),
         out_specs=(vmem, vmem),
         scratch_shapes=[
-            pltpu.VMEM((size, 2 * size), jnp.float32),
+            pltpu.VMEM((2 * size, size), jnp.float32),
             pltpu.VMEM((points, SUB, LANES), jnp.float32),
         ],
         compiler_params=pltpu.CompilerParams(vmem_limit_bytes=16 * 2**20),

time: 33.7 us -> 34.2 us (1.015)
    pallas_call x1, Pallas kernels: 10.3 us -> 10.9 us  [whole_grid(): pl.pallas_call(functools.partial(krylov_kernel, parts, count), out_shape=...]
    pallas_call x1, Pallas kernels: 4.75 us -> 4.28 us  [whole_grid(): pl.pallas_call(functools.partial(gram_kernel, points), out_shape=(out, ou...]
  transfers between devices with their start and end apart: 10 -> 10, of which waited for: 6 -> 2; matrix products, arithmetic and copies ran while one was open for 0% -> 0% of each run, Pallas kernels for 0% -> 32%
where the time goes in v9:
time: 34.2 us; the launch traced here: 34 us
  Pallas kernels  15.7 us (46%)
  starting transfers between devices  9.45 us (28%)
  waiting for transfers between devices  6.59 us (19%)
  between operations  1.31 us (4%)
  other arithmetic  0.93 us (3%)
    pallas_call x1, Pallas kernels, whole_grid(): pl.pallas_call(functools.partial(krylov_kernel, parts, count), out_shape=...  10.9 us
    ppermute x10, starting transfers between devices, swapped(): lax.ppermute(values, axis, [(index ^ mask, index) for index in range(size)])  9.45 us
    ppermute x10, waiting for transfers between devices, swapped(): lax.ppermute(values, axis, [(index ^ mask, index) for index in range(size)])  6.59 us
    pallas_call x1, Pallas kernels, whole_grid(): pl.pallas_call(functools.partial(gram_kernel, points), out_shape=(out, ou...  4.28 us
    concatenate x1, other arithmetic, packed_block(): jnp.concatenate([rows, levels], axis=0)  0.93 us
  transfers between devices with their start and end apart: 10, of which 2 were waited for; matrix products, arithmetic and copies ran while one was open for 0% of the time, Pallas kernels for 32%

profile of v9, /device:TPU:0, one launch (start us, length us, event | category | flops | bytes accessed | tf_op | source)
XLA Modules:
  0.0 34.0 jit_solution(1000380346658634755)
XLA Ops:
  1.3 0.9 %pad_maximum_fusion.rows = f32[272,128]{1,0:T(8,128)S(1)} fusion(f32[16,128]{1,0:T(8,128)} %bitcast.13, f32[256,128]{1,0:T(8,128)} %bitcast.12), kind=kLoop, calls=%fused_computation | loop fusion | flops 34816 | bytes 278528 | tf_op jit(solution)/shard_map/concatenate | solution.py:235
  2.2 0.6 %pack.1 = (f32[272,128]{1,0:T(8,128)S(1)}, f32[8,128]{1,0:T(8,128)S(1)}) custom-call(s32[1,1]{1,0:T(1,128)} %bitcast.11.counts, f32[272,128]{1,0:T(8,128)S(1)} %pad_maximum_fusion.rows), custom_call_target="tpu_custom_call" | custom-call | tf_op jit(solution)/shard_map/pack/pallas_call | solution.py:225
  2.8 3.0 %collective-permute-start.1 = (f32[272,128]{1,0:T(8,128)S(1)}, f32[272,128]{1,0:T(8,128)S(1)}, u32[]{:S(2)}, u32[]{:S(2)}) collective-permute-start(f32[272,128]{1,0:T(8,128)S(1)} %get-tuple-element.12.refs_0_), channel_id=1, source_target_pairs={{2,0},{3,1},{0,2},{1,3},{6,4},{7,5},{4,6},{5,7},{10,8},{11,9},{8,1... | collective-permute-start | bytes 417800 | tf_op jit(solution)/shard_map/ppermute | solution.py:504
  5.8 1.5 %collective-permute-start.3 = (f32[272,128]{1,0:T(8,128)S(1)}, f32[272,128]{1,0:T(8,128)S(1)}, u32[]{:S(2)}, u32[]{:S(2)}) collective-permute-start(f32[272,128]{1,0:T(8,128)S(1)} %get-tuple-element.12.refs_0_), channel_id=1, source_target_pairs={{4,0},{5,1},{6,2},{7,3},{0,4},{1,5},{2,6},{3,7},{12,8},{13,9},{14,... | collective-permute-start | bytes 417800 | tf_op jit(solution)/shard_map/ppermute | solution.py:504
  7.3 0.0 collective-permute-start.5
  7.3 0.0 collective-permute-start
  7.3 2.5 %collective-permute-done.1.refs_2_ = f32[272,128]{1,0:T(8,128)S(1)} collective-permute-done((f32[272,128]{1,0:T(8,128)S(1)}, f32[272,128]{1,0:T(8,128)S(1)}, u32[]{:S(2)}, u32[]{:S(2)}) %collective-permute-start.1) | collective-permute-done | bytes 139296 | tf_op jit(solution)/shard_map/ppermute | solution.py:504
  9.9 0.0 collective-permute-start.2
  9.9 4.0 %collective-permute-done.3.refs_4_ = f32[272,128]{1,0:T(8,128)S(1)} collective-permute-done((f32[272,128]{1,0:T(8,128)S(1)}, f32[272,128]{1,0:T(8,128)S(1)}, u32[]{:S(2)}, u32[]{:S(2)}) %collective-permute-start.3) | collective-permute-done | bytes 139296 | tf_op jit(solution)/shard_map/ppermute | solution.py:504
  13.9 0.0 collective-permute-start.4
  13.9 0.0 collective-permute-done.5.refs_6_
  13.9 0.5 %collective-permute-start.6 = (f32[272,128]{1,0:T(8,128)S(1)}, f32[272,128]{1,0:T(8,128)S(1)}, u32[]{:S(2)}, u32[]{:S(2)}) collective-permute-start(f32[272,128]{1,0:T(8,128)S(1)} %collective-permute-done.5.refs_6_), channel_id=1, source_target_pairs={{1,0},{0,1},{3,2},{2,3},{5,4},{4,5},{7,6},{6,7},{9,8},{8,9},{11,10... | collective-permute-start | bytes 417800 | tf_op jit(solution)/shard_map/ppermute | solution.py:504
  14.4 1.6 %collective-permute-start.7 = (f32[8,128]{1,0:T(8,128)S(1)}, f32[8,128]{1,0:T(8,128)S(1)}, u32[]{:S(2)}, u32[]{:S(2)}) collective-permute-start(f32[8,128]{1,0:T(8,128)S(1)} %get-tuple-element.14.refs_0_), channel_id=1, source_target_pairs={{8,0},{0,8},{24,16},{16,24},{9,1},{1,9},{25,17},{17,25},{10,2},{2,... | collective-permute-start | bytes 12296 | tf_op jit(solution)/shard_map/ppermute | solution.py:504
  16.0 0.0 collective-permute-done.refs_1_
  16.0 2.6 %collective-permute-start.8 = (f32[8,128]{1,0:T(8,128)S(1)}, f32[8,128]{1,0:T(8,128)S(1)}, u32[]{:S(2)}, u32[]{:S(2)}) collective-permute-start(f32[8,128]{1,0:T(8,128)S(1)} %get-tuple-element.14.refs_0_), channel_id=1, source_target_pairs={{16,0},{24,8},{0,16},{8,24},{17,1},{25,9},{1,17},{9,25},{18,2},{26... | collective-permute-start | bytes 12296 | tf_op jit(solution)/shard_map/ppermute | solution.py:504
  18.6 0.0 collective-permute-done.2.refs_3_
  18.6 0.2 collective-permute-start.9
  18.8 0.0 collective-permute-done.4.refs_5_
  18.8 0.0 collective-permute-done.6.refs_7_
  18.8 10.9 %krylov.1 = (f32[16,16,1024]{2,1,0:T(8,128)S(1)}, f32[16,16,1024]{2,1,0:T(8,128)S(1)}, f32[16,16,1024]{2,1,0:T(8,128)S(1)}, f32[16,16,1024]{2,1,0:T(8,128)S(1)},...) custom-call(f32[272,128]{1,0:T(8,128)S(1)} %get-tuple-element.12.ref, ...), custom_call_target="tpu_custom_call" | custom-call | tf_op jit(solution)/shard_map/krylov/pallas_call | solution.py:518
  29.7 0.0 collective-permute-done.7.refs_1_
  29.7 0.0 collective-permute-done.8.refs_2_
  29.7 0.0 collective-permute-done.9.refs_3_
  29.7 4.3 %gram.1 = (f32[2,64,64]{2,1,0:T(8,128)}, f32[2,64,64]{2,1,0:T(8,128)}) custom-call(f32[12,16,128]{2,1,0:T(8,128)S(1)} %get-tuple-element.13.scalars, f32[8,128]{1,0:T(8,128)S(1)} %get-tuple-element.14.refs_0_, f32[8,128]{1,0:T(8,128)S(1)} %collective-permute-done.7.refs_1_, f32[8,128]{1,0:T(8,128)S(1)} %collective-permute-done.8.refs_2_, ...), custom_call_target="tpu_custom_call" | custom-call | tf_op jit(solution)/shard_map/gram/pallas_call | solution.py:534
Async XLA Ops:
  2.8 7.1 %collective-permute-start.1 = (f32[272,128]{1,0:T(8,128)S(1)}, f32[272,128]{1,0:T(8,128)S(1)}, u32[]{:S(2)}, u32[]{:S(2)}) collective-permute-start(f32[272,128]{1,0:T(8,128)S(1)} %get-tuple-element.12.refs_0_), channel_id=1, source_target_pairs={{2,0},{3,1},{0,2},{1,3},{6,4},{7,5},{4,6},{5,7},{10,8},{11,9},{8,1... | collective-permute-start | bytes 417800 | tf_op jit(solution)/shard_map/ppermute | solution.py:504
  5.8 8.1 %collective-permute-start.3 = (f32[272,128]{1,0:T(8,128)S(1)}, f32[272,128]{1,0:T(8,128)S(1)}, u32[]{:S(2)}, u32[]{:S(2)}) collective-permute-start(f32[272,128]{1,0:T(8,128)S(1)} %get-tuple-element.12.refs_0_), channel_id=1, source_target_pairs={{4,0},{5,1},{6,2},{7,3},{0,4},{1,5},{2,6},{3,7},{12,8},{13,9},{14,... | collective-permute-start | bytes 417800 | tf_op jit(solution)/shard_map/ppermute | solution.py:504
  7.3 6.6 %collective-permute-start.5 = (f32[272,128]{1,0:T(8,128)S(1)}, f32[272,128]{1,0:T(8,128)S(1)}, u32[]{:S(2)}, u32[]{:S(2)}) collective-permute-start(f32[272,128]{1,0:T(8,128)S(1)} %get-tuple-element.12.refs_0_), channel_id=1, source_target_pairs={{6,0},{7,1},{4,2},{5,3},{2,4},{3,5},{0,6},{1,7},{14,8},{15,9},{12,... | collective-permute-start | bytes 417800 | tf_op jit(solution)/shard_map/ppermute | solution.py:504
  7.3 8.7 %collective-permute-start = (f32[272,128]{1,0:T(8,128)S(1)}, f32[272,128]{1,0:T(8,128)S(1)}, u32[]{:S(2)}, u32[]{:S(2)}) collective-permute-start(f32[272,128]{1,0:T(8,128)S(1)} %get-tuple-element.12.refs_0_), channel_id=1, source_target_pairs={{1,0},{0,1},{3,2},{2,3},{5,4},{4,5},{7,6},{6,7},{9,8},{8,9},{11,10... | collective-permute-start | bytes 417800 | tf_op jit(solution)/shard_map/ppermute | solution.py:504
  9.9 8.7 %collective-permute-start.2 = (f32[272,128]{1,0:T(8,128)S(1)}, f32[272,128]{1,0:T(8,128)S(1)}, u32[]{:S(2)}, u32[]{:S(2)}) collective-permute-start(f32[272,128]{1,0:T(8,128)S(1)} %collective-permute-done.1.refs_2_), channel_id=1, source_target_pairs={{1,0},{0,1},{3,2},{2,3},{5,4},{4,5},{7,6},{6,7},{9,8},{8,9},{11,10... | collective-permute-start | bytes 417800 | tf_op jit(solution)/shard_map/ppermute | solution.py:504
  13.9 4.9 %collective-permute-start.4 = (f32[272,128]{1,0:T(8,128)S(1)}, f32[272,128]{1,0:T(8,128)S(1)}, u32[]{:S(2)}, u32[]{:S(2)}) collective-permute-start(f32[272,128]{1,0:T(8,128)S(1)} %collective-permute-done.3.refs_4_), channel_id=1, source_target_pairs={{1,0},{0,1},{3,2},{2,3},{5,4},{4,5},{7,6},{6,7},{9,8},{8,9},{11,10... | collective-permute-start | bytes 417800 | tf_op jit(solution)/shard_map/ppermute | solution.py:504
  13.9 4.9 %collective-permute-start.6 = (f32[272,128]{1,0:T(8,128)S(1)}, f32[272,128]{1,0:T(8,128)S(1)}, u32[]{:S(2)}, u32[]{:S(2)}) collective-permute-start(f32[272,128]{1,0:T(8,128)S(1)} %collective-permute-done.5.refs_6_), channel_id=1, source_target_pairs={{1,0},{0,1},{3,2},{2,3},{5,4},{4,5},{7,6},{6,7},{9,8},{8,9},{11,10... | collective-permute-start | bytes 417800 | tf_op jit(solution)/shard_map/ppermute | solution.py:504
  14.4 15.3 %collective-permute-start.7 = (f32[8,128]{1,0:T(8,128)S(1)}, f32[8,128]{1,0:T(8,128)S(1)}, u32[]{:S(2)}, u32[]{:S(2)}) collective-permute-start(f32[8,128]{1,0:T(8,128)S(1)} %get-tuple-element.14.refs_0_), channel_id=1, source_target_pairs={{8,0},{0,8},{24,16},{16,24},{9,1},{1,9},{25,17},{17,25},{10,2},{2,... | collective-permute-start | bytes 12296 | tf_op jit(solution)/shard_map/ppermute | solution.py:504
  16.0 13.7 %collective-permute-start.8 = (f32[8,128]{1,0:T(8,128)S(1)}, f32[8,128]{1,0:T(8,128)S(1)}, u32[]{:S(2)}, u32[]{:S(2)}) collective-permute-start(f32[8,128]{1,0:T(8,128)S(1)} %get-tuple-element.14.refs_0_), channel_id=1, source_target_pairs={{16,0},{24,8},{0,16},{8,24},{17,1},{25,9},{1,17},{9,25},{18,2},{26... | collective-permute-start | bytes 12296 | tf_op jit(solution)/shard_map/ppermute | solution.py:504
  18.6 11.2 %collective-permute-start.9 = (f32[8,128]{1,0:T(8,128)S(1)}, f32[8,128]{1,0:T(8,128)S(1)}, u32[]{:S(2)}, u32[]{:S(2)}) collective-permute-start(f32[8,128]{1,0:T(8,128)S(1)} %get-tuple-element.14.refs_0_), channel_id=1, source_target_pairs={{24,0},{16,8},{8,16},{0,24},{25,1},{17,9},{9,17},{1,25},{26,2},{18... | collective-permute-start | bytes 12296 | tf_op jit(solution)/shard_map/ppermute | solution.py:504

commit v10 on v8

--- a/solution.py
+++ b/solution.py
@@ -167,6 +167,7 @@
 BASIS = ITERS + 1
 CORES = 2
 TOGETHER = 4
+TILE = 128
 H_SCALE = 2.0 / COEF_NEAR
 FAR_SCALED = 0.5 * H_SCALE * COEF_FAR
 
@@ -212,7 +213,7 @@
             value = jnp.where(lane_block == (row + far) % columns, moved, value)
         start = depth * ROWS * SUB * groups + deep * ROWS
         out[start : start + ROWS, :] = value
-    tile[...] = jnp.broadcast_to(counts[...].astype(jnp.float32), (SUB, LANES))
+    tile[...] = jnp.broadcast_to(counts[...].astype(jnp.float32), tile.shape)
 
 
 def packed_block(sources, potential, iter_counts):
@@ -226,7 +227,7 @@
         functools.partial(pack_kernel, depth, count // SUB),
         out_shape=(
             jax.ShapeDtypeStruct((size, LANES), jnp.float32),
-            jax.ShapeDtypeStruct((SUB, LANES), jnp.float32),
+            jax.ShapeDtypeStruct((TILE, LANES), jnp.float32),
         ),
         in_specs=[vmem, vmem],
         out_specs=(vmem, vmem),
@@ -266,8 +267,8 @@
         out = []
         for yi in range(Y_IN):
             line = here[yi * X_IN : (yi + 1) * X_IN]
-            before = [x_prev(line[X_IN - 2], first_x), x_prev(line[X_IN - 1], first_x)]
-            after = [x_next(line[0], last_x), x_next(line[1], last_x)]
+            before = [x_prev(value, first_x) for value in line[X_IN - 2 :]]
+            after = [x_next(value, last_x) for value in line[:2]]
             wide = before + line + after
             for xi in range(X_IN):
                 m = yi * X_IN + xi
@@ -456,9 +457,8 @@
         scalars[i] = jnp.concatenate(value, axis=0)
 
 
-def gram_kernel(points, scalars, *refs):
-    tiles, vectors = refs[:points], refs[points : points + BASIS]
-    out_b, out_a, gram, limits = refs[points + BASIS :]
+def gram_kernel(points, limits, scalars, *refs):
+    vectors, (out_b, out_a, gram) = refs[:BASIS], refs[BASIS:]
     planes, count, _ = vectors[0].shape
     groups = count // SUB
     size = BASIS * count
@@ -469,20 +469,17 @@
         high = values.astype(jnp.bfloat16)
         low = (values - high.astype(jnp.float32)).astype(jnp.bfloat16)
         gram[...] += lax.dot_general(
+            jnp.concatenate([high, low], axis=0),
             high,
-            jnp.concatenate([high, low], axis=0),
             (((1,), (1,)), ((), ())),
             preferred_element_type=jnp.float32,
         )
         return carry
 
     lax.fori_loop(0, planes, gram_turn, 0, unroll=TOGETHER)
-    cross = gram[:, size:]
-    pairs = gram[:, :size] + cross + cross.T
-
-    here = lax.axis_index("point")
-    for far, tile in enumerate(tiles):
-        limits[jnp.bitwise_xor(here, far)] = tile[...]
+    cross = gram[size:, :]
+    pairs = gram[:size, :] + cross + cross.T
+
     bounds = [jnp.concatenate([limits[j]] * groups, axis=0) for j in range(points)]
     alphas = [scalars[i] for i in range(ITERS)]
     norms = [scalars[ITERS + i] for i in range(ITERS)]
@@ -512,8 +509,7 @@
     planes = parts * depth
     block, tile = packed_block(sources, potential, iter_counts)
     even = [block] + [swapped(block, "dom", parts, mask) for mask in range(CORES, parts, CORES)]
-    tiles = [swapped(tile, "point", points, far) for far in range(1, points)]
-    even[2], *tiles = lax.optimization_barrier((even[2], *tiles))
+    limits = lax.all_gather(tile, "point")[:, :SUB]
     odd = [swapped(value, "dom", parts, 1) for value in even]
     blocks = [value for pair in zip(even, odd) for value in pair]
     vmem = pl.BlockSpec(memory_space=pltpu.VMEM)
@@ -530,9 +526,6 @@
             pltpu.VMEM((planes, SUB, ROWS * LANES), jnp.float32),
         ],
         compiler_params=pltpu.CompilerParams(vmem_limit_bytes=16 * 2**20),
-        cost_estimate=pl.CostEstimate(
-            flops=ITERS * count * cells * 30, bytes_accessed=32 * 2**20, transcendentals=0
-        ),
         name="krylov",
     )(*blocks)
     size = BASIS * count
@@ -541,15 +534,12 @@
     return pl.pallas_call(
         functools.partial(gram_kernel, points),
         out_shape=(out, out),
-        in_specs=[vmem] * (1 + points + BASIS),
+        in_specs=[vmem] * (2 + BASIS),
         out_specs=(vmem, vmem),
-        scratch_shapes=[
-            pltpu.VMEM((size, 2 * size), jnp.float32),
-            pltpu.VMEM((points, SUB, LANES), jnp.float32),
-        ],
+        scratch_shapes=[pltpu.VMEM((2 * size, size), jnp.float32)],
         compiler_params=pltpu.CompilerParams(vmem_limit_bytes=16 * 2**20),
         name="gram",
-    )(scalars, tile, *tiles, *vectors)
+    )(limits, scalars, *vectors)
 
 
 def on_device(sources, potential, iter_counts):

time: 33.7 us -> 43 us (1.28)
  blocking collectives: 0 us -> 14.2 us
  starting transfers between devices: 9.19 us -> 4.87 us
  Pallas kernels: 15.6 us -> 15.1 us
    all_gather x0 -> x1, blocking collectives: none -> 14.2 us  [whole_grid(): limits = lax.all_gather(tile, 'point')[:, :SUB]]
    ppermute x10 -> x7, starting transfers between devices: 9.19 us -> 4.87 us  [swapped(): lax.ppermute(values, axis, [(index ^ mask, index) for index in range(size)])]
    pallas_call x1, Pallas kernels: 4.75 us -> 4.27 us  [whole_grid(): pl.pallas_call(functools.partial(gram_kernel, points), out_shape=(out, ou...]
    ppermute x10 -> x7, waiting for transfers between devices: 6.48 us -> 6.26 us  [swapped(): lax.ppermute(values, axis, [(index ^ mask, index) for index in range(size)])]
  transfers between devices with their start and end apart: 10 -> 7, of which waited for: 6 -> 3; matrix products, arithmetic and copies ran while one was open for 0% -> 0% of each run, Pallas kernels for 0% -> 0%
where the time goes in v10:
time: 43 us; the launch traced here: 42.7 us
  Pallas kernels  15.1 us (35%)
  blocking collectives  14.2 us (33%)
  waiting for transfers between devices  6.26 us (15%)
  starting transfers between devices  4.87 us (11%)
  between operations  1.32 us (3%)
  other arithmetic  0.93 us (2%)
    all_gather x1, blocking collectives, whole_grid(): limits = lax.all_gather(tile, 'point')[:, :SUB]  14.2 us
    pallas_call x1, Pallas kernels, whole_grid(): pl.pallas_call(functools.partial(krylov_kernel, parts, count), out_shape=...  10.3 us
    ppermute x7, waiting for transfers between devices, swapped(): lax.ppermute(values, axis, [(index ^ mask, index) for index in range(size)])  6.26 us
    ppermute x7, starting transfers between devices, swapped(): lax.ppermute(values, axis, [(index ^ mask, index) for index in range(size)])  4.87 us
    pallas_call x1, Pallas kernels, whole_grid(): pl.pallas_call(functools.partial(gram_kernel, points), out_shape=(out, ou...  4.27 us
    concatenate x1, other arithmetic, packed_block(): jnp.concatenate([rows, levels], axis=0)  0.93 us
  transfers between devices with their start and end apart: 7, of which 3 were waited for; matrix products, arithmetic and copies ran while one was open for 0% of the time, Pallas kernels for 0%

profile of v10, /device:TPU:0, one launch (start us, length us, event | category | flops | bytes accessed | tf_op | source)
XLA Modules:
  0.0 42.7 jit_solution(14516521986225403606)
XLA Ops:
  1.3 0.9 %pad_maximum_fusion.rows = f32[272,128]{1,0:T(8,128)S(1)} fusion(f32[16,128]{1,0:T(8,128)} %bitcast.15, f32[256,128]{1,0:T(8,128)} %bitcast.14), kind=kLoop, calls=%fused_computation | loop fusion | flops 34816 | bytes 278528 | tf_op jit(solution)/shard_map/concatenate | solution.py:236
  2.2 0.6 %pack.1 = (f32[272,128]{1,0:T(8,128)S(1)}, f32[128,128]{1,0:T(8,128)S(1)}) custom-call(s32[1,1]{1,0:T(1,128)} %bitcast.12.counts, f32[272,128]{1,0:T(8,128)S(1)} %pad_maximum_fusion.rows), custom_call_target="tpu_custom_call" | custom-call | tf_op jit(solution)/shard_map/pack/pallas_call | solution.py:226
  2.8 4.0 %collective-permute-start.5 = (f32[272,128]{1,0:T(8,128)S(1)}, f32[272,128]{1,0:T(8,128)S(1)}, u32[]{:S(2)}, u32[]{:S(2)}) collective-permute-start(f32[272,128]{1,0:T(8,128)S(1)} %get-tuple-element.13.refs_0_), channel_id=1, source_target_pairs={{6,0},{7,1},{4,2},{5,3},{2,4},{3,5},{0,6},{1,7},{14,8},{15,9},{12,... | collective-permute-start | bytes 417800 | tf_op jit(solution)/shard_map/ppermute | solution.py:504
  6.7 0.5 %collective-permute-start.3 = (f32[272,128]{1,0:T(8,128)S(1)}, f32[272,128]{1,0:T(8,128)S(1)}, u32[]{:S(2)}, u32[]{:S(2)}) collective-permute-start(f32[272,128]{1,0:T(8,128)S(1)} %get-tuple-element.13.refs_0_), channel_id=1, source_target_pairs={{4,0},{5,1},{6,2},{7,3},{0,4},{1,5},{2,6},{3,7},{12,8},{13,9},{14,... | collective-permute-start | bytes 417800 | tf_op jit(solution)/shard_map/ppermute | solution.py:504
  7.2 0.1 collective-permute-start.1
  7.4 0.0 collective-permute-start
  7.4 3.4 %collective-permute-done.5.refs_6_ = f32[272,128]{1,0:T(8,128)S(1)} collective-permute-done((f32[272,128]{1,0:T(8,128)S(1)}, f32[272,128]{1,0:T(8,128)S(1)}, u32[]{:S(2)}, u32[]{:S(2)}) %collective-permute-start.5) | collective-permute-done | bytes 139296 | tf_op jit(solution)/shard_map/ppermute | solution.py:504
  10.8 0.0 collective-permute-start.6
  10.8 2.6 %collective-permute-done.3.refs_4_ = f32[272,128]{1,0:T(8,128)S(1)} collective-permute-done((f32[272,128]{1,0:T(8,128)S(1)}, f32[272,128]{1,0:T(8,128)S(1)}, u32[]{:S(2)}, u32[]{:S(2)}) %collective-permute-start.3) | collective-permute-done | bytes 139296 | tf_op jit(solution)/shard_map/ppermute | solution.py:504
  13.4 0.0 collective-permute-start.4
  13.4 0.2 collective-permute-done.1.refs_2_
  13.7 0.3 collective-permute-start.2
  13.9 14.2 %all-gather = f32[512,128]{1,0:T(8,128)S(1)} all-gather(f32[128,128]{1,0:T(8,128)S(1)} %get-tuple-element.12), channel_id=2, replica_groups=mesh['point'=4,'dom'=8] {'point'}, dimensions={0}, use_global_device_ids=true | all-gather | bytes 327680 | tf_op jit(solution)/shard_map/all_gather | solution.py:512
  28.1 0.0 collective-permute-done.refs_1_
  28.1 0.0 collective-permute-done.6.refs_7_
  28.1 0.0 collective-permute-done.4.refs_5_
  28.1 0.0 collective-permute-done.2.refs_3_
  28.2 10.3 %krylov.1 = (f32[16,16,1024]{2,1,0:T(8,128)S(1)}, f32[16,16,1024]{2,1,0:T(8,128)S(1)}, f32[16,16,1024]{2,1,0:T(8,128)S(1)}, f32[16,16,1024]{2,1,0:T(8,128)S(1)},...) custom-call(f32[272,128]{1,0:T(8,128)S(1)} %get-tuple-element.13.ref, ...), custom_call_target="tpu_custom_call" | custom-call | tf_op jit(solution)/shard_map/krylov/pallas_call | solution.py:518
  38.5 4.3 %gram.1 = (f32[2,64,64]{2,1,0:T(8,128)}, f32[2,64,64]{2,1,0:T(8,128)}) custom-call(f32[4,8,128]{2,1,0:T(8,128)S(1)} %slice.4.limits, f32[12,16,128]{2,1,0:T(8,128)S(1)} %get-tuple-element.14.scalars, f32[16,16,1024]{2,1,0:T(8,128)S(1)} %get-tuple-element.15.refs_0_, f32[16,16,1024]{2,1,0:T(8,128)S(1)} %get-tuple-element.16.refs_1_, ...), custom_call_target="tpu_custom_call" | custom-call | tf_op jit(solution)/shard_map/gram/pallas_call | solution.py:534
  (1 shorter events, 0.0 us)
Async XLA Ops:
  2.8 8.0 %collective-permute-start.5 = (f32[272,128]{1,0:T(8,128)S(1)}, f32[272,128]{1,0:T(8,128)S(1)}, u32[]{:S(2)}, u32[]{:S(2)}) collective-permute-start(f32[272,128]{1,0:T(8,128)S(1)} %get-tuple-element.13.refs_0_), channel_id=1, source_target_pairs={{6,0},{7,1},{4,2},{5,3},{2,4},{3,5},{0,6},{1,7},{14,8},{15,9},{12,... | collective-permute-start | bytes 417800 | tf_op jit(solution)/shard_map/ppermute | solution.py:504
  6.7 6.7 %collective-permute-start.3 = (f32[272,128]{1,0:T(8,128)S(1)}, f32[272,128]{1,0:T(8,128)S(1)}, u32[]{:S(2)}, u32[]{:S(2)}) collective-permute-start(f32[272,128]{1,0:T(8,128)S(1)} %get-tuple-element.13.refs_0_), channel_id=1, source_target_pairs={{4,0},{5,1},{6,2},{7,3},{0,4},{1,5},{2,6},{3,7},{12,8},{13,9},{14,... | collective-permute-start | bytes 417800 | tf_op jit(solution)/shard_map/ppermute | solution.py:504
  7.2 6.4 %collective-permute-start.1 = (f32[272,128]{1,0:T(8,128)S(1)}, f32[272,128]{1,0:T(8,128)S(1)}, u32[]{:S(2)}, u32[]{:S(2)}) collective-permute-start(f32[272,128]{1,0:T(8,128)S(1)} %get-tuple-element.13.refs_0_), channel_id=1, source_target_pairs={{2,0},{3,1},{0,2},{1,3},{6,4},{7,5},{4,6},{5,7},{10,8},{11,9},{8,1... | collective-permute-start | bytes 417800 | tf_op jit(solution)/shard_map/ppermute | solution.py:504
  7.4 20.7 %collective-permute-start = (f32[272,128]{1,0:T(8,128)S(1)}, f32[272,128]{1,0:T(8,128)S(1)}, u32[]{:S(2)}, u32[]{:S(2)}) collective-permute-start(f32[272,128]{1,0:T(8,128)S(1)} %get-tuple-element.13.refs_0_), channel_id=1, source_target_pairs={{1,0},{0,1},{3,2},{2,3},{5,4},{4,5},{7,6},{6,7},{9,8},{8,9},{11,10... | collective-permute-start | bytes 417800 | tf_op jit(solution)/shard_map/ppermute | solution.py:504
  10.8 17.3 %collective-permute-start.6 = (f32[272,128]{1,0:T(8,128)S(1)}, f32[272,128]{1,0:T(8,128)S(1)}, u32[]{:S(2)}, u32[]{:S(2)}) collective-permute-start(f32[272,128]{1,0:T(8,128)S(1)} %collective-permute-done.5.refs_6_), channel_id=1, source_target_pairs={{1,0},{0,1},{3,2},{2,3},{5,4},{4,5},{7,6},{6,7},{9,8},{8,9},{11,10... | collective-permute-start | bytes 417800 | tf_op jit(solution)/shard_map/ppermute | solution.py:504
  13.4 14.7 %collective-permute-start.4 = (f32[272,128]{1,0:T(8,128)S(1)}, f32[272,128]{1,0:T(8,128)S(1)}, u32[]{:S(2)}, u32[]{:S(2)}) collective-permute-start(f32[272,128]{1,0:T(8,128)S(1)} %collective-permute-done.3.refs_4_), channel_id=1, source_target_pairs={{1,0},{0,1},{3,2},{2,3},{5,4},{4,5},{7,6},{6,7},{9,8},{8,9},{11,10... | collective-permute-start | bytes 417800 | tf_op jit(solution)/shard_map/ppermute | solution.py:504
  13.7 14.5 %collective-permute-start.2 = (f32[272,128]{1,0:T(8,128)S(1)}, f32[272,128]{1,0:T(8,128)S(1)}, u32[]{:S(2)}, u32[]{:S(2)}) collective-permute-start(f32[272,128]{1,0:T(8,128)S(1)} %collective-permute-done.1.refs_2_), channel_id=1, source_target_pairs={{1,0},{0,1},{3,2},{2,3},{5,4},{4,5},{7,6},{6,7},{9,8},{8,9},{11,10... | collective-permute-start | bytes 417800 | tf_op jit(solution)/shard_map/ppermute | solution.py:504

commit v11 on v8

--- a/solution.py
+++ b/solution.py
@@ -166,7 +166,8 @@
 SUB = 8
 BASIS = ITERS + 1
 CORES = 2
-TOGETHER = 4
+TOGETHER = 2
+UNROLL = 4
 H_SCALE = 2.0 / COEF_NEAR
 FAR_SCALED = 0.5 * H_SCALE * COEF_FAR
 
@@ -266,8 +267,8 @@
         out = []
         for yi in range(Y_IN):
             line = here[yi * X_IN : (yi + 1) * X_IN]
-            before = [x_prev(line[X_IN - 2], first_x), x_prev(line[X_IN - 1], first_x)]
-            after = [x_next(line[0], last_x), x_next(line[1], last_x)]
+            before = [x_prev(value, first_x) for value in line[X_IN - 2 :]]
+            after = [x_next(value, last_x) for value in line[:2]]
             wide = before + line + after
             for xi in range(X_IN):
                 m = yi * X_IN + xi
@@ -426,7 +427,8 @@
                 new_sums.append((curve, norm))
             return tuple(new_sums)
 
-        sums = lax.fori_loop(0, planes // TOGETHER, apply_turn, ((blank, blank),) * groups)
+        start = ((blank, blank),) * groups
+        sums = lax.fori_loop(0, planes // TOGETHER, apply_turn, start, unroll=2)
         if i == 0:
             norms.append([lane_sum(norm) for _, norm in sums])
         alphas.append([ratio(lane_sum(sums[g][0]), norms[i][g]) for g in range(groups)])
@@ -450,7 +452,7 @@
                 new_sums.append(norm)
             return tuple(new_sums)
 
-        sums = lax.fori_loop(0, planes, step_turn, (blank,) * groups, unroll=TOGETHER)
+        sums = lax.fori_loop(0, planes, step_turn, (blank,) * groups, unroll=UNROLL)
         norms.append([lane_sum(norm) for norm in sums])
     for i, value in enumerate(alphas + norms):
         scalars[i] = jnp.concatenate(value, axis=0)
@@ -469,19 +471,20 @@
         high = values.astype(jnp.bfloat16)
         low = (values - high.astype(jnp.float32)).astype(jnp.bfloat16)
         gram[...] += lax.dot_general(
+            jnp.concatenate([high, low], axis=0),
             high,
-            jnp.concatenate([high, low], axis=0),
             (((1,), (1,)), ((), ())),
             preferred_element_type=jnp.float32,
         )
         return carry
 
-    lax.fori_loop(0, planes, gram_turn, 0, unroll=TOGETHER)
-    cross = gram[:, size:]
-    pairs = gram[:, :size] + cross + cross.T
+    lax.fori_loop(0, planes, gram_turn, 0, unroll=UNROLL)
+    cross = gram[size:, :]
+    pairs = gram[:size, :] + cross + cross.T
 
     here = lax.axis_index("point")
-    for far, tile in enumerate(tiles):
+    core = jnp.bitwise_and(lax.axis_index("dom"), CORES - 1)
+    for far, tile in zip((0, 1 + core, 3, 2 - core), tiles):
         limits[jnp.bitwise_xor(here, far)] = tile[...]
     bounds = [jnp.concatenate([limits[j]] * groups, axis=0) for j in range(points)]
     alphas = [scalars[i] for i in range(ITERS)]
@@ -512,8 +515,14 @@
     planes = parts * depth
     block, tile = packed_block(sources, potential, iter_counts)
     even = [block] + [swapped(block, "dom", parts, mask) for mask in range(CORES, parts, CORES)]
-    tiles = [swapped(tile, "point", points, far) for far in range(1, points)]
-    even[2], *tiles = lax.optimization_barrier((even[2], *tiles))
+    mixed = [
+        ((point ^ (1 + part % CORES)) * parts + part, point * parts + part)
+        for point in range(points)
+        for part in range(parts)
+    ]
+    tiles = [lax.ppermute(tile, ("point", "dom"), mixed), swapped(tile, "point", points, 3)]
+    even[1], *tiles = lax.optimization_barrier((even[1], *tiles))
+    tiles.append(swapped(tiles[0], "dom", parts, 1))
     odd = [swapped(value, "dom", parts, 1) for value in even]
     blocks = [value for pair in zip(even, odd) for value in pair]
     vmem = pl.BlockSpec(memory_space=pltpu.VMEM)
@@ -530,9 +539,6 @@
             pltpu.VMEM((planes, SUB, ROWS * LANES), jnp.float32),
         ],
         compiler_params=pltpu.CompilerParams(vmem_limit_bytes=16 * 2**20),
-        cost_estimate=pl.CostEstimate(
-            flops=ITERS * count * cells * 30, bytes_accessed=32 * 2**20, transcendentals=0
-        ),
         name="krylov",
     )(*blocks)
     size = BASIS * count
@@ -544,7 +550,7 @@
         in_specs=[vmem] * (1 + points + BASIS),
         out_specs=(vmem, vmem),
         scratch_shapes=[
-            pltpu.VMEM((size, 2 * size), jnp.float32),
+            pltpu.VMEM((2 * size, size), jnp.float32),
             pltpu.VMEM((points, SUB, LANES), jnp.float32),
         ],
         compiler_params=pltpu.CompilerParams(vmem_limit_bytes=16 * 2**20),

time: 33.7 us -> 31.5 us (0.935)
  waiting for transfers between devices: 6.48 us -> 3.78 us
  starting transfers between devices: 9.19 us -> 10.1 us
  Pallas kernels: 15.6 us -> 15.2 us
    ppermute x10 -> x9, waiting for transfers between devices: 6.48 us -> 3.78 us  [swapped(): lax.ppermute(values, axis, [(index ^ mask, index) for index in range(size)])]
    ppermute x0 -> x1, starting transfers between devices: none -> 2.03 us  [whole_grid(): lax.ppermute(tile, ('point', 'dom'), mixed)]
    ppermute x10 -> x9, starting transfers between devices: 9.19 us -> 8.04 us  [swapped(): lax.ppermute(values, axis, [(index ^ mask, index) for index in range(size)])]
    pallas_call x1, Pallas kernels: 4.75 us -> 4.29 us  [whole_grid(): pl.pallas_call(functools.partial(gram_kernel, points), out_shape=(out, ou...]
  transfers between devices with their start and end apart: 10 -> 10, of which waited for: 6 -> 4; matrix products, arithmetic and copies ran while one was open for 0% -> 0% of each run, Pallas kernels for 0% -> 33%
where the time goes in v11:
time: 31.5 us; the launch traced here: 31.2 us
  Pallas kernels  15.2 us (48%)
  starting transfers between devices  10.1 us (32%)
  waiting for transfers between devices  3.78 us (12%)
  between operations  1.3 us (4%)
  other arithmetic  0.93 us (3%)
    pallas_call x1, Pallas kernels, whole_grid(): pl.pallas_call(functools.partial(krylov_kernel, parts, count), out_shape=...  10.3 us
    ppermute x9, starting transfers between devices, swapped(): lax.ppermute(values, axis, [(index ^ mask, index) for index in range(size)])  8.04 us
    pallas_call x1, Pallas kernels, whole_grid(): pl.pallas_call(functools.partial(gram_kernel, points), out_shape=(out, ou...  4.29 us
    ppermute x9, waiting for transfers between devices, swapped(): lax.ppermute(values, axis, [(index ^ mask, index) for index in range(size)])  3.78 us
    ppermute x1, starting transfers between devices, whole_grid(): lax.ppermute(tile, ('point', 'dom'), mixed)  2.03 us
    concatenate x1, other arithmetic, packed_block(): jnp.concatenate([rows, levels], axis=0)  0.93 us
  transfers between devices with their start and end apart: 10, of which 4 were waited for; matrix products, arithmetic and copies ran while one was open for 0% of the time, Pallas kernels for 33%

profile of v11, /device:TPU:0, one launch (start us, length us, event | category | flops | bytes accessed | tf_op | source)
XLA Modules:
  0.0 31.2 jit_solution(11552298554057436351)
XLA Ops:
  1.3 0.9 %pad_maximum_fusion.rows = f32[272,128]{1,0:T(8,128)S(1)} fusion(f32[16,128]{1,0:T(8,128)} %bitcast.13, f32[256,128]{1,0:T(8,128)} %bitcast.12), kind=kLoop, calls=%fused_computation | loop fusion | flops 34816 | bytes 278528 | tf_op jit(solution)/shard_map/concatenate | solution.py:236
  2.2 0.6 %pack.1 = (f32[272,128]{1,0:T(8,128)S(1)}, f32[8,128]{1,0:T(8,128)S(1)}) custom-call(s32[1,1]{1,0:T(1,128)} %bitcast.11.counts, f32[272,128]{1,0:T(8,128)S(1)} %pad_maximum_fusion.rows), custom_call_target="tpu_custom_call" | custom-call | tf_op jit(solution)/shard_map/pack/pallas_call | solution.py:226
  2.8 3.0 %collective-permute-start.1 = (f32[272,128]{1,0:T(8,128)S(1)}, f32[272,128]{1,0:T(8,128)S(1)}, u32[]{:S(2)}, u32[]{:S(2)}) collective-permute-start(f32[272,128]{1,0:T(8,128)S(1)} %get-tuple-element.15.refs_0_), channel_id=1, source_target_pairs={{2,0},{3,1},{0,2},{1,3},{6,4},{7,5},{4,6},{5,7},{10,8},{11,9},{8,1... | collective-permute-start | bytes 417800 | tf_op jit(solution)/shard_map/ppermute | solution.py:510
  5.8 1.5 %collective-permute-start.5 = (f32[272,128]{1,0:T(8,128)S(1)}, f32[272,128]{1,0:T(8,128)S(1)}, u32[]{:S(2)}, u32[]{:S(2)}) collective-permute-start(f32[272,128]{1,0:T(8,128)S(1)} %get-tuple-element.15.refs_0_), channel_id=1, source_target_pairs={{4,0},{5,1},{6,2},{7,3},{0,4},{1,5},{2,6},{3,7},{12,8},{13,9},{14,... | collective-permute-start | bytes 417800 | tf_op jit(solution)/shard_map/ppermute | solution.py:510
  7.3 0.0 collective-permute-start.7
  7.3 2.0 %collective-permute-start.2 = (f32[8,128]{1,0:T(8,128)S(1)}, f32[8,128]{1,0:T(8,128)S(1)}, u32[]{:S(2)}, u32[]{:S(2)}) collective-permute-start(f32[8,128]{1,0:T(8,128)S(1)} %get-tuple-element.16.refs_0_), channel_id=1, source_target_pairs={{8,0},{17,1},{10,2},{19,3},{12,4},{21,5},{14,6},{23,7},{0,8},{25,9... | collective-permute-start | bytes 12296 | tf_op jit(solution)/shard_map/ppermute | solution.py:523
  9.4 2.5 %collective-permute-start.3 = (f32[8,128]{1,0:T(8,128)S(1)}, f32[8,128]{1,0:T(8,128)S(1)}, u32[]{:S(2)}, u32[]{:S(2)}) collective-permute-start(f32[8,128]{1,0:T(8,128)S(1)} %get-tuple-element.16.refs_0_), channel_id=1, source_target_pairs={{24,0},{16,8},{8,16},{0,24},{25,1},{17,9},{9,17},{1,25},{26,2},{18... | collective-permute-start | bytes 12296 | tf_op jit(solution)/shard_map/ppermute | solution.py:510
  11.8 0.0 collective-permute-done.2.refs_1_
  11.8 0.0 collective-permute-start
  11.8 2.9 %collective-permute-done.3.refs_2_ = f32[8,128]{1,0:T(8,128)S(1)} collective-permute-done((f32[8,128]{1,0:T(8,128)S(1)}, f32[8,128]{1,0:T(8,128)S(1)}, u32[]{:S(2)}, u32[]{:S(2)}) %collective-permute-start.3) | collective-permute-done | bytes 4128 | tf_op jit(solution)/shard_map/ppermute | solution.py:510
  14.8 0.0 collective-permute-done.1.refs_2_
  14.8 0.0 collective-permute-start.4
  14.8 0.0 collective-permute-done.5.refs_4_
  14.8 0.5 %collective-permute-start.6 = (f32[272,128]{1,0:T(8,128)S(1)}, f32[272,128]{1,0:T(8,128)S(1)}, u32[]{:S(2)}, u32[]{:S(2)}) collective-permute-start(f32[272,128]{1,0:T(8,128)S(1)} %collective-permute-done.5.refs_4_), channel_id=1, source_target_pairs={{1,0},{0,1},{3,2},{2,3},{5,4},{4,5},{7,6},{6,7},{9,8},{8,9},{11,10... | collective-permute-start | bytes 417800 | tf_op jit(solution)/shard_map/ppermute | solution.py:510
  15.3 0.0 collective-permute-done.7.refs_6_
  15.3 0.1 collective-permute-start.8
  15.3 0.4 %collective-permute-start.9 = (f32[8,128]{1,0:T(8,128)S(1)}, f32[8,128]{1,0:T(8,128)S(1)}, u32[]{:S(2)}, u32[]{:S(2)}) collective-permute-start(f32[8,128]{1,0:T(8,128)S(1)} %collective-permute-done.2.refs_1_), channel_id=1, source_target_pairs={{1,0},{0,1},{3,2},{2,3},{5,4},{4,5},{7,6},{6,7},{9,8},{8,9},{11,10... | collective-permute-start | bytes 12296 | tf_op jit(solution)/shard_map/ppermute | solution.py:510
  15.8 0.0 collective-permute-done.refs_1_
  15.8 0.3 %collective-permute-done.4.refs_3_ = f32[272,128]{1,0:T(8,128)S(1)} collective-permute-done((f32[272,128]{1,0:T(8,128)S(1)}, f32[272,128]{1,0:T(8,128)S(1)}, u32[]{:S(2)}, u32[]{:S(2)}) %collective-permute-start.4) | collective-permute-done | bytes 139296 | tf_op jit(solution)/shard_map/ppermute | solution.py:510
  16.1 0.2 collective-permute-done.6.refs_5_
  16.3 0.3 %collective-permute-done.8.refs_7_ = f32[272,128]{1,0:T(8,128)S(1)} collective-permute-done((f32[272,128]{1,0:T(8,128)S(1)}, f32[272,128]{1,0:T(8,128)S(1)}, u32[]{:S(2)}, u32[]{:S(2)}) %collective-permute-start.8) | collective-permute-done | bytes 139296 | tf_op jit(solution)/shard_map/ppermute | solution.py:510
  16.6 10.3 %krylov.1 = (f32[16,16,1024]{2,1,0:T(8,128)S(1)}, f32[16,16,1024]{2,1,0:T(8,128)S(1)}, f32[16,16,1024]{2,1,0:T(8,128)S(1)}, f32[16,16,1024]{2,1,0:T(8,128)S(1)},...) custom-call(f32[272,128]{1,0:T(8,128)S(1)} %get-tuple-element.15.ref, ...), custom_call_target="tpu_custom_call" | custom-call | tf_op jit(solution)/shard_map/krylov/pallas_call | solution.py:531
  27.0 0.0 collective-permute-done.9.refs_3_
  27.0 4.3 %gram.1 = (f32[2,64,64]{2,1,0:T(8,128)}, f32[2,64,64]{2,1,0:T(8,128)}) custom-call(f32[12,16,128]{2,1,0:T(8,128)S(1)} %get-tuple-element.18.scalars, f32[8,128]{1,0:T(8,128)S(1)} %get-tuple-element.16.refs_0_, f32[8,128]{1,0:T(8,128)S(1)} %collective-permute-done.2.refs_1_, f32[8,128]{1,0:T(8,128)S(1)} %collective-permute-done.3.refs_2_, ...), custom_call_target="tpu_custom_call" | custom-call | tf_op jit(solution)/shard_map/gram/pallas_call | solution.py:547
Async XLA Ops:
  2.8 12.0 %collective-permute-start.1 = (f32[272,128]{1,0:T(8,128)S(1)}, f32[272,128]{1,0:T(8,128)S(1)}, u32[]{:S(2)}, u32[]{:S(2)}) collective-permute-start(f32[272,128]{1,0:T(8,128)S(1)} %get-tuple-element.15.refs_0_), channel_id=1, source_target_pairs={{2,0},{3,1},{0,2},{1,3},{6,4},{7,5},{4,6},{5,7},{10,8},{11,9},{8,1... | collective-permute-start | bytes 417800 | tf_op jit(solution)/shard_map/ppermute | solution.py:510
  5.8 9.0 %collective-permute-start.5 = (f32[272,128]{1,0:T(8,128)S(1)}, f32[272,128]{1,0:T(8,128)S(1)}, u32[]{:S(2)}, u32[]{:S(2)}) collective-permute-start(f32[272,128]{1,0:T(8,128)S(1)} %get-tuple-element.15.refs_0_), channel_id=1, source_target_pairs={{4,0},{5,1},{6,2},{7,3},{0,4},{1,5},{2,6},{3,7},{12,8},{13,9},{14,... | collective-permute-start | bytes 417800 | tf_op jit(solution)/shard_map/ppermute | solution.py:510
  7.3 8.0 %collective-permute-start.7 = (f32[272,128]{1,0:T(8,128)S(1)}, f32[272,128]{1,0:T(8,128)S(1)}, u32[]{:S(2)}, u32[]{:S(2)}) collective-permute-start(f32[272,128]{1,0:T(8,128)S(1)} %get-tuple-element.15.refs_0_), channel_id=1, source_target_pairs={{6,0},{7,1},{4,2},{5,3},{2,4},{3,5},{0,6},{1,7},{14,8},{15,9},{12,... | collective-permute-start | bytes 417800 | tf_op jit(solution)/shard_map/ppermute | solution.py:510
  7.3 4.5 %collective-permute-start.2 = (f32[8,128]{1,0:T(8,128)S(1)}, f32[8,128]{1,0:T(8,128)S(1)}, u32[]{:S(2)}, u32[]{:S(2)}) collective-permute-start(f32[8,128]{1,0:T(8,128)S(1)} %get-tuple-element.16.refs_0_), channel_id=1, source_target_pairs={{8,0},{17,1},{10,2},{19,3},{12,4},{21,5},{14,6},{23,7},{0,8},{25,9... | collective-permute-start | bytes 12296 | tf_op jit(solution)/shard_map/ppermute | solution.py:523
  9.4 5.4 %collective-permute-start.3 = (f32[8,128]{1,0:T(8,128)S(1)}, f32[8,128]{1,0:T(8,128)S(1)}, u32[]{:S(2)}, u32[]{:S(2)}) collective-permute-start(f32[8,128]{1,0:T(8,128)S(1)} %get-tuple-element.16.refs_0_), channel_id=1, source_target_pairs={{24,0},{16,8},{8,16},{0,24},{25,1},{17,9},{9,17},{1,25},{26,2},{18... | collective-permute-start | bytes 12296 | tf_op jit(solution)/shard_map/ppermute | solution.py:510
  11.8 4.0 %collective-permute-start = (f32[272,128]{1,0:T(8,128)S(1)}, f32[272,128]{1,0:T(8,128)S(1)}, u32[]{:S(2)}, u32[]{:S(2)}) collective-permute-start(f32[272,128]{1,0:T(8,128)S(1)} %get-tuple-element.15.refs_0_), channel_id=1, source_target_pairs={{1,0},{0,1},{3,2},{2,3},{5,4},{4,5},{7,6},{6,7},{9,8},{8,9},{11,10... | collective-permute-start | bytes 417800 | tf_op jit(solution)/shard_map/ppermute | solution.py:510
  14.8 1.4 %collective-permute-start.4 = (f32[272,128]{1,0:T(8,128)S(1)}, f32[272,128]{1,0:T(8,128)S(1)}, u32[]{:S(2)}, u32[]{:S(2)}) collective-permute-start(f32[272,128]{1,0:T(8,128)S(1)} %collective-permute-done.1.refs_2_), channel_id=1, source_target_pairs={{1,0},{0,1},{3,2},{2,3},{5,4},{4,5},{7,6},{6,7},{9,8},{8,9},{11,10... | collective-permute-start | bytes 417800 | tf_op jit(solution)/shard_map/ppermute | solution.py:510
  14.8 1.6 %collective-permute-start.6 = (f32[272,128]{1,0:T(8,128)S(1)}, f32[272,128]{1,0:T(8,128)S(1)}, u32[]{:S(2)}, u32[]{:S(2)}) collective-permute-start(f32[272,128]{1,0:T(8,128)S(1)} %collective-permute-done.5.refs_4_), channel_id=1, source_target_pairs={{1,0},{0,1},{3,2},{2,3},{5,4},{4,5},{7,6},{6,7},{9,8},{8,9},{11,10... | collective-permute-start | bytes 417800 | tf_op jit(solution)/shard_map/ppermute | solution.py:510
  15.3 1.4 %collective-permute-start.8 = (f32[272,128]{1,0:T(8,128)S(1)}, f32[272,128]{1,0:T(8,128)S(1)}, u32[]{:S(2)}, u32[]{:S(2)}) collective-permute-start(f32[272,128]{1,0:T(8,128)S(1)} %collective-permute-done.7.refs_6_), channel_id=1, source_target_pairs={{1,0},{0,1},{3,2},{2,3},{5,4},{4,5},{7,6},{6,7},{9,8},{8,9},{11,10... | collective-permute-start | bytes 417800 | tf_op jit(solution)/shard_map/ppermute | solution.py:510
  15.3 11.6 %collective-permute-start.9 = (f32[8,128]{1,0:T(8,128)S(1)}, f32[8,128]{1,0:T(8,128)S(1)}, u32[]{:S(2)}, u32[]{:S(2)}) collective-permute-start(f32[8,128]{1,0:T(8,128)S(1)} %collective-permute-done.2.refs_1_), channel_id=1, source_target_pairs={{1,0},{0,1},{3,2},{2,3},{5,4},{4,5},{7,6},{6,7},{9,8},{8,9},{11,10... | collective-permute-start | bytes 12296 | tf_op jit(solution)/shard_map/ppermute | solution.py:510

commit v12 on v11

--- a/solution.py
+++ b/solution.py
@@ -244,12 +244,10 @@
     return jnp.where(bottom > 0.0, top / jnp.where(bottom > 0.0, bottom, 1.0), 0.0)
 
 
-def x_next(values, wrap_mask):
-    return jnp.where(wrap_mask, pltpu.roll(values, X_OUT - 1, 1), pltpu.roll(values, LANES - 1, 1))
-
-
-def x_prev(values, wrap_mask):
-    return jnp.where(wrap_mask, pltpu.roll(values, LANES - X_OUT + 1, 1), pltpu.roll(values, 1, 1))
+def tree_sum(values):
+    while len(values) > 1:
+        values = [sum(values[i : i + 2][1:], values[i]) for i in range(0, len(values), 2)]
+    return values[0]
 
 
 def apply_planes(vector, diagonal, first, count, group, last_x, first_x):
@@ -267,8 +265,14 @@
         out = []
         for yi in range(Y_IN):
             line = here[yi * X_IN : (yi + 1) * X_IN]
-            before = [x_prev(value, first_x) for value in line[X_IN - 2 :]]
-            after = [x_next(value, last_x) for value in line[:2]]
+            before = [
+                pltpu.roll(jnp.where(last_x, y_up[yi * X_IN + xi], line[xi]), 1, 1)
+                for xi in range(X_IN - 2, X_IN)
+            ]
+            after = [
+                pltpu.roll(jnp.where(first_x, y_down[yi * X_IN + xi], line[xi]), LANES - 1, 1)
+                for xi in range(2)
+            ]
             wide = before + line + after
             for xi in range(X_IN):
                 m = yi * X_IN + xi
@@ -421,9 +425,9 @@
                 for plane, (value, out) in enumerate(done):
                     for m in range(ROWS):
                         target[first + plane, rows, pl.ds(m * LANES, LANES)] = out[m]
-                        curve = curve + value[m] * out[m]
-                        if i == 0:
-                            norm = norm + value[m] * value[m]
+                    curve = curve + tree_sum([value[m] * out[m] for m in range(ROWS)])
+                    if i == 0:
+                        norm = norm + tree_sum([value[m] * value[m] for m in range(ROWS)])
                 new_sums.append((curve, norm))
             return tuple(new_sums)
 
@@ -440,7 +444,7 @@
             new_sums = []
             for group in range(groups):
                 rows = pl.ds(group * SUB, SUB)
-                norm = sums[group]
+                squares = []
                 for m in range(ROWS):
                     lanes = pl.ds(m * LANES, LANES)
                     value = applied[plane, rows, lanes]
@@ -448,8 +452,8 @@
                     if i:
                         value = value - betas[group] * vectors[i - 1][plane, rows, lanes]
                     vectors[i + 1][plane, rows, lanes] = value
-                    norm = norm + value * value
-                new_sums.append(norm)
+                    squares.append(value * value)
+                new_sums.append(sums[group] + tree_sum(squares))
             return tuple(new_sums)
 
         sums = lax.fori_loop(0, planes, step_turn, (blank,) * groups, unroll=UNROLL)

time: 31.5 us -> 34.3 us (1.089)
  Pallas kernels: 15.2 us -> 18 us
    pallas_call x1, Pallas kernels: 10.3 us -> 13.2 us  [whole_grid(): pl.pallas_call(functools.partial(krylov_kernel, parts, count), out_shape=...]
  transfers between devices with their start and end apart: 10 -> 10, of which waited for: 4 -> 4; matrix products, arithmetic and copies ran while one was open for 0% -> 0% of each run, Pallas kernels for 33% -> 39%
where the time goes in v12:
time: 34.3 us; the launch traced here: 34.1 us
  Pallas kernels  18 us (52%)
  starting transfers between devices  10.1 us (29%)
  waiting for transfers between devices  3.78 us (11%)
  between operations  1.3 us (4%)
  other arithmetic  0.93 us (3%)
    pallas_call x1, Pallas kernels, whole_grid(): pl.pallas_call(functools.partial(krylov_kernel, parts, count), out_shape=...  13.2 us
    ppermute x9, starting transfers between devices, swapped(): lax.ppermute(values, axis, [(index ^ mask, index) for index in range(size)])  8.04 us
    pallas_call x1, Pallas kernels, whole_grid(): pl.pallas_call(functools.partial(gram_kernel, points), out_shape=(out, ou...  4.28 us
    ppermute x9, waiting for transfers between devices, swapped(): lax.ppermute(values, axis, [(index ^ mask, index) for index in range(size)])  3.78 us
    ppermute x1, starting transfers between devices, whole_grid(): lax.ppermute(tile, ('point', 'dom'), mixed)  2.03 us
    concatenate x1, other arithmetic, packed_block(): jnp.concatenate([rows, levels], axis=0)  0.93 us
  transfers between devices with their start and end apart: 10, of which 4 were waited for; matrix products, arithmetic and copies ran while one was open for 0% of the time, Pallas kernels for 39%

profile of v12, /device:TPU:0, one launch (start us, length us, event | category | flops | bytes accessed | tf_op | source)
XLA Modules:
  0.0 34.1 jit_solution(14286440246246081550)
XLA Ops:
  1.3 0.9 %pad_maximum_fusion.rows = f32[272,128]{1,0:T(8,128)S(1)} fusion(f32[16,128]{1,0:T(8,128)} %bitcast.13, f32[256,128]{1,0:T(8,128)} %bitcast.12), kind=kLoop, calls=%fused_computation | loop fusion | flops 34816 | bytes 278528 | tf_op jit(solution)/shard_map/concatenate | solution.py:236
  2.2 0.6 %pack.1 = (f32[272,128]{1,0:T(8,128)S(1)}, f32[8,128]{1,0:T(8,128)S(1)}) custom-call(s32[1,1]{1,0:T(1,128)} %bitcast.11.counts, f32[272,128]{1,0:T(8,128)S(1)} %pad_maximum_fusion.rows), custom_call_target="tpu_custom_call" | custom-call | tf_op jit(solution)/shard_map/pack/pallas_call | solution.py:226
  2.8 3.0 %collective-permute-start.1 = (f32[272,128]{1,0:T(8,128)S(1)}, f32[272,128]{1,0:T(8,128)S(1)}, u32[]{:S(2)}, u32[]{:S(2)}) collective-permute-start(f32[272,128]{1,0:T(8,128)S(1)} %get-tuple-element.15.refs_0_), channel_id=1, source_target_pairs={{2,0},{3,1},{0,2},{1,3},{6,4},{7,5},{4,6},{5,7},{10,8},{11,9},{8,1... | collective-permute-start | bytes 417800 | tf_op jit(solution)/shard_map/ppermute | solution.py:514
  5.8 1.5 %collective-permute-start.5 = (f32[272,128]{1,0:T(8,128)S(1)}, f32[272,128]{1,0:T(8,128)S(1)}, u32[]{:S(2)}, u32[]{:S(2)}) collective-permute-start(f32[272,128]{1,0:T(8,128)S(1)} %get-tuple-element.15.refs_0_), channel_id=1, source_target_pairs={{4,0},{5,1},{6,2},{7,3},{0,4},{1,5},{2,6},{3,7},{12,8},{13,9},{14,... | collective-permute-start | bytes 417800 | tf_op jit(solution)/shard_map/ppermute | solution.py:514
  7.3 0.0 collective-permute-start.7
  7.3 2.0 %collective-permute-start.2 = (f32[8,128]{1,0:T(8,128)S(1)}, f32[8,128]{1,0:T(8,128)S(1)}, u32[]{:S(2)}, u32[]{:S(2)}) collective-permute-start(f32[8,128]{1,0:T(8,128)S(1)} %get-tuple-element.16.refs_0_), channel_id=1, source_target_pairs={{8,0},{17,1},{10,2},{19,3},{12,4},{21,5},{14,6},{23,7},{0,8},{25,9... | collective-permute-start | bytes 12296 | tf_op jit(solution)/shard_map/ppermute | solution.py:527
  9.4 2.5 %collective-permute-start.3 = (f32[8,128]{1,0:T(8,128)S(1)}, f32[8,128]{1,0:T(8,128)S(1)}, u32[]{:S(2)}, u32[]{:S(2)}) collective-permute-start(f32[8,128]{1,0:T(8,128)S(1)} %get-tuple-element.16.refs_0_), channel_id=1, source_target_pairs={{24,0},{16,8},{8,16},{0,24},{25,1},{17,9},{9,17},{1,25},{26,2},{18... | collective-permute-start | bytes 12296 | tf_op jit(solution)/shard_map/ppermute | solution.py:514
  11.8 0.0 collective-permute-done.2.refs_1_
  11.8 0.0 collective-permute-start
  11.8 2.9 %collective-permute-done.3.refs_2_ = f32[8,128]{1,0:T(8,128)S(1)} collective-permute-done((f32[8,128]{1,0:T(8,128)S(1)}, f32[8,128]{1,0:T(8,128)S(1)}, u32[]{:S(2)}, u32[]{:S(2)}) %collective-permute-start.3) | collective-permute-done | bytes 4128 | tf_op jit(solution)/shard_map/ppermute | solution.py:514
  14.8 0.0 collective-permute-done.1.refs_2_
  14.8 0.0 collective-permute-start.4
  14.8 0.0 collective-permute-done.5.refs_4_
  14.8 0.5 %collective-permute-start.6 = (f32[272,128]{1,0:T(8,128)S(1)}, f32[272,128]{1,0:T(8,128)S(1)}, u32[]{:S(2)}, u32[]{:S(2)}) collective-permute-start(f32[272,128]{1,0:T(8,128)S(1)} %collective-permute-done.5.refs_4_), channel_id=1, source_target_pairs={{1,0},{0,1},{3,2},{2,3},{5,4},{4,5},{7,6},{6,7},{9,8},{8,9},{11,10... | collective-permute-start | bytes 417800 | tf_op jit(solution)/shard_map/ppermute | solution.py:514
  15.3 0.0 collective-permute-done.7.refs_6_
  15.3 0.1 collective-permute-start.8
  15.3 0.4 %collective-permute-start.9 = (f32[8,128]{1,0:T(8,128)S(1)}, f32[8,128]{1,0:T(8,128)S(1)}, u32[]{:S(2)}, u32[]{:S(2)}) collective-permute-start(f32[8,128]{1,0:T(8,128)S(1)} %collective-permute-done.2.refs_1_), channel_id=1, source_target_pairs={{1,0},{0,1},{3,2},{2,3},{5,4},{4,5},{7,6},{6,7},{9,8},{8,9},{11,10... | collective-permute-start | bytes 12296 | tf_op jit(solution)/shard_map/ppermute | solution.py:514
  15.8 0.0 collective-permute-done.refs_1_
  15.8 0.3 collective-permute-done.4.refs_3_
  16.1 0.2 collective-permute-done.6.refs_5_
  16.3 0.3 collective-permute-done.8.refs_7_
  16.6 13.2 %krylov.1 = (f32[16,16,1024]{2,1,0:T(8,128)S(1)}, f32[16,16,1024]{2,1,0:T(8,128)S(1)}, f32[16,16,1024]{2,1,0:T(8,128)S(1)}, f32[16,16,1024]{2,1,0:T(8,128)S(1)},...) custom-call(f32[272,128]{1,0:T(8,128)S(1)} %get-tuple-element.15.ref, ...), custom_call_target="tpu_custom_call" | custom-call | tf_op jit(solution)/shard_map/krylov/pallas_call | solution.py:535
  29.8 0.0 collective-permute-done.9.refs_3_
  29.8 4.3 %gram.1 = (f32[2,64,64]{2,1,0:T(8,128)}, f32[2,64,64]{2,1,0:T(8,128)}) custom-call(f32[12,16,128]{2,1,0:T(8,128)S(1)} %get-tuple-element.18.scalars, f32[8,128]{1,0:T(8,128)S(1)} %get-tuple-element.16.refs_0_, f32[8,128]{1,0:T(8,128)S(1)} %collective-permute-done.2.refs_1_, f32[8,128]{1,0:T(8,128)S(1)} %collective-permute-done.3.refs_2_, ...), custom_call_target="tpu_custom_call" | custom-call | tf_op jit(solution)/shard_map/gram/pallas_call | solution.py:551
Async XLA Ops:
  2.8 12.0 %collective-permute-start.1 = (f32[272,128]{1,0:T(8,128)S(1)}, f32[272,128]{1,0:T(8,128)S(1)}, u32[]{:S(2)}, u32[]{:S(2)}) collective-permute-start(f32[272,128]{1,0:T(8,128)S(1)} %get-tuple-element.15.refs_0_), channel_id=1, source_target_pairs={{2,0},{3,1},{0,2},{1,3},{6,4},{7,5},{4,6},{5,7},{10,8},{11,9},{8,1... | collective-permute-start | bytes 417800 | tf_op jit(solution)/shard_map/ppermute | solution.py:514
  5.8 9.0 %collective-permute-start.5 = (f32[272,128]{1,0:T(8,128)S(1)}, f32[272,128]{1,0:T(8,128)S(1)}, u32[]{:S(2)}, u32[]{:S(2)}) collective-permute-start(f32[272,128]{1,0:T(8,128)S(1)} %get-tuple-element.15.refs_0_), channel_id=1, source_target_pairs={{4,0},{5,1},{6,2},{7,3},{0,4},{1,5},{2,6},{3,7},{12,8},{13,9},{14,... | collective-permute-start | bytes 417800 | tf_op jit(solution)/shard_map/ppermute | solution.py:514
  7.3 8.0 %collective-permute-start.7 = (f32[272,128]{1,0:T(8,128)S(1)}, f32[272,128]{1,0:T(8,128)S(1)}, u32[]{:S(2)}, u32[]{:S(2)}) collective-permute-start(f32[272,128]{1,0:T(8,128)S(1)} %get-tuple-element.15.refs_0_), channel_id=1, source_target_pairs={{6,0},{7,1},{4,2},{5,3},{2,4},{3,5},{0,6},{1,7},{14,8},{15,9},{12,... | collective-permute-start | bytes 417800 | tf_op jit(solution)/shard_map/ppermute | solution.py:514
  7.3 4.5 %collective-permute-start.2 = (f32[8,128]{1,0:T(8,128)S(1)}, f32[8,128]{1,0:T(8,128)S(1)}, u32[]{:S(2)}, u32[]{:S(2)}) collective-permute-start(f32[8,128]{1,0:T(8,128)S(1)} %get-tuple-element.16.refs_0_), channel_id=1, source_target_pairs={{8,0},{17,1},{10,2},{19,3},{12,4},{21,5},{14,6},{23,7},{0,8},{25,9... | collective-permute-start | bytes 12296 | tf_op jit(solution)/shard_map/ppermute | solution.py:527
  9.4 5.4 %collective-permute-start.3 = (f32[8,128]{1,0:T(8,128)S(1)}, f32[8,128]{1,0:T(8,128)S(1)}, u32[]{:S(2)}, u32[]{:S(2)}) collective-permute-start(f32[8,128]{1,0:T(8,128)S(1)} %get-tuple-element.16.refs_0_), channel_id=1, source_target_pairs={{24,0},{16,8},{8,16},{0,24},{25,1},{17,9},{9,17},{1,25},{26,2},{18... | collective-permute-start | bytes 12296 | tf_op jit(solution)/shard_map/ppermute | solution.py:514
  11.8 4.0 %collective-permute-start = (f32[272,128]{1,0:T(8,128)S(1)}, f32[272,128]{1,0:T(8,128)S(1)}, u32[]{:S(2)}, u32[]{:S(2)}) collective-permute-start(f32[272,128]{1,0:T(8,128)S(1)} %get-tuple-element.15.refs_0_), channel_id=1, source_target_pairs={{1,0},{0,1},{3,2},{2,3},{5,4},{4,5},{7,6},{6,7},{9,8},{8,9},{11,10... | collective-permute-start | bytes 417800 | tf_op jit(solution)/shard_map/ppermute | solution.py:514
  14.8 1.4 %collective-permute-start.4 = (f32[272,128]{1,0:T(8,128)S(1)}, f32[272,128]{1,0:T(8,128)S(1)}, u32[]{:S(2)}, u32[]{:S(2)}) collective-permute-start(f32[272,128]{1,0:T(8,128)S(1)} %collective-permute-done.1.refs_2_), channel_id=1, source_target_pairs={{1,0},{0,1},{3,2},{2,3},{5,4},{4,5},{7,6},{6,7},{9,8},{8,9},{11,10... | collective-permute-start | bytes 417800 | tf_op jit(solution)/shard_map/ppermute | solution.py:514
  14.8 1.6 %collective-permute-start.6 = (f32[272,128]{1,0:T(8,128)S(1)}, f32[272,128]{1,0:T(8,128)S(1)}, u32[]{:S(2)}, u32[]{:S(2)}) collective-permute-start(f32[272,128]{1,0:T(8,128)S(1)} %collective-permute-done.5.refs_4_), channel_id=1, source_target_pairs={{1,0},{0,1},{3,2},{2,3},{5,4},{4,5},{7,6},{6,7},{9,8},{8,9},{11,10... | collective-permute-start | bytes 417800 | tf_op jit(solution)/shard_map/ppermute | solution.py:514
  15.3 1.4 %collective-permute-start.8 = (f32[272,128]{1,0:T(8,128)S(1)}, f32[272,128]{1,0:T(8,128)S(1)}, u32[]{:S(2)}, u32[]{:S(2)}) collective-permute-start(f32[272,128]{1,0:T(8,128)S(1)} %collective-permute-done.7.refs_6_), channel_id=1, source_target_pairs={{1,0},{0,1},{3,2},{2,3},{5,4},{4,5},{7,6},{6,7},{9,8},{8,9},{11,10... | collective-permute-start | bytes 417800 | tf_op jit(solution)/shard_map/ppermute | solution.py:514
  15.3 14.4 %collective-permute-start.9 = (f32[8,128]{1,0:T(8,128)S(1)}, f32[8,128]{1,0:T(8,128)S(1)}, u32[]{:S(2)}, u32[]{:S(2)}) collective-permute-start(f32[8,128]{1,0:T(8,128)S(1)} %collective-permute-done.2.refs_1_), channel_id=1, source_target_pairs={{1,0},{0,1},{3,2},{2,3},{5,4},{4,5},{7,6},{6,7},{9,8},{8,9},{11,10... | collective-permute-start | bytes 12296 | tf_op jit(solution)/shard_map/ppermute | solution.py:514

commit v13 on v12

--- a/solution.py
+++ b/solution.py
@@ -250,7 +250,35 @@
     return values[0]
 
 
-def apply_planes(vector, diagonal, first, count, group, last_x, first_x):
+def x_next(values, wrap_mask):
+    return jnp.where(wrap_mask, pltpu.roll(values, X_OUT - 1, 1), pltpu.roll(values, LANES - 1, 1))
+
+
+def x_prev(values, wrap_mask):
+    return jnp.where(wrap_mask, pltpu.roll(values, LANES - X_OUT + 1, 1), pltpu.roll(values, 1, 1))
+
+
+def halo_sums(here, last_x, first_x):
+    y_up = [pltpu.roll(value, LANES - X_OUT, 1) for value in here]
+    y_down = [pltpu.roll(value, X_OUT, 1) for value in here]
+    sums = []
+    for yi in range(Y_IN):
+        line = here[yi * X_IN : (yi + 1) * X_IN]
+        before = [x_prev(value, first_x) for value in line[X_IN - 2 :]]
+        after = [x_next(value, last_x) for value in line[:2]]
+        far_x = before + after
+        near_x = [before[1], None, None, after[0]]
+        for xi in range(X_IN):
+            m = yi * X_IN + xi
+            other = (1 - yi) * X_IN + xi
+            near = y_down[other] if yi == 0 else y_up[other]
+            if near_x[xi] is not None:
+                near = near + near_x[xi]
+            sums.append(near + FAR_SCALED * ((y_up[m] + y_down[m]) + far_x[xi]))
+    return sums
+
+
+def apply_planes(vector, halo, diagonal, first, count, group):
     planes = vector.shape[0]
     rows = pl.ds(group * SUB, SUB)
     held = {}
@@ -260,30 +288,16 @@
     for plane in range(count):
         here, above, below = held[plane], held[plane + 1], held[plane - 1]
         above_2, below_2 = held[plane + 2], held[plane - 2]
-        y_up = [pltpu.roll(value, LANES - X_OUT, 1) for value in here]
-        y_down = [pltpu.roll(value, X_OUT, 1) for value in here]
         out = []
-        for yi in range(Y_IN):
-            line = here[yi * X_IN : (yi + 1) * X_IN]
-            before = [
-                pltpu.roll(jnp.where(last_x, y_up[yi * X_IN + xi], line[xi]), 1, 1)
-                for xi in range(X_IN - 2, X_IN)
-            ]
-            after = [
-                pltpu.roll(jnp.where(first_x, y_down[yi * X_IN + xi], line[xi]), LANES - 1, 1)
-                for xi in range(2)
-            ]
-            wide = before + line + after
-            for xi in range(X_IN):
-                m = yi * X_IN + xi
-                other = (1 - yi) * X_IN + xi
-                y_next = here[other] if yi == 0 else y_up[other]
-                y_prev = here[other] if yi == 1 else y_down[other]
-                near = (wide[xi + 1] + wide[xi + 3]) + (y_next + y_prev) + (above[m] + below[m])
-                far = (wide[xi] + wide[xi + 4]) + (y_up[m] + y_down[m])
-                far = far + (above_2[m] + below_2[m])
-                level = diagonal[first + plane, :, pl.ds(m * LANES, LANES)]
-                out.append(level * here[m] - near - FAR_SCALED * far)
+        for m in range(ROWS):
+            lanes = pl.ds(m * LANES, LANES)
+            yi, xi = m // X_IN, m % X_IN
+            near = [here[(1 - yi) * X_IN + xi] + (above[m] + below[m])]
+            near += [here[yi * X_IN + x] for x in (xi - 1, xi + 1) if 0 <= x < X_IN]
+            far = [above_2[m] + below_2[m]]
+            far += [here[yi * X_IN + x] for x in (xi - 2, xi + 2) if 0 <= x < X_IN]
+            value = diagonal[first + plane, :, lanes] * here[m] - halo[first + plane, rows, lanes]
+            out.append((value - sum(near[1:], near[0])) - FAR_SCALED * sum(far[1:], far[0]))
         yield here, out
 
 
@@ -389,7 +403,7 @@
 
 def krylov_kernel(parts, count, *refs):
     blocks, vectors = refs[:parts], refs[parts : parts + BASIS]
-    scalars, applied, diagonal = refs[parts + BASIS :]
+    scalars, applied, halo, diagonal = refs[parts + BASIS :]
     planes = diagonal.shape[0]
     depth = planes // parts
     groups = count // SUB
@@ -400,10 +414,15 @@
     for turn in range(parts):
         slab = jnp.bitwise_xor(here, turn) * depth
         for deep in range(depth):
-            for m in range(ROWS):
-                start = (deep * ROWS + m) * count
-                lanes = pl.ds(m * LANES, LANES)
-                vectors[0][slab + deep, :, lanes] = blocks[turn][start : start + count, :]
+            for group in range(groups):
+                rows = pl.ds(group * SUB, SUB)
+                values = []
+                for m in range(ROWS):
+                    start = (deep * ROWS + m) * count + group * SUB
+                    values.append(blocks[turn][start : start + SUB, :])
+                    vectors[0][slab + deep, rows, m * LANES : (m + 1) * LANES] = values[m]
+                for m, value in enumerate(halo_sums(values, last_x, first_x)):
+                    halo[slab + deep, rows, m * LANES : (m + 1) * LANES] = value
             start = depth * ROWS * count + deep * ROWS
             levels = H_SCALE * (blocks[turn][start : start + ROWS, :] + 3.75)
             for m in range(ROWS):
@@ -421,7 +440,7 @@
             for group in range(groups):
                 rows = pl.ds(group * SUB, SUB)
                 curve, norm = sums[group]
-                done = apply_planes(source, diagonal, first, TOGETHER, group, last_x, first_x)
+                done = apply_planes(source, halo, diagonal, first, TOGETHER, group)
                 for plane, (value, out) in enumerate(done):
                     for m in range(ROWS):
                         target[first + plane, rows, pl.ds(m * LANES, LANES)] = out[m]
@@ -444,7 +463,7 @@
             new_sums = []
             for group in range(groups):
                 rows = pl.ds(group * SUB, SUB)
-                squares = []
+                values = []
                 for m in range(ROWS):
                     lanes = pl.ds(m * LANES, LANES)
                     value = applied[plane, rows, lanes]
@@ -452,8 +471,10 @@
                     if i:
                         value = value - betas[group] * vectors[i - 1][plane, rows, lanes]
                     vectors[i + 1][plane, rows, lanes] = value
-                    squares.append(value * value)
-                new_sums.append(sums[group] + tree_sum(squares))
+                    values.append(value)
+                for m, value in enumerate(halo_sums(values, last_x, first_x)):
+                    halo[plane, rows, pl.ds(m * LANES, LANES)] = value
+                new_sums.append(sums[group] + tree_sum([value * value for value in values]))
             return tuple(new_sums)
 
         sums = lax.fori_loop(0, planes, step_turn, (blank,) * groups, unroll=UNROLL)
@@ -540,6 +561,7 @@
         out_specs=[vmem] * (BASIS + 1),
         scratch_shapes=[
             pltpu.VMEM(vector, jnp.float32),
+            pltpu.VMEM(vector, jnp.float32),
             pltpu.VMEM((planes, SUB, ROWS * LANES), jnp.float32),
         ],
         compiler_params=pltpu.CompilerParams(vmem_limit_bytes=16 * 2**20),

time: 34.3 us -> 32.7 us (0.953)
  Pallas kernels: 18 us -> 16.4 us
    pallas_call x1, Pallas kernels: 13.2 us -> 11.6 us  [whole_grid(): pl.pallas_call(functools.partial(krylov_kernel, parts, count), out_shape=...]
  transfers between devices with their start and end apart: 10 -> 10, of which waited for: 4 -> 4; matrix products, arithmetic and copies ran while one was open for 0% -> 0% of each run, Pallas kernels for 39% -> 36%
where the time goes in v13:
time: 32.7 us; the launch traced here: 32.5 us
  Pallas kernels  16.4 us (50%)
  starting transfers between devices  10.1 us (31%)
  waiting for transfers between devices  3.78 us (12%)
  between operations  1.3 us (4%)
  other arithmetic  0.93 us (3%)
    pallas_call x1, Pallas kernels, whole_grid(): pl.pallas_call(functools.partial(krylov_kernel, parts, count), out_shape=...  11.6 us
    ppermute x9, starting transfers between devices, swapped(): lax.ppermute(values, axis, [(index ^ mask, index) for index in range(size)])  8.04 us
    pallas_call x1, Pallas kernels, whole_grid(): pl.pallas_call(functools.partial(gram_kernel, points), out_shape=(out, ou...  4.27 us
    ppermute x9, waiting for transfers between devices, swapped(): lax.ppermute(values, axis, [(index ^ mask, index) for index in range(size)])  3.78 us
    ppermute x1, starting transfers between devices, whole_grid(): lax.ppermute(tile, ('point', 'dom'), mixed)  2.03 us
    concatenate x1, other arithmetic, packed_block(): jnp.concatenate([rows, levels], axis=0)  0.93 us
  transfers between devices with their start and end apart: 10, of which 4 were waited for; matrix products, arithmetic and copies ran while one was open for 0% of the time, Pallas kernels for 36%

profile of v13, /device:TPU:0, one launch (start us, length us, event | category | flops | bytes accessed | tf_op | source)
XLA Modules:
  0.0 32.5 jit_solution(2550784500351847196)
XLA Ops:
  1.3 0.9 %pad_maximum_fusion.rows = f32[272,128]{1,0:T(8,128)S(1)} fusion(f32[16,128]{1,0:T(8,128)} %bitcast.13, f32[256,128]{1,0:T(8,128)} %bitcast.12), kind=kLoop, calls=%fused_computation | loop fusion | flops 34816 | bytes 278528 | tf_op jit(solution)/shard_map/concatenate | solution.py:236
  2.2 0.6 %pack.1 = (f32[272,128]{1,0:T(8,128)S(1)}, f32[8,128]{1,0:T(8,128)S(1)}) custom-call(s32[1,1]{1,0:T(1,128)} %bitcast.11.counts, f32[272,128]{1,0:T(8,128)S(1)} %pad_maximum_fusion.rows), custom_call_target="tpu_custom_call" | custom-call | tf_op jit(solution)/shard_map/pack/pallas_call | solution.py:226
  2.8 3.0 %collective-permute-start.1 = (f32[272,128]{1,0:T(8,128)S(1)}, f32[272,128]{1,0:T(8,128)S(1)}, u32[]{:S(2)}, u32[]{:S(2)}) collective-permute-start(f32[272,128]{1,0:T(8,128)S(1)} %get-tuple-element.15.refs_0_), channel_id=1, source_target_pairs={{2,0},{3,1},{0,2},{1,3},{6,4},{7,5},{4,6},{5,7},{10,8},{11,9},{8,1... | collective-permute-start | bytes 417800 | tf_op jit(solution)/shard_map/ppermute | solution.py:535
  5.8 1.5 %collective-permute-start.5 = (f32[272,128]{1,0:T(8,128)S(1)}, f32[272,128]{1,0:T(8,128)S(1)}, u32[]{:S(2)}, u32[]{:S(2)}) collective-permute-start(f32[272,128]{1,0:T(8,128)S(1)} %get-tuple-element.15.refs_0_), channel_id=1, source_target_pairs={{4,0},{5,1},{6,2},{7,3},{0,4},{1,5},{2,6},{3,7},{12,8},{13,9},{14,... | collective-permute-start | bytes 417800 | tf_op jit(solution)/shard_map/ppermute | solution.py:535
  7.3 0.0 collective-permute-start.7
  7.3 2.0 %collective-permute-start.2 = (f32[8,128]{1,0:T(8,128)S(1)}, f32[8,128]{1,0:T(8,128)S(1)}, u32[]{:S(2)}, u32[]{:S(2)}) collective-permute-start(f32[8,128]{1,0:T(8,128)S(1)} %get-tuple-element.16.refs_0_), channel_id=1, source_target_pairs={{8,0},{17,1},{10,2},{19,3},{12,4},{21,5},{14,6},{23,7},{0,8},{25,9... | collective-permute-start | bytes 12296 | tf_op jit(solution)/shard_map/ppermute | solution.py:548
  9.4 2.5 %collective-permute-start.3 = (f32[8,128]{1,0:T(8,128)S(1)}, f32[8,128]{1,0:T(8,128)S(1)}, u32[]{:S(2)}, u32[]{:S(2)}) collective-permute-start(f32[8,128]{1,0:T(8,128)S(1)} %get-tuple-element.16.refs_0_), channel_id=1, source_target_pairs={{24,0},{16,8},{8,16},{0,24},{25,1},{17,9},{9,17},{1,25},{26,2},{18... | collective-permute-start | bytes 12296 | tf_op jit(solution)/shard_map/ppermute | solution.py:535
  11.8 0.0 collective-permute-done.2.refs_1_
  11.8 0.0 collective-permute-start
  11.8 2.9 %collective-permute-done.3.refs_2_ = f32[8,128]{1,0:T(8,128)S(1)} collective-permute-done((f32[8,128]{1,0:T(8,128)S(1)}, f32[8,128]{1,0:T(8,128)S(1)}, u32[]{:S(2)}, u32[]{:S(2)}) %collective-permute-start.3) | collective-permute-done | bytes 4128 | tf_op jit(solution)/shard_map/ppermute | solution.py:535
  14.8 0.0 collective-permute-done.1.refs_2_
  14.8 0.0 collective-permute-start.4
  14.8 0.0 collective-permute-done.5.refs_4_
  14.8 0.5 %collective-permute-start.6 = (f32[272,128]{1,0:T(8,128)S(1)}, f32[272,128]{1,0:T(8,128)S(1)}, u32[]{:S(2)}, u32[]{:S(2)}) collective-permute-start(f32[272,128]{1,0:T(8,128)S(1)} %collective-permute-done.5.refs_4_), channel_id=1, source_target_pairs={{1,0},{0,1},{3,2},{2,3},{5,4},{4,5},{7,6},{6,7},{9,8},{8,9},{11,10... | collective-permute-start | bytes 417800 | tf_op jit(solution)/shard_map/ppermute | solution.py:535
  15.3 0.0 collective-permute-done.7.refs_6_
  15.3 0.1 collective-permute-start.8
  15.3 0.4 %collective-permute-start.9 = (f32[8,128]{1,0:T(8,128)S(1)}, f32[8,128]{1,0:T(8,128)S(1)}, u32[]{:S(2)}, u32[]{:S(2)}) collective-permute-start(f32[8,128]{1,0:T(8,128)S(1)} %collective-permute-done.2.refs_1_), channel_id=1, source_target_pairs={{1,0},{0,1},{3,2},{2,3},{5,4},{4,5},{7,6},{6,7},{9,8},{8,9},{11,10... | collective-permute-start | bytes 12296 | tf_op jit(solution)/shard_map/ppermute | solution.py:535
  15.8 0.0 collective-permute-done.refs_1_
  15.8 0.3 %collective-permute-done.4.refs_3_ = f32[272,128]{1,0:T(8,128)S(1)} collective-permute-done((f32[272,128]{1,0:T(8,128)S(1)}, f32[272,128]{1,0:T(8,128)S(1)}, u32[]{:S(2)}, u32[]{:S(2)}) %collective-permute-start.4) | collective-permute-done | bytes 139296 | tf_op jit(solution)/shard_map/ppermute | solution.py:535
  16.1 0.2 collective-permute-done.6.refs_5_
  16.3 0.3 collective-permute-done.8.refs_7_
  16.6 11.6 %krylov.1 = (f32[16,16,1024]{2,1,0:T(8,128)S(1)}, f32[16,16,1024]{2,1,0:T(8,128)S(1)}, f32[16,16,1024]{2,1,0:T(8,128)S(1)}, f32[16,16,1024]{2,1,0:T(8,128)S(1)},...) custom-call(f32[272,128]{1,0:T(8,128)S(1)} %get-tuple-element.15.ref, ...), custom_call_target="tpu_custom_call" | custom-call | tf_op jit(solution)/shard_map/krylov/pallas_call | solution.py:556
  28.2 0.0 collective-permute-done.9.refs_3_
  28.2 4.3 %gram.1 = (f32[2,64,64]{2,1,0:T(8,128)}, f32[2,64,64]{2,1,0:T(8,128)}) custom-call(f32[12,16,128]{2,1,0:T(8,128)S(1)} %get-tuple-element.18.scalars, f32[8,128]{1,0:T(8,128)S(1)} %get-tuple-element.16.refs_0_, f32[8,128]{1,0:T(8,128)S(1)} %collective-permute-done.2.refs_1_, f32[8,128]{1,0:T(8,128)S(1)} %collective-permute-done.3.refs_2_, ...), custom_call_target="tpu_custom_call" | custom-call | tf_op jit(solution)/shard_map/gram/pallas_call | solution.py:573
Async XLA Ops:
  2.8 12.0 %collective-permute-start.1 = (f32[272,128]{1,0:T(8,128)S(1)}, f32[272,128]{1,0:T(8,128)S(1)}, u32[]{:S(2)}, u32[]{:S(2)}) collective-permute-start(f32[272,128]{1,0:T(8,128)S(1)} %get-tuple-element.15.refs_0_), channel_id=1, source_target_pairs={{2,0},{3,1},{0,2},{1,3},{6,4},{7,5},{4,6},{5,7},{10,8},{11,9},{8,1... | collective-permute-start | bytes 417800 | tf_op jit(solution)/shard_map/ppermute | solution.py:535
  5.8 9.0 %collective-permute-start.5 = (f32[272,128]{1,0:T(8,128)S(1)}, f32[272,128]{1,0:T(8,128)S(1)}, u32[]{:S(2)}, u32[]{:S(2)}) collective-permute-start(f32[272,128]{1,0:T(8,128)S(1)} %get-tuple-element.15.refs_0_), channel_id=1, source_target_pairs={{4,0},{5,1},{6,2},{7,3},{0,4},{1,5},{2,6},{3,7},{12,8},{13,9},{14,... | collective-permute-start | bytes 417800 | tf_op jit(solution)/shard_map/ppermute | solution.py:535
  7.3 8.0 %collective-permute-start.7 = (f32[272,128]{1,0:T(8,128)S(1)}, f32[272,128]{1,0:T(8,128)S(1)}, u32[]{:S(2)}, u32[]{:S(2)}) collective-permute-start(f32[272,128]{1,0:T(8,128)S(1)} %get-tuple-element.15.refs_0_), channel_id=1, source_target_pairs={{6,0},{7,1},{4,2},{5,3},{2,4},{3,5},{0,6},{1,7},{14,8},{15,9},{12,... | collective-permute-start | bytes 417800 | tf_op jit(solution)/shard_map/ppermute | solution.py:535
  7.3 4.5 %collective-permute-start.2 = (f32[8,128]{1,0:T(8,128)S(1)}, f32[8,128]{1,0:T(8,128)S(1)}, u32[]{:S(2)}, u32[]{:S(2)}) collective-permute-start(f32[8,128]{1,0:T(8,128)S(1)} %get-tuple-element.16.refs_0_), channel_id=1, source_target_pairs={{8,0},{17,1},{10,2},{19,3},{12,4},{21,5},{14,6},{23,7},{0,8},{25,9... | collective-permute-start | bytes 12296 | tf_op jit(solution)/shard_map/ppermute | solution.py:548
  9.4 5.4 %collective-permute-start.3 = (f32[8,128]{1,0:T(8,128)S(1)}, f32[8,128]{1,0:T(8,128)S(1)}, u32[]{:S(2)}, u32[]{:S(2)}) collective-permute-start(f32[8,128]{1,0:T(8,128)S(1)} %get-tuple-element.16.refs_0_), channel_id=1, source_target_pairs={{24,0},{16,8},{8,16},{0,24},{25,1},{17,9},{9,17},{1,25},{26,2},{18... | collective-permute-start | bytes 12296 | tf_op jit(solution)/shard_map/ppermute | solution.py:535
  11.8 4.0 %collective-permute-start = (f32[272,128]{1,0:T(8,128)S(1)}, f32[272,128]{1,0:T(8,128)S(1)}, u32[]{:S(2)}, u32[]{:S(2)}) collective-permute-start(f32[272,128]{1,0:T(8,128)S(1)} %get-tuple-element.15.refs_0_), channel_id=1, source_target_pairs={{1,0},{0,1},{3,2},{2,3},{5,4},{4,5},{7,6},{6,7},{9,8},{8,9},{11,10... | collective-permute-start | bytes 417800 | tf_op jit(solution)/shard_map/ppermute | solution.py:535
  14.8 1.4 %collective-permute-start.4 = (f32[272,128]{1,0:T(8,128)S(1)}, f32[272,128]{1,0:T(8,128)S(1)}, u32[]{:S(2)}, u32[]{:S(2)}) collective-permute-start(f32[272,128]{1,0:T(8,128)S(1)} %collective-permute-done.1.refs_2_), channel_id=1, source_target_pairs={{1,0},{0,1},{3,2},{2,3},{5,4},{4,5},{7,6},{6,7},{9,8},{8,9},{11,10... | collective-permute-start | bytes 417800 | tf_op jit(solution)/shard_map/ppermute | solution.py:535
  14.8 1.6 %collective-permute-start.6 = (f32[272,128]{1,0:T(8,128)S(1)}, f32[272,128]{1,0:T(8,128)S(1)}, u32[]{:S(2)}, u32[]{:S(2)}) collective-permute-start(f32[272,128]{1,0:T(8,128)S(1)} %collective-permute-done.5.refs_4_), channel_id=1, source_target_pairs={{1,0},{0,1},{3,2},{2,3},{5,4},{4,5},{7,6},{6,7},{9,8},{8,9},{11,10... | collective-permute-start | bytes 417800 | tf_op jit(solution)/shard_map/ppermute | solution.py:535
  15.3 1.4 %collective-permute-start.8 = (f32[272,128]{1,0:T(8,128)S(1)}, f32[272,128]{1,0:T(8,128)S(1)}, u32[]{:S(2)}, u32[]{:S(2)}) collective-permute-start(f32[272,128]{1,0:T(8,128)S(1)} %collective-permute-done.7.refs_6_), channel_id=1, source_target_pairs={{1,0},{0,1},{3,2},{2,3},{5,4},{4,5},{7,6},{6,7},{9,8},{8,9},{11,10... | collective-permute-start | bytes 417800 | tf_op jit(solution)/shard_map/ppermute | solution.py:535
  15.3 12.9 %collective-permute-start.9 = (f32[8,128]{1,0:T(8,128)S(1)}, f32[8,128]{1,0:T(8,128)S(1)}, u32[]{:S(2)}, u32[]{:S(2)}) collective-permute-start(f32[8,128]{1,0:T(8,128)S(1)} %collective-permute-done.2.refs_1_), channel_id=1, source_target_pairs={{1,0},{0,1},{3,2},{2,3},{5,4},{4,5},{7,6},{6,7},{9,8},{8,9},{11,10... | collective-permute-start | bytes 12296 | tf_op jit(solution)/shard_map/ppermute | solution.py:535

commit v14 on v11

--- a/solution.py
+++ b/solution.py
@@ -166,7 +166,6 @@
 SUB = 8
 BASIS = ITERS + 1
 CORES = 2
-TOGETHER = 2
 UNROLL = 4
 H_SCALE = 2.0 / COEF_NEAR
 FAR_SCALED = 0.5 * H_SCALE * COEF_FAR
@@ -252,35 +251,39 @@
     return jnp.where(wrap_mask, pltpu.roll(values, LANES - X_OUT + 1, 1), pltpu.roll(values, 1, 1))
 
 
-def apply_planes(vector, diagonal, first, count, group, last_x, first_x):
+def tree_sum(values):
+    while len(values) > 1:
+        values = [sum(values[i : i + 2][1:], values[i]) for i in range(0, len(values), 2)]
+    return values[0]
+
+
+def apply_plane(vector, diagonal, plane, group, last_x, first_x):
     planes = vector.shape[0]
     rows = pl.ds(group * SUB, SUB)
-    held = {}
-    for far in range(-2, count + 2):
-        index = jnp.bitwise_and(first + (far + planes), planes - 1)
-        held[far] = [vector[index, rows, pl.ds(m * LANES, LANES)] for m in range(ROWS)]
-    for plane in range(count):
-        here, above, below = held[plane], held[plane + 1], held[plane - 1]
-        above_2, below_2 = held[plane + 2], held[plane - 2]
-        y_up = [pltpu.roll(value, LANES - X_OUT, 1) for value in here]
-        y_down = [pltpu.roll(value, X_OUT, 1) for value in here]
-        out = []
-        for yi in range(Y_IN):
-            line = here[yi * X_IN : (yi + 1) * X_IN]
-            before = [x_prev(value, first_x) for value in line[X_IN - 2 :]]
-            after = [x_next(value, last_x) for value in line[:2]]
-            wide = before + line + after
-            for xi in range(X_IN):
-                m = yi * X_IN + xi
-                other = (1 - yi) * X_IN + xi
-                y_next = here[other] if yi == 0 else y_up[other]
-                y_prev = here[other] if yi == 1 else y_down[other]
-                near = (wide[xi + 1] + wide[xi + 3]) + (y_next + y_prev) + (above[m] + below[m])
-                far = (wide[xi] + wide[xi + 4]) + (y_up[m] + y_down[m])
-                far = far + (above_2[m] + below_2[m])
-                level = diagonal[first + plane, :, pl.ds(m * LANES, LANES)]
-                out.append(level * here[m] - near - FAR_SCALED * far)
-        yield here, out
+
+    def plane_at(index):
+        return [vector[index % planes, rows, m * LANES : (m + 1) * LANES] for m in range(ROWS)]
+
+    here, above, below = (plane_at(plane + far) for far in (0, 1, -1))
+    above_2, below_2 = (plane_at(plane + far) for far in (2, -2))
+    y_up = [pltpu.roll(value, LANES - X_OUT, 1) for value in here]
+    y_down = [pltpu.roll(value, X_OUT, 1) for value in here]
+    out = []
+    for yi in range(Y_IN):
+        line = here[yi * X_IN : (yi + 1) * X_IN]
+        before = [x_prev(line[X_IN - 2], first_x), x_prev(line[X_IN - 1], first_x)]
+        after = [x_next(line[0], last_x), x_next(line[1], last_x)]
+        wide = before + line + after
+        for xi in range(X_IN):
+            m = yi * X_IN + xi
+            other = (1 - yi) * X_IN + xi
+            y_next = here[other] if yi == 0 else y_up[other]
+            y_prev = here[other] if yi == 1 else y_down[other]
+            near = (wide[xi + 1] + wide[xi + 3]) + (y_next + y_prev) + (above[m] + below[m])
+            far = (wide[xi] + wide[xi + 4]) + (y_up[m] + y_down[m]) + (above_2[m] + below_2[m])
+            level = diagonal[plane, :, m * LANES : (m + 1) * LANES]
+            out.append(level * here[m] - near - FAR_SCALED * far)
+    return here, out
 
 
 def cmul(first, second):
@@ -384,8 +387,7 @@
 
 
 def krylov_kernel(parts, count, *refs):
-    blocks, vectors = refs[:parts], refs[parts : parts + BASIS]
-    scalars, applied, diagonal = refs[parts + BASIS :]
+    blocks, (vectors, applied, scalars, first_work, second_work, diagonal) = refs[:parts], refs[parts:]
     planes = diagonal.shape[0]
     depth = planes // parts
     groups = count // SUB
@@ -398,76 +400,81 @@
         for deep in range(depth):
             for m in range(ROWS):
                 start = (deep * ROWS + m) * count
-                lanes = pl.ds(m * LANES, LANES)
-                vectors[0][slab + deep, :, lanes] = blocks[turn][start : start + count, :]
+                lanes = slice(m * LANES, (m + 1) * LANES)
+                value = blocks[turn][start : start + count, :]
+                first_work[slab + deep, :, lanes] = value
+                vectors[0, slab + deep, :, lanes] = value
             start = depth * ROWS * count + deep * ROWS
             levels = H_SCALE * (blocks[turn][start : start + ROWS, :] + 3.75)
             for m in range(ROWS):
                 level = jnp.broadcast_to(levels[m : m + 1, :], (SUB, LANES))
                 diagonal[slab + deep, :, m * LANES : (m + 1) * LANES] = level
-
-    blank = jnp.zeros((SUB, LANES), jnp.float32)
-    alphas, norms = [], []
-    for i in range(ITERS):
-        source, target = vectors[i], applied if i < ITERS - 1 else vectors[ITERS]
-
-        def apply_turn(turn, sums, i=i, source=source, target=target):
-            first = turn * TOGETHER
-            new_sums = []
-            for group in range(groups):
-                rows = pl.ds(group * SUB, SUB)
-                curve, norm = sums[group]
-                done = apply_planes(source, diagonal, first, TOGETHER, group, last_x, first_x)
-                for plane, (value, out) in enumerate(done):
-                    for m in range(ROWS):
-                        target[first + plane, rows, pl.ds(m * LANES, LANES)] = out[m]
-                        curve = curve + value[m] * out[m]
-                        if i == 0:
-                            norm = norm + value[m] * value[m]
-                new_sums.append((curve, norm))
-            return tuple(new_sums)
-
-        start = ((blank, blank),) * groups
-        sums = lax.fori_loop(0, planes // TOGETHER, apply_turn, start, unroll=2)
-        if i == 0:
-            norms.append([lane_sum(norm) for _, norm in sums])
-        alphas.append([ratio(lane_sum(sums[g][0]), norms[i][g]) for g in range(groups)])
-        if i == ITERS - 1:
-            break
-        betas = [ratio(norms[i][g], norms[i - 1][g]) for g in range(groups)] if i else None
-
-        def step_turn(plane, sums, i=i, alpha=alphas[i], betas=betas):
-            new_sums = []
-            for group in range(groups):
-                rows = pl.ds(group * SUB, SUB)
-                norm = sums[group]
-                for m in range(ROWS):
-                    lanes = pl.ds(m * LANES, LANES)
-                    value = applied[plane, rows, lanes]
-                    value = value - alpha[group] * vectors[i][plane, rows, lanes]
-                    if i:
-                        value = value - betas[group] * vectors[i - 1][plane, rows, lanes]
-                    vectors[i + 1][plane, rows, lanes] = value
-                    norm = norm + value * value
-                new_sums.append(norm)
-            return tuple(new_sums)
-
-        sums = lax.fori_loop(0, planes, step_turn, (blank,) * groups, unroll=UNROLL)
-        norms.append([lane_sum(norm) for norm in sums])
-    for i, value in enumerate(alphas + norms):
-        scalars[i] = jnp.concatenate(value, axis=0)
+    second_work[...] = jnp.zeros_like(second_work)
+    scalars[ITERS] = jnp.zeros((count, LANES), jnp.float32)
+
+    all_rows = [pl.ds(group * SUB, SUB) for group in range(groups)]
+    all_lanes = [slice(m * LANES, (m + 1) * LANES) for m in range(ROWS)]
+    for group, rows in enumerate(all_rows):
+        norm = []
+        for plane in range(planes):
+            values = [first_work[plane, rows, lanes] for lanes in all_lanes]
+            norm.append(tree_sum([value * value for value in values]))
+        scalars[ITERS + 1, rows, :] = lane_sum(tree_sum(norm))
+
+    def half_turn(i, work, before):
+        curves = []
+        for group, rows in enumerate(all_rows):
+            curve = []
+            for plane in range(planes):
+                value, out = apply_plane(work, diagonal, plane, group, last_x, first_x)
+                for m, lanes in enumerate(all_lanes):
+                    applied[plane, rows, lanes] = out[m]
+                curve.append(tree_sum([value[m] * out[m] for m in range(ROWS)]))
+            curves.append(lane_sum(tree_sum(curve)))
+        alphas = []
+        for group, rows in enumerate(all_rows):
+            alphas.append(ratio(curves[group], scalars[ITERS + 1 + i, rows, :]))
+            scalars[i, rows, :] = alphas[group]
+
+        @pl.when(i < ITERS - 1)
+        def _():
+            norms = []
+            for group, rows in enumerate(all_rows):
+                beta = ratio(scalars[ITERS + 1 + i, rows, :], scalars[ITERS + i, rows, :])
+                norm = []
+                for plane in range(planes):
+                    values = []
+                    for lanes in all_lanes:
+                        value = applied[plane, rows, lanes]
+                        value = value - alphas[group] * work[plane, rows, lanes]
+                        value = value - beta * before[plane, rows, lanes]
+                        before[plane, rows, lanes] = value
+                        vectors[i + 1, plane, rows, lanes] = value
+                        values.append(value * value)
+                    norm.append(tree_sum(values))
+                norms.append(lane_sum(tree_sum(norm)))
+            for group, rows in enumerate(all_rows):
+                scalars[ITERS + 2 + i, rows, :] = norms[group]
+
+    def turn(step, carry):
+        half_turn(2 * step, first_work, second_work)
+        half_turn(2 * step + 1, second_work, first_work)
+        return carry
+
+    lax.fori_loop(0, ITERS // 2, turn, 0)
 
 
 def gram_kernel(points, scalars, *refs):
-    tiles, vectors = refs[:points], refs[points : points + BASIS]
-    out_b, out_a, gram, limits = refs[points + BASIS :]
-    planes, count, _ = vectors[0].shape
+    tiles = refs[:points]
+    archive, applied, out_b, out_a, gram, limits = refs[points:]
+    planes, count, _ = applied.shape
     groups = count // SUB
     size = BASIS * count
     gram[...] = jnp.zeros_like(gram)
 
     def gram_turn(plane, carry):
-        values = jnp.concatenate([vector[plane] for vector in vectors], axis=0)
+        values = [archive[i, plane] for i in range(ITERS)] + [applied[plane]]
+        values = jnp.concatenate(values, axis=0)
         high = values.astype(jnp.bfloat16)
         low = (values - high.astype(jnp.float32)).astype(jnp.bfloat16)
         gram[...] += lax.dot_general(
@@ -488,7 +495,7 @@
         limits[jnp.bitwise_xor(here, far)] = tile[...]
     bounds = [jnp.concatenate([limits[j]] * groups, axis=0) for j in range(points)]
     alphas = [scalars[i] for i in range(ITERS)]
-    norms = [scalars[ITERS + i] for i in range(ITERS)]
+    norms = [scalars[ITERS + 1 + i] for i in range(ITERS)]
     weights = weights_of(alphas, norms, bounds, count)
     real = jnp.concatenate([pair[0] for pair in weights], axis=0)
     imag = jnp.concatenate([pair[1] for pair in weights], axis=0)
@@ -528,13 +535,17 @@
     vmem = pl.BlockSpec(memory_space=pltpu.VMEM)
     vector = (planes, count, ROWS * LANES)
     cells = planes * ROWS * LANES
-    *vectors, scalars = pl.pallas_call(
+    vectors, applied, scalars = pl.pallas_call(
         functools.partial(krylov_kernel, parts, count),
-        out_shape=[jax.ShapeDtypeStruct(vector, jnp.float32)] * BASIS
-        + [jax.ShapeDtypeStruct((2 * ITERS, count, LANES), jnp.float32)],
+        out_shape=(
+            jax.ShapeDtypeStruct((ITERS,) + vector, jnp.float32),
+            jax.ShapeDtypeStruct(vector, jnp.float32),
+            jax.ShapeDtypeStruct((2 * ITERS + 1, count, LANES), jnp.float32),
+        ),
         in_specs=[vmem] * parts,
-        out_specs=[vmem] * (BASIS + 1),
+        out_specs=(vmem,) * 3,
         scratch_shapes=[
+            pltpu.VMEM(vector, jnp.float32),
             pltpu.VMEM(vector, jnp.float32),
             pltpu.VMEM((planes, SUB, ROWS * LANES), jnp.float32),
         ],
@@ -547,7 +558,7 @@
     return pl.pallas_call(
         functools.partial(gram_kernel, points),
         out_shape=(out, out),
-        in_specs=[vmem] * (1 + points + BASIS),
+        in_specs=[vmem] * (3 + points),
         out_specs=(vmem, vmem),
         scratch_shapes=[
             pltpu.VMEM((2 * size, size), jnp.float32),
@@ -555,7 +566,7 @@
         ],
         compiler_params=pltpu.CompilerParams(vmem_limit_bytes=16 * 2**20),
         name="gram",
-    )(scalars, tile, *tiles, *vectors)
+    )(scalars, tile, *tiles, vectors, applied)
 
 
 def on_device(sources, potential, iter_counts):

time: 31.5 us -> 31 us (0.984)
  Pallas kernels: 15.2 us -> 14.7 us
    pallas_call x1, Pallas kernels: 10.3 us -> 9.72 us  [whole_grid(): pl.pallas_call(functools.partial(krylov_kernel, parts, count), out_shape=...]
  transfers between devices with their start and end apart: 10 -> 10, of which waited for: 4 -> 4; matrix products, arithmetic and copies ran while one was open for 0% -> 0% of each run, Pallas kernels for 33% -> 32%
where the time goes in v14:
time: 31 us; the launch traced here: 30.7 us
  Pallas kernels  14.7 us (47%)
  starting transfers between devices  10.1 us (33%)
  waiting for transfers between devices  3.78 us (12%)
  between operations  1.3 us (4%)
  other arithmetic  0.93 us (3%)
    pallas_call x1, Pallas kernels, whole_grid(): pl.pallas_call(functools.partial(krylov_kernel, parts, count), out_shape=...  9.72 us
    ppermute x9, starting transfers between devices, swapped(): lax.ppermute(values, axis, [(index ^ mask, index) for index in range(size)])  8.04 us
    pallas_call x1, Pallas kernels, whole_grid(): pl.pallas_call(functools.partial(gram_kernel, points), out_shape=(out, ou...  4.38 us
    ppermute x9, waiting for transfers between devices, swapped(): lax.ppermute(values, axis, [(index ^ mask, index) for index in range(size)])  3.78 us
    ppermute x1, starting transfers between devices, whole_grid(): lax.ppermute(tile, ('point', 'dom'), mixed)  2.03 us
    concatenate x1, other arithmetic, packed_block(): jnp.concatenate([rows, levels], axis=0)  0.93 us
  transfers between devices with their start and end apart: 10, of which 4 were waited for; matrix products, arithmetic and copies ran while one was open for 0% of the time, Pallas kernels for 32%

profile of v14, /device:TPU:0, one launch (start us, length us, event | category | flops | bytes accessed | tf_op | source)
XLA Modules:
  0.0 30.7 jit_solution(14566592974638706507)
XLA Ops:
  1.3 0.9 %pad_maximum_fusion.rows = f32[272,128]{1,0:T(8,128)S(1)} fusion(f32[16,128]{1,0:T(8,128)} %bitcast.13, f32[256,128]{1,0:T(8,128)} %bitcast.12), kind=kLoop, calls=%fused_computation | loop fusion | flops 34816 | bytes 278528 | tf_op jit(solution)/shard_map/concatenate | solution.py:235
  2.2 0.6 %pack.1 = (f32[272,128]{1,0:T(8,128)S(1)}, f32[8,128]{1,0:T(8,128)S(1)}) custom-call(s32[1,1]{1,0:T(1,128)} %bitcast.11.counts, f32[272,128]{1,0:T(8,128)S(1)} %pad_maximum_fusion.rows), custom_call_target="tpu_custom_call" | custom-call | tf_op jit(solution)/shard_map/pack/pallas_call | solution.py:225
  2.8 3.0 %collective-permute-start.1 = (f32[272,128]{1,0:T(8,128)S(1)}, f32[272,128]{1,0:T(8,128)S(1)}, u32[]{:S(2)}, u32[]{:S(2)}) collective-permute-start(f32[272,128]{1,0:T(8,128)S(1)} %get-tuple-element.10.refs_0_), channel_id=1, source_target_pairs={{2,0},{3,1},{0,2},{1,3},{6,4},{7,5},{4,6},{5,7},{10,8},{11,9},{8,1... | collective-permute-start | bytes 417800 | tf_op jit(solution)/shard_map/ppermute | solution.py:517
  5.8 1.5 %collective-permute-start.5 = (f32[272,128]{1,0:T(8,128)S(1)}, f32[272,128]{1,0:T(8,128)S(1)}, u32[]{:S(2)}, u32[]{:S(2)}) collective-permute-start(f32[272,128]{1,0:T(8,128)S(1)} %get-tuple-element.10.refs_0_), channel_id=1, source_target_pairs={{4,0},{5,1},{6,2},{7,3},{0,4},{1,5},{2,6},{3,7},{12,8},{13,9},{14,... | collective-permute-start | bytes 417800 | tf_op jit(solution)/shard_map/ppermute | solution.py:517
  7.3 0.0 collective-permute-start.7
  7.3 2.0 %collective-permute-start.2 = (f32[8,128]{1,0:T(8,128)S(1)}, f32[8,128]{1,0:T(8,128)S(1)}, u32[]{:S(2)}, u32[]{:S(2)}) collective-permute-start(f32[8,128]{1,0:T(8,128)S(1)} %get-tuple-element.11.refs_0_), channel_id=1, source_target_pairs={{8,0},{17,1},{10,2},{19,3},{12,4},{21,5},{14,6},{23,7},{0,8},{25,9... | collective-permute-start | bytes 12296 | tf_op jit(solution)/shard_map/ppermute | solution.py:530
  9.4 2.5 %collective-permute-start.3 = (f32[8,128]{1,0:T(8,128)S(1)}, f32[8,128]{1,0:T(8,128)S(1)}, u32[]{:S(2)}, u32[]{:S(2)}) collective-permute-start(f32[8,128]{1,0:T(8,128)S(1)} %get-tuple-element.11.refs_0_), channel_id=1, source_target_pairs={{24,0},{16,8},{8,16},{0,24},{25,1},{17,9},{9,17},{1,25},{26,2},{18... | collective-permute-start | bytes 12296 | tf_op jit(solution)/shard_map/ppermute | solution.py:517
  11.8 0.0 collective-permute-done.2.refs_1_
  11.8 0.0 collective-permute-start
  11.8 2.9 %collective-permute-done.3.refs_2_ = f32[8,128]{1,0:T(8,128)S(1)} collective-permute-done((f32[8,128]{1,0:T(8,128)S(1)}, f32[8,128]{1,0:T(8,128)S(1)}, u32[]{:S(2)}, u32[]{:S(2)}) %collective-permute-start.3) | collective-permute-done | bytes 4128 | tf_op jit(solution)/shard_map/ppermute | solution.py:517
  14.8 0.0 collective-permute-done.1.refs_2_
  14.8 0.0 collective-permute-start.4
  14.8 0.0 collective-permute-done.5.refs_4_
  14.8 0.5 %collective-permute-start.6 = (f32[272,128]{1,0:T(8,128)S(1)}, f32[272,128]{1,0:T(8,128)S(1)}, u32[]{:S(2)}, u32[]{:S(2)}) collective-permute-start(f32[272,128]{1,0:T(8,128)S(1)} %collective-permute-done.5.refs_4_), channel_id=1, source_target_pairs={{1,0},{0,1},{3,2},{2,3},{5,4},{4,5},{7,6},{6,7},{9,8},{8,9},{11,10... | collective-permute-start | bytes 417800 | tf_op jit(solution)/shard_map/ppermute | solution.py:517
  15.3 0.0 collective-permute-done.7.refs_6_
  15.3 0.1 collective-permute-start.8
  15.3 0.4 %collective-permute-start.9 = (f32[8,128]{1,0:T(8,128)S(1)}, f32[8,128]{1,0:T(8,128)S(1)}, u32[]{:S(2)}, u32[]{:S(2)}) collective-permute-start(f32[8,128]{1,0:T(8,128)S(1)} %collective-permute-done.2.refs_1_), channel_id=1, source_target_pairs={{1,0},{0,1},{3,2},{2,3},{5,4},{4,5},{7,6},{6,7},{9,8},{8,9},{11,10... | collective-permute-start | bytes 12296 | tf_op jit(solution)/shard_map/ppermute | solution.py:517
  15.8 0.0 collective-permute-done.refs_1_
  15.8 0.3 %collective-permute-done.4.refs_3_ = f32[272,128]{1,0:T(8,128)S(1)} collective-permute-done((f32[272,128]{1,0:T(8,128)S(1)}, f32[272,128]{1,0:T(8,128)S(1)}, u32[]{:S(2)}, u32[]{:S(2)}) %collective-permute-start.4) | collective-permute-done | bytes 139296 | tf_op jit(solution)/shard_map/ppermute | solution.py:517
  16.1 0.2 collective-permute-done.6.refs_5_
  16.3 0.3 %collective-permute-done.8.refs_7_ = f32[272,128]{1,0:T(8,128)S(1)} collective-permute-done((f32[272,128]{1,0:T(8,128)S(1)}, f32[272,128]{1,0:T(8,128)S(1)}, u32[]{:S(2)}, u32[]{:S(2)}) %collective-permute-start.8) | collective-permute-done | bytes 139296 | tf_op jit(solution)/shard_map/ppermute | solution.py:517
  16.6 9.7 %krylov.1 = (f32[6,16,16,1024]{3,2,1,0:T(8,128)S(1)}, f32[16,16,1024]{2,1,0:T(8,128)S(1)}, f32[13,16,128]{2,1,0:T(8,128)S(1)}) custom-call(f32[272,128]{1,0:T(8,128)S(1)} %get-tuple-element.10.refs_0_, f32[272,128]{1,0:T(8,128)S(1)} %collective-permute-done.refs_1_, f32[272,128]{1,0:T(8,128)S(1)} %collective-permute-done.1.refs_2_, ...), custom_call_target="tpu_custom_call" | custom-call | tf_op jit(solution)/shard_map/krylov/pallas_call | solution.py:538
  26.4 0.0 collective-permute-done.9.refs_3_
  26.4 4.4 %gram.1 = (f32[2,64,64]{2,1,0:T(8,128)}, f32[2,64,64]{2,1,0:T(8,128)}) custom-call(f32[13,16,128]{2,1,0:T(8,128)S(1)} %get-tuple-element.13.scalars, f32[8,128]{1,0:T(8,128)S(1)} %get-tuple-element.11.refs_0_, f32[8,128]{1,0:T(8,128)S(1)} %collective-permute-done.2.refs_1_, f32[8,128]{1,0:T(8,128)S(1)} %collective-permute-done.3.refs_2_, ...), custom_call_target="tpu_custom_call" | custom-call | tf_op jit(solution)/shard_map/gram/pallas_call | solution.py:558
Async XLA Ops:
  2.8 12.0 %collective-permute-start.1 = (f32[272,128]{1,0:T(8,128)S(1)}, f32[272,128]{1,0:T(8,128)S(1)}, u32[]{:S(2)}, u32[]{:S(2)}) collective-permute-start(f32[272,128]{1,0:T(8,128)S(1)} %get-tuple-element.10.refs_0_), channel_id=1, source_target_pairs={{2,0},{3,1},{0,2},{1,3},{6,4},{7,5},{4,6},{5,7},{10,8},{11,9},{8,1... | collective-permute-start | bytes 417800 | tf_op jit(solution)/shard_map/ppermute | solution.py:517
  5.8 9.0 %collective-permute-start.5 = (f32[272,128]{1,0:T(8,128)S(1)}, f32[272,128]{1,0:T(8,128)S(1)}, u32[]{:S(2)}, u32[]{:S(2)}) collective-permute-start(f32[272,128]{1,0:T(8,128)S(1)} %get-tuple-element.10.refs_0_), channel_id=1, source_target_pairs={{4,0},{5,1},{6,2},{7,3},{0,4},{1,5},{2,6},{3,7},{12,8},{13,9},{14,... | collective-permute-start | bytes 417800 | tf_op jit(solution)/shard_map/ppermute | solution.py:517
  7.3 8.0 %collective-permute-start.7 = (f32[272,128]{1,0:T(8,128)S(1)}, f32[272,128]{1,0:T(8,128)S(1)}, u32[]{:S(2)}, u32[]{:S(2)}) collective-permute-start(f32[272,128]{1,0:T(8,128)S(1)} %get-tuple-element.10.refs_0_), channel_id=1, source_target_pairs={{6,0},{7,1},{4,2},{5,3},{2,4},{3,5},{0,6},{1,7},{14,8},{15,9},{12,... | collective-permute-start | bytes 417800 | tf_op jit(solution)/shard_map/ppermute | solution.py:517
  7.3 4.5 %collective-permute-start.2 = (f32[8,128]{1,0:T(8,128)S(1)}, f32[8,128]{1,0:T(8,128)S(1)}, u32[]{:S(2)}, u32[]{:S(2)}) collective-permute-start(f32[8,128]{1,0:T(8,128)S(1)} %get-tuple-element.11.refs_0_), channel_id=1, source_target_pairs={{8,0},{17,1},{10,2},{19,3},{12,4},{21,5},{14,6},{23,7},{0,8},{25,9... | collective-permute-start | bytes 12296 | tf_op jit(solution)/shard_map/ppermute | solution.py:530
  9.4 5.4 %collective-permute-start.3 = (f32[8,128]{1,0:T(8,128)S(1)}, f32[8,128]{1,0:T(8,128)S(1)}, u32[]{:S(2)}, u32[]{:S(2)}) collective-permute-start(f32[8,128]{1,0:T(8,128)S(1)} %get-tuple-element.11.refs_0_), channel_id=1, source_target_pairs={{24,0},{16,8},{8,16},{0,24},{25,1},{17,9},{9,17},{1,25},{26,2},{18... | collective-permute-start | bytes 12296 | tf_op jit(solution)/shard_map/ppermute | solution.py:517
  11.8 4.0 %collective-permute-start = (f32[272,128]{1,0:T(8,128)S(1)}, f32[272,128]{1,0:T(8,128)S(1)}, u32[]{:S(2)}, u32[]{:S(2)}) collective-permute-start(f32[272,128]{1,0:T(8,128)S(1)} %get-tuple-element.10.refs_0_), channel_id=1, source_target_pairs={{1,0},{0,1},{3,2},{2,3},{5,4},{4,5},{7,6},{6,7},{9,8},{8,9},{11,10... | collective-permute-start | bytes 417800 | tf_op jit(solution)/shard_map/ppermute | solution.py:517
  14.8 1.4 %collective-permute-start.4 = (f32[272,128]{1,0:T(8,128)S(1)}, f32[272,128]{1,0:T(8,128)S(1)}, u32[]{:S(2)}, u32[]{:S(2)}) collective-permute-start(f32[272,128]{1,0:T(8,128)S(1)} %collective-permute-done.1.refs_2_), channel_id=1, source_target_pairs={{1,0},{0,1},{3,2},{2,3},{5,4},{4,5},{7,6},{6,7},{9,8},{8,9},{11,10... | collective-permute-start | bytes 417800 | tf_op jit(solution)/shard_map/ppermute | solution.py:517
  14.8 1.6 %collective-permute-start.6 = (f32[272,128]{1,0:T(8,128)S(1)}, f32[272,128]{1,0:T(8,128)S(1)}, u32[]{:S(2)}, u32[]{:S(2)}) collective-permute-start(f32[272,128]{1,0:T(8,128)S(1)} %collective-permute-done.5.refs_4_), channel_id=1, source_target_pairs={{1,0},{0,1},{3,2},{2,3},{5,4},{4,5},{7,6},{6,7},{9,8},{8,9},{11,10... | collective-permute-start | bytes 417800 | tf_op jit(solution)/shard_map/ppermute | solution.py:517
  15.3 1.4 %collective-permute-start.8 = (f32[272,128]{1,0:T(8,128)S(1)}, f32[272,128]{1,0:T(8,128)S(1)}, u32[]{:S(2)}, u32[]{:S(2)}) collective-permute-start(f32[272,128]{1,0:T(8,128)S(1)} %collective-permute-done.7.refs_6_), channel_id=1, source_target_pairs={{1,0},{0,1},{3,2},{2,3},{5,4},{4,5},{7,6},{6,7},{9,8},{8,9},{11,10... | collective-permute-start | bytes 417800 | tf_op jit(solution)/shard_map/ppermute | solution.py:517
  15.3 11.0 %collective-permute-start.9 = (f32[8,128]{1,0:T(8,128)S(1)}, f32[8,128]{1,0:T(8,128)S(1)}, u32[]{:S(2)}, u32[]{:S(2)}) collective-permute-start(f32[8,128]{1,0:T(8,128)S(1)} %collective-permute-done.2.refs_1_), channel_id=1, source_target_pairs={{1,0},{0,1},{3,2},{2,3},{5,4},{4,5},{7,6},{6,7},{9,8},{8,9},{11,10... | collective-permute-start | bytes 12296 | tf_op jit(solution)/shard_map/ppermute | solution.py:517

commit v15 on v14

--- a/solution.py
+++ b/solution.py
@@ -243,14 +243,6 @@
     return jnp.where(bottom > 0.0, top / jnp.where(bottom > 0.0, bottom, 1.0), 0.0)
 
 
-def x_next(values, wrap_mask):
-    return jnp.where(wrap_mask, pltpu.roll(values, X_OUT - 1, 1), pltpu.roll(values, LANES - 1, 1))
-
-
-def x_prev(values, wrap_mask):
-    return jnp.where(wrap_mask, pltpu.roll(values, LANES - X_OUT + 1, 1), pltpu.roll(values, 1, 1))
-
-
 def tree_sum(values):
     while len(values) > 1:
         values = [sum(values[i : i + 2][1:], values[i]) for i in range(0, len(values), 2)]
@@ -271,8 +263,14 @@
     out = []
     for yi in range(Y_IN):
         line = here[yi * X_IN : (yi + 1) * X_IN]
-        before = [x_prev(line[X_IN - 2], first_x), x_prev(line[X_IN - 1], first_x)]
-        after = [x_next(line[0], last_x), x_next(line[1], last_x)]
+        before = [
+            pltpu.roll(jnp.where(last_x, y_up[yi * X_IN + xi], line[xi]), 1, 1)
+            for xi in range(X_IN - 2, X_IN)
+        ]
+        after = [
+            pltpu.roll(jnp.where(first_x, y_down[yi * X_IN + xi], line[xi]), LANES - 1, 1)
+            for xi in range(2)
+        ]
         wide = before + line + after
         for xi in range(X_IN):
             m = yi * X_IN + xi

time: 31 us -> 38 us (1.23)
  Pallas kernels: 14.7 us -> 21.7 us
    pallas_call x1, Pallas kernels: 9.72 us -> 16.8 us  [whole_grid(): pl.pallas_call(functools.partial(krylov_kernel, parts, count), out_shape=...]
  transfers between devices with their start and end apart: 10 -> 10, of which waited for: 4 -> 4; matrix products, arithmetic and copies ran while one was open for 0% -> 0% of each run, Pallas kernels for 32% -> 44%
where the time goes in v15:
time: 38 us; the launch traced here: 37.8 us
  Pallas kernels  21.7 us (57%)
  starting transfers between devices  10.1 us (27%)
  waiting for transfers between devices  3.78 us (10%)
  between operations  1.3 us (3%)
  other arithmetic  0.93 us (2%)
    pallas_call x1, Pallas kernels, whole_grid(): pl.pallas_call(functools.partial(krylov_kernel, parts, count), out_shape=...  16.8 us
    ppermute x9, starting transfers between devices, swapped(): lax.ppermute(values, axis, [(index ^ mask, index) for index in range(size)])  8.04 us
    pallas_call x1, Pallas kernels, whole_grid(): pl.pallas_call(functools.partial(gram_kernel, points), out_shape=(out, ou...  4.39 us
    ppermute x9, waiting for transfers between devices, swapped(): lax.ppermute(values, axis, [(index ^ mask, index) for index in range(size)])  3.78 us
    ppermute x1, starting transfers between devices, whole_grid(): lax.ppermute(tile, ('point', 'dom'), mixed)  2.03 us
    concatenate x1, other arithmetic, packed_block(): jnp.concatenate([rows, levels], axis=0)  0.93 us
  transfers between devices with their start and end apart: 10, of which 4 were waited for; matrix products, arithmetic and copies ran while one was open for 0% of the time, Pallas kernels for 44%

profile of v15, /device:TPU:0, one launch (start us, length us, event | category | flops | bytes accessed | tf_op | source)
XLA Modules:
  0.0 37.8 jit_solution(12836230873441380851)
XLA Ops:
  1.3 0.9 %pad_maximum_fusion.rows = f32[272,128]{1,0:T(8,128)S(1)} fusion(f32[16,128]{1,0:T(8,128)} %bitcast.13, f32[256,128]{1,0:T(8,128)} %bitcast.12), kind=kLoop, calls=%fused_computation | loop fusion | flops 34816 | bytes 278528 | tf_op jit(solution)/shard_map/concatenate | solution.py:235
  2.2 0.6 %pack.1 = (f32[272,128]{1,0:T(8,128)S(1)}, f32[8,128]{1,0:T(8,128)S(1)}) custom-call(s32[1,1]{1,0:T(1,128)} %bitcast.11.counts, f32[272,128]{1,0:T(8,128)S(1)} %pad_maximum_fusion.rows), custom_call_target="tpu_custom_call" | custom-call | tf_op jit(solution)/shard_map/pack/pallas_call | solution.py:225
  2.8 3.0 %collective-permute-start.1 = (f32[272,128]{1,0:T(8,128)S(1)}, f32[272,128]{1,0:T(8,128)S(1)}, u32[]{:S(2)}, u32[]{:S(2)}) collective-permute-start(f32[272,128]{1,0:T(8,128)S(1)} %get-tuple-element.10.refs_0_), channel_id=1, source_target_pairs={{2,0},{3,1},{0,2},{1,3},{6,4},{7,5},{4,6},{5,7},{10,8},{11,9},{8,1... | collective-permute-start | bytes 417800 | tf_op jit(solution)/shard_map/ppermute | solution.py:515
  5.8 1.5 %collective-permute-start.5 = (f32[272,128]{1,0:T(8,128)S(1)}, f32[272,128]{1,0:T(8,128)S(1)}, u32[]{:S(2)}, u32[]{:S(2)}) collective-permute-start(f32[272,128]{1,0:T(8,128)S(1)} %get-tuple-element.10.refs_0_), channel_id=1, source_target_pairs={{4,0},{5,1},{6,2},{7,3},{0,4},{1,5},{2,6},{3,7},{12,8},{13,9},{14,... | collective-permute-start | bytes 417800 | tf_op jit(solution)/shard_map/ppermute | solution.py:515
  7.3 0.0 collective-permute-start.7
  7.3 2.0 %collective-permute-start.2 = (f32[8,128]{1,0:T(8,128)S(1)}, f32[8,128]{1,0:T(8,128)S(1)}, u32[]{:S(2)}, u32[]{:S(2)}) collective-permute-start(f32[8,128]{1,0:T(8,128)S(1)} %get-tuple-element.11.refs_0_), channel_id=1, source_target_pairs={{8,0},{17,1},{10,2},{19,3},{12,4},{21,5},{14,6},{23,7},{0,8},{25,9... | collective-permute-start | bytes 12296 | tf_op jit(solution)/shard_map/ppermute | solution.py:528
  9.4 2.5 %collective-permute-start.3 = (f32[8,128]{1,0:T(8,128)S(1)}, f32[8,128]{1,0:T(8,128)S(1)}, u32[]{:S(2)}, u32[]{:S(2)}) collective-permute-start(f32[8,128]{1,0:T(8,128)S(1)} %get-tuple-element.11.refs_0_), channel_id=1, source_target_pairs={{24,0},{16,8},{8,16},{0,24},{25,1},{17,9},{9,17},{1,25},{26,2},{18... | collective-permute-start | bytes 12296 | tf_op jit(solution)/shard_map/ppermute | solution.py:515
  11.8 0.0 collective-permute-done.2.refs_1_
  11.8 0.0 collective-permute-start
  11.8 2.9 %collective-permute-done.3.refs_2_ = f32[8,128]{1,0:T(8,128)S(1)} collective-permute-done((f32[8,128]{1,0:T(8,128)S(1)}, f32[8,128]{1,0:T(8,128)S(1)}, u32[]{:S(2)}, u32[]{:S(2)}) %collective-permute-start.3) | collective-permute-done | bytes 4128 | tf_op jit(solution)/shard_map/ppermute | solution.py:515
  14.8 0.0 collective-permute-done.1.refs_2_
  14.8 0.0 collective-permute-start.4
  14.8 0.0 collective-permute-done.5.refs_4_
  14.8 0.5 %collective-permute-start.6 = (f32[272,128]{1,0:T(8,128)S(1)}, f32[272,128]{1,0:T(8,128)S(1)}, u32[]{:S(2)}, u32[]{:S(2)}) collective-permute-start(f32[272,128]{1,0:T(8,128)S(1)} %collective-permute-done.5.refs_4_), channel_id=1, source_target_pairs={{1,0},{0,1},{3,2},{2,3},{5,4},{4,5},{7,6},{6,7},{9,8},{8,9},{11,10... | collective-permute-start | bytes 417800 | tf_op jit(solution)/shard_map/ppermute | solution.py:515
  15.3 0.0 collective-permute-done.7.refs_6_
  15.3 0.1 collective-permute-start.8
  15.3 0.4 %collective-permute-start.9 = (f32[8,128]{1,0:T(8,128)S(1)}, f32[8,128]{1,0:T(8,128)S(1)}, u32[]{:S(2)}, u32[]{:S(2)}) collective-permute-start(f32[8,128]{1,0:T(8,128)S(1)} %collective-permute-done.2.refs_1_), channel_id=1, source_target_pairs={{1,0},{0,1},{3,2},{2,3},{5,4},{4,5},{7,6},{6,7},{9,8},{8,9},{11,10... | collective-permute-start | bytes 12296 | tf_op jit(solution)/shard_map/ppermute | solution.py:515
  15.8 0.0 collective-permute-done.refs_1_
  15.8 0.3 collective-permute-done.4.refs_3_
  16.1 0.2 collective-permute-done.6.refs_5_
  16.3 0.3 collective-permute-done.8.refs_7_
  16.6 16.8 %krylov.1 = (f32[6,16,16,1024]{3,2,1,0:T(8,128)S(1)}, f32[16,16,1024]{2,1,0:T(8,128)S(1)}, f32[13,16,128]{2,1,0:T(8,128)S(1)}) custom-call(f32[272,128]{1,0:T(8,128)S(1)} %get-tuple-element.10.refs_0_, f32[272,128]{1,0:T(8,128)S(1)} %collective-permute-done.refs_1_, f32[272,128]{1,0:T(8,128)S(1)} %collective-permute-done.1.refs_2_, ...), custom_call_target="tpu_custom_call" | custom-call | tf_op jit(solution)/shard_map/krylov/pallas_call | solution.py:536
  33.4 0.0 collective-permute-done.9.refs_3_
  33.4 4.4 %gram.1 = (f32[2,64,64]{2,1,0:T(8,128)}, f32[2,64,64]{2,1,0:T(8,128)}) custom-call(f32[13,16,128]{2,1,0:T(8,128)S(1)} %get-tuple-element.13.scalars, f32[8,128]{1,0:T(8,128)S(1)} %get-tuple-element.11.refs_0_, f32[8,128]{1,0:T(8,128)S(1)} %collective-permute-done.2.refs_1_, f32[8,128]{1,0:T(8,128)S(1)} %collective-permute-done.3.refs_2_, ...), custom_call_target="tpu_custom_call" | custom-call | tf_op jit(solution)/shard_map/gram/pallas_call | solution.py:556
Async XLA Ops:
  2.8 12.0 %collective-permute-start.1 = (f32[272,128]{1,0:T(8,128)S(1)}, f32[272,128]{1,0:T(8,128)S(1)}, u32[]{:S(2)}, u32[]{:S(2)}) collective-permute-start(f32[272,128]{1,0:T(8,128)S(1)} %get-tuple-element.10.refs_0_), channel_id=1, source_target_pairs={{2,0},{3,1},{0,2},{1,3},{6,4},{7,5},{4,6},{5,7},{10,8},{11,9},{8,1... | collective-permute-start | bytes 417800 | tf_op jit(solution)/shard_map/ppermute | solution.py:515
  5.8 9.0 %collective-permute-start.5 = (f32[272,128]{1,0:T(8,128)S(1)}, f32[272,128]{1,0:T(8,128)S(1)}, u32[]{:S(2)}, u32[]{:S(2)}) collective-permute-start(f32[272,128]{1,0:T(8,128)S(1)} %get-tuple-element.10.refs_0_), channel_id=1, source_target_pairs={{4,0},{5,1},{6,2},{7,3},{0,4},{1,5},{2,6},{3,7},{12,8},{13,9},{14,... | collective-permute-start | bytes 417800 | tf_op jit(solution)/shard_map/ppermute | solution.py:515
  7.3 8.0 %collective-permute-start.7 = (f32[272,128]{1,0:T(8,128)S(1)}, f32[272,128]{1,0:T(8,128)S(1)}, u32[]{:S(2)}, u32[]{:S(2)}) collective-permute-start(f32[272,128]{1,0:T(8,128)S(1)} %get-tuple-element.10.refs_0_), channel_id=1, source_target_pairs={{6,0},{7,1},{4,2},{5,3},{2,4},{3,5},{0,6},{1,7},{14,8},{15,9},{12,... | collective-permute-start | bytes 417800 | tf_op jit(solution)/shard_map/ppermute | solution.py:515
  7.3 4.5 %collective-permute-start.2 = (f32[8,128]{1,0:T(8,128)S(1)}, f32[8,128]{1,0:T(8,128)S(1)}, u32[]{:S(2)}, u32[]{:S(2)}) collective-permute-start(f32[8,128]{1,0:T(8,128)S(1)} %get-tuple-element.11.refs_0_), channel_id=1, source_target_pairs={{8,0},{17,1},{10,2},{19,3},{12,4},{21,5},{14,6},{23,7},{0,8},{25,9... | collective-permute-start | bytes 12296 | tf_op jit(solution)/shard_map/ppermute | solution.py:528
  9.4 5.4 %collective-permute-start.3 = (f32[8,128]{1,0:T(8,128)S(1)}, f32[8,128]{1,0:T(8,128)S(1)}, u32[]{:S(2)}, u32[]{:S(2)}) collective-permute-start(f32[8,128]{1,0:T(8,128)S(1)} %get-tuple-element.11.refs_0_), channel_id=1, source_target_pairs={{24,0},{16,8},{8,16},{0,24},{25,1},{17,9},{9,17},{1,25},{26,2},{18... | collective-permute-start | bytes 12296 | tf_op jit(solution)/shard_map/ppermute | solution.py:515
  11.8 4.0 %collective-permute-start = (f32[272,128]{1,0:T(8,128)S(1)}, f32[272,128]{1,0:T(8,128)S(1)}, u32[]{:S(2)}, u32[]{:S(2)}) collective-permute-start(f32[272,128]{1,0:T(8,128)S(1)} %get-tuple-element.10.refs_0_), channel_id=1, source_target_pairs={{1,0},{0,1},{3,2},{2,3},{5,4},{4,5},{7,6},{6,7},{9,8},{8,9},{11,10... | collective-permute-start | bytes 417800 | tf_op jit(solution)/shard_map/ppermute | solution.py:515
  14.8 1.4 %collective-permute-start.4 = (f32[272,128]{1,0:T(8,128)S(1)}, f32[272,128]{1,0:T(8,128)S(1)}, u32[]{:S(2)}, u32[]{:S(2)}) collective-permute-start(f32[272,128]{1,0:T(8,128)S(1)} %collective-permute-done.1.refs_2_), channel_id=1, source_target_pairs={{1,0},{0,1},{3,2},{2,3},{5,4},{4,5},{7,6},{6,7},{9,8},{8,9},{11,10... | collective-permute-start | bytes 417800 | tf_op jit(solution)/shard_map/ppermute | solution.py:515
  14.8 1.6 %collective-permute-start.6 = (f32[272,128]{1,0:T(8,128)S(1)}, f32[272,128]{1,0:T(8,128)S(1)}, u32[]{:S(2)}, u32[]{:S(2)}) collective-permute-start(f32[272,128]{1,0:T(8,128)S(1)} %collective-permute-done.5.refs_4_), channel_id=1, source_target_pairs={{1,0},{0,1},{3,2},{2,3},{5,4},{4,5},{7,6},{6,7},{9,8},{8,9},{11,10... | collective-permute-start | bytes 417800 | tf_op jit(solution)/shard_map/ppermute | solution.py:515
  15.3 1.4 %collective-permute-start.8 = (f32[272,128]{1,0:T(8,128)S(1)}, f32[272,128]{1,0:T(8,128)S(1)}, u32[]{:S(2)}, u32[]{:S(2)}) collective-permute-start(f32[272,128]{1,0:T(8,128)S(1)} %collective-permute-done.7.refs_6_), channel_id=1, source_target_pairs={{1,0},{0,1},{3,2},{2,3},{5,4},{4,5},{7,6},{6,7},{9,8},{8,9},{11,10... | collective-permute-start | bytes 417800 | tf_op jit(solution)/shard_map/ppermute | solution.py:515
  15.3 18.1 %collective-permute-start.9 = (f32[8,128]{1,0:T(8,128)S(1)}, f32[8,128]{1,0:T(8,128)S(1)}, u32[]{:S(2)}, u32[]{:S(2)}) collective-permute-start(f32[8,128]{1,0:T(8,128)S(1)} %collective-permute-done.2.refs_1_), channel_id=1, source_target_pairs={{1,0},{0,1},{3,2},{2,3},{5,4},{4,5},{7,6},{6,7},{9,8},{8,9},{11,10... | collective-permute-start | bytes 12296 | tf_op jit(solution)/shard_map/ppermute | solution.py:515

commit v16 on v14

--- a/solution.py
+++ b/solution.py
@@ -243,37 +243,42 @@
     return jnp.where(bottom > 0.0, top / jnp.where(bottom > 0.0, bottom, 1.0), 0.0)
 
 
-def x_next(values, wrap_mask):
-    return jnp.where(wrap_mask, pltpu.roll(values, X_OUT - 1, 1), pltpu.roll(values, LANES - 1, 1))
-
-
-def x_prev(values, wrap_mask):
-    return jnp.where(wrap_mask, pltpu.roll(values, LANES - X_OUT + 1, 1), pltpu.roll(values, 1, 1))
-
-
 def tree_sum(values):
     while len(values) > 1:
         values = [sum(values[i : i + 2][1:], values[i]) for i in range(0, len(values), 2)]
     return values[0]
 
 
-def apply_plane(vector, diagonal, plane, group, last_x, first_x):
-    planes = vector.shape[0]
-    rows = pl.ds(group * SUB, SUB)
-
-    def plane_at(index):
-        return [vector[index % planes, rows, m * LANES : (m + 1) * LANES] for m in range(ROWS)]
-
-    here, above, below = (plane_at(plane + far) for far in (0, 1, -1))
-    above_2, below_2 = (plane_at(plane + far) for far in (2, -2))
+def plane_rows(vector, plane, rows):
+    return [vector[plane, rows, m * LANES : (m + 1) * LANES] for m in range(ROWS)]
+
+
+def plane_rolls(here):
     y_up = [pltpu.roll(value, LANES - X_OUT, 1) for value in here]
     y_down = [pltpu.roll(value, X_OUT, 1) for value in here]
+    before, after = [], []
+    for yi in range(Y_IN):
+        line = here[yi * X_IN : (yi + 1) * X_IN]
+        for value in line[X_IN - 2 :]:
+            before.append((pltpu.roll(value, LANES - X_OUT + 1, 1), pltpu.roll(value, 1, 1)))
+        for value in line[:2]:
+            after.append((pltpu.roll(value, X_OUT - 1, 1), pltpu.roll(value, LANES - 1, 1)))
+    return y_up, y_down, before, after
+
+
+def apply_plane(vector, diagonal, plane, rows, rolls, last_x, first_x):
+    planes = vector.shape[0]
+    here = plane_rows(vector, plane, rows)
+    above, below, above_2, below_2 = (
+        plane_rows(vector, (plane + far) % planes, rows) for far in (1, -1, 2, -2)
+    )
+    y_up, y_down, before, after = rolls
     out = []
     for yi in range(Y_IN):
         line = here[yi * X_IN : (yi + 1) * X_IN]
-        before = [x_prev(line[X_IN - 2], first_x), x_prev(line[X_IN - 1], first_x)]
-        after = [x_next(line[0], last_x), x_next(line[1], last_x)]
-        wide = before + line + after
+        low = [jnp.where(first_x, *pair) for pair in before[2 * yi : 2 * yi + 2]]
+        high = [jnp.where(last_x, *pair) for pair in after[2 * yi : 2 * yi + 2]]
+        wide = low + line + high
         for xi in range(X_IN):
             m = yi * X_IN + xi
             other = (1 - yi) * X_IN + xi
@@ -422,15 +427,19 @@
         scalars[ITERS + 1, rows, :] = lane_sum(tree_sum(norm))
 
     def half_turn(i, work, before):
-        curves = []
-        for group, rows in enumerate(all_rows):
-            curve = []
-            for plane in range(planes):
-                value, out = apply_plane(work, diagonal, plane, group, last_x, first_x)
-                for m, lanes in enumerate(all_lanes):
-                    applied[plane, rows, lanes] = out[m]
-                curve.append(tree_sum([value[m] * out[m] for m in range(ROWS)]))
-            curves.append(lane_sum(tree_sum(curve)))
+        units = [(plane, group) for plane in range(planes) for group in range(groups)]
+        curve = [[] for _ in range(groups)]
+        ahead = plane_rolls(plane_rows(work, 0, all_rows[0]))
+        for (plane, group), coming in zip(units, units[1:] + [None]):
+            rolls = ahead
+            if coming is not None:
+                ahead = plane_rolls(plane_rows(work, coming[0], all_rows[coming[1]]))
+            rows = all_rows[group]
+            value, out = apply_plane(work, diagonal, plane, rows, rolls, last_x, first_x)
+            for m, lanes in enumerate(all_lanes):
+                applied[plane, rows, lanes] = out[m]
+            curve[group].append(tree_sum([value[m] * out[m] for m in range(ROWS)]))
+        curves = [lane_sum(tree_sum(parts_of)) for parts_of in curve]
         alphas = []
         for group, rows in enumerate(all_rows):
             alphas.append(ratio(curves[group], scalars[ITERS + 1 + i, rows, :]))

time: 31 us -> 30.5 us (0.984)
  Pallas kernels: 14.7 us -> 14.2 us
    pallas_call x1, Pallas kernels: 9.72 us -> 9.26 us  [whole_grid(): pl.pallas_call(functools.partial(krylov_kernel, parts, count), out_shape=...]
  transfers between devices with their start and end apart: 10 -> 10, of which waited for: 4 -> 4; matrix products, arithmetic and copies ran while one was open for 0% -> 0% of each run, Pallas kernels for 32% -> 31%
where the time goes in v16:
time: 30.5 us; the launch traced here: 30.3 us
  Pallas kernels  14.2 us (47%)
  starting transfers between devices  10.1 us (33%)
  waiting for transfers between devices  3.78 us (12%)
  between operations  1.3 us (4%)
  other arithmetic  0.93 us (3%)
    pallas_call x1, Pallas kernels, whole_grid(): pl.pallas_call(functools.partial(krylov_kernel, parts, count), out_shape=...  9.26 us
    ppermute x9, starting transfers between devices, swapped(): lax.ppermute(values, axis, [(index ^ mask, index) for index in range(size)])  8.04 us
    pallas_call x1, Pallas kernels, whole_grid(): pl.pallas_call(functools.partial(gram_kernel, points), out_shape=(out, ou...  4.39 us
    ppermute x9, waiting for transfers between devices, swapped(): lax.ppermute(values, axis, [(index ^ mask, index) for index in range(size)])  3.78 us
    ppermute x1, starting transfers between devices, whole_grid(): lax.ppermute(tile, ('point', 'dom'), mixed)  2.03 us
    concatenate x1, other arithmetic, packed_block(): jnp.concatenate([rows, levels], axis=0)  0.93 us
  transfers between devices with their start and end apart: 10, of which 4 were waited for; matrix products, arithmetic and copies ran while one was open for 0% of the time, Pallas kernels for 31%

profile of v16, /device:TPU:0, one launch (start us, length us, event | category | flops | bytes accessed | tf_op | source)
XLA Modules:
  0.0 30.3 jit_solution(16801241912852677304)
XLA Ops:
  1.3 0.9 %pad_maximum_fusion.rows = f32[272,128]{1,0:T(8,128)S(1)} fusion(f32[16,128]{1,0:T(8,128)} %bitcast.13, f32[256,128]{1,0:T(8,128)} %bitcast.12), kind=kLoop, calls=%fused_computation | loop fusion | flops 34816 | bytes 278528 | tf_op jit(solution)/shard_map/concatenate | solution.py:235
  2.2 0.6 %pack.1 = (f32[272,128]{1,0:T(8,128)S(1)}, f32[8,128]{1,0:T(8,128)S(1)}) custom-call(s32[1,1]{1,0:T(1,128)} %bitcast.11.counts, f32[272,128]{1,0:T(8,128)S(1)} %pad_maximum_fusion.rows), custom_call_target="tpu_custom_call" | custom-call | tf_op jit(solution)/shard_map/pack/pallas_call | solution.py:225
  2.8 3.0 %collective-permute-start.1 = (f32[272,128]{1,0:T(8,128)S(1)}, f32[272,128]{1,0:T(8,128)S(1)}, u32[]{:S(2)}, u32[]{:S(2)}) collective-permute-start(f32[272,128]{1,0:T(8,128)S(1)} %get-tuple-element.10.refs_0_), channel_id=1, source_target_pairs={{2,0},{3,1},{0,2},{1,3},{6,4},{7,5},{4,6},{5,7},{10,8},{11,9},{8,1... | collective-permute-start | bytes 417800 | tf_op jit(solution)/shard_map/ppermute | solution.py:526
  5.8 1.5 %collective-permute-start.5 = (f32[272,128]{1,0:T(8,128)S(1)}, f32[272,128]{1,0:T(8,128)S(1)}, u32[]{:S(2)}, u32[]{:S(2)}) collective-permute-start(f32[272,128]{1,0:T(8,128)S(1)} %get-tuple-element.10.refs_0_), channel_id=1, source_target_pairs={{4,0},{5,1},{6,2},{7,3},{0,4},{1,5},{2,6},{3,7},{12,8},{13,9},{14,... | collective-permute-start | bytes 417800 | tf_op jit(solution)/shard_map/ppermute | solution.py:526
  7.3 0.0 collective-permute-start.7
  7.3 2.0 %collective-permute-start.2 = (f32[8,128]{1,0:T(8,128)S(1)}, f32[8,128]{1,0:T(8,128)S(1)}, u32[]{:S(2)}, u32[]{:S(2)}) collective-permute-start(f32[8,128]{1,0:T(8,128)S(1)} %get-tuple-element.11.refs_0_), channel_id=1, source_target_pairs={{8,0},{17,1},{10,2},{19,3},{12,4},{21,5},{14,6},{23,7},{0,8},{25,9... | collective-permute-start | bytes 12296 | tf_op jit(solution)/shard_map/ppermute | solution.py:539
  9.4 2.5 %collective-permute-start.3 = (f32[8,128]{1,0:T(8,128)S(1)}, f32[8,128]{1,0:T(8,128)S(1)}, u32[]{:S(2)}, u32[]{:S(2)}) collective-permute-start(f32[8,128]{1,0:T(8,128)S(1)} %get-tuple-element.11.refs_0_), channel_id=1, source_target_pairs={{24,0},{16,8},{8,16},{0,24},{25,1},{17,9},{9,17},{1,25},{26,2},{18... | collective-permute-start | bytes 12296 | tf_op jit(solution)/shard_map/ppermute | solution.py:526
  11.8 0.0 collective-permute-done.2.refs_1_
  11.8 0.0 collective-permute-start
  11.8 2.9 %collective-permute-done.3.refs_2_ = f32[8,128]{1,0:T(8,128)S(1)} collective-permute-done((f32[8,128]{1,0:T(8,128)S(1)}, f32[8,128]{1,0:T(8,128)S(1)}, u32[]{:S(2)}, u32[]{:S(2)}) %collective-permute-start.3) | collective-permute-done | bytes 4128 | tf_op jit(solution)/shard_map/ppermute | solution.py:526
  14.8 0.0 collective-permute-done.1.refs_2_
  14.8 0.0 collective-permute-start.4
  14.8 0.0 collective-permute-done.5.refs_4_
  14.8 0.5 %collective-permute-start.6 = (f32[272,128]{1,0:T(8,128)S(1)}, f32[272,128]{1,0:T(8,128)S(1)}, u32[]{:S(2)}, u32[]{:S(2)}) collective-permute-start(f32[272,128]{1,0:T(8,128)S(1)} %collective-permute-done.5.refs_4_), channel_id=1, source_target_pairs={{1,0},{0,1},{3,2},{2,3},{5,4},{4,5},{7,6},{6,7},{9,8},{8,9},{11,10... | collective-permute-start | bytes 417800 | tf_op jit(solution)/shard_map/ppermute | solution.py:526
  15.3 0.0 collective-permute-done.7.refs_6_
  15.3 0.1 collective-permute-start.8
  15.3 0.4 %collective-permute-start.9 = (f32[8,128]{1,0:T(8,128)S(1)}, f32[8,128]{1,0:T(8,128)S(1)}, u32[]{:S(2)}, u32[]{:S(2)}) collective-permute-start(f32[8,128]{1,0:T(8,128)S(1)} %collective-permute-done.2.refs_1_), channel_id=1, source_target_pairs={{1,0},{0,1},{3,2},{2,3},{5,4},{4,5},{7,6},{6,7},{9,8},{8,9},{11,10... | collective-permute-start | bytes 12296 | tf_op jit(solution)/shard_map/ppermute | solution.py:526
  15.8 0.0 collective-permute-done.refs_1_
  15.8 0.3 %collective-permute-done.4.refs_3_ = f32[272,128]{1,0:T(8,128)S(1)} collective-permute-done((f32[272,128]{1,0:T(8,128)S(1)}, f32[272,128]{1,0:T(8,128)S(1)}, u32[]{:S(2)}, u32[]{:S(2)}) %collective-permute-start.4) | collective-permute-done | bytes 139296 | tf_op jit(solution)/shard_map/ppermute | solution.py:526
  16.1 0.2 collective-permute-done.6.refs_5_
  16.3 0.3 %collective-permute-done.8.refs_7_ = f32[272,128]{1,0:T(8,128)S(1)} collective-permute-done((f32[272,128]{1,0:T(8,128)S(1)}, f32[272,128]{1,0:T(8,128)S(1)}, u32[]{:S(2)}, u32[]{:S(2)}) %collective-permute-start.8) | collective-permute-done | bytes 139296 | tf_op jit(solution)/shard_map/ppermute | solution.py:526
  16.6 9.3 %krylov.1 = (f32[6,16,16,1024]{3,2,1,0:T(8,128)S(1)}, f32[16,16,1024]{2,1,0:T(8,128)S(1)}, f32[13,16,128]{2,1,0:T(8,128)S(1)}) custom-call(f32[272,128]{1,0:T(8,128)S(1)} %get-tuple-element.10.refs_0_, f32[272,128]{1,0:T(8,128)S(1)} %collective-permute-done.refs_1_, f32[272,128]{1,0:T(8,128)S(1)} %collective-permute-done.1.refs_2_, ...), custom_call_target="tpu_custom_call" | custom-call | tf_op jit(solution)/shard_map/krylov/pallas_call | solution.py:547
  25.9 0.0 collective-permute-done.9.refs_3_
  25.9 4.4 %gram.1 = (f32[2,64,64]{2,1,0:T(8,128)}, f32[2,64,64]{2,1,0:T(8,128)}) custom-call(f32[13,16,128]{2,1,0:T(8,128)S(1)} %get-tuple-element.13.scalars, f32[8,128]{1,0:T(8,128)S(1)} %get-tuple-element.11.refs_0_, f32[8,128]{1,0:T(8,128)S(1)} %collective-permute-done.2.refs_1_, f32[8,128]{1,0:T(8,128)S(1)} %collective-permute-done.3.refs_2_, ...), custom_call_target="tpu_custom_call" | custom-call | tf_op jit(solution)/shard_map/gram/pallas_call | solution.py:567
Async XLA Ops:
  2.8 12.0 %collective-permute-start.1 = (f32[272,128]{1,0:T(8,128)S(1)}, f32[272,128]{1,0:T(8,128)S(1)}, u32[]{:S(2)}, u32[]{:S(2)}) collective-permute-start(f32[272,128]{1,0:T(8,128)S(1)} %get-tuple-element.10.refs_0_), channel_id=1, source_target_pairs={{2,0},{3,1},{0,2},{1,3},{6,4},{7,5},{4,6},{5,7},{10,8},{11,9},{8,1... | collective-permute-start | bytes 417800 | tf_op jit(solution)/shard_map/ppermute | solution.py:526
  5.8 9.0 %collective-permute-start.5 = (f32[272,128]{1,0:T(8,128)S(1)}, f32[272,128]{1,0:T(8,128)S(1)}, u32[]{:S(2)}, u32[]{:S(2)}) collective-permute-start(f32[272,128]{1,0:T(8,128)S(1)} %get-tuple-element.10.refs_0_), channel_id=1, source_target_pairs={{4,0},{5,1},{6,2},{7,3},{0,4},{1,5},{2,6},{3,7},{12,8},{13,9},{14,... | collective-permute-start | bytes 417800 | tf_op jit(solution)/shard_map/ppermute | solution.py:526
  7.3 8.0 %collective-permute-start.7 = (f32[272,128]{1,0:T(8,128)S(1)}, f32[272,128]{1,0:T(8,128)S(1)}, u32[]{:S(2)}, u32[]{:S(2)}) collective-permute-start(f32[272,128]{1,0:T(8,128)S(1)} %get-tuple-element.10.refs_0_), channel_id=1, source_target_pairs={{6,0},{7,1},{4,2},{5,3},{2,4},{3,5},{0,6},{1,7},{14,8},{15,9},{12,... | collective-permute-start | bytes 417800 | tf_op jit(solution)/shard_map/ppermute | solution.py:526
  7.3 4.5 %collective-permute-start.2 = (f32[8,128]{1,0:T(8,128)S(1)}, f32[8,128]{1,0:T(8,128)S(1)}, u32[]{:S(2)}, u32[]{:S(2)}) collective-permute-start(f32[8,128]{1,0:T(8,128)S(1)} %get-tuple-element.11.refs_0_), channel_id=1, source_target_pairs={{8,0},{17,1},{10,2},{19,3},{12,4},{21,5},{14,6},{23,7},{0,8},{25,9... | collective-permute-start | bytes 12296 | tf_op jit(solution)/shard_map/ppermute | solution.py:539
  9.4 5.4 %collective-permute-start.3 = (f32[8,128]{1,0:T(8,128)S(1)}, f32[8,128]{1,0:T(8,128)S(1)}, u32[]{:S(2)}, u32[]{:S(2)}) collective-permute-start(f32[8,128]{1,0:T(8,128)S(1)} %get-tuple-element.11.refs_0_), channel_id=1, source_target_pairs={{24,0},{16,8},{8,16},{0,24},{25,1},{17,9},{9,17},{1,25},{26,2},{18... | collective-permute-start | bytes 12296 | tf_op jit(solution)/shard_map/ppermute | solution.py:526
  11.8 4.0 %collective-permute-start = (f32[272,128]{1,0:T(8,128)S(1)}, f32[272,128]{1,0:T(8,128)S(1)}, u32[]{:S(2)}, u32[]{:S(2)}) collective-permute-start(f32[272,128]{1,0:T(8,128)S(1)} %get-tuple-element.10.refs_0_), channel_id=1, source_target_pairs={{1,0},{0,1},{3,2},{2,3},{5,4},{4,5},{7,6},{6,7},{9,8},{8,9},{11,10... | collective-permute-start | bytes 417800 | tf_op jit(solution)/shard_map/ppermute | solution.py:526
  14.8 1.4 %collective-permute-start.4 = (f32[272,128]{1,0:T(8,128)S(1)}, f32[272,128]{1,0:T(8,128)S(1)}, u32[]{:S(2)}, u32[]{:S(2)}) collective-permute-start(f32[272,128]{1,0:T(8,128)S(1)} %collective-permute-done.1.refs_2_), channel_id=1, source_target_pairs={{1,0},{0,1},{3,2},{2,3},{5,4},{4,5},{7,6},{6,7},{9,8},{8,9},{11,10... | collective-permute-start | bytes 417800 | tf_op jit(solution)/shard_map/ppermute | solution.py:526
  14.8 1.6 %collective-permute-start.6 = (f32[272,128]{1,0:T(8,128)S(1)}, f32[272,128]{1,0:T(8,128)S(1)}, u32[]{:S(2)}, u32[]{:S(2)}) collective-permute-start(f32[272,128]{1,0:T(8,128)S(1)} %collective-permute-done.5.refs_4_), channel_id=1, source_target_pairs={{1,0},{0,1},{3,2},{2,3},{5,4},{4,5},{7,6},{6,7},{9,8},{8,9},{11,10... | collective-permute-start | bytes 417800 | tf_op jit(solution)/shard_map/ppermute | solution.py:526
  15.3 1.4 %collective-permute-start.8 = (f32[272,128]{1,0:T(8,128)S(1)}, f32[272,128]{1,0:T(8,128)S(1)}, u32[]{:S(2)}, u32[]{:S(2)}) collective-permute-start(f32[272,128]{1,0:T(8,128)S(1)} %collective-permute-done.7.refs_6_), channel_id=1, source_target_pairs={{1,0},{0,1},{3,2},{2,3},{5,4},{4,5},{7,6},{6,7},{9,8},{8,9},{11,10... | collective-permute-start | bytes 417800 | tf_op jit(solution)/shard_map/ppermute | solution.py:526
  15.3 10.6 %collective-permute-start.9 = (f32[8,128]{1,0:T(8,128)S(1)}, f32[8,128]{1,0:T(8,128)S(1)}, u32[]{:S(2)}, u32[]{:S(2)}) collective-permute-start(f32[8,128]{1,0:T(8,128)S(1)} %collective-permute-done.2.refs_1_), channel_id=1, source_target_pairs={{1,0},{0,1},{3,2},{2,3},{5,4},{4,5},{7,6},{6,7},{9,8},{8,9},{11,10... | collective-permute-start | bytes 12296 | tf_op jit(solution)/shard_map/ppermute | solution.py:526

commit v17 on v16

--- a/solution.py
+++ b/solution.py
@@ -392,7 +392,8 @@
 
 
 def krylov_kernel(parts, count, *refs):
-    blocks, (vectors, applied, scalars, first_work, second_work, diagonal) = refs[:parts], refs[parts:]
+    blocks = refs[:parts]
+    vectors, applied, scalars, first_work, second_work, diagonal, partial = refs[parts:]
     planes = diagonal.shape[0]
     depth = planes // parts
     groups = count // SUB
@@ -422,52 +423,76 @@
     for group, rows in enumerate(all_rows):
         norm = []
         for plane in range(planes):
-            values = [first_work[plane, rows, lanes] for lanes in all_lanes]
+            values = plane_rows(first_work, plane, rows)
             norm.append(tree_sum([value * value for value in values]))
-        scalars[ITERS + 1, rows, :] = lane_sum(tree_sum(norm))
-
-    def half_turn(i, work, before):
-        units = [(plane, group) for plane in range(planes) for group in range(groups)]
-        curve = [[] for _ in range(groups)]
-        ahead = plane_rolls(plane_rows(work, 0, all_rows[0]))
-        for (plane, group), coming in zip(units, units[1:] + [None]):
+        partial[rows, :] = tree_sum(norm)
+
+    def stencil_pass(work, group, between):
+        rows = all_rows[group]
+        curve = []
+        ahead = plane_rolls(plane_rows(work, 0, rows))
+        for plane in range(planes):
             rolls = ahead
-            if coming is not None:
-                ahead = plane_rolls(plane_rows(work, coming[0], all_rows[coming[1]]))
-            rows = all_rows[group]
+            if plane + 1 < planes:
+                ahead = plane_rolls(plane_rows(work, plane + 1, rows))
             value, out = apply_plane(work, diagonal, plane, rows, rolls, last_x, first_x)
             for m, lanes in enumerate(all_lanes):
                 applied[plane, rows, lanes] = out[m]
-            curve[group].append(tree_sum([value[m] * out[m] for m in range(ROWS)]))
-        curves = [lane_sum(tree_sum(parts_of)) for parts_of in curve]
-        alphas = []
-        for group, rows in enumerate(all_rows):
-            alphas.append(ratio(curves[group], scalars[ITERS + 1 + i, rows, :]))
-            scalars[i, rows, :] = alphas[group]
-
-        @pl.when(i < ITERS - 1)
-        def _():
-            norms = []
+            curve.append(tree_sum([value[m] * out[m] for m in range(ROWS)]))
+            if plane == planes // 2:
+                between()
+        return tree_sum(curve)
+
+    def update_pass(i, work, before, group, alpha, beta, between):
+        rows = all_rows[group]
+        norm = []
+        for plane in range(planes):
+            values = []
+            for lanes in all_lanes:
+                value = applied[plane, rows, lanes]
+                value = value - alpha * work[plane, rows, lanes]
+                value = value - beta * before[plane, rows, lanes]
+                before[plane, rows, lanes] = value
+                vectors[i + 1, plane, rows, lanes] = value
+                values.append(value * value)
+            norm.append(tree_sum(values))
+            if plane == planes // 2:
+                between()
+        partial[rows, :] = tree_sum(norm)
+
+    def half_turn(i, work, before, may_end):
+        norms = [lane_sum(partial[rows, :]) for rows in all_rows]
+        last_norms = [scalars[ITERS + i, rows, :] for rows in all_rows]
+        alphas, betas = [], []
+
+        def finish_norms():
             for group, rows in enumerate(all_rows):
-                beta = ratio(scalars[ITERS + 1 + i, rows, :], scalars[ITERS + i, rows, :])
-                norm = []
-                for plane in range(planes):
-                    values = []
-                    for lanes in all_lanes:
-                        value = applied[plane, rows, lanes]
-                        value = value - alphas[group] * work[plane, rows, lanes]
-                        value = value - beta * before[plane, rows, lanes]
-                        before[plane, rows, lanes] = value
-                        vectors[i + 1, plane, rows, lanes] = value
-                        values.append(value * value)
-                    norm.append(tree_sum(values))
-                norms.append(lane_sum(tree_sum(norm)))
-            for group, rows in enumerate(all_rows):
-                scalars[ITERS + 2 + i, rows, :] = norms[group]
+                scalars[ITERS + 1 + i, rows, :] = norms[group]
+                betas.append(ratio(norms[group], last_norms[group]))
+
+        def finish_alpha(group, curve):
+            alphas.append(ratio(curve, norms[group]))
+            scalars[i, all_rows[group], :] = alphas[group]
+
+        curves = [lane_sum(stencil_pass(work, 0, finish_norms))]
+        curves.append(lane_sum(stencil_pass(work, 1, lambda: finish_alpha(0, curves[0]))))
+        if may_end:
+            finish_alpha(1, curves[1])
+
+            @pl.when(i < ITERS - 1)
+            def _():
+                for group in range(groups):
+                    update_pass(
+                        i, work, before, group, alphas[group], betas[group], lambda: None
+                    )
+        else:
+            later = [lambda: finish_alpha(1, curves[1]), lambda: None]
+            for group in range(groups):
+                update_pass(i, work, before, group, alphas[group], betas[group], later[group])
 
     def turn(step, carry):
-        half_turn(2 * step, first_work, second_work)
-        half_turn(2 * step + 1, second_work, first_work)
+        half_turn(2 * step, first_work, second_work, False)
+        half_turn(2 * step + 1, second_work, first_work, True)
         return carry
 
     lax.fori_loop(0, ITERS // 2, turn, 0)
@@ -537,9 +562,10 @@
         for part in range(parts)
     ]
     tiles = [lax.ppermute(tile, ("point", "dom"), mixed), swapped(tile, "point", points, 3)]
-    even[1], *tiles = lax.optimization_barrier((even[1], *tiles))
+    odd = [swapped(value, "dom", parts, 1) for value in even[1:]]
+    own, _, *tiles = lax.optimization_barrier((block, odd[0], *tiles))
     tiles.append(swapped(tiles[0], "dom", parts, 1))
-    odd = [swapped(value, "dom", parts, 1) for value in even]
+    odd.insert(0, swapped(own, "dom", parts, 1))
     blocks = [value for pair in zip(even, odd) for value in pair]
     vmem = pl.BlockSpec(memory_space=pltpu.VMEM)
     vector = (planes, count, ROWS * LANES)
@@ -557,6 +583,7 @@
             pltpu.VMEM(vector, jnp.float32),
             pltpu.VMEM(vector, jnp.float32),
             pltpu.VMEM((planes, SUB, ROWS * LANES), jnp.float32),
+            pltpu.VMEM((count, LANES), jnp.float32),
         ],
         compiler_params=pltpu.CompilerParams(vmem_limit_bytes=16 * 2**20),
         name="krylov",

time: 30.5 us -> 33.4 us (1.095)
  waiting for transfers between devices: 3.78 us -> 5.8 us
  Pallas kernels: 14.2 us -> 15.1 us
    ppermute x9, waiting for transfers between devices: 3.78 us -> 5.8 us  [swapped(): lax.ppermute(values, axis, [(index ^ mask, index) for index in range(size)])]
    pallas_call x1, Pallas kernels: 9.26 us -> 10.2 us  [whole_grid(): pl.pallas_call(functools.partial(krylov_kernel, parts, count), out_shape=...]
  transfers between devices with their start and end apart: 10 -> 10, of which waited for: 4 -> 3; matrix products, arithmetic and copies ran while one was open for 0% -> 0% of each run, Pallas kernels for 31% -> 31%
where the time goes in v17:
time: 33.4 us; the launch traced here: 33.2 us
  Pallas kernels  15.1 us (45%)
  starting transfers between devices  10 us (30%)
  waiting for transfers between devices  5.8 us (17%)
  between operations  1.3 us (4%)
  other arithmetic  0.93 us (3%)
    pallas_call x1, Pallas kernels, whole_grid(): pl.pallas_call(functools.partial(krylov_kernel, parts, count), out_shape=...  10.2 us
    ppermute x9, starting transfers between devices, swapped(): lax.ppermute(values, axis, [(index ^ mask, index) for index in range(size)])  8.05 us
    ppermute x9, waiting for transfers between devices, swapped(): lax.ppermute(values, axis, [(index ^ mask, index) for index in range(size)])  5.8 us
    pallas_call x1, Pallas kernels, whole_grid(): pl.pallas_call(functools.partial(gram_kernel, points), out_shape=(out, ou...  4.37 us
    ppermute x1, starting transfers between devices, whole_grid(): lax.ppermute(tile, ('point', 'dom'), mixed)  1.97 us
    concatenate x1, other arithmetic, packed_block(): jnp.concatenate([rows, levels], axis=0)  0.93 us
  transfers between devices with their start and end apart: 10, of which 3 were waited for; matrix products, arithmetic and copies ran while one was open for 0% of the time, Pallas kernels for 31%

profile of v17, /device:TPU:0, one launch (start us, length us, event | category | flops | bytes accessed | tf_op | source)
XLA Modules:
  0.0 33.2 jit_solution(17896533311731685077)
XLA Ops:
  1.3 0.9 %pad_maximum_fusion.rows = f32[272,128]{1,0:T(8,128)S(1)} fusion(f32[16,128]{1,0:T(8,128)} %bitcast.13, f32[256,128]{1,0:T(8,128)} %bitcast.12), kind=kLoop, calls=%fused_computation | loop fusion | flops 34816 | bytes 278528 | tf_op jit(solution)/shard_map/concatenate | solution.py:235
  2.2 0.6 %pack.1 = (f32[272,128]{1,0:T(8,128)S(1)}, f32[8,128]{1,0:T(8,128)S(1)}) custom-call(s32[1,1]{1,0:T(1,128)} %bitcast.11.counts, f32[272,128]{1,0:T(8,128)S(1)} %pad_maximum_fusion.rows), custom_call_target="tpu_custom_call" | custom-call | tf_op jit(solution)/shard_map/pack/pallas_call | solution.py:225
  2.8 3.0 %collective-permute-start = (f32[272,128]{1,0:T(8,128)S(1)}, f32[272,128]{1,0:T(8,128)S(1)}, u32[]{:S(2)}, u32[]{:S(2)}) collective-permute-start(f32[272,128]{1,0:T(8,128)S(1)} %get-tuple-element.12.refs_0_), channel_id=1, source_target_pairs={{2,0},{3,1},{0,2},{1,3},{6,4},{7,5},{4,6},{5,7},{10,8},{11,9},{8,1... | collective-permute-start | bytes 417800 | tf_op jit(solution)/shard_map/ppermute | solution.py:551
  5.8 1.5 %collective-permute-start.5 = (f32[272,128]{1,0:T(8,128)S(1)}, f32[272,128]{1,0:T(8,128)S(1)}, u32[]{:S(2)}, u32[]{:S(2)}) collective-permute-start(f32[272,128]{1,0:T(8,128)S(1)} %get-tuple-element.12.refs_0_), channel_id=1, source_target_pairs={{4,0},{5,1},{6,2},{7,3},{0,4},{1,5},{2,6},{3,7},{12,8},{13,9},{14,... | collective-permute-start | bytes 417800 | tf_op jit(solution)/shard_map/ppermute | solution.py:551
  7.3 0.0 collective-permute-start.7
  7.3 2.5 %collective-permute-done.refs_2_ = f32[272,128]{1,0:T(8,128)S(1)} collective-permute-done((f32[272,128]{1,0:T(8,128)S(1)}, f32[272,128]{1,0:T(8,128)S(1)}, u32[]{:S(2)}, u32[]{:S(2)}) %collective-permute-start) | collective-permute-done | bytes 139296 | tf_op jit(solution)/shard_map/ppermute | solution.py:551
  9.9 0.0 collective-permute-start.1
  9.9 2.0 %collective-permute-start.2 = (f32[8,128]{1,0:T(8,128)S(1)}, f32[8,128]{1,0:T(8,128)S(1)}, u32[]{:S(2)}, u32[]{:S(2)}) collective-permute-start(f32[8,128]{1,0:T(8,128)S(1)} %get-tuple-element.11.refs_0_), channel_id=1, source_target_pairs={{8,0},{17,1},{10,2},{19,3},{12,4},{21,5},{14,6},{23,7},{0,8},{25,9... | collective-permute-start | bytes 12296 | tf_op jit(solution)/shard_map/ppermute | solution.py:564
  11.8 2.5 %collective-permute-start.3 = (f32[8,128]{1,0:T(8,128)S(1)}, f32[8,128]{1,0:T(8,128)S(1)}, u32[]{:S(2)}, u32[]{:S(2)}) collective-permute-start(f32[8,128]{1,0:T(8,128)S(1)} %get-tuple-element.11.refs_0_), channel_id=1, source_target_pairs={{24,0},{16,8},{8,16},{0,24},{25,1},{17,9},{9,17},{1,25},{26,2},{18... | collective-permute-start | bytes 12296 | tf_op jit(solution)/shard_map/ppermute | solution.py:551
  14.3 0.0 collective-permute-done.5.refs_4_
  14.3 0.0 collective-permute-start.6
  14.3 0.0 collective-permute-done.7.refs_6_
  14.3 0.5 %collective-permute-start.8 = (f32[272,128]{1,0:T(8,128)S(1)}, f32[272,128]{1,0:T(8,128)S(1)}, u32[]{:S(2)}, u32[]{:S(2)}) collective-permute-start(f32[272,128]{1,0:T(8,128)S(1)} %collective-permute-done.7.refs_6_), channel_id=1, source_target_pairs={{1,0},{0,1},{3,2},{2,3},{5,4},{4,5},{7,6},{6,7},{9,8},{8,9},{11,10... | collective-permute-start | bytes 417800 | tf_op jit(solution)/shard_map/ppermute | solution.py:551
  14.8 0.0 collective-permute-done.2.refs_1_
  14.8 2.4 %collective-permute-done.3.refs_2_ = f32[8,128]{1,0:T(8,128)S(1)} collective-permute-done((f32[8,128]{1,0:T(8,128)S(1)}, f32[8,128]{1,0:T(8,128)S(1)}, u32[]{:S(2)}, u32[]{:S(2)}) %collective-permute-start.3) | collective-permute-done | bytes 4128 | tf_op jit(solution)/shard_map/ppermute | solution.py:551
  17.2 0.0 collective-permute-done.1.refs_3_
  17.2 0.1 collective-permute-start.4
  17.4 0.4 %collective-permute-start.9 = (f32[8,128]{1,0:T(8,128)S(1)}, f32[8,128]{1,0:T(8,128)S(1)}, u32[]{:S(2)}, u32[]{:S(2)}) collective-permute-start(f32[8,128]{1,0:T(8,128)S(1)} %collective-permute-done.2.refs_1_), channel_id=1, source_target_pairs={{1,0},{0,1},{3,2},{2,3},{5,4},{4,5},{7,6},{6,7},{9,8},{8,9},{11,10... | collective-permute-start | bytes 12296 | tf_op jit(solution)/shard_map/ppermute | solution.py:551
  17.8 0.0 collective-permute-done.6.refs_5_
  17.8 0.0 collective-permute-done.8.refs_7_
  17.8 0.8 %collective-permute-done.4.refs_1_ = f32[272,128]{1,0:T(8,128)S(1)} collective-permute-done((f32[272,128]{1,0:T(8,128)S(1)}, f32[272,128]{1,0:T(8,128)S(1)}, u32[]{:S(2)}, u32[]{:S(2)}) %collective-permute-start.4) | collective-permute-done | bytes 139296 | tf_op jit(solution)/shard_map/ppermute | solution.py:551
  18.6 10.2 %krylov.1 = (f32[6,16,16,1024]{3,2,1,0:T(8,128)S(1)}, f32[16,16,1024]{2,1,0:T(8,128)S(1)}, f32[13,16,128]{2,1,0:T(8,128)S(1)}) custom-call(f32[272,128]{1,0:T(8,128)S(1)} %get-tuple-element.12.refs_0_, f32[272,128]{1,0:T(8,128)S(1)} %collective-permute-done.4.refs_1_, f32[272,128]{1,0:T(8,128)S(1)} %collective-permute-done.refs_2_, ...), custom_call_target="tpu_custom_call" | custom-call | tf_op jit(solution)/shard_map/krylov/pallas_call | solution.py:573
  28.8 0.0 collective-permute-done.9.refs_3_
  28.8 4.4 %gram.1 = (f32[2,64,64]{2,1,0:T(8,128)}, f32[2,64,64]{2,1,0:T(8,128)}) custom-call(f32[13,16,128]{2,1,0:T(8,128)S(1)} %get-tuple-element.13.scalars, f32[8,128]{1,0:T(8,128)S(1)} %get-tuple-element.11.refs_0_, f32[8,128]{1,0:T(8,128)S(1)} %collective-permute-done.2.refs_1_, f32[8,128]{1,0:T(8,128)S(1)} %collective-permute-done.3.refs_2_, ...), custom_call_target="tpu_custom_call" | custom-call | tf_op jit(solution)/shard_map/gram/pallas_call | solution.py:594
Async XLA Ops:
  2.8 7.1 %collective-permute-start = (f32[272,128]{1,0:T(8,128)S(1)}, f32[272,128]{1,0:T(8,128)S(1)}, u32[]{:S(2)}, u32[]{:S(2)}) collective-permute-start(f32[272,128]{1,0:T(8,128)S(1)} %get-tuple-element.12.refs_0_), channel_id=1, source_target_pairs={{2,0},{3,1},{0,2},{1,3},{6,4},{7,5},{4,6},{5,7},{10,8},{11,9},{8,1... | collective-permute-start | bytes 417800 | tf_op jit(solution)/shard_map/ppermute | solution.py:551
  5.8 8.5 %collective-permute-start.5 = (f32[272,128]{1,0:T(8,128)S(1)}, f32[272,128]{1,0:T(8,128)S(1)}, u32[]{:S(2)}, u32[]{:S(2)}) collective-permute-start(f32[272,128]{1,0:T(8,128)S(1)} %get-tuple-element.12.refs_0_), channel_id=1, source_target_pairs={{4,0},{5,1},{6,2},{7,3},{0,4},{1,5},{2,6},{3,7},{12,8},{13,9},{14,... | collective-permute-start | bytes 417800 | tf_op jit(solution)/shard_map/ppermute | solution.py:551
  7.3 7.0 %collective-permute-start.7 = (f32[272,128]{1,0:T(8,128)S(1)}, f32[272,128]{1,0:T(8,128)S(1)}, u32[]{:S(2)}, u32[]{:S(2)}) collective-permute-start(f32[272,128]{1,0:T(8,128)S(1)} %get-tuple-element.12.refs_0_), channel_id=1, source_target_pairs={{6,0},{7,1},{4,2},{5,3},{2,4},{3,5},{0,6},{1,7},{14,8},{15,9},{12,... | collective-permute-start | bytes 417800 | tf_op jit(solution)/shard_map/ppermute | solution.py:551
  9.9 7.4 %collective-permute-start.1 = (f32[272,128]{1,0:T(8,128)S(1)}, f32[272,128]{1,0:T(8,128)S(1)}, u32[]{:S(2)}, u32[]{:S(2)}) collective-permute-start(f32[272,128]{1,0:T(8,128)S(1)} %collective-permute-done.refs_2_), channel_id=1, source_target_pairs={{1,0},{0,1},{3,2},{2,3},{5,4},{4,5},{7,6},{6,7},{9,8},{8,9},{11,10... | collective-permute-start | bytes 417800 | tf_op jit(solution)/shard_map/ppermute | solution.py:551
  9.9 5.0 %collective-permute-start.2 = (f32[8,128]{1,0:T(8,128)S(1)}, f32[8,128]{1,0:T(8,128)S(1)}, u32[]{:S(2)}, u32[]{:S(2)}) collective-permute-start(f32[8,128]{1,0:T(8,128)S(1)} %get-tuple-element.11.refs_0_), channel_id=1, source_target_pairs={{8,0},{17,1},{10,2},{19,3},{12,4},{21,5},{14,6},{23,7},{0,8},{25,9... | collective-permute-start | bytes 12296 | tf_op jit(solution)/shard_map/ppermute | solution.py:564
  11.8 5.4 %collective-permute-start.3 = (f32[8,128]{1,0:T(8,128)S(1)}, f32[8,128]{1,0:T(8,128)S(1)}, u32[]{:S(2)}, u32[]{:S(2)}) collective-permute-start(f32[8,128]{1,0:T(8,128)S(1)} %get-tuple-element.11.refs_0_), channel_id=1, source_target_pairs={{24,0},{16,8},{8,16},{0,24},{25,1},{17,9},{9,17},{1,25},{26,2},{18... | collective-permute-start | bytes 12296 | tf_op jit(solution)/shard_map/ppermute | solution.py:551
  14.3 3.4 %collective-permute-start.6 = (f32[272,128]{1,0:T(8,128)S(1)}, f32[272,128]{1,0:T(8,128)S(1)}, u32[]{:S(2)}, u32[]{:S(2)}) collective-permute-start(f32[272,128]{1,0:T(8,128)S(1)} %collective-permute-done.5.refs_4_), channel_id=1, source_target_pairs={{1,0},{0,1},{3,2},{2,3},{5,4},{4,5},{7,6},{6,7},{9,8},{8,9},{11,10... | collective-permute-start | bytes 417800 | tf_op jit(solution)/shard_map/ppermute | solution.py:551
  14.3 3.4 %collective-permute-start.8 = (f32[272,128]{1,0:T(8,128)S(1)}, f32[272,128]{1,0:T(8,128)S(1)}, u32[]{:S(2)}, u32[]{:S(2)}) collective-permute-start(f32[272,128]{1,0:T(8,128)S(1)} %collective-permute-done.7.refs_6_), channel_id=1, source_target_pairs={{1,0},{0,1},{3,2},{2,3},{5,4},{4,5},{7,6},{6,7},{9,8},{8,9},{11,10... | collective-permute-start | bytes 417800 | tf_op jit(solution)/shard_map/ppermute | solution.py:551
  17.2 1.4 %collective-permute-start.4 = (f32[272,128]{1,0:T(8,128)S(1)}, f32[272,128]{1,0:T(8,128)S(1)}, u32[]{:S(2)}, u32[]{:S(2)}) collective-permute-start(f32[272,128]{1,0:T(8,128)S(1)} %get-tuple-element.12.refs_0_), channel_id=1, source_target_pairs={{1,0},{0,1},{3,2},{2,3},{5,4},{4,5},{7,6},{6,7},{9,8},{8,9},{11,10... | collective-permute-start | bytes 417800 | tf_op jit(solution)/shard_map/ppermute | solution.py:551
  17.4 11.5 %collective-permute-start.9 = (f32[8,128]{1,0:T(8,128)S(1)}, f32[8,128]{1,0:T(8,128)S(1)}, u32[]{:S(2)}, u32[]{:S(2)}) collective-permute-start(f32[8,128]{1,0:T(8,128)S(1)} %collective-permute-done.2.refs_1_), channel_id=1, source_target_pairs={{1,0},{0,1},{3,2},{2,3},{5,4},{4,5},{7,6},{6,7},{9,8},{8,9},{11,10... | collective-permute-start | bytes 12296 | tf_op jit(solution)/shard_map/ppermute | solution.py:551

commit v18 on v16

--- a/solution.py
+++ b/solution.py
@@ -253,42 +253,62 @@
     return [vector[plane, rows, m * LANES : (m + 1) * LANES] for m in range(ROWS)]
 
 
-def plane_rolls(here):
-    y_up = [pltpu.roll(value, LANES - X_OUT, 1) for value in here]
-    y_down = [pltpu.roll(value, X_OUT, 1) for value in here]
-    before, after = [], []
+def y_rolls(here):
+    return [
+        (pltpu.roll(value, LANES - X_OUT, 1), pltpu.roll(value, X_OUT, 1)) for value in here
+    ]
+
+
+def x_rolls(here):
+    halos = []
     for yi in range(Y_IN):
         line = here[yi * X_IN : (yi + 1) * X_IN]
-        for value in line[X_IN - 2 :]:
-            before.append((pltpu.roll(value, LANES - X_OUT + 1, 1), pltpu.roll(value, 1, 1)))
-        for value in line[:2]:
-            after.append((pltpu.roll(value, X_OUT - 1, 1), pltpu.roll(value, LANES - 1, 1)))
-    return y_up, y_down, before, after
-
-
-def apply_plane(vector, diagonal, plane, rows, rolls, last_x, first_x):
+        halo = [
+            (pltpu.roll(value, LANES - X_OUT + 1, 1), pltpu.roll(value, 1, 1))
+            for value in line[X_IN - 2 :]
+        ]
+        halo += [
+            (pltpu.roll(value, X_OUT - 1, 1), pltpu.roll(value, LANES - 1, 1))
+            for value in line[:2]
+        ]
+        halos.append(halo)
+    return halos
+
+
+def apply_plane(vector, diagonal, plane, rows, here, rolled, ahead, last_x, first_x):
     planes = vector.shape[0]
-    here = plane_rows(vector, plane, rows)
     above, below, above_2, below_2 = (
         plane_rows(vector, (plane + far) % planes, rows) for far in (1, -1, 2, -2)
     )
-    y_up, y_down, before, after = rolls
+    near = [above[m] + below[m] for m in range(ROWS)]
+    far = [above_2[m] + below_2[m] for m in range(ROWS)]
+    halos = x_rolls(here)
+    for m in range(ROWS):
+        other = m + X_IN if m < X_IN else m - X_IN
+        near[m] = near[m] + (here[other] + rolled[other][1 if m < X_IN else 0])
+        far[m] = far[m] + (rolled[m][0] + rolled[m][1])
+    for m in range(ROWS):
+        yi, xi = m // X_IN, m % X_IN
+        for x in (xi - 1, xi + 1):
+            if 0 <= x < X_IN:
+                near[m] = near[m] + here[yi * X_IN + x]
+        for x in (xi - 2, xi + 2):
+            if 0 <= x < X_IN:
+                far[m] = far[m] + here[yi * X_IN + x]
+    coming = ahead()
     out = []
     for yi in range(Y_IN):
-        line = here[yi * X_IN : (yi + 1) * X_IN]
-        low = [jnp.where(first_x, *pair) for pair in before[2 * yi : 2 * yi + 2]]
-        high = [jnp.where(last_x, *pair) for pair in after[2 * yi : 2 * yi + 2]]
-        wide = low + line + high
-        for xi in range(X_IN):
-            m = yi * X_IN + xi
-            other = (1 - yi) * X_IN + xi
-            y_next = here[other] if yi == 0 else y_up[other]
-            y_prev = here[other] if yi == 1 else y_down[other]
-            near = (wide[xi + 1] + wide[xi + 3]) + (y_next + y_prev) + (above[m] + below[m])
-            far = (wide[xi] + wide[xi + 4]) + (y_up[m] + y_down[m]) + (above_2[m] + below_2[m])
+        low = [jnp.where(first_x, *pair) for pair in halos[yi][:2]]
+        high = [jnp.where(last_x, *pair) for pair in halos[yi][2:]]
+        first, last = yi * X_IN, (yi + 1) * X_IN - 1
+        near[first] = near[first] + low[1]
+        near[last] = near[last] + high[0]
+        for m, halo in zip((first, first + 1, last - 1, last), low + high):
+            far[m] = far[m] + halo
+        for m in range(first, last + 1):
             level = diagonal[plane, :, m * LANES : (m + 1) * LANES]
-            out.append(level * here[m] - near - FAR_SCALED * far)
-    return here, out
+            out.append(level * here[m] - near[m] - FAR_SCALED * far[m])
+    return out, coming
 
 
 def cmul(first, second):
@@ -429,13 +449,21 @@
     def half_turn(i, work, before):
         units = [(plane, group) for plane in range(planes) for group in range(groups)]
         curve = [[] for _ in range(groups)]
-        ahead = plane_rolls(plane_rows(work, 0, all_rows[0]))
+        here = plane_rows(work, 0, all_rows[0])
+        state = (here, y_rolls(here))
         for (plane, group), coming in zip(units, units[1:] + [None]):
-            rolls = ahead
-            if coming is not None:
-                ahead = plane_rolls(plane_rows(work, coming[0], all_rows[coming[1]]))
+
+            def ahead(coming=coming):
+                if coming is None:
+                    return None
+                here = plane_rows(work, coming[0], all_rows[coming[1]])
+                return here, y_rolls(here)
+
             rows = all_rows[group]
-            value, out = apply_plane(work, diagonal, plane, rows, rolls, last_x, first_x)
+            value = state[0]
+            out, state = apply_plane(
+                work, diagonal, plane, rows, *state, ahead, last_x, first_x
+            )
             for m, lanes in enumerate(all_lanes):
                 applied[plane, rows, lanes] = out[m]
             curve[group].append(tree_sum([value[m] * out[m] for m in range(ROWS)]))

time: 30.5 us -> 30.5 us (level)
  transfers between devices with their start and end apart: 10 -> 10, of which waited for: 4 -> 4; matrix products, arithmetic and copies ran while one was open for 0% -> 0% of each run, Pallas kernels for 31% -> 30%
where the time goes in v18:
time: 30.5 us; the launch traced here: 30.3 us
  Pallas kernels  14.2 us (47%)
  starting transfers between devices  10.1 us (33%)
  waiting for transfers between devices  3.78 us (12%)
  between operations  1.3 us (4%)
  other arithmetic  0.93 us (3%)
    pallas_call x1, Pallas kernels, whole_grid(): pl.pallas_call(functools.partial(krylov_kernel, parts, count), out_shape=...  9.23 us
    ppermute x9, starting transfers between devices, swapped(): lax.ppermute(values, axis, [(index ^ mask, index) for index in range(size)])  8.04 us
    pallas_call x1, Pallas kernels, whole_grid(): pl.pallas_call(functools.partial(gram_kernel, points), out_shape=(out, ou...  4.39 us
    ppermute x9, waiting for transfers between devices, swapped(): lax.ppermute(values, axis, [(index ^ mask, index) for index in range(size)])  3.78 us
    ppermute x1, starting transfers between devices, whole_grid(): lax.ppermute(tile, ('point', 'dom'), mixed)  2.03 us
    concatenate x1, other arithmetic, packed_block(): jnp.concatenate([rows, levels], axis=0)  0.93 us
  transfers between devices with their start and end apart: 10, of which 4 were waited for; matrix products, arithmetic and copies ran while one was open for 0% of the time, Pallas kernels for 30%

profile of v18, /device:TPU:0, one launch (start us, length us, event | category | flops | bytes accessed | tf_op | source)
XLA Modules:
  0.0 30.3 jit_solution(13106255779004445339)
XLA Ops:
  1.3 0.9 %pad_maximum_fusion.rows = f32[272,128]{1,0:T(8,128)S(1)} fusion(f32[16,128]{1,0:T(8,128)} %bitcast.13, f32[256,128]{1,0:T(8,128)} %bitcast.12), kind=kLoop, calls=%fused_computation | loop fusion | flops 34816 | bytes 278528 | tf_op jit(solution)/shard_map/concatenate | solution.py:235
  2.2 0.6 %pack.1 = (f32[272,128]{1,0:T(8,128)S(1)}, f32[8,128]{1,0:T(8,128)S(1)}) custom-call(s32[1,1]{1,0:T(1,128)} %bitcast.11.counts, f32[272,128]{1,0:T(8,128)S(1)} %pad_maximum_fusion.rows), custom_call_target="tpu_custom_call" | custom-call | tf_op jit(solution)/shard_map/pack/pallas_call | solution.py:225
  2.8 3.0 %collective-permute-start.1 = (f32[272,128]{1,0:T(8,128)S(1)}, f32[272,128]{1,0:T(8,128)S(1)}, u32[]{:S(2)}, u32[]{:S(2)}) collective-permute-start(f32[272,128]{1,0:T(8,128)S(1)} %get-tuple-element.10.refs_0_), channel_id=1, source_target_pairs={{2,0},{3,1},{0,2},{1,3},{6,4},{7,5},{4,6},{5,7},{10,8},{11,9},{8,1... | collective-permute-start | bytes 417800 | tf_op jit(solution)/shard_map/ppermute | solution.py:554
  5.8 1.5 %collective-permute-start.5 = (f32[272,128]{1,0:T(8,128)S(1)}, f32[272,128]{1,0:T(8,128)S(1)}, u32[]{:S(2)}, u32[]{:S(2)}) collective-permute-start(f32[272,128]{1,0:T(8,128)S(1)} %get-tuple-element.10.refs_0_), channel_id=1, source_target_pairs={{4,0},{5,1},{6,2},{7,3},{0,4},{1,5},{2,6},{3,7},{12,8},{13,9},{14,... | collective-permute-start | bytes 417800 | tf_op jit(solution)/shard_map/ppermute | solution.py:554
  7.3 0.0 collective-permute-start.7
  7.3 2.0 %collective-permute-start.2 = (f32[8,128]{1,0:T(8,128)S(1)}, f32[8,128]{1,0:T(8,128)S(1)}, u32[]{:S(2)}, u32[]{:S(2)}) collective-permute-start(f32[8,128]{1,0:T(8,128)S(1)} %get-tuple-element.11.refs_0_), channel_id=1, source_target_pairs={{8,0},{17,1},{10,2},{19,3},{12,4},{21,5},{14,6},{23,7},{0,8},{25,9... | collective-permute-start | bytes 12296 | tf_op jit(solution)/shard_map/ppermute | solution.py:567
  9.4 2.5 %collective-permute-start.3 = (f32[8,128]{1,0:T(8,128)S(1)}, f32[8,128]{1,0:T(8,128)S(1)}, u32[]{:S(2)}, u32[]{:S(2)}) collective-permute-start(f32[8,128]{1,0:T(8,128)S(1)} %get-tuple-element.11.refs_0_), channel_id=1, source_target_pairs={{24,0},{16,8},{8,16},{0,24},{25,1},{17,9},{9,17},{1,25},{26,2},{18... | collective-permute-start | bytes 12296 | tf_op jit(solution)/shard_map/ppermute | solution.py:554
  11.8 0.0 collective-permute-done.2.refs_1_
  11.8 0.0 collective-permute-start
  11.8 2.9 %collective-permute-done.3.refs_2_ = f32[8,128]{1,0:T(8,128)S(1)} collective-permute-done((f32[8,128]{1,0:T(8,128)S(1)}, f32[8,128]{1,0:T(8,128)S(1)}, u32[]{:S(2)}, u32[]{:S(2)}) %collective-permute-start.3) | collective-permute-done | bytes 4128 | tf_op jit(solution)/shard_map/ppermute | solution.py:554
  14.8 0.0 collective-permute-done.1.refs_2_
  14.8 0.0 collective-permute-start.4
  14.8 0.0 collective-permute-done.5.refs_4_
  14.8 0.5 %collective-permute-start.6 = (f32[272,128]{1,0:T(8,128)S(1)}, f32[272,128]{1,0:T(8,128)S(1)}, u32[]{:S(2)}, u32[]{:S(2)}) collective-permute-start(f32[272,128]{1,0:T(8,128)S(1)} %collective-permute-done.5.refs_4_), channel_id=1, source_target_pairs={{1,0},{0,1},{3,2},{2,3},{5,4},{4,5},{7,6},{6,7},{9,8},{8,9},{11,10... | collective-permute-start | bytes 417800 | tf_op jit(solution)/shard_map/ppermute | solution.py:554
  15.3 0.0 collective-permute-done.7.refs_6_
  15.3 0.1 collective-permute-start.8
  15.3 0.4 %collective-permute-start.9 = (f32[8,128]{1,0:T(8,128)S(1)}, f32[8,128]{1,0:T(8,128)S(1)}, u32[]{:S(2)}, u32[]{:S(2)}) collective-permute-start(f32[8,128]{1,0:T(8,128)S(1)} %collective-permute-done.2.refs_1_), channel_id=1, source_target_pairs={{1,0},{0,1},{3,2},{2,3},{5,4},{4,5},{7,6},{6,7},{9,8},{8,9},{11,10... | collective-permute-start | bytes 12296 | tf_op jit(solution)/shard_map/ppermute | solution.py:554
  15.8 0.0 collective-permute-done.refs_1_
  15.8 0.3 %collective-permute-done.4.refs_3_ = f32[272,128]{1,0:T(8,128)S(1)} collective-permute-done((f32[272,128]{1,0:T(8,128)S(1)}, f32[272,128]{1,0:T(8,128)S(1)}, u32[]{:S(2)}, u32[]{:S(2)}) %collective-permute-start.4) | collective-permute-done | bytes 139296 | tf_op jit(solution)/shard_map/ppermute | solution.py:554
  16.1 0.2 collective-permute-done.6.refs_5_
  16.3 0.3 %collective-permute-done.8.refs_7_ = f32[272,128]{1,0:T(8,128)S(1)} collective-permute-done((f32[272,128]{1,0:T(8,128)S(1)}, f32[272,128]{1,0:T(8,128)S(1)}, u32[]{:S(2)}, u32[]{:S(2)}) %collective-permute-start.8) | collective-permute-done | bytes 139296 | tf_op jit(solution)/shard_map/ppermute | solution.py:554
  16.6 9.2 %krylov.1 = (f32[6,16,16,1024]{3,2,1,0:T(8,128)S(1)}, f32[16,16,1024]{2,1,0:T(8,128)S(1)}, f32[13,16,128]{2,1,0:T(8,128)S(1)}) custom-call(f32[272,128]{1,0:T(8,128)S(1)} %get-tuple-element.10.refs_0_, f32[272,128]{1,0:T(8,128)S(1)} %collective-permute-done.refs_1_, f32[272,128]{1,0:T(8,128)S(1)} %collective-permute-done.1.refs_2_, ...), custom_call_target="tpu_custom_call" | custom-call | tf_op jit(solution)/shard_map/krylov/pallas_call | solution.py:575
  25.9 0.0 collective-permute-done.9.refs_3_
  25.9 4.4 %gram.1 = (f32[2,64,64]{2,1,0:T(8,128)}, f32[2,64,64]{2,1,0:T(8,128)}) custom-call(f32[13,16,128]{2,1,0:T(8,128)S(1)} %get-tuple-element.13.scalars, f32[8,128]{1,0:T(8,128)S(1)} %get-tuple-element.11.refs_0_, f32[8,128]{1,0:T(8,128)S(1)} %collective-permute-done.2.refs_1_, f32[8,128]{1,0:T(8,128)S(1)} %collective-permute-done.3.refs_2_, ...), custom_call_target="tpu_custom_call" | custom-call | tf_op jit(solution)/shard_map/gram/pallas_call | solution.py:595
Async XLA Ops:
  2.8 12.0 %collective-permute-start.1 = (f32[272,128]{1,0:T(8,128)S(1)}, f32[272,128]{1,0:T(8,128)S(1)}, u32[]{:S(2)}, u32[]{:S(2)}) collective-permute-start(f32[272,128]{1,0:T(8,128)S(1)} %get-tuple-element.10.refs_0_), channel_id=1, source_target_pairs={{2,0},{3,1},{0,2},{1,3},{6,4},{7,5},{4,6},{5,7},{10,8},{11,9},{8,1... | collective-permute-start | bytes 417800 | tf_op jit(solution)/shard_map/ppermute | solution.py:554
  5.8 9.0 %collective-permute-start.5 = (f32[272,128]{1,0:T(8,128)S(1)}, f32[272,128]{1,0:T(8,128)S(1)}, u32[]{:S(2)}, u32[]{:S(2)}) collective-permute-start(f32[272,128]{1,0:T(8,128)S(1)} %get-tuple-element.10.refs_0_), channel_id=1, source_target_pairs={{4,0},{5,1},{6,2},{7,3},{0,4},{1,5},{2,6},{3,7},{12,8},{13,9},{14,... | collective-permute-start | bytes 417800 | tf_op jit(solution)/shard_map/ppermute | solution.py:554
  7.3 8.0 %collective-permute-start.7 = (f32[272,128]{1,0:T(8,128)S(1)}, f32[272,128]{1,0:T(8,128)S(1)}, u32[]{:S(2)}, u32[]{:S(2)}) collective-permute-start(f32[272,128]{1,0:T(8,128)S(1)} %get-tuple-element.10.refs_0_), channel_id=1, source_target_pairs={{6,0},{7,1},{4,2},{5,3},{2,4},{3,5},{0,6},{1,7},{14,8},{15,9},{12,... | collective-permute-start | bytes 417800 | tf_op jit(solution)/shard_map/ppermute | solution.py:554
  7.3 4.5 %collective-permute-start.2 = (f32[8,128]{1,0:T(8,128)S(1)}, f32[8,128]{1,0:T(8,128)S(1)}, u32[]{:S(2)}, u32[]{:S(2)}) collective-permute-start(f32[8,128]{1,0:T(8,128)S(1)} %get-tuple-element.11.refs_0_), channel_id=1, source_target_pairs={{8,0},{17,1},{10,2},{19,3},{12,4},{21,5},{14,6},{23,7},{0,8},{25,9... | collective-permute-start | bytes 12296 | tf_op jit(solution)/shard_map/ppermute | solution.py:567
  9.4 5.4 %collective-permute-start.3 = (f32[8,128]{1,0:T(8,128)S(1)}, f32[8,128]{1,0:T(8,128)S(1)}, u32[]{:S(2)}, u32[]{:S(2)}) collective-permute-start(f32[8,128]{1,0:T(8,128)S(1)} %get-tuple-element.11.refs_0_), channel_id=1, source_target_pairs={{24,0},{16,8},{8,16},{0,24},{25,1},{17,9},{9,17},{1,25},{26,2},{18... | collective-permute-start | bytes 12296 | tf_op jit(solution)/shard_map/ppermute | solution.py:554
  11.8 4.0 %collective-permute-start = (f32[272,128]{1,0:T(8,128)S(1)}, f32[272,128]{1,0:T(8,128)S(1)}, u32[]{:S(2)}, u32[]{:S(2)}) collective-permute-start(f32[272,128]{1,0:T(8,128)S(1)} %get-tuple-element.10.refs_0_), channel_id=1, source_target_pairs={{1,0},{0,1},{3,2},{2,3},{5,4},{4,5},{7,6},{6,7},{9,8},{8,9},{11,10... | collective-permute-start | bytes 417800 | tf_op jit(solution)/shard_map/ppermute | solution.py:554
  14.8 1.4 %collective-permute-start.4 = (f32[272,128]{1,0:T(8,128)S(1)}, f32[272,128]{1,0:T(8,128)S(1)}, u32[]{:S(2)}, u32[]{:S(2)}) collective-permute-start(f32[272,128]{1,0:T(8,128)S(1)} %collective-permute-done.1.refs_2_), channel_id=1, source_target_pairs={{1,0},{0,1},{3,2},{2,3},{5,4},{4,5},{7,6},{6,7},{9,8},{8,9},{11,10... | collective-permute-start | bytes 417800 | tf_op jit(solution)/shard_map/ppermute | solution.py:554
  14.8 1.6 %collective-permute-start.6 = (f32[272,128]{1,0:T(8,128)S(1)}, f32[272,128]{1,0:T(8,128)S(1)}, u32[]{:S(2)}, u32[]{:S(2)}) collective-permute-start(f32[272,128]{1,0:T(8,128)S(1)} %collective-permute-done.5.refs_4_), channel_id=1, source_target_pairs={{1,0},{0,1},{3,2},{2,3},{5,4},{4,5},{7,6},{6,7},{9,8},{8,9},{11,10... | collective-permute-start | bytes 417800 | tf_op jit(solution)/shard_map/ppermute | solution.py:554
  15.3 1.4 %collective-permute-start.8 = (f32[272,128]{1,0:T(8,128)S(1)}, f32[272,128]{1,0:T(8,128)S(1)}, u32[]{:S(2)}, u32[]{:S(2)}) collective-permute-start(f32[272,128]{1,0:T(8,128)S(1)} %collective-permute-done.7.refs_6_), channel_id=1, source_target_pairs={{1,0},{0,1},{3,2},{2,3},{5,4},{4,5},{7,6},{6,7},{9,8},{8,9},{11,10... | collective-permute-start | bytes 417800 | tf_op jit(solution)/shard_map/ppermute | solution.py:554
  15.3 10.5 %collective-permute-start.9 = (f32[8,128]{1,0:T(8,128)S(1)}, f32[8,128]{1,0:T(8,128)S(1)}, u32[]{:S(2)}, u32[]{:S(2)}) collective-permute-start(f32[8,128]{1,0:T(8,128)S(1)} %collective-permute-done.2.refs_1_), channel_id=1, source_target_pairs={{1,0},{0,1},{3,2},{2,3},{5,4},{4,5},{7,6},{6,7},{9,8},{8,9},{11,10... | collective-permute-start | bytes 12296 | tf_op jit(solution)/shard_map/ppermute | solution.py:554

commit v19 on v18

--- a/solution.py
+++ b/solution.py
@@ -259,17 +259,17 @@
     ]
 
 
-def x_rolls(here):
+def x_rolls(here, rolled, last_x, first_x):
     halos = []
     for yi in range(Y_IN):
-        line = here[yi * X_IN : (yi + 1) * X_IN]
+        first = yi * X_IN
         halo = [
-            (pltpu.roll(value, LANES - X_OUT + 1, 1), pltpu.roll(value, 1, 1))
-            for value in line[X_IN - 2 :]
+            pltpu.roll(jnp.where(last_x, rolled[m][0], here[m]), 1, 1)
+            for m in range(first + X_IN - 2, first + X_IN)
         ]
         halo += [
-            (pltpu.roll(value, X_OUT - 1, 1), pltpu.roll(value, LANES - 1, 1))
-            for value in line[:2]
+            pltpu.roll(jnp.where(first_x, rolled[m][1], here[m]), LANES - 1, 1)
+            for m in range(first, first + 2)
         ]
         halos.append(halo)
     return halos
@@ -282,7 +282,7 @@
     )
     near = [above[m] + below[m] for m in range(ROWS)]
     far = [above_2[m] + below_2[m] for m in range(ROWS)]
-    halos = x_rolls(here)
+    halos = x_rolls(here, rolled, last_x, first_x)
     for m in range(ROWS):
         other = m + X_IN if m < X_IN else m - X_IN
         near[m] = near[m] + (here[other] + rolled[other][1 if m < X_IN else 0])
@@ -298,8 +298,7 @@
     coming = ahead()
     out = []
     for yi in range(Y_IN):
-        low = [jnp.where(first_x, *pair) for pair in halos[yi][:2]]
-        high = [jnp.where(last_x, *pair) for pair in halos[yi][2:]]
+        low, high = halos[yi][:2], halos[yi][2:]
         first, last = yi * X_IN, (yi + 1) * X_IN - 1
         near[first] = near[first] + low[1]
         near[last] = near[last] + high[0]

time: 30.5 us -> 37.8 us (1.24)
  Pallas kernels: 14.2 us -> 21.5 us
    pallas_call x1, Pallas kernels: 9.23 us -> 16.6 us  [whole_grid(): pl.pallas_call(functools.partial(krylov_kernel, parts, count), out_shape=...]
  transfers between devices with their start and end apart: 10 -> 10, of which waited for: 4 -> 4; matrix products, arithmetic and copies ran while one was open for 0% -> 0% of each run, Pallas kernels for 30% -> 44%
where the time goes in v19:
time: 37.8 us; the launch traced here: 37.6 us
  Pallas kernels  21.5 us (57%)
  starting transfers between devices  10.1 us (27%)
  waiting for transfers between devices  3.78 us (10%)
  between operations  1.3 us (3%)
  other arithmetic  0.93 us (2%)
    pallas_call x1, Pallas kernels, whole_grid(): pl.pallas_call(functools.partial(krylov_kernel, parts, count), out_shape=...  16.6 us
    ppermute x9, starting transfers between devices, swapped(): lax.ppermute(values, axis, [(index ^ mask, index) for index in range(size)])  8.04 us
    pallas_call x1, Pallas kernels, whole_grid(): pl.pallas_call(functools.partial(gram_kernel, points), out_shape=(out, ou...  4.37 us
    ppermute x9, waiting for transfers between devices, swapped(): lax.ppermute(values, axis, [(index ^ mask, index) for index in range(size)])  3.78 us
    ppermute x1, starting transfers between devices, whole_grid(): lax.ppermute(tile, ('point', 'dom'), mixed)  2.03 us
    concatenate x1, other arithmetic, packed_block(): jnp.concatenate([rows, levels], axis=0)  0.93 us
  transfers between devices with their start and end apart: 10, of which 4 were waited for; matrix products, arithmetic and copies ran while one was open for 0% of the time, Pallas kernels for 44%

profile of v19, /device:TPU:0, one launch (start us, length us, event | category | flops | bytes accessed | tf_op | source)
XLA Modules:
  0.0 37.6 jit_solution(2616531401488495699)
XLA Ops:
  1.3 0.9 %pad_maximum_fusion.rows = f32[272,128]{1,0:T(8,128)S(1)} fusion(f32[16,128]{1,0:T(8,128)} %bitcast.13, f32[256,128]{1,0:T(8,128)} %bitcast.12), kind=kLoop, calls=%fused_computation | loop fusion | flops 34816 | bytes 278528 | tf_op jit(solution)/shard_map/concatenate | solution.py:235
  2.2 0.6 %pack.1 = (f32[272,128]{1,0:T(8,128)S(1)}, f32[8,128]{1,0:T(8,128)S(1)}) custom-call(s32[1,1]{1,0:T(1,128)} %bitcast.11.counts, f32[272,128]{1,0:T(8,128)S(1)} %pad_maximum_fusion.rows), custom_call_target="tpu_custom_call" | custom-call | tf_op jit(solution)/shard_map/pack/pallas_call | solution.py:225
  2.8 3.0 %collective-permute-start.1 = (f32[272,128]{1,0:T(8,128)S(1)}, f32[272,128]{1,0:T(8,128)S(1)}, u32[]{:S(2)}, u32[]{:S(2)}) collective-permute-start(f32[272,128]{1,0:T(8,128)S(1)} %get-tuple-element.10.refs_0_), channel_id=1, source_target_pairs={{2,0},{3,1},{0,2},{1,3},{6,4},{7,5},{4,6},{5,7},{10,8},{11,9},{8,1... | collective-permute-start | bytes 417800 | tf_op jit(solution)/shard_map/ppermute | solution.py:553
  5.8 1.5 %collective-permute-start.5 = (f32[272,128]{1,0:T(8,128)S(1)}, f32[272,128]{1,0:T(8,128)S(1)}, u32[]{:S(2)}, u32[]{:S(2)}) collective-permute-start(f32[272,128]{1,0:T(8,128)S(1)} %get-tuple-element.10.refs_0_), channel_id=1, source_target_pairs={{4,0},{5,1},{6,2},{7,3},{0,4},{1,5},{2,6},{3,7},{12,8},{13,9},{14,... | collective-permute-start | bytes 417800 | tf_op jit(solution)/shard_map/ppermute | solution.py:553
  7.3 0.0 collective-permute-start.7
  7.3 2.0 %collective-permute-start.2 = (f32[8,128]{1,0:T(8,128)S(1)}, f32[8,128]{1,0:T(8,128)S(1)}, u32[]{:S(2)}, u32[]{:S(2)}) collective-permute-start(f32[8,128]{1,0:T(8,128)S(1)} %get-tuple-element.11.refs_0_), channel_id=1, source_target_pairs={{8,0},{17,1},{10,2},{19,3},{12,4},{21,5},{14,6},{23,7},{0,8},{25,9... | collective-permute-start | bytes 12296 | tf_op jit(solution)/shard_map/ppermute | solution.py:566
  9.4 2.5 %collective-permute-start.3 = (f32[8,128]{1,0:T(8,128)S(1)}, f32[8,128]{1,0:T(8,128)S(1)}, u32[]{:S(2)}, u32[]{:S(2)}) collective-permute-start(f32[8,128]{1,0:T(8,128)S(1)} %get-tuple-element.11.refs_0_), channel_id=1, source_target_pairs={{24,0},{16,8},{8,16},{0,24},{25,1},{17,9},{9,17},{1,25},{26,2},{18... | collective-permute-start | bytes 12296 | tf_op jit(solution)/shard_map/ppermute | solution.py:553
  11.8 0.0 collective-permute-done.2.refs_1_
  11.8 0.0 collective-permute-start
  11.8 2.9 %collective-permute-done.3.refs_2_ = f32[8,128]{1,0:T(8,128)S(1)} collective-permute-done((f32[8,128]{1,0:T(8,128)S(1)}, f32[8,128]{1,0:T(8,128)S(1)}, u32[]{:S(2)}, u32[]{:S(2)}) %collective-permute-start.3) | collective-permute-done | bytes 4128 | tf_op jit(solution)/shard_map/ppermute | solution.py:553
  14.8 0.0 collective-permute-done.1.refs_2_
  14.8 0.0 collective-permute-start.4
  14.8 0.0 collective-permute-done.5.refs_4_
  14.8 0.5 %collective-permute-start.6 = (f32[272,128]{1,0:T(8,128)S(1)}, f32[272,128]{1,0:T(8,128)S(1)}, u32[]{:S(2)}, u32[]{:S(2)}) collective-permute-start(f32[272,128]{1,0:T(8,128)S(1)} %collective-permute-done.5.refs_4_), channel_id=1, source_target_pairs={{1,0},{0,1},{3,2},{2,3},{5,4},{4,5},{7,6},{6,7},{9,8},{8,9},{11,10... | collective-permute-start | bytes 417800 | tf_op jit(solution)/shard_map/ppermute | solution.py:553
  15.3 0.0 collective-permute-done.7.refs_6_
  15.3 0.1 collective-permute-start.8
  15.3 0.4 %collective-permute-start.9 = (f32[8,128]{1,0:T(8,128)S(1)}, f32[8,128]{1,0:T(8,128)S(1)}, u32[]{:S(2)}, u32[]{:S(2)}) collective-permute-start(f32[8,128]{1,0:T(8,128)S(1)} %collective-permute-done.2.refs_1_), channel_id=1, source_target_pairs={{1,0},{0,1},{3,2},{2,3},{5,4},{4,5},{7,6},{6,7},{9,8},{8,9},{11,10... | collective-permute-start | bytes 12296 | tf_op jit(solution)/shard_map/ppermute | solution.py:553
  15.8 0.0 collective-permute-done.refs_1_
  15.8 0.3 collective-permute-done.4.refs_3_
  16.1 0.2 collective-permute-done.6.refs_5_
  16.3 0.3 collective-permute-done.8.refs_7_
  16.6 16.6 %krylov.1 = (f32[6,16,16,1024]{3,2,1,0:T(8,128)S(1)}, f32[16,16,1024]{2,1,0:T(8,128)S(1)}, f32[13,16,128]{2,1,0:T(8,128)S(1)}) custom-call(f32[272,128]{1,0:T(8,128)S(1)} %get-tuple-element.10.refs_0_, f32[272,128]{1,0:T(8,128)S(1)} %collective-permute-done.refs_1_, f32[272,128]{1,0:T(8,128)S(1)} %collective-permute-done.1.refs_2_, ...), custom_call_target="tpu_custom_call" | custom-call | tf_op jit(solution)/shard_map/krylov/pallas_call | solution.py:574
  33.3 0.0 collective-permute-done.9.refs_3_
  33.3 4.4 %gram.1 = (f32[2,64,64]{2,1,0:T(8,128)}, f32[2,64,64]{2,1,0:T(8,128)}) custom-call(f32[13,16,128]{2,1,0:T(8,128)S(1)} %get-tuple-element.13.scalars, f32[8,128]{1,0:T(8,128)S(1)} %get-tuple-element.11.refs_0_, f32[8,128]{1,0:T(8,128)S(1)} %collective-permute-done.2.refs_1_, f32[8,128]{1,0:T(8,128)S(1)} %collective-permute-done.3.refs_2_, ...), custom_call_target="tpu_custom_call" | custom-call | tf_op jit(solution)/shard_map/gram/pallas_call | solution.py:594
Async XLA Ops:
  2.8 12.0 %collective-permute-start.1 = (f32[272,128]{1,0:T(8,128)S(1)}, f32[272,128]{1,0:T(8,128)S(1)}, u32[]{:S(2)}, u32[]{:S(2)}) collective-permute-start(f32[272,128]{1,0:T(8,128)S(1)} %get-tuple-element.10.refs_0_), channel_id=1, source_target_pairs={{2,0},{3,1},{0,2},{1,3},{6,4},{7,5},{4,6},{5,7},{10,8},{11,9},{8,1... | collective-permute-start | bytes 417800 | tf_op jit(solution)/shard_map/ppermute | solution.py:553
  5.8 9.0 %collective-permute-start.5 = (f32[272,128]{1,0:T(8,128)S(1)}, f32[272,128]{1,0:T(8,128)S(1)}, u32[]{:S(2)}, u32[]{:S(2)}) collective-permute-start(f32[272,128]{1,0:T(8,128)S(1)} %get-tuple-element.10.refs_0_), channel_id=1, source_target_pairs={{4,0},{5,1},{6,2},{7,3},{0,4},{1,5},{2,6},{3,7},{12,8},{13,9},{14,... | collective-permute-start | bytes 417800 | tf_op jit(solution)/shard_map/ppermute | solution.py:553
  7.3 8.0 %collective-permute-start.7 = (f32[272,128]{1,0:T(8,128)S(1)}, f32[272,128]{1,0:T(8,128)S(1)}, u32[]{:S(2)}, u32[]{:S(2)}) collective-permute-start(f32[272,128]{1,0:T(8,128)S(1)} %get-tuple-element.10.refs_0_), channel_id=1, source_target_pairs={{6,0},{7,1},{4,2},{5,3},{2,4},{3,5},{0,6},{1,7},{14,8},{15,9},{12,... | collective-permute-start | bytes 417800 | tf_op jit(solution)/shard_map/ppermute | solution.py:553
  7.3 4.5 %collective-permute-start.2 = (f32[8,128]{1,0:T(8,128)S(1)}, f32[8,128]{1,0:T(8,128)S(1)}, u32[]{:S(2)}, u32[]{:S(2)}) collective-permute-start(f32[8,128]{1,0:T(8,128)S(1)} %get-tuple-element.11.refs_0_), channel_id=1, source_target_pairs={{8,0},{17,1},{10,2},{19,3},{12,4},{21,5},{14,6},{23,7},{0,8},{25,9... | collective-permute-start | bytes 12296 | tf_op jit(solution)/shard_map/ppermute | solution.py:566
  9.4 5.4 %collective-permute-start.3 = (f32[8,128]{1,0:T(8,128)S(1)}, f32[8,128]{1,0:T(8,128)S(1)}, u32[]{:S(2)}, u32[]{:S(2)}) collective-permute-start(f32[8,128]{1,0:T(8,128)S(1)} %get-tuple-element.11.refs_0_), channel_id=1, source_target_pairs={{24,0},{16,8},{8,16},{0,24},{25,1},{17,9},{9,17},{1,25},{26,2},{18... | collective-permute-start | bytes 12296 | tf_op jit(solution)/shard_map/ppermute | solution.py:553
  11.8 4.0 %collective-permute-start = (f32[272,128]{1,0:T(8,128)S(1)}, f32[272,128]{1,0:T(8,128)S(1)}, u32[]{:S(2)}, u32[]{:S(2)}) collective-permute-start(f32[272,128]{1,0:T(8,128)S(1)} %get-tuple-element.10.refs_0_), channel_id=1, source_target_pairs={{1,0},{0,1},{3,2},{2,3},{5,4},{4,5},{7,6},{6,7},{9,8},{8,9},{11,10... | collective-permute-start | bytes 417800 | tf_op jit(solution)/shard_map/ppermute | solution.py:553
  14.8 1.4 %collective-permute-start.4 = (f32[272,128]{1,0:T(8,128)S(1)}, f32[272,128]{1,0:T(8,128)S(1)}, u32[]{:S(2)}, u32[]{:S(2)}) collective-permute-start(f32[272,128]{1,0:T(8,128)S(1)} %collective-permute-done.1.refs_2_), channel_id=1, source_target_pairs={{1,0},{0,1},{3,2},{2,3},{5,4},{4,5},{7,6},{6,7},{9,8},{8,9},{11,10... | collective-permute-start | bytes 417800 | tf_op jit(solution)/shard_map/ppermute | solution.py:553
  14.8 1.6 %collective-permute-start.6 = (f32[272,128]{1,0:T(8,128)S(1)}, f32[272,128]{1,0:T(8,128)S(1)}, u32[]{:S(2)}, u32[]{:S(2)}) collective-permute-start(f32[272,128]{1,0:T(8,128)S(1)} %collective-permute-done.5.refs_4_), channel_id=1, source_target_pairs={{1,0},{0,1},{3,2},{2,3},{5,4},{4,5},{7,6},{6,7},{9,8},{8,9},{11,10... | collective-permute-start | bytes 417800 | tf_op jit(solution)/shard_map/ppermute | solution.py:553
  15.3 1.4 %collective-permute-start.8 = (f32[272,128]{1,0:T(8,128)S(1)}, f32[272,128]{1,0:T(8,128)S(1)}, u32[]{:S(2)}, u32[]{:S(2)}) collective-permute-start(f32[272,128]{1,0:T(8,128)S(1)} %collective-permute-done.7.refs_6_), channel_id=1, source_target_pairs={{1,0},{0,1},{3,2},{2,3},{5,4},{4,5},{7,6},{6,7},{9,8},{8,9},{11,10... | collective-permute-start | bytes 417800 | tf_op jit(solution)/shard_map/ppermute | solution.py:553
  15.3 17.9 %collective-permute-start.9 = (f32[8,128]{1,0:T(8,128)S(1)}, f32[8,128]{1,0:T(8,128)S(1)}, u32[]{:S(2)}, u32[]{:S(2)}) collective-permute-start(f32[8,128]{1,0:T(8,128)S(1)} %collective-permute-done.2.refs_1_), channel_id=1, source_target_pairs={{1,0},{0,1},{3,2},{2,3},{5,4},{4,5},{7,6},{6,7},{9,8},{8,9},{11,10... | collective-permute-start | bytes 12296 | tf_op jit(solution)/shard_map/ppermute | solution.py:553

commit v20 on v14

--- a/solution.py
+++ b/solution.py
@@ -166,7 +166,6 @@
 SUB = 8
 BASIS = ITERS + 1
 CORES = 2
-UNROLL = 4
 H_SCALE = 2.0 / COEF_NEAR
 FAR_SCALED = 0.5 * H_SCALE * COEF_FAR
 
@@ -243,46 +242,53 @@
     return jnp.where(bottom > 0.0, top / jnp.where(bottom > 0.0, bottom, 1.0), 0.0)
 
 
-def x_next(values, wrap_mask):
-    return jnp.where(wrap_mask, pltpu.roll(values, X_OUT - 1, 1), pltpu.roll(values, LANES - 1, 1))
-
-
-def x_prev(values, wrap_mask):
-    return jnp.where(wrap_mask, pltpu.roll(values, LANES - X_OUT + 1, 1), pltpu.roll(values, 1, 1))
-
-
 def tree_sum(values):
     while len(values) > 1:
         values = [sum(values[i : i + 2][1:], values[i]) for i in range(0, len(values), 2)]
     return values[0]
 
 
-def apply_plane(vector, diagonal, plane, group, last_x, first_x):
-    planes = vector.shape[0]
-    rows = pl.ds(group * SUB, SUB)
-
-    def plane_at(index):
-        return [vector[index % planes, rows, m * LANES : (m + 1) * LANES] for m in range(ROWS)]
-
-    here, above, below = (plane_at(plane + far) for far in (0, 1, -1))
-    above_2, below_2 = (plane_at(plane + far) for far in (2, -2))
+def plane_rows(vector, plane, rows):
+    return [vector[plane, rows, m * LANES : (m + 1) * LANES] for m in range(ROWS)]
+
+
+def y_parts(here, last_x, first_x):
     y_up = [pltpu.roll(value, LANES - X_OUT, 1) for value in here]
     y_down = [pltpu.roll(value, X_OUT, 1) for value in here]
+    sums, edges = [], []
+    for m in range(ROWS):
+        near = y_down[m + X_IN] if m < X_IN else y_up[m - X_IN]
+        sums.append(near + FAR_SCALED * (y_up[m] + y_down[m]))
+        if m % X_IN < 2:
+            edges.append(jnp.where(first_x, y_down[m], here[m]))
+        else:
+            edges.append(jnp.where(last_x, y_up[m], here[m]))
+    return sums, edges
+
+
+def apply_plane(vector, sums, edges, diagonal, plane, rows):
+    planes = vector.shape[0]
+    halos = []
+    for m, edge in enumerate(plane_rows(edges, plane, rows)):
+        halos.append(pltpu.roll(edge, LANES - 1 if m % X_IN < 2 else 1, 1))
+    here, above, below, above_2, below_2 = (
+        plane_rows(vector, (plane + far) % planes, rows) for far in (0, 1, -1, 2, -2)
+    )
+    y_sums = plane_rows(sums, plane, rows)
     out = []
     for yi in range(Y_IN):
-        line = here[yi * X_IN : (yi + 1) * X_IN]
-        before = [x_prev(line[X_IN - 2], first_x), x_prev(line[X_IN - 1], first_x)]
-        after = [x_next(line[0], last_x), x_next(line[1], last_x)]
-        wide = before + line + after
+        first = yi * X_IN
+        line, halo = here[first : first + X_IN], halos[first : first + X_IN]
+        wide = halo[2:] + line + halo[:2]
         for xi in range(X_IN):
-            m = yi * X_IN + xi
-            other = (1 - yi) * X_IN + xi
-            y_next = here[other] if yi == 0 else y_up[other]
-            y_prev = here[other] if yi == 1 else y_down[other]
-            near = (wide[xi + 1] + wide[xi + 3]) + (y_next + y_prev) + (above[m] + below[m])
-            far = (wide[xi] + wide[xi + 4]) + (y_up[m] + y_down[m]) + (above_2[m] + below_2[m])
+            m = first + xi
+            other = m + X_IN if yi == 0 else m - X_IN
+            near = here[other] + (above[m] + below[m])
+            far = above_2[m] + below_2[m]
+            near = near + (wide[xi + 1] + wide[xi + 3])
+            far = far + (wide[xi] + wide[xi + 4])
             level = diagonal[plane, :, m * LANES : (m + 1) * LANES]
-            out.append(level * here[m] - near - FAR_SCALED * far)
+            out.append((level * here[m] - y_sums[m]) - near - FAR_SCALED * far)
     return here, out
 
 
@@ -293,87 +299,87 @@
     )
 
 
-def moment_coeffs(point, points, count):
+def picked(index, values):
+    result = jnp.float32(values[0])
+    for i, value in enumerate(values[1:], 1):
+        result = jnp.where(index == i, jnp.float32(value), result)
+    return result
+
+
+def moment_coeffs(point, angles, count):
     lane = lax.broadcasted_iota(jnp.int32, (1, LANES), 1)
     moment = lax.rem(lane, MOMENTS * count) // count
-    angle = 2.0 * math.pi * (point + 0.5) / points
     parts = []
     for func in (math.cos, math.sin):
-        value = jnp.full((1, LANES), 0.25 * func(angle), jnp.float32)
-        for k in range(1, MOMENTS):
-            value = jnp.where(moment == k, 0.25 * func((k + 1) * angle), value)
+        value = jnp.zeros((1, LANES), jnp.float32)
+        for k in range(MOMENTS):
+            coeff = picked(point, [0.25 * func((k + 1) * angle) for angle in angles])
+            value = jnp.where(moment == k, coeff, value)
         parts.append(value)
     return parts
 
 
-def weights_of(alphas, norms, limits, count):
-    points = len(limits)
-    shape = (count, LANES)
-    half = MOMENTS * count
+def weights_of(point, points, alphas, norms, limit):
+    shape = alphas[0].shape
+    count = shape[0]
     lane = lax.broadcasted_iota(jnp.int32, shape, 1)
     source = lax.broadcasted_iota(jnp.int32, shape, 0)
     own = lax.rem(lane, count) == source
-    left_half = lane < half
+    left_half = lane < MOMENTS * count
     betas = [ratio(norms[i + 1], norms[i]) for i in range(ITERS - 1)]
-    sums = [[jnp.zeros(shape, jnp.float32)] * 2 for _ in range(BASIS)]
     zero = jnp.zeros(shape, jnp.float32)
     one = jnp.ones(shape, jnp.float32)
-    for point in range(points):
-        angle = 2.0 * math.pi * (point + 0.5) / points
-        shift = (GAMMA + RADIUS * math.cos(angle), RADIUS * math.sin(angle))
-        scaled_shift = (H_SCALE * shift[0], H_SCALE * shift[1])
-        limit = limits[point]
-        product = (one, zero)
-        products = [product]
-        links = []
-        pivot = (scaled_shift[0] - alphas[0], zero + scaled_shift[1])
-        for i in range(ITERS):
-            size = 1.0 / (pivot[0] * pivot[0] + pivot[1] * pivot[1])
-            inverse = (pivot[0] * size, -pivot[1] * size)
-            product = cmul(product, inverse)
-            products.append(product)
-            if i < ITERS - 1:
-                link = (betas[i] * inverse[0], betas[i] * inverse[1])
-                links.append(link)
-                pivot = (scaled_shift[0] - alphas[i + 1] - link[0], scaled_shift[1] - link[1])
-        solved = [None] * ITERS
-        for i in reversed(range(ITERS)):
-            value = (H_SCALE * products[i + 1][0], H_SCALE * products[i + 1][1])
-            if i < ITERS - 1:
-                step = cmul(links[i], solved[i + 1])
-                value = (value[0] + step[0], value[1] + step[1])
-            used = limit > i
-            solved[i] = (jnp.where(used, value[0], 0.0), jnp.where(used, value[1], 0.0))
-        applied = []
-        for i in range(BASIS):
-            left = limit == i
-            rest = (
-                jnp.where(left, products[i][0], 0.0),
-                jnp.where(left, products[i][1], 0.0),
-            )
-            if i < ITERS:
-                turned = (
-                    shift[0] * solved[i][0] - shift[1] * solved[i][1],
-                    shift[0] * solved[i][1] + shift[1] * solved[i][0],
-                )
-                rest = (rest[0] + turned[0], rest[1] + turned[1])
-            if i == 0:
-                rest = (rest[0] - 1.0, rest[1])
-            applied.append(rest)
-        tail = applied[ITERS]
-        for back, factor in ((1, alphas[ITERS - 1]), (2, betas[ITERS - 2])):
-            part = applied[ITERS - back]
-            applied[ITERS - back] = (part[0] - factor * tail[0], part[1] - factor * tail[1])
-        moment = moment_coeffs(point, points, count)
-        for i in range(BASIS):
-            left = solved[i] if i < ITERS else (zero, zero)
-            both = (
-                jnp.where(left_half, left[0], applied[i][0]),
-                jnp.where(left_half, left[1], applied[i][1]),
-            )
-            term = cmul(moment, both)
-            sums[i] = [sums[i][0] + term[0], sums[i][1] + term[1]]
-    return [[jnp.where(own, part, 0.0) for part in pair] for pair in sums]
+    angles = [2.0 * math.pi * (j + 0.5) / points for j in range(points)]
+    shift = (
+        picked(point, [GAMMA + RADIUS * math.cos(angle) for angle in angles]),
+        picked(point, [RADIUS * math.sin(angle) for angle in angles]),
+    )
+    scaled_shift = (H_SCALE * shift[0], H_SCALE * shift[1])
+    product = (one, zero)
+    products = [product]
+    links = []
+    pivot = (scaled_shift[0] - alphas[0], zero + scaled_shift[1])
+    for i in range(ITERS):
+        size = 1.0 / (pivot[0] * pivot[0] + pivot[1] * pivot[1])
+        inverse = (pivot[0] * size, -pivot[1] * size)
+        product = cmul(product, inverse)
+        products.append(product)
+        if i < ITERS - 1:
+            link = (betas[i] * inverse[0], betas[i] * inverse[1])
+            links.append(link)
+            pivot = (scaled_shift[0] - alphas[i + 1] - link[0], scaled_shift[1] - link[1])
+    solved = [None] * ITERS
+    for i in reversed(range(ITERS)):
+        value = (H_SCALE * products[i + 1][0], H_SCALE * products[i + 1][1])
+        if i < ITERS - 1:
+            step = cmul(links[i], solved[i + 1])
+            value = (value[0] + step[0], value[1] + step[1])
+        used = limit > i
+        solved[i] = (jnp.where(used, value[0], 0.0), jnp.where(used, value[1], 0.0))
+    applied = []
+    for i in range(BASIS):
+        left = limit == i
+        rest = (jnp.where(left, products[i][0], 0.0), jnp.where(left, products[i][1], 0.0))
+        if i < ITERS:
+            turned = cmul(shift, solved[i])
+            rest = (rest[0] + turned[0], rest[1] + turned[1])
+        if i == 0:
+            rest = (rest[0] - 1.0, rest[1])
+        applied.append(rest)
+    tail = applied[ITERS]
+    for back, factor in ((1, alphas[ITERS - 1]), (2, betas[ITERS - 2])):
+        part = applied[ITERS - back]
+        applied[ITERS - back] = (part[0] - factor * tail[0], part[1] - factor * tail[1])
+    moment = moment_coeffs(point, angles, count)
+    weights = []
+    for i in range(BASIS):
+        left = solved[i] if i < ITERS else (zero, zero)
+        both = (
+            jnp.where(left_half, left[0], applied[i][0]),
+            jnp.where(left_half, left[1], applied[i][1]),
+        )
+        weights.append([jnp.where(own, part, 0.0) for part in cmul(moment, both)])
+    return weights
 
 
 def exact_dot(first, second, dims):
@@ -387,7 +393,8 @@
 
 
 def krylov_kernel(parts, count, *refs):
-    blocks, (vectors, applied, scalars, first_work, second_work, diagonal) = refs[:parts], refs[parts:]
+    blocks, (vectors, applied, scalars) = refs[:parts], refs[parts : parts + 3]
+    first_work, second_work, diagonal, sums, edges = refs[parts + 3 :]
     planes = diagonal.shape[0]
     depth = planes // parts
     groups = count // SUB
@@ -414,23 +421,28 @@
 
     all_rows = [pl.ds(group * SUB, SUB) for group in range(groups)]
     all_lanes = [slice(m * LANES, (m + 1) * LANES) for m in range(ROWS)]
+    def keep_y_parts(plane, rows, values):
+        for ref, parts_of in zip((sums, edges), y_parts(values, last_x, first_x)):
+            for lanes, part in zip(all_lanes, parts_of):
+                ref[plane, rows, lanes] = part
+
     for group, rows in enumerate(all_rows):
         norm = []
         for plane in range(planes):
-            values = [first_work[plane, rows, lanes] for lanes in all_lanes]
+            values = plane_rows(first_work, plane, rows)
+            keep_y_parts(plane, rows, values)
             norm.append(tree_sum([value * value for value in values]))
         scalars[ITERS + 1, rows, :] = lane_sum(tree_sum(norm))
 
     def half_turn(i, work, before):
-        curves = []
-        for group, rows in enumerate(all_rows):
-            curve = []
-            for plane in range(planes):
-                value, out = apply_plane(work, diagonal, plane, group, last_x, first_x)
+        curve = [[] for _ in range(groups)]
+        for plane in range(planes):
+            for group, rows in enumerate(all_rows):
+                value, out = apply_plane(work, sums, edges, diagonal, plane, rows)
                 for m, lanes in enumerate(all_lanes):
                     applied[plane, rows, lanes] = out[m]
-                curve.append(tree_sum([value[m] * out[m] for m in range(ROWS)]))
-            curves.append(lane_sum(tree_sum(curve)))
+                curve[group].append(tree_sum([value[m] * out[m] for m in range(ROWS)]))
+        curves = [lane_sum(tree_sum(parts_of)) for parts_of in curve]
         alphas = []
         for group, rows in enumerate(all_rows):
             alphas.append(ratio(curves[group], scalars[ITERS + 1 + i, rows, :]))
@@ -450,8 +462,9 @@
                         value = value - beta * before[plane, rows, lanes]
                         before[plane, rows, lanes] = value
                         vectors[i + 1, plane, rows, lanes] = value
-                        values.append(value * value)
-                    norm.append(tree_sum(values))
+                        values.append(value)
+                    keep_y_parts(plane, rows, values)
+                    norm.append(tree_sum([value * value for value in values]))
                 norms.append(lane_sum(tree_sum(norm)))
             for group, rows in enumerate(all_rows):
                 scalars[ITERS + 2 + i, rows, :] = norms[group]
@@ -466,40 +479,46 @@
 
 def gram_kernel(points, scalars, *refs):
     tiles = refs[:points]
-    archive, applied, out_b, out_a, gram, limits = refs[points:]
+    archive, applied, out_b, out_a, gram, limits, weights = refs[points:]
     planes, count, _ = applied.shape
     groups = count // SUB
     size = BASIS * count
-    gram[...] = jnp.zeros_like(gram)
-
-    def gram_turn(plane, carry):
-        values = [archive[i, plane] for i in range(ITERS)] + [applied[plane]]
-        values = jnp.concatenate(values, axis=0)
-        high = values.astype(jnp.bfloat16)
-        low = (values - high.astype(jnp.float32)).astype(jnp.bfloat16)
-        gram[...] += lax.dot_general(
-            jnp.concatenate([high, low], axis=0),
-            high,
-            (((1,), (1,)), ((), ())),
-            preferred_element_type=jnp.float32,
-        )
-        return carry
-
-    lax.fori_loop(0, planes, gram_turn, 0, unroll=UNROLL)
-    cross = gram[size:, :]
-    pairs = gram[:size, :] + cross + cross.T
-
     here = lax.axis_index("point")
     core = jnp.bitwise_and(lax.axis_index("dom"), CORES - 1)
     for far, tile in zip((0, 1 + core, 3, 2 - core), tiles):
         limits[jnp.bitwise_xor(here, far)] = tile[...]
-    bounds = [jnp.concatenate([limits[j]] * groups, axis=0) for j in range(points)]
-    alphas = [scalars[i] for i in range(ITERS)]
-    norms = [scalars[ITERS + 1 + i] for i in range(ITERS)]
-    weights = weights_of(alphas, norms, bounds, count)
-    real = jnp.concatenate([pair[0] for pair in weights], axis=0)
-    imag = jnp.concatenate([pair[1] for pair in weights], axis=0)
-    right = exact_dot(pairs, jnp.concatenate([real, imag], axis=1), ((1,), (0,)))
+    gram[...] = jnp.zeros_like(gram)
+    weights[...] = jnp.zeros_like(weights)
+
+    def turn(point, carry):
+        limit = jnp.concatenate([limits[point]] * groups, axis=0)
+        alphas = [scalars[i] for i in range(ITERS)]
+        norms = [scalars[ITERS + 1 + i] for i in range(ITERS)]
+        total = None
+        for deep in range(planes // points):
+            plane = point * (planes // points) + deep
+            values = [archive[i, plane] for i in range(ITERS)] + [applied[plane]]
+            values = jnp.concatenate(values, axis=0)
+            high = values.astype(jnp.bfloat16)
+            low = (values - high.astype(jnp.float32)).astype(jnp.bfloat16)
+            product = lax.dot_general(
+                jnp.concatenate([high, low], axis=0),
+                high,
+                (((1,), (1,)), ((), ())),
+                preferred_element_type=jnp.float32,
+            )
+            total = product if total is None else total + product
+        gram[...] += total
+        for i, pair in enumerate(weights_of(point, points, alphas, norms, limit)):
+            for part, value in enumerate(pair):
+                weights[i * count : (i + 1) * count, part * LANES : (part + 1) * LANES] += value
+        return carry
+
+    lax.fori_loop(0, points, turn, 0)
+    cross = gram[size:, :]
+    pairs = gram[:size, :] + cross + cross.T
+    right = exact_dot(pairs, weights[...], ((1,), (0,)))
+    real, imag = weights[:, :LANES], weights[:, LANES:]
     half = MOMENTS * count
     left = jnp.concatenate([real[:, :half], imag[:, :half]], axis=1)
     joined = exact_dot(left.T, right, ((1,), (0,)))
@@ -548,6 +567,8 @@
             pltpu.VMEM(vector, jnp.float32),
             pltpu.VMEM(vector, jnp.float32),
             pltpu.VMEM((planes, SUB, ROWS * LANES), jnp.float32),
+            pltpu.VMEM(vector, jnp.float32),
+            pltpu.VMEM(vector, jnp.float32),
         ],
         compiler_params=pltpu.CompilerParams(vmem_limit_bytes=16 * 2**20),
         name="krylov",
@@ -563,6 +584,7 @@
         scratch_shapes=[
             pltpu.VMEM((2 * size, size), jnp.float32),
             pltpu.VMEM((points, SUB, LANES), jnp.float32),
+            pltpu.VMEM((size, 2 * LANES), jnp.float32),
         ],
         compiler_params=pltpu.CompilerParams(vmem_limit_bytes=16 * 2**20),
         name="gram",

time: 31 us -> 29 us (0.935)
  Pallas kernels: 14.7 us -> 12.7 us
    pallas_call x1, Pallas kernels: 9.72 us -> 7.83 us  [whole_grid(): pl.pallas_call(functools.partial(krylov_kernel, parts, count), out_shape=...]
  transfers between devices with their start and end apart: 10 -> 10, of which waited for: 4 -> 4; matrix products, arithmetic and copies ran while one was open for 0% -> 0% of each run, Pallas kernels for 32% -> 27%
where the time goes in v20:
time: 29 us; the launch traced here: 28.7 us
  Pallas kernels  12.7 us (44%)
  starting transfers between devices  10.1 us (35%)
  waiting for transfers between devices  3.78 us (13%)
  between operations  1.3 us (4%)
  other arithmetic  0.93 us (3%)
    ppermute x9, starting transfers between devices, swapped(): lax.ppermute(values, axis, [(index ^ mask, index) for index in range(size)])  8.04 us
    pallas_call x1, Pallas kernels, whole_grid(): pl.pallas_call(functools.partial(krylov_kernel, parts, count), out_shape=...  7.83 us
    pallas_call x1, Pallas kernels, whole_grid(): pl.pallas_call(functools.partial(gram_kernel, points), out_shape=(out, ou...  4.27 us
    ppermute x9, waiting for transfers between devices, swapped(): lax.ppermute(values, axis, [(index ^ mask, index) for index in range(size)])  3.78 us
    ppermute x1, starting transfers between devices, whole_grid(): lax.ppermute(tile, ('point', 'dom'), mixed)  2.03 us
    concatenate x1, other arithmetic, packed_block(): jnp.concatenate([rows, levels], axis=0)  0.93 us
  transfers between devices with their start and end apart: 10, of which 4 were waited for; matrix products, arithmetic and copies ran while one was open for 0% of the time, Pallas kernels for 27%

profile of v20, /device:TPU:0, one launch (start us, length us, event | category | flops | bytes accessed | tf_op | source)
XLA Modules:
  0.0 28.7 jit_solution(7778823715253193613)
XLA Ops:
  1.3 0.9 %pad_maximum_fusion.rows = f32[272,128]{1,0:T(8,128)S(1)} fusion(f32[16,128]{1,0:T(8,128)} %bitcast.13, f32[256,128]{1,0:T(8,128)} %bitcast.12), kind=kLoop, calls=%fused_computation | loop fusion | flops 34816 | bytes 278528 | tf_op jit(solution)/shard_map/concatenate | solution.py:234
  2.2 0.6 %pack.1 = (f32[272,128]{1,0:T(8,128)S(1)}, f32[8,128]{1,0:T(8,128)S(1)}) custom-call(s32[1,1]{1,0:T(1,128)} %bitcast.11.counts, f32[272,128]{1,0:T(8,128)S(1)} %pad_maximum_fusion.rows), custom_call_target="tpu_custom_call" | custom-call | tf_op jit(solution)/shard_map/pack/pallas_call | solution.py:224
  2.8 3.0 %collective-permute-start.1 = (f32[272,128]{1,0:T(8,128)S(1)}, f32[272,128]{1,0:T(8,128)S(1)}, u32[]{:S(2)}, u32[]{:S(2)}) collective-permute-start(f32[272,128]{1,0:T(8,128)S(1)} %get-tuple-element.10.refs_0_), channel_id=1, source_target_pairs={{2,0},{3,1},{0,2},{1,3},{6,4},{7,5},{4,6},{5,7},{10,8},{11,9},{8,1... | collective-permute-start | bytes 417800 | tf_op jit(solution)/shard_map/ppermute | solution.py:536
  5.8 1.5 %collective-permute-start.5 = (f32[272,128]{1,0:T(8,128)S(1)}, f32[272,128]{1,0:T(8,128)S(1)}, u32[]{:S(2)}, u32[]{:S(2)}) collective-permute-start(f32[272,128]{1,0:T(8,128)S(1)} %get-tuple-element.10.refs_0_), channel_id=1, source_target_pairs={{4,0},{5,1},{6,2},{7,3},{0,4},{1,5},{2,6},{3,7},{12,8},{13,9},{14,... | collective-permute-start | bytes 417800 | tf_op jit(solution)/shard_map/ppermute | solution.py:536
  7.3 0.0 collective-permute-start.7
  7.3 2.0 %collective-permute-start.2 = (f32[8,128]{1,0:T(8,128)S(1)}, f32[8,128]{1,0:T(8,128)S(1)}, u32[]{:S(2)}, u32[]{:S(2)}) collective-permute-start(f32[8,128]{1,0:T(8,128)S(1)} %get-tuple-element.11.refs_0_), channel_id=1, source_target_pairs={{8,0},{17,1},{10,2},{19,3},{12,4},{21,5},{14,6},{23,7},{0,8},{25,9... | collective-permute-start | bytes 12296 | tf_op jit(solution)/shard_map/ppermute | solution.py:549
  9.4 2.5 %collective-permute-start.3 = (f32[8,128]{1,0:T(8,128)S(1)}, f32[8,128]{1,0:T(8,128)S(1)}, u32[]{:S(2)}, u32[]{:S(2)}) collective-permute-start(f32[8,128]{1,0:T(8,128)S(1)} %get-tuple-element.11.refs_0_), channel_id=1, source_target_pairs={{24,0},{16,8},{8,16},{0,24},{25,1},{17,9},{9,17},{1,25},{26,2},{18... | collective-permute-start | bytes 12296 | tf_op jit(solution)/shard_map/ppermute | solution.py:536
  11.8 0.0 collective-permute-done.2.refs_1_
  11.8 0.0 collective-permute-start
  11.8 2.9 %collective-permute-done.3.refs_2_ = f32[8,128]{1,0:T(8,128)S(1)} collective-permute-done((f32[8,128]{1,0:T(8,128)S(1)}, f32[8,128]{1,0:T(8,128)S(1)}, u32[]{:S(2)}, u32[]{:S(2)}) %collective-permute-start.3) | collective-permute-done | bytes 4128 | tf_op jit(solution)/shard_map/ppermute | solution.py:536
  14.8 0.0 collective-permute-done.1.refs_2_
  14.8 0.0 collective-permute-start.4
  14.8 0.0 collective-permute-done.5.refs_4_
  14.8 0.5 %collective-permute-start.6 = (f32[272,128]{1,0:T(8,128)S(1)}, f32[272,128]{1,0:T(8,128)S(1)}, u32[]{:S(2)}, u32[]{:S(2)}) collective-permute-start(f32[272,128]{1,0:T(8,128)S(1)} %collective-permute-done.5.refs_4_), channel_id=1, source_target_pairs={{1,0},{0,1},{3,2},{2,3},{5,4},{4,5},{7,6},{6,7},{9,8},{8,9},{11,10... | collective-permute-start | bytes 417800 | tf_op jit(solution)/shard_map/ppermute | solution.py:536
  15.3 0.0 collective-permute-done.7.refs_6_
  15.3 0.1 collective-permute-start.8
  15.3 0.4 %collective-permute-start.9 = (f32[8,128]{1,0:T(8,128)S(1)}, f32[8,128]{1,0:T(8,128)S(1)}, u32[]{:S(2)}, u32[]{:S(2)}) collective-permute-start(f32[8,128]{1,0:T(8,128)S(1)} %collective-permute-done.2.refs_1_), channel_id=1, source_target_pairs={{1,0},{0,1},{3,2},{2,3},{5,4},{4,5},{7,6},{6,7},{9,8},{8,9},{11,10... | collective-permute-start | bytes 12296 | tf_op jit(solution)/shard_map/ppermute | solution.py:536
  15.8 0.0 collective-permute-done.refs_1_
  15.8 0.3 %collective-permute-done.4.refs_3_ = f32[272,128]{1,0:T(8,128)S(1)} collective-permute-done((f32[272,128]{1,0:T(8,128)S(1)}, f32[272,128]{1,0:T(8,128)S(1)}, u32[]{:S(2)}, u32[]{:S(2)}) %collective-permute-start.4) | collective-permute-done | bytes 139296 | tf_op jit(solution)/shard_map/ppermute | solution.py:536
  16.1 0.2 collective-permute-done.6.refs_5_
  16.3 0.3 %collective-permute-done.8.refs_7_ = f32[272,128]{1,0:T(8,128)S(1)} collective-permute-done((f32[272,128]{1,0:T(8,128)S(1)}, f32[272,128]{1,0:T(8,128)S(1)}, u32[]{:S(2)}, u32[]{:S(2)}) %collective-permute-start.8) | collective-permute-done | bytes 139296 | tf_op jit(solution)/shard_map/ppermute | solution.py:536
  16.6 7.8 %krylov.1 = (f32[6,16,16,1024]{3,2,1,0:T(8,128)S(1)}, f32[16,16,1024]{2,1,0:T(8,128)S(1)}, f32[13,16,128]{2,1,0:T(8,128)S(1)}) custom-call(f32[272,128]{1,0:T(8,128)S(1)} %get-tuple-element.10.refs_0_, f32[272,128]{1,0:T(8,128)S(1)} %collective-permute-done.refs_1_, f32[272,128]{1,0:T(8,128)S(1)} %collective-permute-done.1.refs_2_, ...), custom_call_target="tpu_custom_call" | custom-call | tf_op jit(solution)/shard_map/krylov/pallas_call | solution.py:557
  24.5 0.0 collective-permute-done.9.refs_3_
  24.5 4.3 %gram.1 = (f32[2,64,64]{2,1,0:T(8,128)}, f32[2,64,64]{2,1,0:T(8,128)}) custom-call(f32[13,16,128]{2,1,0:T(8,128)S(1)} %get-tuple-element.13.scalars, f32[8,128]{1,0:T(8,128)S(1)} %get-tuple-element.11.refs_0_, f32[8,128]{1,0:T(8,128)S(1)} %collective-permute-done.2.refs_1_, f32[8,128]{1,0:T(8,128)S(1)} %collective-permute-done.3.refs_2_, ...), custom_call_target="tpu_custom_call" | custom-call | tf_op jit(solution)/shard_map/gram/pallas_call | solution.py:579
Async XLA Ops:
  2.8 12.0 %collective-permute-start.1 = (f32[272,128]{1,0:T(8,128)S(1)}, f32[272,128]{1,0:T(8,128)S(1)}, u32[]{:S(2)}, u32[]{:S(2)}) collective-permute-start(f32[272,128]{1,0:T(8,128)S(1)} %get-tuple-element.10.refs_0_), channel_id=1, source_target_pairs={{2,0},{3,1},{0,2},{1,3},{6,4},{7,5},{4,6},{5,7},{10,8},{11,9},{8,1... | collective-permute-start | bytes 417800 | tf_op jit(solution)/shard_map/ppermute | solution.py:536
  5.8 9.0 %collective-permute-start.5 = (f32[272,128]{1,0:T(8,128)S(1)}, f32[272,128]{1,0:T(8,128)S(1)}, u32[]{:S(2)}, u32[]{:S(2)}) collective-permute-start(f32[272,128]{1,0:T(8,128)S(1)} %get-tuple-element.10.refs_0_), channel_id=1, source_target_pairs={{4,0},{5,1},{6,2},{7,3},{0,4},{1,5},{2,6},{3,7},{12,8},{13,9},{14,... | collective-permute-start | bytes 417800 | tf_op jit(solution)/shard_map/ppermute | solution.py:536
  7.3 8.0 %collective-permute-start.7 = (f32[272,128]{1,0:T(8,128)S(1)}, f32[272,128]{1,0:T(8,128)S(1)}, u32[]{:S(2)}, u32[]{:S(2)}) collective-permute-start(f32[272,128]{1,0:T(8,128)S(1)} %get-tuple-element.10.refs_0_), channel_id=1, source_target_pairs={{6,0},{7,1},{4,2},{5,3},{2,4},{3,5},{0,6},{1,7},{14,8},{15,9},{12,... | collective-permute-start | bytes 417800 | tf_op jit(solution)/shard_map/ppermute | solution.py:536
  7.3 4.5 %collective-permute-start.2 = (f32[8,128]{1,0:T(8,128)S(1)}, f32[8,128]{1,0:T(8,128)S(1)}, u32[]{:S(2)}, u32[]{:S(2)}) collective-permute-start(f32[8,128]{1,0:T(8,128)S(1)} %get-tuple-element.11.refs_0_), channel_id=1, source_target_pairs={{8,0},{17,1},{10,2},{19,3},{12,4},{21,5},{14,6},{23,7},{0,8},{25,9... | collective-permute-start | bytes 12296 | tf_op jit(solution)/shard_map/ppermute | solution.py:549
  9.4 5.4 %collective-permute-start.3 = (f32[8,128]{1,0:T(8,128)S(1)}, f32[8,128]{1,0:T(8,128)S(1)}, u32[]{:S(2)}, u32[]{:S(2)}) collective-permute-start(f32[8,128]{1,0:T(8,128)S(1)} %get-tuple-element.11.refs_0_), channel_id=1, source_target_pairs={{24,0},{16,8},{8,16},{0,24},{25,1},{17,9},{9,17},{1,25},{26,2},{18... | collective-permute-start | bytes 12296 | tf_op jit(solution)/shard_map/ppermute | solution.py:536
  11.8 4.0 %collective-permute-start = (f32[272,128]{1,0:T(8,128)S(1)}, f32[272,128]{1,0:T(8,128)S(1)}, u32[]{:S(2)}, u32[]{:S(2)}) collective-permute-start(f32[272,128]{1,0:T(8,128)S(1)} %get-tuple-element.10.refs_0_), channel_id=1, source_target_pairs={{1,0},{0,1},{3,2},{2,3},{5,4},{4,5},{7,6},{6,7},{9,8},{8,9},{11,10... | collective-permute-start | bytes 417800 | tf_op jit(solution)/shard_map/ppermute | solution.py:536
  14.8 1.4 %collective-permute-start.4 = (f32[272,128]{1,0:T(8,128)S(1)}, f32[272,128]{1,0:T(8,128)S(1)}, u32[]{:S(2)}, u32[]{:S(2)}) collective-permute-start(f32[272,128]{1,0:T(8,128)S(1)} %collective-permute-done.1.refs_2_), channel_id=1, source_target_pairs={{1,0},{0,1},{3,2},{2,3},{5,4},{4,5},{7,6},{6,7},{9,8},{8,9},{11,10... | collective-permute-start | bytes 417800 | tf_op jit(solution)/shard_map/ppermute | solution.py:536
  14.8 1.6 %collective-permute-start.6 = (f32[272,128]{1,0:T(8,128)S(1)}, f32[272,128]{1,0:T(8,128)S(1)}, u32[]{:S(2)}, u32[]{:S(2)}) collective-permute-start(f32[272,128]{1,0:T(8,128)S(1)} %collective-permute-done.5.refs_4_), channel_id=1, source_target_pairs={{1,0},{0,1},{3,2},{2,3},{5,4},{4,5},{7,6},{6,7},{9,8},{8,9},{11,10... | collective-permute-start | bytes 417800 | tf_op jit(solution)/shard_map/ppermute | solution.py:536
  15.3 1.4 %collective-permute-start.8 = (f32[272,128]{1,0:T(8,128)S(1)}, f32[272,128]{1,0:T(8,128)S(1)}, u32[]{:S(2)}, u32[]{:S(2)}) collective-permute-start(f32[272,128]{1,0:T(8,128)S(1)} %collective-permute-done.7.refs_6_), channel_id=1, source_target_pairs={{1,0},{0,1},{3,2},{2,3},{5,4},{4,5},{7,6},{6,7},{9,8},{8,9},{11,10... | collective-permute-start | bytes 417800 | tf_op jit(solution)/shard_map/ppermute | solution.py:536
  15.3 9.1 %collective-permute-start.9 = (f32[8,128]{1,0:T(8,128)S(1)}, f32[8,128]{1,0:T(8,128)S(1)}, u32[]{:S(2)}, u32[]{:S(2)}) collective-permute-start(f32[8,128]{1,0:T(8,128)S(1)} %collective-permute-done.2.refs_1_), channel_id=1, source_target_pairs={{1,0},{0,1},{3,2},{2,3},{5,4},{4,5},{7,6},{6,7},{9,8},{8,9},{11,10... | collective-permute-start | bytes 12296 | tf_op jit(solution)/shard_map/ppermute | solution.py:536

commit v21 on v20

--- a/solution.py
+++ b/solution.py
@@ -392,9 +392,14 @@
     )
 
 
+def split(values):
+    high = values.astype(jnp.bfloat16)
+    return high, (values - high.astype(jnp.float32)).astype(jnp.bfloat16)
+
+
 def krylov_kernel(parts, count, *refs):
-    blocks, (vectors, applied, scalars) = refs[:parts], refs[parts : parts + 3]
-    first_work, second_work, diagonal, sums, edges = refs[parts + 3 :]
+    blocks, (highs, lows, applied, scalars) = refs[:parts], refs[parts : parts + 4]
+    first_work, second_work, diagonal, sums, edges, partial = refs[parts + 4 :]
     planes = diagonal.shape[0]
     depth = planes // parts
     groups = count // SUB
@@ -410,7 +415,7 @@
                 lanes = slice(m * LANES, (m + 1) * LANES)
                 value = blocks[turn][start : start + count, :]
                 first_work[slab + deep, :, lanes] = value
-                vectors[0, slab + deep, :, lanes] = value
+                highs[0, slab + deep, :, lanes], lows[0, slab + deep, :, lanes] = split(value)
             start = depth * ROWS * count + deep * ROWS
             levels = H_SCALE * (blocks[turn][start : start + ROWS, :] + 3.75)
             for m in range(ROWS):
@@ -432,9 +437,37 @@
             values = plane_rows(first_work, plane, rows)
             keep_y_parts(plane, rows, values)
             norm.append(tree_sum([value * value for value in values]))
-        scalars[ITERS + 1, rows, :] = lane_sum(tree_sum(norm))
-
-    def half_turn(i, work, before):
+        partial[rows, :] = tree_sum(norm)
+
+    def update_pass(i, work, before, alphas, betas):
+        norm = [[] for _ in range(groups)]
+        for plane in range(planes):
+            columns = []
+            for group, rows in enumerate(all_rows):
+                values = []
+                for lanes in all_lanes:
+                    value = applied[plane, rows, lanes] - betas[group] * before[plane, rows, lanes]
+                    value = value - alphas[group] * work[plane, rows, lanes]
+                    before[plane, rows, lanes] = value
+                    values.append(value)
+                keep_y_parts(plane, rows, values)
+                norm[group].append(tree_sum([value * value for value in values]))
+                columns.append(values)
+            for lanes, *column in zip(all_lanes, *columns):
+                high, low = split(jnp.concatenate(column, axis=0))
+                highs[i + 1, plane, :, lanes] = high
+                lows[i + 1, plane, :, lanes] = low
+        for rows, terms in zip(all_rows, norm):
+            partial[rows, :] = tree_sum(terms)
+
+    def half_turn(i, work, before, may_end):
+        norms = [lane_sum(partial[rows, :]) for rows in all_rows]
+        betas = [
+            ratio(norm, scalars[ITERS + i, rows, :]) for norm, rows in zip(norms, all_rows)
+        ]
+        inverses = [ratio(jnp.ones_like(norm), norm) for norm in norms]
+        for norm, rows in zip(norms, all_rows):
+            scalars[ITERS + 1 + i, rows, :] = norm
         curve = [[] for _ in range(groups)]
         for plane in range(planes):
             for group, rows in enumerate(all_rows):
@@ -442,36 +475,17 @@
                 for m, lanes in enumerate(all_lanes):
                     applied[plane, rows, lanes] = out[m]
                 curve[group].append(tree_sum([value[m] * out[m] for m in range(ROWS)]))
-        curves = [lane_sum(tree_sum(parts_of)) for parts_of in curve]
-        alphas = []
-        for group, rows in enumerate(all_rows):
-            alphas.append(ratio(curves[group], scalars[ITERS + 1 + i, rows, :]))
-            scalars[i, rows, :] = alphas[group]
-
-        @pl.when(i < ITERS - 1)
-        def _():
-            norms = []
-            for group, rows in enumerate(all_rows):
-                beta = ratio(scalars[ITERS + 1 + i, rows, :], scalars[ITERS + i, rows, :])
-                norm = []
-                for plane in range(planes):
-                    values = []
-                    for lanes in all_lanes:
-                        value = applied[plane, rows, lanes]
-                        value = value - alphas[group] * work[plane, rows, lanes]
-                        value = value - beta * before[plane, rows, lanes]
-                        before[plane, rows, lanes] = value
-                        vectors[i + 1, plane, rows, lanes] = value
-                        values.append(value)
-                    keep_y_parts(plane, rows, values)
-                    norm.append(tree_sum([value * value for value in values]))
-                norms.append(lane_sum(tree_sum(norm)))
-            for group, rows in enumerate(all_rows):
-                scalars[ITERS + 2 + i, rows, :] = norms[group]
+        alphas = [lane_sum(tree_sum(curve[g])) * inverses[g] for g in range(groups)]
+        for alpha, rows in zip(alphas, all_rows):
+            scalars[i, rows, :] = alpha
+        if may_end:
+            pl.when(i < ITERS - 1)(lambda: update_pass(i, work, before, alphas, betas))
+        else:
+            update_pass(i, work, before, alphas, betas)
 
     def turn(step, carry):
-        half_turn(2 * step, first_work, second_work)
-        half_turn(2 * step + 1, second_work, first_work)
+        half_turn(2 * step, first_work, second_work, False)
+        half_turn(2 * step + 1, second_work, first_work, True)
         return carry
 
     lax.fori_loop(0, ITERS // 2, turn, 0)
@@ -479,7 +493,7 @@
 
 def gram_kernel(points, scalars, *refs):
     tiles = refs[:points]
-    archive, applied, out_b, out_a, gram, limits, weights = refs[points:]
+    highs, lows, applied, out_b, out_a, gram, limits, weights = refs[points:]
     planes, count, _ = applied.shape
     groups = count // SUB
     size = BASIS * count
@@ -497,10 +511,9 @@
         total = None
         for deep in range(planes // points):
             plane = point * (planes // points) + deep
-            values = [archive[i, plane] for i in range(ITERS)] + [applied[plane]]
-            values = jnp.concatenate(values, axis=0)
-            high = values.astype(jnp.bfloat16)
-            low = (values - high.astype(jnp.float32)).astype(jnp.bfloat16)
+            last_high, last_low = split(applied[plane])
+            high = jnp.concatenate([highs[i, plane] for i in range(ITERS)] + [last_high], axis=0)
+            low = jnp.concatenate([lows[i, plane] for i in range(ITERS)] + [last_low], axis=0)
             product = lax.dot_general(
                 jnp.concatenate([high, low], axis=0),
                 high,
@@ -554,21 +567,23 @@
     vmem = pl.BlockSpec(memory_space=pltpu.VMEM)
     vector = (planes, count, ROWS * LANES)
     cells = planes * ROWS * LANES
-    vectors, applied, scalars = pl.pallas_call(
+    highs, lows, applied, scalars = pl.pallas_call(
         functools.partial(krylov_kernel, parts, count),
         out_shape=(
-            jax.ShapeDtypeStruct((ITERS,) + vector, jnp.float32),
+            jax.ShapeDtypeStruct((ITERS,) + vector, jnp.bfloat16),
+            jax.ShapeDtypeStruct((ITERS,) + vector, jnp.bfloat16),
             jax.ShapeDtypeStruct(vector, jnp.float32),
             jax.ShapeDtypeStruct((2 * ITERS + 1, count, LANES), jnp.float32),
         ),
         in_specs=[vmem] * parts,
-        out_specs=(vmem,) * 3,
+        out_specs=(vmem,) * 4,
         scratch_shapes=[
             pltpu.VMEM(vector, jnp.float32),
             pltpu.VMEM(vector, jnp.float32),
             pltpu.VMEM((planes, SUB, ROWS * LANES), jnp.float32),
             pltpu.VMEM(vector, jnp.float32),
             pltpu.VMEM(vector, jnp.float32),
+            pltpu.VMEM((count, LANES), jnp.float32),
         ],
         compiler_params=pltpu.CompilerParams(vmem_limit_bytes=16 * 2**20),
         name="krylov",
@@ -579,7 +594,7 @@
     return pl.pallas_call(
         functools.partial(gram_kernel, points),
         out_shape=(out, out),
-        in_specs=[vmem] * (3 + points),
+        in_specs=[vmem] * (4 + points),
         out_specs=(vmem, vmem),
         scratch_shapes=[
             pltpu.VMEM((2 * size, size), jnp.float32),
@@ -588,7 +603,7 @@
         ],
         compiler_params=pltpu.CompilerParams(vmem_limit_bytes=16 * 2**20),
         name="gram",
-    )(scalars, tile, *tiles, vectors, applied)
+    )(scalars, tile, *tiles, highs, lows, applied)
 
 
 def on_device(sources, potential, iter_counts):

time: 29 us -> 28.9 us (level)
  transfers between devices with their start and end apart: 10 -> 10, of which waited for: 4 -> 4; matrix products, arithmetic and copies ran while one was open for 0% -> 0% of each run, Pallas kernels for 27% -> 28%
where the time goes in v21:
time: 28.9 us; the launch traced here: 28.7 us
  Pallas kernels  12.6 us (44%)
  starting transfers between devices  10.1 us (35%)
  waiting for transfers between devices  3.78 us (13%)
  between operations  1.3 us (4%)
  other arithmetic  0.93 us (3%)
    ppermute x9, starting transfers between devices, swapped(): lax.ppermute(values, axis, [(index ^ mask, index) for index in range(size)])  8.04 us
    pallas_call x1, Pallas kernels, whole_grid(): pl.pallas_call(functools.partial(krylov_kernel, parts, count), out_shape=...  7.95 us
    pallas_call x1, Pallas kernels, whole_grid(): pl.pallas_call(functools.partial(gram_kernel, points), out_shape=(out, ou...  4.09 us
    ppermute x9, waiting for transfers between devices, swapped(): lax.ppermute(values, axis, [(index ^ mask, index) for index in range(size)])  3.78 us
    ppermute x1, starting transfers between devices, whole_grid(): lax.ppermute(tile, ('point', 'dom'), mixed)  2.03 us
    concatenate x1, other arithmetic, packed_block(): jnp.concatenate([rows, levels], axis=0)  0.93 us
  transfers between devices with their start and end apart: 10, of which 4 were waited for; matrix products, arithmetic and copies ran while one was open for 0% of the time, Pallas kernels for 28%

profile of v21, /device:TPU:0, one launch (start us, length us, event | category | flops | bytes accessed | tf_op | source)
XLA Modules:
  0.0 28.7 jit_solution(4420256209349820623)
XLA Ops:
  1.3 0.9 %pad_maximum_fusion.rows = f32[272,128]{1,0:T(8,128)S(1)} fusion(f32[16,128]{1,0:T(8,128)} %bitcast.13, f32[256,128]{1,0:T(8,128)} %bitcast.12), kind=kLoop, calls=%fused_computation | loop fusion | flops 34816 | bytes 278528 | tf_op jit(solution)/shard_map/concatenate | solution.py:234
  2.2 0.6 %pack.1 = (f32[272,128]{1,0:T(8,128)S(1)}, f32[8,128]{1,0:T(8,128)S(1)}) custom-call(s32[1,1]{1,0:T(1,128)} %bitcast.11.counts, f32[272,128]{1,0:T(8,128)S(1)} %pad_maximum_fusion.rows), custom_call_target="tpu_custom_call" | custom-call | tf_op jit(solution)/shard_map/pack/pallas_call | solution.py:224
  2.8 3.0 %collective-permute-start.1 = (f32[272,128]{1,0:T(8,128)S(1)}, f32[272,128]{1,0:T(8,128)S(1)}, u32[]{:S(2)}, u32[]{:S(2)}) collective-permute-start(f32[272,128]{1,0:T(8,128)S(1)} %get-tuple-element.11.refs_0_), channel_id=1, source_target_pairs={{2,0},{3,1},{0,2},{1,3},{6,4},{7,5},{4,6},{5,7},{10,8},{11,9},{8,1... | collective-permute-start | bytes 417800 | tf_op jit(solution)/shard_map/ppermute | solution.py:549
  5.8 1.5 %collective-permute-start.5 = (f32[272,128]{1,0:T(8,128)S(1)}, f32[272,128]{1,0:T(8,128)S(1)}, u32[]{:S(2)}, u32[]{:S(2)}) collective-permute-start(f32[272,128]{1,0:T(8,128)S(1)} %get-tuple-element.11.refs_0_), channel_id=1, source_target_pairs={{4,0},{5,1},{6,2},{7,3},{0,4},{1,5},{2,6},{3,7},{12,8},{13,9},{14,... | collective-permute-start | bytes 417800 | tf_op jit(solution)/shard_map/ppermute | solution.py:549
  7.3 0.0 collective-permute-start.7
  7.3 2.0 %collective-permute-start.2 = (f32[8,128]{1,0:T(8,128)S(1)}, f32[8,128]{1,0:T(8,128)S(1)}, u32[]{:S(2)}, u32[]{:S(2)}) collective-permute-start(f32[8,128]{1,0:T(8,128)S(1)} %get-tuple-element.12.refs_0_), channel_id=1, source_target_pairs={{8,0},{17,1},{10,2},{19,3},{12,4},{21,5},{14,6},{23,7},{0,8},{25,9... | collective-permute-start | bytes 12296 | tf_op jit(solution)/shard_map/ppermute | solution.py:562
  9.4 2.5 %collective-permute-start.3 = (f32[8,128]{1,0:T(8,128)S(1)}, f32[8,128]{1,0:T(8,128)S(1)}, u32[]{:S(2)}, u32[]{:S(2)}) collective-permute-start(f32[8,128]{1,0:T(8,128)S(1)} %get-tuple-element.12.refs_0_), channel_id=1, source_target_pairs={{24,0},{16,8},{8,16},{0,24},{25,1},{17,9},{9,17},{1,25},{26,2},{18... | collective-permute-start | bytes 12296 | tf_op jit(solution)/shard_map/ppermute | solution.py:549
  11.8 0.0 collective-permute-done.2.refs_1_
  11.8 0.0 collective-permute-start
  11.8 2.9 %collective-permute-done.3.refs_2_ = f32[8,128]{1,0:T(8,128)S(1)} collective-permute-done((f32[8,128]{1,0:T(8,128)S(1)}, f32[8,128]{1,0:T(8,128)S(1)}, u32[]{:S(2)}, u32[]{:S(2)}) %collective-permute-start.3) | collective-permute-done | bytes 4128 | tf_op jit(solution)/shard_map/ppermute | solution.py:549
  14.8 0.0 collective-permute-done.1.refs_2_
  14.8 0.0 collective-permute-start.4
  14.8 0.0 collective-permute-done.5.refs_4_
  14.8 0.5 %collective-permute-start.6 = (f32[272,128]{1,0:T(8,128)S(1)}, f32[272,128]{1,0:T(8,128)S(1)}, u32[]{:S(2)}, u32[]{:S(2)}) collective-permute-start(f32[272,128]{1,0:T(8,128)S(1)} %collective-permute-done.5.refs_4_), channel_id=1, source_target_pairs={{1,0},{0,1},{3,2},{2,3},{5,4},{4,5},{7,6},{6,7},{9,8},{8,9},{11,10... | collective-permute-start | bytes 417800 | tf_op jit(solution)/shard_map/ppermute | solution.py:549
  15.3 0.0 collective-permute-done.7.refs_6_
  15.3 0.1 collective-permute-start.8
  15.3 0.4 %collective-permute-start.9 = (f32[8,128]{1,0:T(8,128)S(1)}, f32[8,128]{1,0:T(8,128)S(1)}, u32[]{:S(2)}, u32[]{:S(2)}) collective-permute-start(f32[8,128]{1,0:T(8,128)S(1)} %collective-permute-done.2.refs_1_), channel_id=1, source_target_pairs={{1,0},{0,1},{3,2},{2,3},{5,4},{4,5},{7,6},{6,7},{9,8},{8,9},{11,10... | collective-permute-start | bytes 12296 | tf_op jit(solution)/shard_map/ppermute | solution.py:549
  15.8 0.0 collective-permute-done.refs_1_
  15.8 0.3 %collective-permute-done.4.refs_3_ = f32[272,128]{1,0:T(8,128)S(1)} collective-permute-done((f32[272,128]{1,0:T(8,128)S(1)}, f32[272,128]{1,0:T(8,128)S(1)}, u32[]{:S(2)}, u32[]{:S(2)}) %collective-permute-start.4) | collective-permute-done | bytes 139296 | tf_op jit(solution)/shard_map/ppermute | solution.py:549
  16.1 0.2 collective-permute-done.6.refs_5_
  16.3 0.3 %collective-permute-done.8.refs_7_ = f32[272,128]{1,0:T(8,128)S(1)} collective-permute-done((f32[272,128]{1,0:T(8,128)S(1)}, f32[272,128]{1,0:T(8,128)S(1)}, u32[]{:S(2)}, u32[]{:S(2)}) %collective-permute-start.8) | collective-permute-done | bytes 139296 | tf_op jit(solution)/shard_map/ppermute | solution.py:549
  16.6 7.9 %krylov.1 = (bf16[6,16,16,1024]{3,2,1,0:T(8,128)(2,1)S(1)}, bf16[6,16,16,1024]{3,2,1,0:T(8,128)(2,1)S(1)}, f32[16,16,1024]{2,1,0:T(8,128)S(1)}, f32[13,16,128]{2,1,0:T(8,128)S(1)}) custom-call(f32[272,128]{1,0:T(8,128)S(1)} %get-tuple-element.11.refs_0_, f32[272,128]{1,0:T(8,128)S(1)} %collective-permute-done.refs_1_, ...), custom_call_target="tpu_custom_call" | custom-call | tf_op jit(solution)/shard_map/krylov/pallas_call | solution.py:570
  24.6 0.0 collective-permute-done.9.refs_3_
  24.6 4.1 %gram.1 = (f32[2,64,64]{2,1,0:T(8,128)}, f32[2,64,64]{2,1,0:T(8,128)}) custom-call(f32[13,16,128]{2,1,0:T(8,128)S(1)} %get-tuple-element.14.scalars, f32[8,128]{1,0:T(8,128)S(1)} %get-tuple-element.12.refs_0_, f32[8,128]{1,0:T(8,128)S(1)} %collective-permute-done.2.refs_1_, f32[8,128]{1,0:T(8,128)S(1)} %collective-permute-done.3.refs_2_, ...), custom_call_target="tpu_custom_call" | custom-call | tf_op jit(solution)/shard_map/gram/pallas_call | solution.py:594
Async XLA Ops:
  2.8 12.0 %collective-permute-start.1 = (f32[272,128]{1,0:T(8,128)S(1)}, f32[272,128]{1,0:T(8,128)S(1)}, u32[]{:S(2)}, u32[]{:S(2)}) collective-permute-start(f32[272,128]{1,0:T(8,128)S(1)} %get-tuple-element.11.refs_0_), channel_id=1, source_target_pairs={{2,0},{3,1},{0,2},{1,3},{6,4},{7,5},{4,6},{5,7},{10,8},{11,9},{8,1... | collective-permute-start | bytes 417800 | tf_op jit(solution)/shard_map/ppermute | solution.py:549
  5.8 9.0 %collective-permute-start.5 = (f32[272,128]{1,0:T(8,128)S(1)}, f32[272,128]{1,0:T(8,128)S(1)}, u32[]{:S(2)}, u32[]{:S(2)}) collective-permute-start(f32[272,128]{1,0:T(8,128)S(1)} %get-tuple-element.11.refs_0_), channel_id=1, source_target_pairs={{4,0},{5,1},{6,2},{7,3},{0,4},{1,5},{2,6},{3,7},{12,8},{13,9},{14,... | collective-permute-start | bytes 417800 | tf_op jit(solution)/shard_map/ppermute | solution.py:549
  7.3 8.0 %collective-permute-start.7 = (f32[272,128]{1,0:T(8,128)S(1)}, f32[272,128]{1,0:T(8,128)S(1)}, u32[]{:S(2)}, u32[]{:S(2)}) collective-permute-start(f32[272,128]{1,0:T(8,128)S(1)} %get-tuple-element.11.refs_0_), channel_id=1, source_target_pairs={{6,0},{7,1},{4,2},{5,3},{2,4},{3,5},{0,6},{1,7},{14,8},{15,9},{12,... | collective-permute-start | bytes 417800 | tf_op jit(solution)/shard_map/ppermute | solution.py:549
  7.3 4.5 %collective-permute-start.2 = (f32[8,128]{1,0:T(8,128)S(1)}, f32[8,128]{1,0:T(8,128)S(1)}, u32[]{:S(2)}, u32[]{:S(2)}) collective-permute-start(f32[8,128]{1,0:T(8,128)S(1)} %get-tuple-element.12.refs_0_), channel_id=1, source_target_pairs={{8,0},{17,1},{10,2},{19,3},{12,4},{21,5},{14,6},{23,7},{0,8},{25,9... | collective-permute-start | bytes 12296 | tf_op jit(solution)/shard_map/ppermute | solution.py:562
  9.4 5.4 %collective-permute-start.3 = (f32[8,128]{1,0:T(8,128)S(1)}, f32[8,128]{1,0:T(8,128)S(1)}, u32[]{:S(2)}, u32[]{:S(2)}) collective-permute-start(f32[8,128]{1,0:T(8,128)S(1)} %get-tuple-element.12.refs_0_), channel_id=1, source_target_pairs={{24,0},{16,8},{8,16},{0,24},{25,1},{17,9},{9,17},{1,25},{26,2},{18... | collective-permute-start | bytes 12296 | tf_op jit(solution)/shard_map/ppermute | solution.py:549
  11.8 4.0 %collective-permute-start = (f32[272,128]{1,0:T(8,128)S(1)}, f32[272,128]{1,0:T(8,128)S(1)}, u32[]{:S(2)}, u32[]{:S(2)}) collective-permute-start(f32[272,128]{1,0:T(8,128)S(1)} %get-tuple-element.11.refs_0_), channel_id=1, source_target_pairs={{1,0},{0,1},{3,2},{2,3},{5,4},{4,5},{7,6},{6,7},{9,8},{8,9},{11,10... | collective-permute-start | bytes 417800 | tf_op jit(solution)/shard_map/ppermute | solution.py:549
  14.8 1.4 %collective-permute-start.4 = (f32[272,128]{1,0:T(8,128)S(1)}, f32[272,128]{1,0:T(8,128)S(1)}, u32[]{:S(2)}, u32[]{:S(2)}) collective-permute-start(f32[272,128]{1,0:T(8,128)S(1)} %collective-permute-done.1.refs_2_), channel_id=1, source_target_pairs={{1,0},{0,1},{3,2},{2,3},{5,4},{4,5},{7,6},{6,7},{9,8},{8,9},{11,10... | collective-permute-start | bytes 417800 | tf_op jit(solution)/shard_map/ppermute | solution.py:549
  14.8 1.6 %collective-permute-start.6 = (f32[272,128]{1,0:T(8,128)S(1)}, f32[272,128]{1,0:T(8,128)S(1)}, u32[]{:S(2)}, u32[]{:S(2)}) collective-permute-start(f32[272,128]{1,0:T(8,128)S(1)} %collective-permute-done.5.refs_4_), channel_id=1, source_target_pairs={{1,0},{0,1},{3,2},{2,3},{5,4},{4,5},{7,6},{6,7},{9,8},{8,9},{11,10... | collective-permute-start | bytes 417800 | tf_op jit(solution)/shard_map/ppermute | solution.py:549
  15.3 1.4 %collective-permute-start.8 = (f32[272,128]{1,0:T(8,128)S(1)}, f32[272,128]{1,0:T(8,128)S(1)}, u32[]{:S(2)}, u32[]{:S(2)}) collective-permute-start(f32[272,128]{1,0:T(8,128)S(1)} %collective-permute-done.7.refs_6_), channel_id=1, source_target_pairs={{1,0},{0,1},{3,2},{2,3},{5,4},{4,5},{7,6},{6,7},{9,8},{8,9},{11,10... | collective-permute-start | bytes 417800 | tf_op jit(solution)/shard_map/ppermute | solution.py:549
  15.3 9.2 %collective-permute-start.9 = (f32[8,128]{1,0:T(8,128)S(1)}, f32[8,128]{1,0:T(8,128)S(1)}, u32[]{:S(2)}, u32[]{:S(2)}) collective-permute-start(f32[8,128]{1,0:T(8,128)S(1)} %collective-permute-done.2.refs_1_), channel_id=1, source_target_pairs={{1,0},{0,1},{3,2},{2,3},{5,4},{4,5},{7,6},{6,7},{9,8},{8,9},{11,10... | collective-permute-start | bytes 12296 | tf_op jit(solution)/shard_map/ppermute | solution.py:549

commit v22 on v21

--- a/solution.py
+++ b/solution.py
@@ -397,6 +397,17 @@
     return high, (values - high.astype(jnp.float32)).astype(jnp.bfloat16)
 
 
+def split_dot(first, second):
+    high, low = split(first)
+    high_2, low_2 = split(second)
+    return lax.dot_general(
+        jnp.concatenate([high, high, low], axis=1),
+        jnp.concatenate([high_2, low_2, high_2], axis=0),
+        (((1,), (0,)), ((), ())),
+        preferred_element_type=jnp.float32,
+    )
+
+
 def krylov_kernel(parts, count, *refs):
     blocks, (highs, lows, applied, scalars) = refs[:parts], refs[parts : parts + 4]
     first_work, second_work, diagonal, sums, edges, partial = refs[parts + 4 :]
@@ -496,7 +507,7 @@
     highs, lows, applied, out_b, out_a, gram, limits, weights = refs[points:]
     planes, count, _ = applied.shape
     groups = count // SUB
-    size = BASIS * count
+    size = gram.shape[1]
     here = lax.axis_index("point")
     core = jnp.bitwise_and(lax.axis_index("dom"), CORES - 1)
     for far, tile in zip((0, 1 + core, 3, 2 - core), tiles):
@@ -512,8 +523,11 @@
         for deep in range(planes // points):
             plane = point * (planes // points) + deep
             last_high, last_low = split(applied[plane])
-            high = jnp.concatenate([highs[i, plane] for i in range(ITERS)] + [last_high], axis=0)
-            low = jnp.concatenate([lows[i, plane] for i in range(ITERS)] + [last_low], axis=0)
+            pad = [jnp.zeros((size - BASIS * count, ROWS * LANES), jnp.bfloat16)]
+            high = [highs[i, plane] for i in range(ITERS)] + [last_high]
+            high = jnp.concatenate(high + pad, axis=0)
+            low = [lows[i, plane] for i in range(ITERS)] + [last_low]
+            low = jnp.concatenate(low + pad, axis=0)
             product = lax.dot_general(
                 jnp.concatenate([high, low], axis=0),
                 high,
@@ -530,11 +544,11 @@
     lax.fori_loop(0, points, turn, 0)
     cross = gram[size:, :]
     pairs = gram[:size, :] + cross + cross.T
-    right = exact_dot(pairs, weights[...], ((1,), (0,)))
+    right = split_dot(pairs, weights[...])
     real, imag = weights[:, :LANES], weights[:, LANES:]
     half = MOMENTS * count
     left = jnp.concatenate([real[:, :half], imag[:, :half]], axis=1)
-    joined = exact_dot(left.T, right, ((1,), (0,)))
+    joined = split_dot(left.T, right)
     scale = 1.0 / (planes * ROWS * LANES)
     width = 2 * half
     real = (joined[:half, :width] + joined[half:, width:]) * scale
@@ -588,7 +602,7 @@
         compiler_params=pltpu.CompilerParams(vmem_limit_bytes=16 * 2**20),
         name="krylov",
     )(*blocks)
-    size = BASIS * count
+    size = -(-BASIS * count // LANES) * LANES
     width = MOMENTS * count
     out = jax.ShapeDtypeStruct((2, width, width), jnp.float32)
     return pl.pallas_call(

time: 28.9 us -> 28.9 us (level)
  no operation moved by 1% of the time
where the time goes in v22:
time: 28.9 us; the launch traced here: 28.7 us
  Pallas kernels  12.6 us (44%)
  starting transfers between devices  10.1 us (35%)
  waiting for transfers between devices  3.78 us (13%)
  between operations  1.3 us (4%)
  other arithmetic  0.93 us (3%)
    ppermute x9, starting transfers between devices, swapped(): lax.ppermute(values, axis, [(index ^ mask, index) for index in range(size)])  8.04 us
    pallas_call x1, Pallas kernels, whole_grid(): pl.pallas_call(functools.partial(krylov_kernel, parts, count), out_shape=...  7.95 us
    pallas_call x1, Pallas kernels, whole_grid(): pl.pallas_call(functools.partial(gram_kernel, points), out_shape=(out, ou...  4.12 us
    ppermute x9, waiting for transfers between devices, swapped(): lax.ppermute(values, axis, [(index ^ mask, index) for index in range(size)])  3.78 us
    ppermute x1, starting transfers between devices, whole_grid(): lax.ppermute(tile, ('point', 'dom'), mixed)  2.03 us
    concatenate x1, other arithmetic, packed_block(): jnp.concatenate([rows, levels], axis=0)  0.93 us
  transfers between devices with their start and end apart: 10, of which 4 were waited for; matrix products, arithmetic and copies ran while one was open for 0% of the time, Pallas kernels for 28%

profile of v22, /device:TPU:0, one launch (start us, length us, event | category | flops | bytes accessed | tf_op | source)
XLA Modules:
  0.0 28.7 jit_solution(2476723622633833558)
XLA Ops:
  1.3 0.9 %pad_maximum_fusion.rows = f32[272,128]{1,0:T(8,128)S(1)} fusion(f32[16,128]{1,0:T(8,128)} %bitcast.13, f32[256,128]{1,0:T(8,128)} %bitcast.12), kind=kLoop, calls=%fused_computation | loop fusion | flops 34816 | bytes 278528 | tf_op jit(solution)/shard_map/concatenate | solution.py:234
  2.2 0.6 %pack.1 = (f32[272,128]{1,0:T(8,128)S(1)}, f32[8,128]{1,0:T(8,128)S(1)}) custom-call(s32[1,1]{1,0:T(1,128)} %bitcast.11.counts, f32[272,128]{1,0:T(8,128)S(1)} %pad_maximum_fusion.rows), custom_call_target="tpu_custom_call" | custom-call | tf_op jit(solution)/shard_map/pack/pallas_call | solution.py:224
  2.8 3.0 %collective-permute-start.1 = (f32[272,128]{1,0:T(8,128)S(1)}, f32[272,128]{1,0:T(8,128)S(1)}, u32[]{:S(2)}, u32[]{:S(2)}) collective-permute-start(f32[272,128]{1,0:T(8,128)S(1)} %get-tuple-element.11.refs_0_), channel_id=1, source_target_pairs={{2,0},{3,1},{0,2},{1,3},{6,4},{7,5},{4,6},{5,7},{10,8},{11,9},{8,1... | collective-permute-start | bytes 417800 | tf_op jit(solution)/shard_map/ppermute | solution.py:563
  5.8 1.5 %collective-permute-start.5 = (f32[272,128]{1,0:T(8,128)S(1)}, f32[272,128]{1,0:T(8,128)S(1)}, u32[]{:S(2)}, u32[]{:S(2)}) collective-permute-start(f32[272,128]{1,0:T(8,128)S(1)} %get-tuple-element.11.refs_0_), channel_id=1, source_target_pairs={{4,0},{5,1},{6,2},{7,3},{0,4},{1,5},{2,6},{3,7},{12,8},{13,9},{14,... | collective-permute-start | bytes 417800 | tf_op jit(solution)/shard_map/ppermute | solution.py:563
  7.3 0.0 collective-permute-start.7
  7.3 2.0 %collective-permute-start.2 = (f32[8,128]{1,0:T(8,128)S(1)}, f32[8,128]{1,0:T(8,128)S(1)}, u32[]{:S(2)}, u32[]{:S(2)}) collective-permute-start(f32[8,128]{1,0:T(8,128)S(1)} %get-tuple-element.12.refs_0_), channel_id=1, source_target_pairs={{8,0},{17,1},{10,2},{19,3},{12,4},{21,5},{14,6},{23,7},{0,8},{25,9... | collective-permute-start | bytes 12296 | tf_op jit(solution)/shard_map/ppermute | solution.py:576
  9.4 2.5 %collective-permute-start.3 = (f32[8,128]{1,0:T(8,128)S(1)}, f32[8,128]{1,0:T(8,128)S(1)}, u32[]{:S(2)}, u32[]{:S(2)}) collective-permute-start(f32[8,128]{1,0:T(8,128)S(1)} %get-tuple-element.12.refs_0_), channel_id=1, source_target_pairs={{24,0},{16,8},{8,16},{0,24},{25,1},{17,9},{9,17},{1,25},{26,2},{18... | collective-permute-start | bytes 12296 | tf_op jit(solution)/shard_map/ppermute | solution.py:563
  11.8 0.0 collective-permute-done.2.refs_1_
  11.8 0.0 collective-permute-start
  11.8 2.9 %collective-permute-done.3.refs_2_ = f32[8,128]{1,0:T(8,128)S(1)} collective-permute-done((f32[8,128]{1,0:T(8,128)S(1)}, f32[8,128]{1,0:T(8,128)S(1)}, u32[]{:S(2)}, u32[]{:S(2)}) %collective-permute-start.3) | collective-permute-done | bytes 4128 | tf_op jit(solution)/shard_map/ppermute | solution.py:563
  14.8 0.0 collective-permute-done.1.refs_2_
  14.8 0.0 collective-permute-start.4
  14.8 0.0 collective-permute-done.5.refs_4_
  14.8 0.5 %collective-permute-start.6 = (f32[272,128]{1,0:T(8,128)S(1)}, f32[272,128]{1,0:T(8,128)S(1)}, u32[]{:S(2)}, u32[]{:S(2)}) collective-permute-start(f32[272,128]{1,0:T(8,128)S(1)} %collective-permute-done.5.refs_4_), channel_id=1, source_target_pairs={{1,0},{0,1},{3,2},{2,3},{5,4},{4,5},{7,6},{6,7},{9,8},{8,9},{11,10... | collective-permute-start | bytes 417800 | tf_op jit(solution)/shard_map/ppermute | solution.py:563
  15.3 0.0 collective-permute-done.7.refs_6_
  15.3 0.1 collective-permute-start.8
  15.3 0.4 %collective-permute-start.9 = (f32[8,128]{1,0:T(8,128)S(1)}, f32[8,128]{1,0:T(8,128)S(1)}, u32[]{:S(2)}, u32[]{:S(2)}) collective-permute-start(f32[8,128]{1,0:T(8,128)S(1)} %collective-permute-done.2.refs_1_), channel_id=1, source_target_pairs={{1,0},{0,1},{3,2},{2,3},{5,4},{4,5},{7,6},{6,7},{9,8},{8,9},{11,10... | collective-permute-start | bytes 12296 | tf_op jit(solution)/shard_map/ppermute | solution.py:563
  15.8 0.0 collective-permute-done.refs_1_
  15.8 0.3 %collective-permute-done.4.refs_3_ = f32[272,128]{1,0:T(8,128)S(1)} collective-permute-done((f32[272,128]{1,0:T(8,128)S(1)}, f32[272,128]{1,0:T(8,128)S(1)}, u32[]{:S(2)}, u32[]{:S(2)}) %collective-permute-start.4) | collective-permute-done | bytes 139296 | tf_op jit(solution)/shard_map/ppermute | solution.py:563
  16.1 0.2 collective-permute-done.6.refs_5_
  16.3 0.3 %collective-permute-done.8.refs_7_ = f32[272,128]{1,0:T(8,128)S(1)} collective-permute-done((f32[272,128]{1,0:T(8,128)S(1)}, f32[272,128]{1,0:T(8,128)S(1)}, u32[]{:S(2)}, u32[]{:S(2)}) %collective-permute-start.8) | collective-permute-done | bytes 139296 | tf_op jit(solution)/shard_map/ppermute | solution.py:563
  16.6 7.9 %krylov.1 = (bf16[6,16,16,1024]{3,2,1,0:T(8,128)(2,1)S(1)}, bf16[6,16,16,1024]{3,2,1,0:T(8,128)(2,1)S(1)}, f32[16,16,1024]{2,1,0:T(8,128)S(1)}, f32[13,16,128]{2,1,0:T(8,128)S(1)}) custom-call(f32[272,128]{1,0:T(8,128)S(1)} %get-tuple-element.11.refs_0_, f32[272,128]{1,0:T(8,128)S(1)} %collective-permute-done.refs_1_, ...), custom_call_target="tpu_custom_call" | custom-call | tf_op jit(solution)/shard_map/krylov/pallas_call | solution.py:584
  24.6 0.0 collective-permute-done.9.refs_3_
  24.6 4.1 %gram.1 = (f32[2,64,64]{2,1,0:T(8,128)}, f32[2,64,64]{2,1,0:T(8,128)}) custom-call(f32[13,16,128]{2,1,0:T(8,128)S(1)} %get-tuple-element.14.scalars, f32[8,128]{1,0:T(8,128)S(1)} %get-tuple-element.12.refs_0_, f32[8,128]{1,0:T(8,128)S(1)} %collective-permute-done.2.refs_1_, f32[8,128]{1,0:T(8,128)S(1)} %collective-permute-done.3.refs_2_, ...), custom_call_target="tpu_custom_call" | custom-call | tf_op jit(solution)/shard_map/gram/pallas_call | solution.py:608
Async XLA Ops:
  2.8 12.0 %collective-permute-start.1 = (f32[272,128]{1,0:T(8,128)S(1)}, f32[272,128]{1,0:T(8,128)S(1)}, u32[]{:S(2)}, u32[]{:S(2)}) collective-permute-start(f32[272,128]{1,0:T(8,128)S(1)} %get-tuple-element.11.refs_0_), channel_id=1, source_target_pairs={{2,0},{3,1},{0,2},{1,3},{6,4},{7,5},{4,6},{5,7},{10,8},{11,9},{8,1... | collective-permute-start | bytes 417800 | tf_op jit(solution)/shard_map/ppermute | solution.py:563
  5.8 9.0 %collective-permute-start.5 = (f32[272,128]{1,0:T(8,128)S(1)}, f32[272,128]{1,0:T(8,128)S(1)}, u32[]{:S(2)}, u32[]{:S(2)}) collective-permute-start(f32[272,128]{1,0:T(8,128)S(1)} %get-tuple-element.11.refs_0_), channel_id=1, source_target_pairs={{4,0},{5,1},{6,2},{7,3},{0,4},{1,5},{2,6},{3,7},{12,8},{13,9},{14,... | collective-permute-start | bytes 417800 | tf_op jit(solution)/shard_map/ppermute | solution.py:563
  7.3 8.0 %collective-permute-start.7 = (f32[272,128]{1,0:T(8,128)S(1)}, f32[272,128]{1,0:T(8,128)S(1)}, u32[]{:S(2)}, u32[]{:S(2)}) collective-permute-start(f32[272,128]{1,0:T(8,128)S(1)} %get-tuple-element.11.refs_0_), channel_id=1, source_target_pairs={{6,0},{7,1},{4,2},{5,3},{2,4},{3,5},{0,6},{1,7},{14,8},{15,9},{12,... | collective-permute-start | bytes 417800 | tf_op jit(solution)/shard_map/ppermute | solution.py:563
  7.3 4.5 %collective-permute-start.2 = (f32[8,128]{1,0:T(8,128)S(1)}, f32[8,128]{1,0:T(8,128)S(1)}, u32[]{:S(2)}, u32[]{:S(2)}) collective-permute-start(f32[8,128]{1,0:T(8,128)S(1)} %get-tuple-element.12.refs_0_), channel_id=1, source_target_pairs={{8,0},{17,1},{10,2},{19,3},{12,4},{21,5},{14,6},{23,7},{0,8},{25,9... | collective-permute-start | bytes 12296 | tf_op jit(solution)/shard_map/ppermute | solution.py:576
  9.4 5.4 %collective-permute-start.3 = (f32[8,128]{1,0:T(8,128)S(1)}, f32[8,128]{1,0:T(8,128)S(1)}, u32[]{:S(2)}, u32[]{:S(2)}) collective-permute-start(f32[8,128]{1,0:T(8,128)S(1)} %get-tuple-element.12.refs_0_), channel_id=1, source_target_pairs={{24,0},{16,8},{8,16},{0,24},{25,1},{17,9},{9,17},{1,25},{26,2},{18... | collective-permute-start | bytes 12296 | tf_op jit(solution)/shard_map/ppermute | solution.py:563
  11.8 4.0 %collective-permute-start = (f32[272,128]{1,0:T(8,128)S(1)}, f32[272,128]{1,0:T(8,128)S(1)}, u32[]{:S(2)}, u32[]{:S(2)}) collective-permute-start(f32[272,128]{1,0:T(8,128)S(1)} %get-tuple-element.11.refs_0_), channel_id=1, source_target_pairs={{1,0},{0,1},{3,2},{2,3},{5,4},{4,5},{7,6},{6,7},{9,8},{8,9},{11,10... | collective-permute-start | bytes 417800 | tf_op jit(solution)/shard_map/ppermute | solution.py:563
  14.8 1.4 %collective-permute-start.4 = (f32[272,128]{1,0:T(8,128)S(1)}, f32[272,128]{1,0:T(8,128)S(1)}, u32[]{:S(2)}, u32[]{:S(2)}) collective-permute-start(f32[272,128]{1,0:T(8,128)S(1)} %collective-permute-done.1.refs_2_), channel_id=1, source_target_pairs={{1,0},{0,1},{3,2},{2,3},{5,4},{4,5},{7,6},{6,7},{9,8},{8,9},{11,10... | collective-permute-start | bytes 417800 | tf_op jit(solution)/shard_map/ppermute | solution.py:563
  14.8 1.6 %collective-permute-start.6 = (f32[272,128]{1,0:T(8,128)S(1)}, f32[272,128]{1,0:T(8,128)S(1)}, u32[]{:S(2)}, u32[]{:S(2)}) collective-permute-start(f32[272,128]{1,0:T(8,128)S(1)} %collective-permute-done.5.refs_4_), channel_id=1, source_target_pairs={{1,0},{0,1},{3,2},{2,3},{5,4},{4,5},{7,6},{6,7},{9,8},{8,9},{11,10... | collective-permute-start | bytes 417800 | tf_op jit(solution)/shard_map/ppermute | solution.py:563
  15.3 1.4 %collective-permute-start.8 = (f32[272,128]{1,0:T(8,128)S(1)}, f32[272,128]{1,0:T(8,128)S(1)}, u32[]{:S(2)}, u32[]{:S(2)}) collective-permute-start(f32[272,128]{1,0:T(8,128)S(1)} %collective-permute-done.7.refs_6_), channel_id=1, source_target_pairs={{1,0},{0,1},{3,2},{2,3},{5,4},{4,5},{7,6},{6,7},{9,8},{8,9},{11,10... | collective-permute-start | bytes 417800 | tf_op jit(solution)/shard_map/ppermute | solution.py:563
  15.3 9.2 %collective-permute-start.9 = (f32[8,128]{1,0:T(8,128)S(1)}, f32[8,128]{1,0:T(8,128)S(1)}, u32[]{:S(2)}, u32[]{:S(2)}) collective-permute-start(f32[8,128]{1,0:T(8,128)S(1)} %collective-permute-done.2.refs_1_), channel_id=1, source_target_pairs={{1,0},{0,1},{3,2},{2,3},{5,4},{4,5},{7,6},{6,7},{9,8},{8,9},{11,10... | collective-permute-start | bytes 12296 | tf_op jit(solution)/shard_map/ppermute | solution.py:563

commit v23 on v21

--- a/solution.py
+++ b/solution.py
@@ -299,46 +299,48 @@
     )
 
 
-def picked(index, values):
-    result = jnp.float32(values[0])
-    for i, value in enumerate(values[1:], 1):
-        result = jnp.where(index == i, jnp.float32(value), result)
-    return result
-
-
-def moment_coeffs(point, angles, count):
-    lane = lax.broadcasted_iota(jnp.int32, (1, LANES), 1)
+def moment_coeffs(angle, shape):
+    count = shape[0]
+    lane = lax.broadcasted_iota(jnp.int32, shape, 1)
     moment = lax.rem(lane, MOMENTS * count) // count
     parts = []
     for func in (math.cos, math.sin):
-        value = jnp.zeros((1, LANES), jnp.float32)
-        for k in range(MOMENTS):
-            coeff = picked(point, [0.25 * func((k + 1) * angle) for angle in angles])
-            value = jnp.where(moment == k, coeff, value)
+        value = jnp.full(shape, 0.25 * func(angle), jnp.float32)
+        for k in range(1, MOMENTS):
+            value = jnp.where(moment == k, 0.25 * func((k + 1) * angle), value)
         parts.append(value)
     return parts
 
 
-def weights_of(point, points, alphas, norms, limit):
-    shape = alphas[0].shape
-    count = shape[0]
+def weights_of(alphas, norms, limits):
+    points = len(limits)
+    count = limits[0].shape[0]
+    shape = (points * count, LANES)
     lane = lax.broadcasted_iota(jnp.int32, shape, 1)
-    source = lax.broadcasted_iota(jnp.int32, shape, 0)
-    own = lax.rem(lane, count) == source
     left_half = lane < MOMENTS * count
-    betas = [ratio(norms[i + 1], norms[i]) for i in range(ITERS - 1)]
+    own = lax.rem(lane[:count], count) == lax.broadcasted_iota(jnp.int32, (count, LANES), 0)
+
+    def stacked(values):
+        return jnp.concatenate(values, axis=0)
+
+    def constant(values):
+        return stacked([jnp.full((count, LANES), value, jnp.float32) for value in values])
+
+    limit = stacked(limits)
+    betas = [stacked([ratio(norms[i + 1], norms[i])] * points) for i in range(ITERS - 1)]
+    alphas = [stacked([alpha] * points) for alpha in alphas]
     zero = jnp.zeros(shape, jnp.float32)
     one = jnp.ones(shape, jnp.float32)
     angles = [2.0 * math.pi * (j + 0.5) / points for j in range(points)]
     shift = (
-        picked(point, [GAMMA + RADIUS * math.cos(angle) for angle in angles]),
-        picked(point, [RADIUS * math.sin(angle) for angle in angles]),
+        constant([GAMMA + RADIUS * math.cos(angle) for angle in angles]),
+        constant([RADIUS * math.sin(angle) for angle in angles]),
     )
     scaled_shift = (H_SCALE * shift[0], H_SCALE * shift[1])
     product = (one, zero)
     products = [product]
     links = []
-    pivot = (scaled_shift[0] - alphas[0], zero + scaled_shift[1])
+    pivot = (scaled_shift[0] - alphas[0], scaled_shift[1])
     for i in range(ITERS):
         size = 1.0 / (pivot[0] * pivot[0] + pivot[1] * pivot[1])
         inverse = (pivot[0] * size, -pivot[1] * size)
@@ -370,7 +372,8 @@
     for back, factor in ((1, alphas[ITERS - 1]), (2, betas[ITERS - 2])):
         part = applied[ITERS - back]
         applied[ITERS - back] = (part[0] - factor * tail[0], part[1] - factor * tail[1])
-    moment = moment_coeffs(point, angles, count)
+    moments = [moment_coeffs(angle, (count, LANES)) for angle in angles]
+    moment = tuple(stacked([pair[part] for pair in moments]) for part in range(2))
     weights = []
     for i in range(BASIS):
         left = solved[i] if i < ITERS else (zero, zero)
@@ -378,7 +381,13 @@
             jnp.where(left_half, left[0], applied[i][0]),
             jnp.where(left_half, left[1], applied[i][1]),
         )
-        weights.append([jnp.where(own, part, 0.0) for part in cmul(moment, both)])
+        terms = cmul(moment, both)
+        weights.append(
+            [
+                jnp.where(own, tree_sum([part[j * count :][:count] for j in range(points)]), 0.0)
+                for part in terms
+            ]
+        )
     return weights
 
 
@@ -493,7 +502,7 @@
 
 def gram_kernel(points, scalars, *refs):
     tiles = refs[:points]
-    highs, lows, applied, out_b, out_a, gram, limits, weights = refs[points:]
+    highs, lows, applied, out_b, out_a, limits = refs[points:]
     planes, count, _ = applied.shape
     groups = count // SUB
     size = BASIS * count
@@ -501,37 +510,28 @@
     core = jnp.bitwise_and(lax.axis_index("dom"), CORES - 1)
     for far, tile in zip((0, 1 + core, 3, 2 - core), tiles):
         limits[jnp.bitwise_xor(here, far)] = tile[...]
-    gram[...] = jnp.zeros_like(gram)
-    weights[...] = jnp.zeros_like(weights)
-
-    def turn(point, carry):
-        limit = jnp.concatenate([limits[point]] * groups, axis=0)
-        alphas = [scalars[i] for i in range(ITERS)]
-        norms = [scalars[ITERS + 1 + i] for i in range(ITERS)]
-        total = None
-        for deep in range(planes // points):
-            plane = point * (planes // points) + deep
-            last_high, last_low = split(applied[plane])
-            high = jnp.concatenate([highs[i, plane] for i in range(ITERS)] + [last_high], axis=0)
-            low = jnp.concatenate([lows[i, plane] for i in range(ITERS)] + [last_low], axis=0)
-            product = lax.dot_general(
-                jnp.concatenate([high, low], axis=0),
-                high,
-                (((1,), (1,)), ((), ())),
-                preferred_element_type=jnp.float32,
-            )
-            total = product if total is None else total + product
-        gram[...] += total
-        for i, pair in enumerate(weights_of(point, points, alphas, norms, limit)):
-            for part, value in enumerate(pair):
-                weights[i * count : (i + 1) * count, part * LANES : (part + 1) * LANES] += value
-        return carry
-
-    lax.fori_loop(0, points, turn, 0)
+
+    bounds = [jnp.concatenate([limits[j]] * groups, axis=0) for j in range(points)]
+    alphas = [scalars[i] for i in range(ITERS)]
+    norms = [scalars[ITERS + 1 + i] for i in range(ITERS)]
+    weights = weights_of(alphas, norms, bounds)
+    real = jnp.concatenate([pair[0] for pair in weights], axis=0)
+    imag = jnp.concatenate([pair[1] for pair in weights], axis=0)
+    gram = None
+    for plane in range(planes):
+        last_high, last_low = split(applied[plane])
+        high = jnp.concatenate([highs[i, plane] for i in range(ITERS)] + [last_high], axis=0)
+        low = jnp.concatenate([lows[i, plane] for i in range(ITERS)] + [last_low], axis=0)
+        product = lax.dot_general(
+            jnp.concatenate([high, low], axis=0),
+            high,
+            (((1,), (1,)), ((), ())),
+            preferred_element_type=jnp.float32,
+        )
+        gram = product if gram is None else gram + product
     cross = gram[size:, :]
     pairs = gram[:size, :] + cross + cross.T
-    right = exact_dot(pairs, weights[...], ((1,), (0,)))
-    real, imag = weights[:, :LANES], weights[:, LANES:]
+    right = exact_dot(pairs, jnp.concatenate([real, imag], axis=1), ((1,), (0,)))
     half = MOMENTS * count
     left = jnp.concatenate([real[:, :half], imag[:, :half]], axis=1)
     joined = exact_dot(left.T, right, ((1,), (0,)))
@@ -588,7 +588,6 @@
         compiler_params=pltpu.CompilerParams(vmem_limit_bytes=16 * 2**20),
         name="krylov",
     )(*blocks)
-    size = BASIS * count
     width = MOMENTS * count
     out = jax.ShapeDtypeStruct((2, width, width), jnp.float32)
     return pl.pallas_call(
@@ -596,11 +595,7 @@
         out_shape=(out, out),
         in_specs=[vmem] * (4 + points),
         out_specs=(vmem, vmem),
-        scratch_shapes=[
-            pltpu.VMEM((2 * size, size), jnp.float32),
-            pltpu.VMEM((points, SUB, LANES), jnp.float32),
-            pltpu.VMEM((size, 2 * LANES), jnp.float32),
-        ],
+        scratch_shapes=[pltpu.VMEM((points, SUB, LANES), jnp.float32)],
         compiler_params=pltpu.CompilerParams(vmem_limit_bytes=16 * 2**20),
         name="gram",
     )(scalars, tile, *tiles, highs, lows, applied)

time: 28.9 us -> 28.7 us (level)
  no operation moved by 1% of the time
where the time goes in v23:
time: 28.7 us; the launch traced here: 28.5 us
  Pallas kernels  12.4 us (43%)
  starting transfers between devices  10.1 us (35%)
  waiting for transfers between devices  3.78 us (13%)
  between operations  1.3 us (5%)
  other arithmetic  0.93 us (3%)
    ppermute x9, starting transfers between devices, swapped(): lax.ppermute(values, axis, [(index ^ mask, index) for index in range(size)])  8.04 us
    pallas_call x1, Pallas kernels, whole_grid(): pl.pallas_call(functools.partial(krylov_kernel, parts, count), out_shape=...  7.95 us
    pallas_call x1, Pallas kernels, whole_grid(): pl.pallas_call(functools.partial(gram_kernel, points), out_shape=(out, ou...  3.88 us
    ppermute x9, waiting for transfers between devices, swapped(): lax.ppermute(values, axis, [(index ^ mask, index) for index in range(size)])  3.78 us
    ppermute x1, starting transfers between devices, whole_grid(): lax.ppermute(tile, ('point', 'dom'), mixed)  2.03 us
    concatenate x1, other arithmetic, packed_block(): jnp.concatenate([rows, levels], axis=0)  0.93 us
  transfers between devices with their start and end apart: 10, of which 4 were waited for; matrix products, arithmetic and copies ran while one was open for 0% of the time, Pallas kernels for 28%

profile of v23, /device:TPU:0, one launch (start us, length us, event | category | flops | bytes accessed | tf_op | source)
XLA Modules:
  0.0 28.5 jit_solution(3739470279162803903)
XLA Ops:
  1.3 0.9 %pad_maximum_fusion.rows = f32[272,128]{1,0:T(8,128)S(1)} fusion(f32[16,128]{1,0:T(8,128)} %bitcast.13, f32[256,128]{1,0:T(8,128)} %bitcast.12), kind=kLoop, calls=%fused_computation | loop fusion | flops 34816 | bytes 278528 | tf_op jit(solution)/shard_map/concatenate | solution.py:234
  2.2 0.6 %pack.1 = (f32[272,128]{1,0:T(8,128)S(1)}, f32[8,128]{1,0:T(8,128)S(1)}) custom-call(s32[1,1]{1,0:T(1,128)} %bitcast.11.counts, f32[272,128]{1,0:T(8,128)S(1)} %pad_maximum_fusion.rows), custom_call_target="tpu_custom_call" | custom-call | tf_op jit(solution)/shard_map/pack/pallas_call | solution.py:224
  2.8 3.0 %collective-permute-start.1 = (f32[272,128]{1,0:T(8,128)S(1)}, f32[272,128]{1,0:T(8,128)S(1)}, u32[]{:S(2)}, u32[]{:S(2)}) collective-permute-start(f32[272,128]{1,0:T(8,128)S(1)} %get-tuple-element.11.refs_0_), channel_id=1, source_target_pairs={{2,0},{3,1},{0,2},{1,3},{6,4},{7,5},{4,6},{5,7},{10,8},{11,9},{8,1... | collective-permute-start | bytes 417800 | tf_op jit(solution)/shard_map/ppermute | solution.py:549
  5.8 1.5 %collective-permute-start.5 = (f32[272,128]{1,0:T(8,128)S(1)}, f32[272,128]{1,0:T(8,128)S(1)}, u32[]{:S(2)}, u32[]{:S(2)}) collective-permute-start(f32[272,128]{1,0:T(8,128)S(1)} %get-tuple-element.11.refs_0_), channel_id=1, source_target_pairs={{4,0},{5,1},{6,2},{7,3},{0,4},{1,5},{2,6},{3,7},{12,8},{13,9},{14,... | collective-permute-start | bytes 417800 | tf_op jit(solution)/shard_map/ppermute | solution.py:549
  7.3 0.0 collective-permute-start.7
  7.3 2.0 %collective-permute-start.2 = (f32[8,128]{1,0:T(8,128)S(1)}, f32[8,128]{1,0:T(8,128)S(1)}, u32[]{:S(2)}, u32[]{:S(2)}) collective-permute-start(f32[8,128]{1,0:T(8,128)S(1)} %get-tuple-element.12.refs_0_), channel_id=1, source_target_pairs={{8,0},{17,1},{10,2},{19,3},{12,4},{21,5},{14,6},{23,7},{0,8},{25,9... | collective-permute-start | bytes 12296 | tf_op jit(solution)/shard_map/ppermute | solution.py:562
  9.4 2.5 %collective-permute-start.3 = (f32[8,128]{1,0:T(8,128)S(1)}, f32[8,128]{1,0:T(8,128)S(1)}, u32[]{:S(2)}, u32[]{:S(2)}) collective-permute-start(f32[8,128]{1,0:T(8,128)S(1)} %get-tuple-element.12.refs_0_), channel_id=1, source_target_pairs={{24,0},{16,8},{8,16},{0,24},{25,1},{17,9},{9,17},{1,25},{26,2},{18... | collective-permute-start | bytes 12296 | tf_op jit(solution)/shard_map/ppermute | solution.py:549
  11.8 0.0 collective-permute-done.2.refs_1_
  11.8 0.0 collective-permute-start
  11.8 2.9 %collective-permute-done.3.refs_2_ = f32[8,128]{1,0:T(8,128)S(1)} collective-permute-done((f32[8,128]{1,0:T(8,128)S(1)}, f32[8,128]{1,0:T(8,128)S(1)}, u32[]{:S(2)}, u32[]{:S(2)}) %collective-permute-start.3) | collective-permute-done | bytes 4128 | tf_op jit(solution)/shard_map/ppermute | solution.py:549
  14.8 0.0 collective-permute-done.1.refs_2_
  14.8 0.0 collective-permute-start.4
  14.8 0.0 collective-permute-done.5.refs_4_
  14.8 0.5 %collective-permute-start.6 = (f32[272,128]{1,0:T(8,128)S(1)}, f32[272,128]{1,0:T(8,128)S(1)}, u32[]{:S(2)}, u32[]{:S(2)}) collective-permute-start(f32[272,128]{1,0:T(8,128)S(1)} %collective-permute-done.5.refs_4_), channel_id=1, source_target_pairs={{1,0},{0,1},{3,2},{2,3},{5,4},{4,5},{7,6},{6,7},{9,8},{8,9},{11,10... | collective-permute-start | bytes 417800 | tf_op jit(solution)/shard_map/ppermute | solution.py:549
  15.3 0.0 collective-permute-done.7.refs_6_
  15.3 0.1 collective-permute-start.8
  15.3 0.4 %collective-permute-start.9 = (f32[8,128]{1,0:T(8,128)S(1)}, f32[8,128]{1,0:T(8,128)S(1)}, u32[]{:S(2)}, u32[]{:S(2)}) collective-permute-start(f32[8,128]{1,0:T(8,128)S(1)} %collective-permute-done.2.refs_1_), channel_id=1, source_target_pairs={{1,0},{0,1},{3,2},{2,3},{5,4},{4,5},{7,6},{6,7},{9,8},{8,9},{11,10... | collective-permute-start | bytes 12296 | tf_op jit(solution)/shard_map/ppermute | solution.py:549
  15.8 0.0 collective-permute-done.refs_1_
  15.8 0.3 %collective-permute-done.4.refs_3_ = f32[272,128]{1,0:T(8,128)S(1)} collective-permute-done((f32[272,128]{1,0:T(8,128)S(1)}, f32[272,128]{1,0:T(8,128)S(1)}, u32[]{:S(2)}, u32[]{:S(2)}) %collective-permute-start.4) | collective-permute-done | bytes 139296 | tf_op jit(solution)/shard_map/ppermute | solution.py:549
  16.1 0.2 collective-permute-done.6.refs_5_
  16.3 0.3 %collective-permute-done.8.refs_7_ = f32[272,128]{1,0:T(8,128)S(1)} collective-permute-done((f32[272,128]{1,0:T(8,128)S(1)}, f32[272,128]{1,0:T(8,128)S(1)}, u32[]{:S(2)}, u32[]{:S(2)}) %collective-permute-start.8) | collective-permute-done | bytes 139296 | tf_op jit(solution)/shard_map/ppermute | solution.py:549
  16.6 7.9 %krylov.1 = (bf16[6,16,16,1024]{3,2,1,0:T(8,128)(2,1)S(1)}, bf16[6,16,16,1024]{3,2,1,0:T(8,128)(2,1)S(1)}, f32[16,16,1024]{2,1,0:T(8,128)S(1)}, f32[13,16,128]{2,1,0:T(8,128)S(1)}) custom-call(f32[272,128]{1,0:T(8,128)S(1)} %get-tuple-element.11.refs_0_, f32[272,128]{1,0:T(8,128)S(1)} %collective-permute-done.refs_1_, ...), custom_call_target="tpu_custom_call" | custom-call | tf_op jit(solution)/shard_map/krylov/pallas_call | solution.py:570
  24.6 0.0 collective-permute-done.9.refs_3_
  24.6 3.9 %gram.1 = (f32[2,64,64]{2,1,0:T(8,128)}, f32[2,64,64]{2,1,0:T(8,128)}) custom-call(f32[13,16,128]{2,1,0:T(8,128)S(1)} %get-tuple-element.14.scalars, f32[8,128]{1,0:T(8,128)S(1)} %get-tuple-element.12.refs_0_, f32[8,128]{1,0:T(8,128)S(1)} %collective-permute-done.2.refs_1_, f32[8,128]{1,0:T(8,128)S(1)} %collective-permute-done.3.refs_2_, ...), custom_call_target="tpu_custom_call" | custom-call | tf_op jit(solution)/shard_map/gram/pallas_call | solution.py:593
Async XLA Ops:
  2.8 12.0 %collective-permute-start.1 = (f32[272,128]{1,0:T(8,128)S(1)}, f32[272,128]{1,0:T(8,128)S(1)}, u32[]{:S(2)}, u32[]{:S(2)}) collective-permute-start(f32[272,128]{1,0:T(8,128)S(1)} %get-tuple-element.11.refs_0_), channel_id=1, source_target_pairs={{2,0},{3,1},{0,2},{1,3},{6,4},{7,5},{4,6},{5,7},{10,8},{11,9},{8,1... | collective-permute-start | bytes 417800 | tf_op jit(solution)/shard_map/ppermute | solution.py:549
  5.8 9.0 %collective-permute-start.5 = (f32[272,128]{1,0:T(8,128)S(1)}, f32[272,128]{1,0:T(8,128)S(1)}, u32[]{:S(2)}, u32[]{:S(2)}) collective-permute-start(f32[272,128]{1,0:T(8,128)S(1)} %get-tuple-element.11.refs_0_), channel_id=1, source_target_pairs={{4,0},{5,1},{6,2},{7,3},{0,4},{1,5},{2,6},{3,7},{12,8},{13,9},{14,... | collective-permute-start | bytes 417800 | tf_op jit(solution)/shard_map/ppermute | solution.py:549
  7.3 8.0 %collective-permute-start.7 = (f32[272,128]{1,0:T(8,128)S(1)}, f32[272,128]{1,0:T(8,128)S(1)}, u32[]{:S(2)}, u32[]{:S(2)}) collective-permute-start(f32[272,128]{1,0:T(8,128)S(1)} %get-tuple-element.11.refs_0_), channel_id=1, source_target_pairs={{6,0},{7,1},{4,2},{5,3},{2,4},{3,5},{0,6},{1,7},{14,8},{15,9},{12,... | collective-permute-start | bytes 417800 | tf_op jit(solution)/shard_map/ppermute | solution.py:549
  7.3 4.5 %collective-permute-start.2 = (f32[8,128]{1,0:T(8,128)S(1)}, f32[8,128]{1,0:T(8,128)S(1)}, u32[]{:S(2)}, u32[]{:S(2)}) collective-permute-start(f32[8,128]{1,0:T(8,128)S(1)} %get-tuple-element.12.refs_0_), channel_id=1, source_target_pairs={{8,0},{17,1},{10,2},{19,3},{12,4},{21,5},{14,6},{23,7},{0,8},{25,9... | collective-permute-start | bytes 12296 | tf_op jit(solution)/shard_map/ppermute | solution.py:562
  9.4 5.4 %collective-permute-start.3 = (f32[8,128]{1,0:T(8,128)S(1)}, f32[8,128]{1,0:T(8,128)S(1)}, u32[]{:S(2)}, u32[]{:S(2)}) collective-permute-start(f32[8,128]{1,0:T(8,128)S(1)} %get-tuple-element.12.refs_0_), channel_id=1, source_target_pairs={{24,0},{16,8},{8,16},{0,24},{25,1},{17,9},{9,17},{1,25},{26,2},{18... | collective-permute-start | bytes 12296 | tf_op jit(solution)/shard_map/ppermute | solution.py:549
  11.8 4.0 %collective-permute-start = (f32[272,128]{1,0:T(8,128)S(1)}, f32[272,128]{1,0:T(8,128)S(1)}, u32[]{:S(2)}, u32[]{:S(2)}) collective-permute-start(f32[272,128]{1,0:T(8,128)S(1)} %get-tuple-element.11.refs_0_), channel_id=1, source_target_pairs={{1,0},{0,1},{3,2},{2,3},{5,4},{4,5},{7,6},{6,7},{9,8},{8,9},{11,10... | collective-permute-start | bytes 417800 | tf_op jit(solution)/shard_map/ppermute | solution.py:549
  14.8 1.4 %collective-permute-start.4 = (f32[272,128]{1,0:T(8,128)S(1)}, f32[272,128]{1,0:T(8,128)S(1)}, u32[]{:S(2)}, u32[]{:S(2)}) collective-permute-start(f32[272,128]{1,0:T(8,128)S(1)} %collective-permute-done.1.refs_2_), channel_id=1, source_target_pairs={{1,0},{0,1},{3,2},{2,3},{5,4},{4,5},{7,6},{6,7},{9,8},{8,9},{11,10... | collective-permute-start | bytes 417800 | tf_op jit(solution)/shard_map/ppermute | solution.py:549
  14.8 1.6 %collective-permute-start.6 = (f32[272,128]{1,0:T(8,128)S(1)}, f32[272,128]{1,0:T(8,128)S(1)}, u32[]{:S(2)}, u32[]{:S(2)}) collective-permute-start(f32[272,128]{1,0:T(8,128)S(1)} %collective-permute-done.5.refs_4_), channel_id=1, source_target_pairs={{1,0},{0,1},{3,2},{2,3},{5,4},{4,5},{7,6},{6,7},{9,8},{8,9},{11,10... | collective-permute-start | bytes 417800 | tf_op jit(solution)/shard_map/ppermute | solution.py:549
  15.3 1.4 %collective-permute-start.8 = (f32[272,128]{1,0:T(8,128)S(1)}, f32[272,128]{1,0:T(8,128)S(1)}, u32[]{:S(2)}, u32[]{:S(2)}) collective-permute-start(f32[272,128]{1,0:T(8,128)S(1)} %collective-permute-done.7.refs_6_), channel_id=1, source_target_pairs={{1,0},{0,1},{3,2},{2,3},{5,4},{4,5},{7,6},{6,7},{9,8},{8,9},{11,10... | collective-permute-start | bytes 417800 | tf_op jit(solution)/shard_map/ppermute | solution.py:549
  15.3 9.2 %collective-permute-start.9 = (f32[8,128]{1,0:T(8,128)S(1)}, f32[8,128]{1,0:T(8,128)S(1)}, u32[]{:S(2)}, u32[]{:S(2)}) collective-permute-start(f32[8,128]{1,0:T(8,128)S(1)} %collective-permute-done.2.refs_1_), channel_id=1, source_target_pairs={{1,0},{0,1},{3,2},{2,3},{5,4},{4,5},{7,6},{6,7},{9,8},{8,9},{11,10... | collective-permute-start | bytes 12296 | tf_op jit(solution)/shard_map/ppermute | solution.py:549

commit v24 on v23

--- a/solution.py
+++ b/solution.py
@@ -166,6 +166,7 @@
 SUB = 8
 BASIS = ITERS + 1
 CORES = 2
+TOGETHER = 4
 H_SCALE = 2.0 / COEF_NEAR
 FAR_SCALED = 0.5 * H_SCALE * COEF_FAR
 
@@ -272,7 +273,8 @@
     for m, edge in enumerate(plane_rows(edges, plane, rows)):
         halos.append(pltpu.roll(edge, LANES - 1 if m % X_IN < 2 else 1, 1))
     here, above, below, above_2, below_2 = (
-        plane_rows(vector, (plane + far) % planes, rows) for far in (0, 1, -1, 2, -2)
+        plane_rows(vector, jnp.bitwise_and(plane + (far + planes), planes - 1), rows)
+        for far in (0, 1, -1, 2, -2)
     )
     y_sums = plane_rows(sums, plane, rows)
     out = []
@@ -440,18 +442,33 @@
             for lanes, part in zip(all_lanes, parts_of):
                 ref[plane, rows, lanes] = part
 
-    for group, rows in enumerate(all_rows):
-        norm = []
-        for plane in range(planes):
+    def over_planes(one_plane):
+        def turn(step, sums):
+            for deep in range(TOGETHER):
+                terms = one_plane(step * TOGETHER + deep)
+                sums = [total + term for total, term in zip(sums, terms)]
+            return tuple(sums)
+
+        blank = jnp.zeros((SUB, LANES), jnp.float32)
+        return lax.fori_loop(0, planes // TOGETHER, turn, (blank,) * groups)
+
+    def keep_norms(terms):
+        for rows, term in zip(all_rows, terms):
+            partial[rows, :] = term
+
+    def first_plane(plane):
+        terms = []
+        for rows in all_rows:
             values = plane_rows(first_work, plane, rows)
             keep_y_parts(plane, rows, values)
-            norm.append(tree_sum([value * value for value in values]))
-        partial[rows, :] = tree_sum(norm)
+            terms.append(tree_sum([value * value for value in values]))
+        return terms
+
+    keep_norms(over_planes(first_plane))
 
     def update_pass(i, work, before, alphas, betas):
-        norm = [[] for _ in range(groups)]
-        for plane in range(planes):
-            columns = []
+        def one_plane(plane):
+            columns, terms = [], []
             for group, rows in enumerate(all_rows):
                 values = []
                 for lanes in all_lanes:
@@ -460,14 +477,15 @@
                     before[plane, rows, lanes] = value
                     values.append(value)
                 keep_y_parts(plane, rows, values)
-                norm[group].append(tree_sum([value * value for value in values]))
+                terms.append(tree_sum([value * value for value in values]))
                 columns.append(values)
             for lanes, *column in zip(all_lanes, *columns):
                 high, low = split(jnp.concatenate(column, axis=0))
                 highs[i + 1, plane, :, lanes] = high
                 lows[i + 1, plane, :, lanes] = low
-        for rows, terms in zip(all_rows, norm):
-            partial[rows, :] = tree_sum(terms)
+            return terms
+
+        keep_norms(over_planes(one_plane))
 
     def half_turn(i, work, before, may_end):
         norms = [lane_sum(partial[rows, :]) for rows in all_rows]
@@ -477,14 +495,18 @@
         inverses = [ratio(jnp.ones_like(norm), norm) for norm in norms]
         for norm, rows in zip(norms, all_rows):
             scalars[ITERS + 1 + i, rows, :] = norm
-        curve = [[] for _ in range(groups)]
-        for plane in range(planes):
-            for group, rows in enumerate(all_rows):
+
+        def one_plane(plane):
+            terms = []
+            for rows in all_rows:
                 value, out = apply_plane(work, sums, edges, diagonal, plane, rows)
                 for m, lanes in enumerate(all_lanes):
                     applied[plane, rows, lanes] = out[m]
-                curve[group].append(tree_sum([value[m] * out[m] for m in range(ROWS)]))
-        alphas = [lane_sum(tree_sum(curve[g])) * inverses[g] for g in range(groups)]
+                terms.append(tree_sum([value[m] * out[m] for m in range(ROWS)]))
+            return terms
+
+        curves = over_planes(one_plane)
+        alphas = [lane_sum(curves[g]) * inverses[g] for g in range(groups)]
         for alpha, rows in zip(alphas, all_rows):
             scalars[i, rows, :] = alpha
         if may_end:

time: 28.7 us -> 31.1 us (1.084)
  Pallas kernels: 12.4 us -> 14.8 us
    pallas_call x1, Pallas kernels: 7.95 us -> 10.4 us  [whole_grid(): pl.pallas_call(functools.partial(krylov_kernel, parts, count), out_shape=...]
  transfers between devices with their start and end apart: 10 -> 10, of which waited for: 4 -> 4; matrix products, arithmetic and copies ran while one was open for 0% -> 0% of each run, Pallas kernels for 28% -> 34%
where the time goes in v24:
time: 31.1 us; the launch traced here: 30.9 us
  Pallas kernels  14.8 us (48%)
  starting transfers between devices  10.1 us (32%)
  waiting for transfers between devices  3.78 us (12%)
  between operations  1.3 us (4%)
  other arithmetic  0.93 us (3%)
    pallas_call x1, Pallas kernels, whole_grid(): pl.pallas_call(functools.partial(krylov_kernel, parts, count), out_shape=...  10.4 us
    ppermute x9, starting transfers between devices, swapped(): lax.ppermute(values, axis, [(index ^ mask, index) for index in range(size)])  8.04 us
    pallas_call x1, Pallas kernels, whole_grid(): pl.pallas_call(functools.partial(gram_kernel, points), out_shape=(out, ou...  3.88 us
    ppermute x9, waiting for transfers between devices, swapped(): lax.ppermute(values, axis, [(index ^ mask, index) for index in range(size)])  3.78 us
    ppermute x1, starting transfers between devices, whole_grid(): lax.ppermute(tile, ('point', 'dom'), mixed)  2.03 us
    concatenate x1, other arithmetic, packed_block(): jnp.concatenate([rows, levels], axis=0)  0.93 us
  transfers between devices with their start and end apart: 10, of which 4 were waited for; matrix products, arithmetic and copies ran while one was open for 0% of the time, Pallas kernels for 34%

profile of v24, /device:TPU:0, one launch (start us, length us, event | category | flops | bytes accessed | tf_op | source)
XLA Modules:
  0.0 30.9 jit_solution(1999936974596808793)
XLA Ops:
  1.3 0.9 %pad_maximum_fusion.rows = f32[272,128]{1,0:T(8,128)S(1)} fusion(f32[16,128]{1,0:T(8,128)} %bitcast.13, f32[256,128]{1,0:T(8,128)} %bitcast.12), kind=kLoop, calls=%fused_computation | loop fusion | flops 34816 | bytes 278528 | tf_op jit(solution)/shard_map/concatenate | solution.py:235
  2.2 0.6 %pack.1 = (f32[272,128]{1,0:T(8,128)S(1)}, f32[8,128]{1,0:T(8,128)S(1)}) custom-call(s32[1,1]{1,0:T(1,128)} %bitcast.11.counts, f32[272,128]{1,0:T(8,128)S(1)} %pad_maximum_fusion.rows), custom_call_target="tpu_custom_call" | custom-call | tf_op jit(solution)/shard_map/pack/pallas_call | solution.py:225
  2.8 3.0 %collective-permute-start.1 = (f32[272,128]{1,0:T(8,128)S(1)}, f32[272,128]{1,0:T(8,128)S(1)}, u32[]{:S(2)}, u32[]{:S(2)}) collective-permute-start(f32[272,128]{1,0:T(8,128)S(1)} %get-tuple-element.11.refs_0_), channel_id=1, source_target_pairs={{2,0},{3,1},{0,2},{1,3},{6,4},{7,5},{4,6},{5,7},{10,8},{11,9},{8,1... | collective-permute-start | bytes 417800 | tf_op jit(solution)/shard_map/ppermute | solution.py:571
  5.8 1.5 %collective-permute-start.5 = (f32[272,128]{1,0:T(8,128)S(1)}, f32[272,128]{1,0:T(8,128)S(1)}, u32[]{:S(2)}, u32[]{:S(2)}) collective-permute-start(f32[272,128]{1,0:T(8,128)S(1)} %get-tuple-element.11.refs_0_), channel_id=1, source_target_pairs={{4,0},{5,1},{6,2},{7,3},{0,4},{1,5},{2,6},{3,7},{12,8},{13,9},{14,... | collective-permute-start | bytes 417800 | tf_op jit(solution)/shard_map/ppermute | solution.py:571
  7.3 0.0 collective-permute-start.7
  7.3 2.0 %collective-permute-start.2 = (f32[8,128]{1,0:T(8,128)S(1)}, f32[8,128]{1,0:T(8,128)S(1)}, u32[]{:S(2)}, u32[]{:S(2)}) collective-permute-start(f32[8,128]{1,0:T(8,128)S(1)} %get-tuple-element.12.refs_0_), channel_id=1, source_target_pairs={{8,0},{17,1},{10,2},{19,3},{12,4},{21,5},{14,6},{23,7},{0,8},{25,9... | collective-permute-start | bytes 12296 | tf_op jit(solution)/shard_map/ppermute | solution.py:584
  9.4 2.5 %collective-permute-start.3 = (f32[8,128]{1,0:T(8,128)S(1)}, f32[8,128]{1,0:T(8,128)S(1)}, u32[]{:S(2)}, u32[]{:S(2)}) collective-permute-start(f32[8,128]{1,0:T(8,128)S(1)} %get-tuple-element.12.refs_0_), channel_id=1, source_target_pairs={{24,0},{16,8},{8,16},{0,24},{25,1},{17,9},{9,17},{1,25},{26,2},{18... | collective-permute-start | bytes 12296 | tf_op jit(solution)/shard_map/ppermute | solution.py:571
  11.8 0.0 collective-permute-done.2.refs_1_
  11.8 0.0 collective-permute-start
  11.8 2.9 %collective-permute-done.3.refs_2_ = f32[8,128]{1,0:T(8,128)S(1)} collective-permute-done((f32[8,128]{1,0:T(8,128)S(1)}, f32[8,128]{1,0:T(8,128)S(1)}, u32[]{:S(2)}, u32[]{:S(2)}) %collective-permute-start.3) | collective-permute-done | bytes 4128 | tf_op jit(solution)/shard_map/ppermute | solution.py:571
  14.8 0.0 collective-permute-done.1.refs_2_
  14.8 0.0 collective-permute-start.4
  14.8 0.0 collective-permute-done.5.refs_4_
  14.8 0.5 %collective-permute-start.6 = (f32[272,128]{1,0:T(8,128)S(1)}, f32[272,128]{1,0:T(8,128)S(1)}, u32[]{:S(2)}, u32[]{:S(2)}) collective-permute-start(f32[272,128]{1,0:T(8,128)S(1)} %collective-permute-done.5.refs_4_), channel_id=1, source_target_pairs={{1,0},{0,1},{3,2},{2,3},{5,4},{4,5},{7,6},{6,7},{9,8},{8,9},{11,10... | collective-permute-start | bytes 417800 | tf_op jit(solution)/shard_map/ppermute | solution.py:571
  15.3 0.0 collective-permute-done.7.refs_6_
  15.3 0.1 collective-permute-start.8
  15.3 0.4 %collective-permute-start.9 = (f32[8,128]{1,0:T(8,128)S(1)}, f32[8,128]{1,0:T(8,128)S(1)}, u32[]{:S(2)}, u32[]{:S(2)}) collective-permute-start(f32[8,128]{1,0:T(8,128)S(1)} %collective-permute-done.2.refs_1_), channel_id=1, source_target_pairs={{1,0},{0,1},{3,2},{2,3},{5,4},{4,5},{7,6},{6,7},{9,8},{8,9},{11,10... | collective-permute-start | bytes 12296 | tf_op jit(solution)/shard_map/ppermute | solution.py:571
  15.8 0.0 collective-permute-done.refs_1_
  15.8 0.3 %collective-permute-done.4.refs_3_ = f32[272,128]{1,0:T(8,128)S(1)} collective-permute-done((f32[272,128]{1,0:T(8,128)S(1)}, f32[272,128]{1,0:T(8,128)S(1)}, u32[]{:S(2)}, u32[]{:S(2)}) %collective-permute-start.4) | collective-permute-done | bytes 139296 | tf_op jit(solution)/shard_map/ppermute | solution.py:571
  16.1 0.2 collective-permute-done.6.refs_5_
  16.3 0.3 %collective-permute-done.8.refs_7_ = f32[272,128]{1,0:T(8,128)S(1)} collective-permute-done((f32[272,128]{1,0:T(8,128)S(1)}, f32[272,128]{1,0:T(8,128)S(1)}, u32[]{:S(2)}, u32[]{:S(2)}) %collective-permute-start.8) | collective-permute-done | bytes 139296 | tf_op jit(solution)/shard_map/ppermute | solution.py:571
  16.6 10.4 %krylov.1 = (bf16[6,16,16,1024]{3,2,1,0:T(8,128)(2,1)S(1)}, bf16[6,16,16,1024]{3,2,1,0:T(8,128)(2,1)S(1)}, f32[16,16,1024]{2,1,0:T(8,128)S(1)}, f32[13,16,128]{2,1,0:T(8,128)S(1)}) custom-call(f32[272,128]{1,0:T(8,128)S(1)} %get-tuple-element.11.refs_0_, f32[272,128]{1,0:T(8,128)S(1)} %collective-permute-done.refs_1_, ...), custom_call_target="tpu_custom_call" | custom-call | tf_op jit(solution)/shard_map/krylov/pallas_call | solution.py:592
  27.0 0.0 collective-permute-done.9.refs_3_
  27.0 3.9 %gram.1 = (f32[2,64,64]{2,1,0:T(8,128)}, f32[2,64,64]{2,1,0:T(8,128)}) custom-call(f32[13,16,128]{2,1,0:T(8,128)S(1)} %get-tuple-element.14.scalars, f32[8,128]{1,0:T(8,128)S(1)} %get-tuple-element.12.refs_0_, f32[8,128]{1,0:T(8,128)S(1)} %collective-permute-done.2.refs_1_, f32[8,128]{1,0:T(8,128)S(1)} %collective-permute-done.3.refs_2_, ...), custom_call_target="tpu_custom_call" | custom-call | tf_op jit(solution)/shard_map/gram/pallas_call | solution.py:615
Async XLA Ops:
  2.8 12.0 %collective-permute-start.1 = (f32[272,128]{1,0:T(8,128)S(1)}, f32[272,128]{1,0:T(8,128)S(1)}, u32[]{:S(2)}, u32[]{:S(2)}) collective-permute-start(f32[272,128]{1,0:T(8,128)S(1)} %get-tuple-element.11.refs_0_), channel_id=1, source_target_pairs={{2,0},{3,1},{0,2},{1,3},{6,4},{7,5},{4,6},{5,7},{10,8},{11,9},{8,1... | collective-permute-start | bytes 417800 | tf_op jit(solution)/shard_map/ppermute | solution.py:571
  5.8 9.0 %collective-permute-start.5 = (f32[272,128]{1,0:T(8,128)S(1)}, f32[272,128]{1,0:T(8,128)S(1)}, u32[]{:S(2)}, u32[]{:S(2)}) collective-permute-start(f32[272,128]{1,0:T(8,128)S(1)} %get-tuple-element.11.refs_0_), channel_id=1, source_target_pairs={{4,0},{5,1},{6,2},{7,3},{0,4},{1,5},{2,6},{3,7},{12,8},{13,9},{14,... | collective-permute-start | bytes 417800 | tf_op jit(solution)/shard_map/ppermute | solution.py:571
  7.3 8.0 %collective-permute-start.7 = (f32[272,128]{1,0:T(8,128)S(1)}, f32[272,128]{1,0:T(8,128)S(1)}, u32[]{:S(2)}, u32[]{:S(2)}) collective-permute-start(f32[272,128]{1,0:T(8,128)S(1)} %get-tuple-element.11.refs_0_), channel_id=1, source_target_pairs={{6,0},{7,1},{4,2},{5,3},{2,4},{3,5},{0,6},{1,7},{14,8},{15,9},{12,... | collective-permute-start | bytes 417800 | tf_op jit(solution)/shard_map/ppermute | solution.py:571
  7.3 4.5 %collective-permute-start.2 = (f32[8,128]{1,0:T(8,128)S(1)}, f32[8,128]{1,0:T(8,128)S(1)}, u32[]{:S(2)}, u32[]{:S(2)}) collective-permute-start(f32[8,128]{1,0:T(8,128)S(1)} %get-tuple-element.12.refs_0_), channel_id=1, source_target_pairs={{8,0},{17,1},{10,2},{19,3},{12,4},{21,5},{14,6},{23,7},{0,8},{25,9... | collective-permute-start | bytes 12296 | tf_op jit(solution)/shard_map/ppermute | solution.py:584
  9.4 5.4 %collective-permute-start.3 = (f32[8,128]{1,0:T(8,128)S(1)}, f32[8,128]{1,0:T(8,128)S(1)}, u32[]{:S(2)}, u32[]{:S(2)}) collective-permute-start(f32[8,128]{1,0:T(8,128)S(1)} %get-tuple-element.12.refs_0_), channel_id=1, source_target_pairs={{24,0},{16,8},{8,16},{0,24},{25,1},{17,9},{9,17},{1,25},{26,2},{18... | collective-permute-start | bytes 12296 | tf_op jit(solution)/shard_map/ppermute | solution.py:571
  11.8 4.0 %collective-permute-start = (f32[272,128]{1,0:T(8,128)S(1)}, f32[272,128]{1,0:T(8,128)S(1)}, u32[]{:S(2)}, u32[]{:S(2)}) collective-permute-start(f32[272,128]{1,0:T(8,128)S(1)} %get-tuple-element.11.refs_0_), channel_id=1, source_target_pairs={{1,0},{0,1},{3,2},{2,3},{5,4},{4,5},{7,6},{6,7},{9,8},{8,9},{11,10... | collective-permute-start | bytes 417800 | tf_op jit(solution)/shard_map/ppermute | solution.py:571
  14.8 1.4 %collective-permute-start.4 = (f32[272,128]{1,0:T(8,128)S(1)}, f32[272,128]{1,0:T(8,128)S(1)}, u32[]{:S(2)}, u32[]{:S(2)}) collective-permute-start(f32[272,128]{1,0:T(8,128)S(1)} %collective-permute-done.1.refs_2_), channel_id=1, source_target_pairs={{1,0},{0,1},{3,2},{2,3},{5,4},{4,5},{7,6},{6,7},{9,8},{8,9},{11,10... | collective-permute-start | bytes 417800 | tf_op jit(solution)/shard_map/ppermute | solution.py:571
  14.8 1.6 %collective-permute-start.6 = (f32[272,128]{1,0:T(8,128)S(1)}, f32[272,128]{1,0:T(8,128)S(1)}, u32[]{:S(2)}, u32[]{:S(2)}) collective-permute-start(f32[272,128]{1,0:T(8,128)S(1)} %collective-permute-done.5.refs_4_), channel_id=1, source_target_pairs={{1,0},{0,1},{3,2},{2,3},{5,4},{4,5},{7,6},{6,7},{9,8},{8,9},{11,10... | collective-permute-start | bytes 417800 | tf_op jit(solution)/shard_map/ppermute | solution.py:571
  15.3 1.4 %collective-permute-start.8 = (f32[272,128]{1,0:T(8,128)S(1)}, f32[272,128]{1,0:T(8,128)S(1)}, u32[]{:S(2)}, u32[]{:S(2)}) collective-permute-start(f32[272,128]{1,0:T(8,128)S(1)} %collective-permute-done.7.refs_6_), channel_id=1, source_target_pairs={{1,0},{0,1},{3,2},{2,3},{5,4},{4,5},{7,6},{6,7},{9,8},{8,9},{11,10... | collective-permute-start | bytes 417800 | tf_op jit(solution)/shard_map/ppermute | solution.py:571
  15.3 11.7 %collective-permute-start.9 = (f32[8,128]{1,0:T(8,128)S(1)}, f32[8,128]{1,0:T(8,128)S(1)}, u32[]{:S(2)}, u32[]{:S(2)}) collective-permute-start(f32[8,128]{1,0:T(8,128)S(1)} %collective-permute-done.2.refs_1_), channel_id=1, source_target_pairs={{1,0},{0,1},{3,2},{2,3},{5,4},{4,5},{7,6},{6,7},{9,8},{8,9},{11,10... | collective-permute-start | bytes 12296 | tf_op jit(solution)/shard_map/ppermute | solution.py:571

commit v25 on v23

--- a/solution.py
+++ b/solution.py
@@ -211,7 +211,7 @@
             value = jnp.where(lane_block == (row + far) % columns, moved, value)
         start = depth * ROWS * SUB * groups + deep * ROWS
         out[start : start + ROWS, :] = value
-    tile[...] = jnp.broadcast_to(counts[...].astype(jnp.float32), (SUB, LANES))
+    tile[...] = jnp.broadcast_to(counts[...].astype(jnp.float32), tile.shape)
 
 
 def packed_block(sources, potential, iter_counts):
@@ -225,7 +225,7 @@
         functools.partial(pack_kernel, depth, count // SUB),
         out_shape=(
             jax.ShapeDtypeStruct((size, LANES), jnp.float32),
-            jax.ShapeDtypeStruct((SUB, LANES), jnp.float32),
+            jax.ShapeDtypeStruct((136, LANES), jnp.float32),
         ),
         in_specs=[vmem, vmem],
         out_specs=(vmem, vmem),
@@ -509,7 +509,7 @@
     here = lax.axis_index("point")
     core = jnp.bitwise_and(lax.axis_index("dom"), CORES - 1)
     for far, tile in zip((0, 1 + core, 3, 2 - core), tiles):
-        limits[jnp.bitwise_xor(here, far)] = tile[...]
+        limits[jnp.bitwise_xor(here, far)] = tile[:SUB, :]
 
     bounds = [jnp.concatenate([limits[j]] * groups, axis=0) for j in range(points)]
     alphas = [scalars[i] for i in range(ITERS)]
@@ -560,9 +560,10 @@
         for part in range(parts)
     ]
     tiles = [lax.ppermute(tile, ("point", "dom"), mixed), swapped(tile, "point", points, 3)]
-    even[1], *tiles = lax.optimization_barrier((even[1], *tiles))
+    tiles = list(lax.optimization_barrier(tuple(tiles)))
     tiles.append(swapped(tiles[0], "dom", parts, 1))
-    odd = [swapped(value, "dom", parts, 1) for value in even]
+    own, even[1] = lax.optimization_barrier((block, even[1]))
+    odd = [swapped(value, "dom", parts, 1) for value in [own] + even[1:]]
     blocks = [value for pair in zip(even, odd) for value in pair]
     vmem = pl.BlockSpec(memory_space=pltpu.VMEM)
     vector = (planes, count, ROWS * LANES)

time: 28.7 us -> 27.8 us (0.969)
  waiting for transfers between devices: 3.78 us -> 2.87 us
    ppermute x9, waiting for transfers between devices: 3.78 us -> 2.87 us  [swapped(): lax.ppermute(values, axis, [(index ^ mask, index) for index in range(size)])]
  transfers between devices with their start and end apart: 10 -> 10, of which waited for: 4 -> 2; matrix products, arithmetic and copies ran while one was open for 0% -> 0% of each run, Pallas kernels for 28% -> 29%
where the time goes in v25:
time: 27.8 us; the launch traced here: 27.6 us
  Pallas kernels  12.4 us (45%)
  starting transfers between devices  10.1 us (36%)
  waiting for transfers between devices  2.87 us (10%)
  between operations  1.32 us (5%)
  other arithmetic  0.93 us (3%)
    ppermute x9, starting transfers between devices, swapped(): lax.ppermute(values, axis, [(index ^ mask, index) for index in range(size)])  8.04 us
    pallas_call x1, Pallas kernels, whole_grid(): pl.pallas_call(functools.partial(krylov_kernel, parts, count), out_shape=...  7.95 us
    pallas_call x1, Pallas kernels, whole_grid(): pl.pallas_call(functools.partial(gram_kernel, points), out_shape=(out, ou...  3.88 us
    ppermute x9, waiting for transfers between devices, swapped(): lax.ppermute(values, axis, [(index ^ mask, index) for index in range(size)])  2.87 us
    ppermute x1, starting transfers between devices, whole_grid(): lax.ppermute(tile, ('point', 'dom'), mixed)  2.03 us
    concatenate x1, other arithmetic, packed_block(): jnp.concatenate([rows, levels], axis=0)  0.93 us
    pallas_call x1, Pallas kernels, packed_block(): pl.pallas_call(functools.partial(pack_kernel, depth, count // SUB), out_s...  0.56 us
  transfers between devices with their start and end apart: 10, of which 2 were waited for; matrix products, arithmetic and copies ran while one was open for 0% of the time, Pallas kernels for 29%

profile of v25, /device:TPU:0, one launch (start us, length us, event | category | flops | bytes accessed | tf_op | source)
XLA Modules:
  0.0 27.6 jit_solution(10365891012501361257)
XLA Ops:
  1.3 0.9 %pad_maximum_fusion.rows = f32[272,128]{1,0:T(8,128)S(1)} fusion(f32[16,128]{1,0:T(8,128)} %bitcast.13, f32[256,128]{1,0:T(8,128)} %bitcast.12), kind=kLoop, calls=%fused_computation | loop fusion | flops 34816 | bytes 278528 | tf_op jit(solution)/shard_map/concatenate | solution.py:234
  2.2 0.6 %pack.1 = (f32[272,128]{1,0:T(8,128)S(1)}, f32[136,128]{1,0:T(8,128)S(1)}) custom-call(s32[1,1]{1,0:T(1,128)} %bitcast.11.counts, f32[272,128]{1,0:T(8,128)S(1)} %pad_maximum_fusion.rows), custom_call_target="tpu_custom_call" | custom-call | tf_op jit(solution)/shard_map/pack/pallas_call | solution.py:224
  2.8 3.0 %collective-permute-start = (f32[272,128]{1,0:T(8,128)S(1)}, f32[272,128]{1,0:T(8,128)S(1)}, u32[]{:S(2)}, u32[]{:S(2)}) collective-permute-start(f32[272,128]{1,0:T(8,128)S(1)} %get-tuple-element.13.refs_0_), channel_id=1, source_target_pairs={{2,0},{3,1},{0,2},{1,3},{6,4},{7,5},{4,6},{5,7},{10,8},{11,9},{8,1... | collective-permute-start | bytes 417800 | tf_op jit(solution)/shard_map/ppermute | solution.py:549
  5.8 1.5 %collective-permute-start.3 = (f32[272,128]{1,0:T(8,128)S(1)}, f32[272,128]{1,0:T(8,128)S(1)}, u32[]{:S(2)}, u32[]{:S(2)}) collective-permute-start(f32[272,128]{1,0:T(8,128)S(1)} %get-tuple-element.13.refs_0_), channel_id=1, source_target_pairs={{4,0},{5,1},{6,2},{7,3},{0,4},{1,5},{2,6},{3,7},{12,8},{13,9},{14,... | collective-permute-start | bytes 417800 | tf_op jit(solution)/shard_map/ppermute | solution.py:549
  7.3 0.0 collective-permute-start.5
  7.3 2.0 %collective-permute-start.7 = (f32[136,128]{1,0:T(8,128)S(1)}, f32[136,128]{1,0:T(8,128)S(1)}, u32[]{:S(2)}, u32[]{:S(2)}) collective-permute-start(f32[136,128]{1,0:T(8,128)S(1)} %get-tuple-element.16.refs_0_), channel_id=1, source_target_pairs={{8,0},{17,1},{10,2},{19,3},{12,4},{21,5},{14,6},{23,7},{0,8},{25,9... | collective-permute-start | bytes 208904 | tf_op jit(solution)/shard_map/ppermute | solution.py:562
  9.4 2.5 %collective-permute-start.8 = (f32[136,128]{1,0:T(8,128)S(1)}, f32[136,128]{1,0:T(8,128)S(1)}, u32[]{:S(2)}, u32[]{:S(2)}) collective-permute-start(f32[136,128]{1,0:T(8,128)S(1)} %get-tuple-element.16.refs_0_), channel_id=1, source_target_pairs={{24,0},{16,8},{8,16},{0,24},{25,1},{17,9},{9,17},{1,25},{26,2},{18... | collective-permute-start | bytes 208904 | tf_op jit(solution)/shard_map/ppermute | solution.py:549
  11.8 0.0 collective-permute-done.refs_2_
  11.8 0.0 collective-permute-start.2
  11.8 0.0 collective-permute-done.7.refs_1_
  11.8 0.5 %collective-permute-start.1 = (f32[272,128]{1,0:T(8,128)S(1)}, f32[272,128]{1,0:T(8,128)S(1)}, u32[]{:S(2)}, u32[]{:S(2)}) collective-permute-start(f32[272,128]{1,0:T(8,128)S(1)} %get-tuple-element.13.refs_0_), channel_id=1, source_target_pairs={{1,0},{0,1},{3,2},{2,3},{5,4},{4,5},{7,6},{6,7},{9,8},{8,9},{11,10... | collective-permute-start | bytes 417800 | tf_op jit(solution)/shard_map/ppermute | solution.py:549
  12.4 1.5 %collective-permute-done.3.refs_4_ = f32[272,128]{1,0:T(8,128)S(1)} collective-permute-done((f32[272,128]{1,0:T(8,128)S(1)}, f32[272,128]{1,0:T(8,128)S(1)}, u32[]{:S(2)}, u32[]{:S(2)}) %collective-permute-start.3) | collective-permute-done | bytes 139296 | tf_op jit(solution)/shard_map/ppermute | solution.py:549
  13.9 0.0 collective-permute-start.4
  13.9 0.0 collective-permute-done.5.refs_6_
  13.9 0.5 %collective-permute-start.6 = (f32[272,128]{1,0:T(8,128)S(1)}, f32[272,128]{1,0:T(8,128)S(1)}, u32[]{:S(2)}, u32[]{:S(2)}) collective-permute-start(f32[272,128]{1,0:T(8,128)S(1)} %collective-permute-done.5.refs_6_), channel_id=1, source_target_pairs={{1,0},{0,1},{3,2},{2,3},{5,4},{4,5},{7,6},{6,7},{9,8},{8,9},{11,10... | collective-permute-start | bytes 417800 | tf_op jit(solution)/shard_map/ppermute | solution.py:549
  14.4 1.3 %collective-permute-done.8.refs_2_ = f32[136,128]{1,0:T(8,128)S(1)} collective-permute-done((f32[136,128]{1,0:T(8,128)S(1)}, f32[136,128]{1,0:T(8,128)S(1)}, u32[]{:S(2)}, u32[]{:S(2)}) %collective-permute-start.8) | collective-permute-done | bytes 69664 | tf_op jit(solution)/shard_map/ppermute | solution.py:549
  15.7 0.0 collective-permute-start.9
  15.7 0.0 collective-permute-done.2.refs_3_
  15.7 0.0 collective-permute-done.1.refs_1_
  15.7 0.0 collective-permute-done.4.refs_5_
  15.7 0.0 collective-permute-done.6.refs_7_
  15.7 8.0 %krylov.1 = (bf16[6,16,16,1024]{3,2,1,0:T(8,128)(2,1)S(1)}, bf16[6,16,16,1024]{3,2,1,0:T(8,128)(2,1)S(1)}, f32[16,16,1024]{2,1,0:T(8,128)S(1)}, f32[13,16,128]{2,1,0:T(8,128)S(1)}) custom-call(f32[272,128]{1,0:T(8,128)S(1)} %get-tuple-element.13.refs_0_, f32[272,128]{1,0:T(8,128)S(1)} %collective-permute-done.1.refs_1_, ...), custom_call_target="tpu_custom_call" | custom-call | tf_op jit(solution)/shard_map/krylov/pallas_call | solution.py:571
  23.7 0.0 collective-permute-done.9.refs_3_
  23.7 3.9 %gram.1 = (f32[2,64,64]{2,1,0:T(8,128)}, f32[2,64,64]{2,1,0:T(8,128)}) custom-call(f32[13,16,128]{2,1,0:T(8,128)S(1)} %get-tuple-element.15.scalars, f32[136,128]{1,0:T(8,128)S(1)} %get-tuple-element.16.refs_0_, f32[136,128]{1,0:T(8,128)S(1)} %collective-permute-done.7.refs_1_, f32[136,128]{1,0:T(8,128)S(1)} %collective-permute-done.8.refs_2_, ...), custom_call_target="tpu_custom_call" | custom-call | tf_op jit(solution)/shard_map/gram/pallas_call | solution.py:594
Async XLA Ops:
  2.8 9.1 %collective-permute-start = (f32[272,128]{1,0:T(8,128)S(1)}, f32[272,128]{1,0:T(8,128)S(1)}, u32[]{:S(2)}, u32[]{:S(2)}) collective-permute-start(f32[272,128]{1,0:T(8,128)S(1)} %get-tuple-element.13.refs_0_), channel_id=1, source_target_pairs={{2,0},{3,1},{0,2},{1,3},{6,4},{7,5},{4,6},{5,7},{10,8},{11,9},{8,1... | collective-permute-start | bytes 417800 | tf_op jit(solution)/shard_map/ppermute | solution.py:549
  5.8 8.1 %collective-permute-start.3 = (f32[272,128]{1,0:T(8,128)S(1)}, f32[272,128]{1,0:T(8,128)S(1)}, u32[]{:S(2)}, u32[]{:S(2)}) collective-permute-start(f32[272,128]{1,0:T(8,128)S(1)} %get-tuple-element.13.refs_0_), channel_id=1, source_target_pairs={{4,0},{5,1},{6,2},{7,3},{0,4},{1,5},{2,6},{3,7},{12,8},{13,9},{14,... | collective-permute-start | bytes 417800 | tf_op jit(solution)/shard_map/ppermute | solution.py:549
  7.3 6.6 %collective-permute-start.5 = (f32[272,128]{1,0:T(8,128)S(1)}, f32[272,128]{1,0:T(8,128)S(1)}, u32[]{:S(2)}, u32[]{:S(2)}) collective-permute-start(f32[272,128]{1,0:T(8,128)S(1)} %get-tuple-element.13.refs_0_), channel_id=1, source_target_pairs={{6,0},{7,1},{4,2},{5,3},{2,4},{3,5},{0,6},{1,7},{14,8},{15,9},{12,... | collective-permute-start | bytes 417800 | tf_op jit(solution)/shard_map/ppermute | solution.py:549
  7.3 4.5 %collective-permute-start.7 = (f32[136,128]{1,0:T(8,128)S(1)}, f32[136,128]{1,0:T(8,128)S(1)}, u32[]{:S(2)}, u32[]{:S(2)}) collective-permute-start(f32[136,128]{1,0:T(8,128)S(1)} %get-tuple-element.16.refs_0_), channel_id=1, source_target_pairs={{8,0},{17,1},{10,2},{19,3},{12,4},{21,5},{14,6},{23,7},{0,8},{25,9... | collective-permute-start | bytes 208904 | tf_op jit(solution)/shard_map/ppermute | solution.py:562
  9.4 6.4 %collective-permute-start.8 = (f32[136,128]{1,0:T(8,128)S(1)}, f32[136,128]{1,0:T(8,128)S(1)}, u32[]{:S(2)}, u32[]{:S(2)}) collective-permute-start(f32[136,128]{1,0:T(8,128)S(1)} %get-tuple-element.16.refs_0_), channel_id=1, source_target_pairs={{24,0},{16,8},{8,16},{0,24},{25,1},{17,9},{9,17},{1,25},{26,2},{18... | collective-permute-start | bytes 208904 | tf_op jit(solution)/shard_map/ppermute | solution.py:549
  11.8 3.9 %collective-permute-start.2 = (f32[272,128]{1,0:T(8,128)S(1)}, f32[272,128]{1,0:T(8,128)S(1)}, u32[]{:S(2)}, u32[]{:S(2)}) collective-permute-start(f32[272,128]{1,0:T(8,128)S(1)} %collective-permute-done.refs_2_), channel_id=1, source_target_pairs={{1,0},{0,1},{3,2},{2,3},{5,4},{4,5},{7,6},{6,7},{9,8},{8,9},{11,10... | collective-permute-start | bytes 417800 | tf_op jit(solution)/shard_map/ppermute | solution.py:549
  11.8 3.9 %collective-permute-start.1 = (f32[272,128]{1,0:T(8,128)S(1)}, f32[272,128]{1,0:T(8,128)S(1)}, u32[]{:S(2)}, u32[]{:S(2)}) collective-permute-start(f32[272,128]{1,0:T(8,128)S(1)} %get-tuple-element.13.refs_0_), channel_id=1, source_target_pairs={{1,0},{0,1},{3,2},{2,3},{5,4},{4,5},{7,6},{6,7},{9,8},{8,9},{11,10... | collective-permute-start | bytes 417800 | tf_op jit(solution)/shard_map/ppermute | solution.py:549
  13.9 1.8 %collective-permute-start.4 = (f32[272,128]{1,0:T(8,128)S(1)}, f32[272,128]{1,0:T(8,128)S(1)}, u32[]{:S(2)}, u32[]{:S(2)}) collective-permute-start(f32[272,128]{1,0:T(8,128)S(1)} %collective-permute-done.3.refs_4_), channel_id=1, source_target_pairs={{1,0},{0,1},{3,2},{2,3},{5,4},{4,5},{7,6},{6,7},{9,8},{8,9},{11,10... | collective-permute-start | bytes 417800 | tf_op jit(solution)/shard_map/ppermute | solution.py:549
  13.9 1.8 %collective-permute-start.6 = (f32[272,128]{1,0:T(8,128)S(1)}, f32[272,128]{1,0:T(8,128)S(1)}, u32[]{:S(2)}, u32[]{:S(2)}) collective-permute-start(f32[272,128]{1,0:T(8,128)S(1)} %collective-permute-done.5.refs_6_), channel_id=1, source_target_pairs={{1,0},{0,1},{3,2},{2,3},{5,4},{4,5},{7,6},{6,7},{9,8},{8,9},{11,10... | collective-permute-start | bytes 417800 | tf_op jit(solution)/shard_map/ppermute | solution.py:549
  15.7 8.0 %collective-permute-start.9 = (f32[136,128]{1,0:T(8,128)S(1)}, f32[136,128]{1,0:T(8,128)S(1)}, u32[]{:S(2)}, u32[]{:S(2)}) collective-permute-start(f32[136,128]{1,0:T(8,128)S(1)} %collective-permute-done.7.refs_1_), channel_id=1, source_target_pairs={{1,0},{0,1},{3,2},{2,3},{5,4},{4,5},{7,6},{6,7},{9,8},{8,9},{11,10... | collective-permute-start | bytes 208904 | tf_op jit(solution)/shard_map/ppermute | solution.py:549

commit v26 on v25

--- a/solution.py
+++ b/solution.py
@@ -166,11 +166,12 @@
 SUB = 8
 BASIS = ITERS + 1
 CORES = 2
+TILE = 136
 H_SCALE = 2.0 / COEF_NEAR
 FAR_SCALED = 0.5 * H_SCALE * COEF_FAR
 
 
-def pack_kernel(depth, groups, counts, rows, out, tile):
+def pack_kernel(depth, groups, rows, out):
     columns = rows.shape[0] // (SUB * groups * depth + depth)
     first_level = columns * SUB * groups * depth
     source = lax.broadcasted_iota(jnp.int32, (LANES, LANES), 0)
@@ -211,10 +212,9 @@
             value = jnp.where(lane_block == (row + far) % columns, moved, value)
         start = depth * ROWS * SUB * groups + deep * ROWS
         out[start : start + ROWS, :] = value
-    tile[...] = jnp.broadcast_to(counts[...].astype(jnp.float32), tile.shape)
-
-
-def packed_block(sources, potential, iter_counts):
+
+
+def packed_block(sources, potential):
     count, depth, cells = sources.shape
     columns = cells // LANES
     rows = sources.reshape(count, depth, columns, LANES).transpose(0, 2, 1, 3).reshape(-1, LANES)
@@ -223,15 +223,12 @@
     size = depth * ROWS * (count + 1)
     return pl.pallas_call(
         functools.partial(pack_kernel, depth, count // SUB),
-        out_shape=(
-            jax.ShapeDtypeStruct((size, LANES), jnp.float32),
-            jax.ShapeDtypeStruct((136, LANES), jnp.float32),
-        ),
-        in_specs=[vmem, vmem],
-        out_specs=(vmem, vmem),
+        out_shape=jax.ShapeDtypeStruct((size, LANES), jnp.float32),
+        in_specs=[vmem],
+        out_specs=vmem,
         compiler_params=pltpu.CompilerParams(vmem_limit_bytes=4 * 2**20),
         name="pack",
-    )(iter_counts.reshape(1, 1), jnp.concatenate([rows, levels], axis=0))
+    )(jnp.concatenate([rows, levels], axis=0))
 
 
 def lane_sum(values):
@@ -508,7 +505,7 @@
     size = BASIS * count
     here = lax.axis_index("point")
     core = jnp.bitwise_and(lax.axis_index("dom"), CORES - 1)
-    for far, tile in zip((0, 1 + core, 3, 2 - core), tiles):
+    for far, tile in zip((0, 3, 1 + core, 2 - core), tiles):
         limits[jnp.bitwise_xor(here, far)] = tile[:SUB, :]
 
     bounds = [jnp.concatenate([limits[j]] * groups, axis=0) for j in range(points)]
@@ -552,16 +549,18 @@
 def whole_grid(sources, potential, iter_counts, *, parts, points):
     count, depth, _ = sources.shape
     planes = parts * depth
-    block, tile = packed_block(sources, potential, iter_counts)
+    block = packed_block(sources, potential)
+    tile = jnp.broadcast_to(iter_counts.astype(jnp.float32), (TILE, LANES))
+    tile = lax.optimization_barrier(tile)
     even = [block] + [swapped(block, "dom", parts, mask) for mask in range(CORES, parts, CORES)]
     mixed = [
         ((point ^ (1 + part % CORES)) * parts + part, point * parts + part)
         for point in range(points)
         for part in range(parts)
     ]
-    tiles = [lax.ppermute(tile, ("point", "dom"), mixed), swapped(tile, "point", points, 3)]
+    tiles = [swapped(tile, "point", points, 3), lax.ppermute(tile, ("point", "dom"), mixed)]
     tiles = list(lax.optimization_barrier(tuple(tiles)))
-    tiles.append(swapped(tiles[0], "dom", parts, 1))
+    tiles.append(swapped(tiles[1], "dom", parts, 1))
     own, even[1] = lax.optimization_barrier((block, even[1]))
     odd = [swapped(value, "dom", parts, 1) for value in [own] + even[1:]]
     blocks = [value for pair in zip(even, odd) for value in pair]

time: 27.8 us -> 28.3 us (1.018)
  waiting for transfers between devices: 2.87 us -> 4.08 us
  starting transfers between devices: 10.1 us -> 9.25 us
    ppermute x1, starting transfers between devices: 2.03 us -> 0.01 us  [whole_grid(): lax.ppermute(tile, ('point', 'dom'), mixed)]
    ppermute x1, waiting for transfers between devices: 0.01 us -> 1.29 us  [whole_grid(): lax.ppermute(tile, ('point', 'dom'), mixed)]
    ppermute x9, starting transfers between devices: 8.04 us -> 9.25 us  [swapped(): lax.ppermute(values, axis, [(index ^ mask, index) for index in range(size)])]
  transfers between devices with their start and end apart: 10 -> 10, of which waited for: 2 -> 2; matrix products, arithmetic and copies ran while one was open for 0% -> 0% of each run, Pallas kernels for 29% -> 28%
where the time goes in v26:
time: 28.3 us; the launch traced here: 28 us
  Pallas kernels  12.4 us (44%)
  starting transfers between devices  9.25 us (33%)
  waiting for transfers between devices  4.08 us (14%)
  between operations  1.33 us (5%)
  other arithmetic  0.93 us (3%)
    ppermute x9, starting transfers between devices, swapped(): lax.ppermute(values, axis, [(index ^ mask, index) for index in range(size)])  9.25 us
    pallas_call x1, Pallas kernels, whole_grid(): pl.pallas_call(functools.partial(krylov_kernel, parts, count), out_shape=...  7.95 us
    pallas_call x1, Pallas kernels, whole_grid(): pl.pallas_call(functools.partial(gram_kernel, points), out_shape=(out, ou...  3.88 us
    ppermute x9, waiting for transfers between devices, swapped(): lax.ppermute(values, axis, [(index ^ mask, index) for index in range(size)])  2.8 us
    ppermute x1, waiting for transfers between devices, whole_grid(): lax.ppermute(tile, ('point', 'dom'), mixed)  1.29 us
    concatenate x1, other arithmetic, packed_block(): jnp.concatenate([rows, levels], axis=0)  0.93 us
  transfers between devices with their start and end apart: 10, of which 2 were waited for; matrix products, arithmetic and copies ran while one was open for 0% of the time, Pallas kernels for 28%

profile of v26, /device:TPU:0, one launch (start us, length us, event | category | flops | bytes accessed | tf_op | source)
XLA Modules:
  0.0 28.0 jit_solution(8069008261955029075)
XLA Ops:
  0.6 0.9 %pad_maximum_fusion.rows = f32[272,128]{1,0:T(8,128)S(1)} fusion(f32[16,128]{1,0:T(8,128)} %bitcast.12, f32[256,128]{1,0:T(8,128)} %bitcast.11), kind=kLoop, calls=%fused_computation | loop fusion | flops 34816 | bytes 278528 | tf_op jit(solution)/shard_map/concatenate | solution.py:231
  1.6 0.6 %pack.1.refs_0_ = f32[272,128]{1,0:T(8,128)S(1)} custom-call(f32[272,128]{1,0:T(8,128)S(1)} %pad_maximum_fusion.rows), custom_call_target="tpu_custom_call" | custom-call | tf_op jit(solution)/shard_map/pack/pallas_call | solution.py:224
  2.1 3.0 %collective-permute-start = (f32[272,128]{1,0:T(8,128)S(1)}, f32[272,128]{1,0:T(8,128)S(1)}, u32[]{:S(2)}, u32[]{:S(2)}) collective-permute-start(f32[272,128]{1,0:T(8,128)S(1)} %pack.1.refs_0_), channel_id=1, source_target_pairs={{2,0},{3,1},{0,2},{1,3},{6,4},{7,5},{4,6},{5,7},{10,8},{11,9},{8,1... | collective-permute-start | bytes 417800 | tf_op jit(solution)/shard_map/ppermute | solution.py:546
  5.1 1.5 %collective-permute-start.3 = (f32[272,128]{1,0:T(8,128)S(1)}, f32[272,128]{1,0:T(8,128)S(1)}, u32[]{:S(2)}, u32[]{:S(2)}) collective-permute-start(f32[272,128]{1,0:T(8,128)S(1)} %pack.1.refs_0_), channel_id=1, source_target_pairs={{4,0},{5,1},{6,2},{7,3},{0,4},{1,5},{2,6},{3,7},{12,8},{13,9},{14,... | collective-permute-start | bytes 417800 | tf_op jit(solution)/shard_map/ppermute | solution.py:546
  6.7 0.0 collective-permute-start.5
  7.3 4.1 %collective-permute-start.7 = (f32[136,128]{1,0:T(8,128)S(1)}, f32[136,128]{1,0:T(8,128)S(1)}, u32[]{:S(2)}, u32[]{:S(2)}) collective-permute-start(f32[136,128]{1,0:T(8,128)S(1)} %broadcast_in_dim.2.refs_0_), channel_id=1, source_target_pairs={{24,0},{16,8},{8,16},{0,24},{25,1},{17,9},{9,17},{1,25},{26,2},{18... | collective-permute-start | bytes 208904 | tf_op jit(solution)/shard_map/ppermute | solution.py:546
  11.5 0.0 collective-permute-start.8
  11.5 0.0 collective-permute-done.refs_2_
  11.5 0.0 collective-permute-start.2
  11.5 2.8 %collective-permute-done.7.refs_1_ = f32[136,128]{1,0:T(8,128)S(1)} collective-permute-done((f32[136,128]{1,0:T(8,128)S(1)}, f32[136,128]{1,0:T(8,128)S(1)}, u32[]{:S(2)}, u32[]{:S(2)}) %collective-permute-start.7) | collective-permute-done | bytes 69664 | tf_op jit(solution)/shard_map/ppermute | solution.py:546
  14.3 0.0 collective-permute-start.1
  14.3 0.0 collective-permute-done.3.refs_4_
  14.3 0.5 %collective-permute-start.4 = (f32[272,128]{1,0:T(8,128)S(1)}, f32[272,128]{1,0:T(8,128)S(1)}, u32[]{:S(2)}, u32[]{:S(2)}) collective-permute-start(f32[272,128]{1,0:T(8,128)S(1)} %collective-permute-done.3.refs_4_), channel_id=1, source_target_pairs={{1,0},{0,1},{3,2},{2,3},{5,4},{4,5},{7,6},{6,7},{9,8},{8,9},{11,10... | collective-permute-start | bytes 417800 | tf_op jit(solution)/shard_map/ppermute | solution.py:546
  14.8 0.0 collective-permute-done.5.refs_6_
  14.8 0.1 collective-permute-start.6
  14.8 1.3 %collective-permute-done.8.refs_2_ = f32[136,128]{1,0:T(8,128)S(1)} collective-permute-done((f32[136,128]{1,0:T(8,128)S(1)}, f32[136,128]{1,0:T(8,128)S(1)}, u32[]{:S(2)}, u32[]{:S(2)}) %collective-permute-start.8) | collective-permute-done | bytes 69664 | tf_op jit(solution)/shard_map/ppermute | solution.py:561
  16.1 0.0 collective-permute-start.9
  16.1 0.0 collective-permute-done.2.refs_3_
  16.1 0.0 collective-permute-done.1.refs_1_
  16.1 0.0 collective-permute-done.4.refs_5_
  16.1 0.0 collective-permute-done.6.refs_7_
  16.2 8.0 %krylov.1 = (bf16[6,16,16,1024]{3,2,1,0:T(8,128)(2,1)S(1)}, bf16[6,16,16,1024]{3,2,1,0:T(8,128)(2,1)S(1)}, f32[16,16,1024]{2,1,0:T(8,128)S(1)}, f32[13,16,128]{2,1,0:T(8,128)S(1)}) custom-call(f32[272,128]{1,0:T(8,128)S(1)} %pack.1.refs_0_, f32[272,128]{1,0:T(8,128)S(1)} %collective-permute-done.1.refs_1_, f32[272,128]{1,0:T(8,128)S(1)} %collective-permute-done.refs_2_, ...), custom_call_target="tpu_custom_call" | custom-call | tf_op jit(solution)/shard_map/krylov/pallas_call | solution.py:570
  24.1 0.0 collective-permute-done.9.refs_3_
  24.1 3.9 %gram.1 = (f32[2,64,64]{2,1,0:T(8,128)}, f32[2,64,64]{2,1,0:T(8,128)}) custom-call(f32[13,16,128]{2,1,0:T(8,128)S(1)} %get-tuple-element.12.scalars, f32[136,128]{1,0:T(8,128)S(1)} %broadcast_in_dim.2.refs_0_, f32[136,128]{1,0:T(8,128)S(1)} %collective-permute-done.7.refs_1_, f32[136,128]{1,0:T(8,128)S(1)} %collective-permute-done.8.refs_2_, ...), custom_call_target="tpu_custom_call" | custom-call | tf_op jit(solution)/shard_map/gram/pallas_call | solution.py:593
  (1 shorter events, 0.0 us)
Async XLA Ops:
  2.1 9.3 %collective-permute-start = (f32[272,128]{1,0:T(8,128)S(1)}, f32[272,128]{1,0:T(8,128)S(1)}, u32[]{:S(2)}, u32[]{:S(2)}) collective-permute-start(f32[272,128]{1,0:T(8,128)S(1)} %pack.1.refs_0_), channel_id=1, source_target_pairs={{2,0},{3,1},{0,2},{1,3},{6,4},{7,5},{4,6},{5,7},{10,8},{11,9},{8,1... | collective-permute-start | bytes 417800 | tf_op jit(solution)/shard_map/ppermute | solution.py:546
  5.1 9.1 %collective-permute-start.3 = (f32[272,128]{1,0:T(8,128)S(1)}, f32[272,128]{1,0:T(8,128)S(1)}, u32[]{:S(2)}, u32[]{:S(2)}) collective-permute-start(f32[272,128]{1,0:T(8,128)S(1)} %pack.1.refs_0_), channel_id=1, source_target_pairs={{4,0},{5,1},{6,2},{7,3},{0,4},{1,5},{2,6},{3,7},{12,8},{13,9},{14,... | collective-permute-start | bytes 417800 | tf_op jit(solution)/shard_map/ppermute | solution.py:546
  6.7 8.1 %collective-permute-start.5 = (f32[272,128]{1,0:T(8,128)S(1)}, f32[272,128]{1,0:T(8,128)S(1)}, u32[]{:S(2)}, u32[]{:S(2)}) collective-permute-start(f32[272,128]{1,0:T(8,128)S(1)} %pack.1.refs_0_), channel_id=1, source_target_pairs={{6,0},{7,1},{4,2},{5,3},{2,4},{3,5},{0,6},{1,7},{14,8},{15,9},{12,... | collective-permute-start | bytes 417800 | tf_op jit(solution)/shard_map/ppermute | solution.py:546
  7.3 6.9 %collective-permute-start.7 = (f32[136,128]{1,0:T(8,128)S(1)}, f32[136,128]{1,0:T(8,128)S(1)}, u32[]{:S(2)}, u32[]{:S(2)}) collective-permute-start(f32[136,128]{1,0:T(8,128)S(1)} %broadcast_in_dim.2.refs_0_), channel_id=1, source_target_pairs={{24,0},{16,8},{8,16},{0,24},{25,1},{17,9},{9,17},{1,25},{26,2},{18... | collective-permute-start | bytes 208904 | tf_op jit(solution)/shard_map/ppermute | solution.py:546
  11.5 4.7 %collective-permute-start.8 = (f32[136,128]{1,0:T(8,128)S(1)}, f32[136,128]{1,0:T(8,128)S(1)}, u32[]{:S(2)}, u32[]{:S(2)}) collective-permute-start(f32[136,128]{1,0:T(8,128)S(1)} %broadcast_in_dim.2.refs_0_), channel_id=1, source_target_pairs={{8,0},{17,1},{10,2},{19,3},{12,4},{21,5},{14,6},{23,7},{0,8},{25,9... | collective-permute-start | bytes 208904 | tf_op jit(solution)/shard_map/ppermute | solution.py:561
  11.5 4.7 %collective-permute-start.2 = (f32[272,128]{1,0:T(8,128)S(1)}, f32[272,128]{1,0:T(8,128)S(1)}, u32[]{:S(2)}, u32[]{:S(2)}) collective-permute-start(f32[272,128]{1,0:T(8,128)S(1)} %collective-permute-done.refs_2_), channel_id=1, source_target_pairs={{1,0},{0,1},{3,2},{2,3},{5,4},{4,5},{7,6},{6,7},{9,8},{8,9},{11,10... | collective-permute-start | bytes 417800 | tf_op jit(solution)/shard_map/ppermute | solution.py:546
  14.3 1.9 %collective-permute-start.1 = (f32[272,128]{1,0:T(8,128)S(1)}, f32[272,128]{1,0:T(8,128)S(1)}, u32[]{:S(2)}, u32[]{:S(2)}) collective-permute-start(f32[272,128]{1,0:T(8,128)S(1)} %pack.1.refs_0_), channel_id=1, source_target_pairs={{1,0},{0,1},{3,2},{2,3},{5,4},{4,5},{7,6},{6,7},{9,8},{8,9},{11,10... | collective-permute-start | bytes 417800 | tf_op jit(solution)/shard_map/ppermute | solution.py:546
  14.3 1.9 %collective-permute-start.4 = (f32[272,128]{1,0:T(8,128)S(1)}, f32[272,128]{1,0:T(8,128)S(1)}, u32[]{:S(2)}, u32[]{:S(2)}) collective-permute-start(f32[272,128]{1,0:T(8,128)S(1)} %collective-permute-done.3.refs_4_), channel_id=1, source_target_pairs={{1,0},{0,1},{3,2},{2,3},{5,4},{4,5},{7,6},{6,7},{9,8},{8,9},{11,10... | collective-permute-start | bytes 417800 | tf_op jit(solution)/shard_map/ppermute | solution.py:546
  14.8 1.4 %collective-permute-start.6 = (f32[272,128]{1,0:T(8,128)S(1)}, f32[272,128]{1,0:T(8,128)S(1)}, u32[]{:S(2)}, u32[]{:S(2)}) collective-permute-start(f32[272,128]{1,0:T(8,128)S(1)} %collective-permute-done.5.refs_6_), channel_id=1, source_target_pairs={{1,0},{0,1},{3,2},{2,3},{5,4},{4,5},{7,6},{6,7},{9,8},{8,9},{11,10... | collective-permute-start | bytes 417800 | tf_op jit(solution)/shard_map/ppermute | solution.py:546
  16.1 8.0 %collective-permute-start.9 = (f32[136,128]{1,0:T(8,128)S(1)}, f32[136,128]{1,0:T(8,128)S(1)}, u32[]{:S(2)}, u32[]{:S(2)}) collective-permute-start(f32[136,128]{1,0:T(8,128)S(1)} %collective-permute-done.8.refs_2_), channel_id=1, source_target_pairs={{1,0},{0,1},{3,2},{2,3},{5,4},{4,5},{7,6},{6,7},{9,8},{8,9},{11,10... | collective-permute-start | bytes 208904 | tf_op jit(solution)/shard_map/ppermute | solution.py:546

commit v27 on v26

--- a/solution.py
+++ b/solution.py
@@ -505,7 +505,7 @@
     size = BASIS * count
     here = lax.axis_index("point")
     core = jnp.bitwise_and(lax.axis_index("dom"), CORES - 1)
-    for far, tile in zip((0, 3, 1 + core, 2 - core), tiles):
+    for far, tile in zip((0, 1 + core, 3, 2 - core), tiles):
         limits[jnp.bitwise_xor(here, far)] = tile[:SUB, :]
 
     bounds = [jnp.concatenate([limits[j]] * groups, axis=0) for j in range(points)]
@@ -558,9 +558,9 @@
         for point in range(points)
         for part in range(parts)
     ]
-    tiles = [swapped(tile, "point", points, 3), lax.ppermute(tile, ("point", "dom"), mixed)]
+    tiles = [lax.ppermute(tile, ("point", "dom"), mixed), swapped(tile, "point", points, 3)]
     tiles = list(lax.optimization_barrier(tuple(tiles)))
-    tiles.append(swapped(tiles[1], "dom", parts, 1))
+    tiles.append(swapped(tiles[0], "dom", parts, 1))
     own, even[1] = lax.optimization_barrier((block, even[1]))
     odd = [swapped(value, "dom", parts, 1) for value in [own] + even[1:]]
     blocks = [value for pair in zip(even, odd) for value in pair]

time: 28.3 us -> 27.9 us (0.986)
  waiting for transfers between devices: 4.08 us -> 2.87 us
  starting transfers between devices: 9.25 us -> 10.1 us
    ppermute x1, starting transfers between devices: 0.01 us -> 2.1 us  [whole_grid(): lax.ppermute(tile, ('point', 'dom'), mixed)]
    ppermute x1, waiting for transfers between devices: 1.29 us -> 0.01 us  [whole_grid(): lax.ppermute(tile, ('point', 'dom'), mixed)]
    ppermute x9, starting transfers between devices: 9.25 us -> 8.04 us  [swapped(): lax.ppermute(values, axis, [(index ^ mask, index) for index in range(size)])]
  transfers between devices with their start and end apart: 10 -> 10, of which waited for: 2 -> 2; matrix products, arithmetic and copies ran while one was open for 0% -> 0% of each run, Pallas kernels for 28% -> 29%
where the time goes in v27:
time: 27.9 us; the launch traced here: 27.7 us
  Pallas kernels  12.4 us (44%)
  starting transfers between devices  10.1 us (36%)
  waiting for transfers between devices  2.87 us (10%)
  between operations  1.33 us (5%)
  other arithmetic  0.93 us (3%)
    ppermute x9, starting transfers between devices, swapped(): lax.ppermute(values, axis, [(index ^ mask, index) for index in range(size)])  8.04 us
    pallas_call x1, Pallas kernels, whole_grid(): pl.pallas_call(functools.partial(krylov_kernel, parts, count), out_shape=...  7.95 us
    pallas_call x1, Pallas kernels, whole_grid(): pl.pallas_call(functools.partial(gram_kernel, points), out_shape=(out, ou...  3.88 us
    ppermute x9, waiting for transfers between devices, swapped(): lax.ppermute(values, axis, [(index ^ mask, index) for index in range(size)])  2.87 us
    ppermute x1, starting transfers between devices, whole_grid(): lax.ppermute(tile, ('point', 'dom'), mixed)  2.1 us
    concatenate x1, other arithmetic, packed_block(): jnp.concatenate([rows, levels], axis=0)  0.93 us
  transfers between devices with their start and end apart: 10, of which 2 were waited for; matrix products, arithmetic and copies ran while one was open for 0% of the time, Pallas kernels for 29%

profile of v27, /device:TPU:0, one launch (start us, length us, event | category | flops | bytes accessed | tf_op | source)
XLA Modules:
  0.0 27.7 jit_solution(13287895153362793050)
XLA Ops:
  0.6 0.9 %pad_maximum_fusion.rows = f32[272,128]{1,0:T(8,128)S(1)} fusion(f32[16,128]{1,0:T(8,128)} %bitcast.12, f32[256,128]{1,0:T(8,128)} %bitcast.11), kind=kLoop, calls=%fused_computation | loop fusion | flops 34816 | bytes 278528 | tf_op jit(solution)/shard_map/concatenate | solution.py:231
  1.6 0.6 %pack.1.refs_0_ = f32[272,128]{1,0:T(8,128)S(1)} custom-call(f32[272,128]{1,0:T(8,128)S(1)} %pad_maximum_fusion.rows), custom_call_target="tpu_custom_call" | custom-call | tf_op jit(solution)/shard_map/pack/pallas_call | solution.py:224
  2.1 3.0 %collective-permute-start = (f32[272,128]{1,0:T(8,128)S(1)}, f32[272,128]{1,0:T(8,128)S(1)}, u32[]{:S(2)}, u32[]{:S(2)}) collective-permute-start(f32[272,128]{1,0:T(8,128)S(1)} %pack.1.refs_0_), channel_id=1, source_target_pairs={{2,0},{3,1},{0,2},{1,3},{6,4},{7,5},{4,6},{5,7},{10,8},{11,9},{8,1... | collective-permute-start | bytes 417800 | tf_op jit(solution)/shard_map/ppermute | solution.py:546
  5.1 1.5 %collective-permute-start.3 = (f32[272,128]{1,0:T(8,128)S(1)}, f32[272,128]{1,0:T(8,128)S(1)}, u32[]{:S(2)}, u32[]{:S(2)}) collective-permute-start(f32[272,128]{1,0:T(8,128)S(1)} %pack.1.refs_0_), channel_id=1, source_target_pairs={{4,0},{5,1},{6,2},{7,3},{0,4},{1,5},{2,6},{3,7},{12,8},{13,9},{14,... | collective-permute-start | bytes 417800 | tf_op jit(solution)/shard_map/ppermute | solution.py:546
  6.7 0.0 collective-permute-start.5
  7.3 2.1 %collective-permute-start.7 = (f32[136,128]{1,0:T(8,128)S(1)}, f32[136,128]{1,0:T(8,128)S(1)}, u32[]{:S(2)}, u32[]{:S(2)}) collective-permute-start(f32[136,128]{1,0:T(8,128)S(1)} %broadcast_in_dim.2.refs_0_), channel_id=1, source_target_pairs={{8,0},{17,1},{10,2},{19,3},{12,4},{21,5},{14,6},{23,7},{0,8},{25,9... | collective-permute-start | bytes 208904 | tf_op jit(solution)/shard_map/ppermute | solution.py:561
  9.4 2.5 %collective-permute-start.8 = (f32[136,128]{1,0:T(8,128)S(1)}, f32[136,128]{1,0:T(8,128)S(1)}, u32[]{:S(2)}, u32[]{:S(2)}) collective-permute-start(f32[136,128]{1,0:T(8,128)S(1)} %broadcast_in_dim.2.refs_0_), channel_id=1, source_target_pairs={{24,0},{16,8},{8,16},{0,24},{25,1},{17,9},{9,17},{1,25},{26,2},{18... | collective-permute-start | bytes 208904 | tf_op jit(solution)/shard_map/ppermute | solution.py:546
  11.9 0.0 collective-permute-done.refs_2_
  11.9 0.0 collective-permute-start.2
  11.9 0.0 collective-permute-done.7.refs_1_
  11.9 0.5 %collective-permute-start.1 = (f32[272,128]{1,0:T(8,128)S(1)}, f32[272,128]{1,0:T(8,128)S(1)}, u32[]{:S(2)}, u32[]{:S(2)}) collective-permute-start(f32[272,128]{1,0:T(8,128)S(1)} %pack.1.refs_0_), channel_id=1, source_target_pairs={{1,0},{0,1},{3,2},{2,3},{5,4},{4,5},{7,6},{6,7},{9,8},{8,9},{11,10... | collective-permute-start | bytes 417800 | tf_op jit(solution)/shard_map/ppermute | solution.py:546
  12.4 0.8 %collective-permute-done.3.refs_4_ = f32[272,128]{1,0:T(8,128)S(1)} collective-permute-done((f32[272,128]{1,0:T(8,128)S(1)}, f32[272,128]{1,0:T(8,128)S(1)}, u32[]{:S(2)}, u32[]{:S(2)}) %collective-permute-start.3) | collective-permute-done | bytes 139296 | tf_op jit(solution)/shard_map/ppermute | solution.py:546
  13.2 0.0 collective-permute-start.4
  13.2 0.0 collective-permute-done.5.refs_6_
  13.3 0.5 %collective-permute-start.6 = (f32[272,128]{1,0:T(8,128)S(1)}, f32[272,128]{1,0:T(8,128)S(1)}, u32[]{:S(2)}, u32[]{:S(2)}) collective-permute-start(f32[272,128]{1,0:T(8,128)S(1)} %collective-permute-done.5.refs_6_), channel_id=1, source_target_pairs={{1,0},{0,1},{3,2},{2,3},{5,4},{4,5},{7,6},{6,7},{9,8},{8,9},{11,10... | collective-permute-start | bytes 417800 | tf_op jit(solution)/shard_map/ppermute | solution.py:546
  13.8 2.0 %collective-permute-done.8.refs_2_ = f32[136,128]{1,0:T(8,128)S(1)} collective-permute-done((f32[136,128]{1,0:T(8,128)S(1)}, f32[136,128]{1,0:T(8,128)S(1)}, u32[]{:S(2)}, u32[]{:S(2)}) %collective-permute-start.8) | collective-permute-done | bytes 69664 | tf_op jit(solution)/shard_map/ppermute | solution.py:546
  15.8 0.0 collective-permute-start.9
  15.8 0.0 collective-permute-done.2.refs_3_
  15.8 0.0 collective-permute-done.1.refs_1_
  15.8 0.0 collective-permute-done.4.refs_5_
  15.8 0.0 collective-permute-done.6.refs_7_
  15.8 8.0 %krylov.1 = (bf16[6,16,16,1024]{3,2,1,0:T(8,128)(2,1)S(1)}, bf16[6,16,16,1024]{3,2,1,0:T(8,128)(2,1)S(1)}, f32[16,16,1024]{2,1,0:T(8,128)S(1)}, f32[13,16,128]{2,1,0:T(8,128)S(1)}) custom-call(f32[272,128]{1,0:T(8,128)S(1)} %pack.1.refs_0_, f32[272,128]{1,0:T(8,128)S(1)} %collective-permute-done.1.refs_1_, f32[272,128]{1,0:T(8,128)S(1)} %collective-permute-done.refs_2_, ...), custom_call_target="tpu_custom_call" | custom-call | tf_op jit(solution)/shard_map/krylov/pallas_call | solution.py:570
  23.8 0.0 collective-permute-done.9.refs_3_
  23.8 3.9 %gram.1 = (f32[2,64,64]{2,1,0:T(8,128)}, f32[2,64,64]{2,1,0:T(8,128)}) custom-call(f32[13,16,128]{2,1,0:T(8,128)S(1)} %get-tuple-element.12.scalars, f32[136,128]{1,0:T(8,128)S(1)} %broadcast_in_dim.2.refs_0_, f32[136,128]{1,0:T(8,128)S(1)} %collective-permute-done.7.refs_1_, f32[136,128]{1,0:T(8,128)S(1)} %collective-permute-done.8.refs_2_, ...), custom_call_target="tpu_custom_call" | custom-call | tf_op jit(solution)/shard_map/gram/pallas_call | solution.py:593
  (1 shorter events, 0.0 us)
Async XLA Ops:
  2.1 9.8 %collective-permute-start = (f32[272,128]{1,0:T(8,128)S(1)}, f32[272,128]{1,0:T(8,128)S(1)}, u32[]{:S(2)}, u32[]{:S(2)}) collective-permute-start(f32[272,128]{1,0:T(8,128)S(1)} %pack.1.refs_0_), channel_id=1, source_target_pairs={{2,0},{3,1},{0,2},{1,3},{6,4},{7,5},{4,6},{5,7},{10,8},{11,9},{8,1... | collective-permute-start | bytes 417800 | tf_op jit(solution)/shard_map/ppermute | solution.py:546
  5.1 8.1 %collective-permute-start.3 = (f32[272,128]{1,0:T(8,128)S(1)}, f32[272,128]{1,0:T(8,128)S(1)}, u32[]{:S(2)}, u32[]{:S(2)}) collective-permute-start(f32[272,128]{1,0:T(8,128)S(1)} %pack.1.refs_0_), channel_id=1, source_target_pairs={{4,0},{5,1},{6,2},{7,3},{0,4},{1,5},{2,6},{3,7},{12,8},{13,9},{14,... | collective-permute-start | bytes 417800 | tf_op jit(solution)/shard_map/ppermute | solution.py:546
  6.7 6.6 %collective-permute-start.5 = (f32[272,128]{1,0:T(8,128)S(1)}, f32[272,128]{1,0:T(8,128)S(1)}, u32[]{:S(2)}, u32[]{:S(2)}) collective-permute-start(f32[272,128]{1,0:T(8,128)S(1)} %pack.1.refs_0_), channel_id=1, source_target_pairs={{6,0},{7,1},{4,2},{5,3},{2,4},{3,5},{0,6},{1,7},{14,8},{15,9},{12,... | collective-permute-start | bytes 417800 | tf_op jit(solution)/shard_map/ppermute | solution.py:546
  7.3 4.6 %collective-permute-start.7 = (f32[136,128]{1,0:T(8,128)S(1)}, f32[136,128]{1,0:T(8,128)S(1)}, u32[]{:S(2)}, u32[]{:S(2)}) collective-permute-start(f32[136,128]{1,0:T(8,128)S(1)} %broadcast_in_dim.2.refs_0_), channel_id=1, source_target_pairs={{8,0},{17,1},{10,2},{19,3},{12,4},{21,5},{14,6},{23,7},{0,8},{25,9... | collective-permute-start | bytes 208904 | tf_op jit(solution)/shard_map/ppermute | solution.py:561
  9.4 6.4 %collective-permute-start.8 = (f32[136,128]{1,0:T(8,128)S(1)}, f32[136,128]{1,0:T(8,128)S(1)}, u32[]{:S(2)}, u32[]{:S(2)}) collective-permute-start(f32[136,128]{1,0:T(8,128)S(1)} %broadcast_in_dim.2.refs_0_), channel_id=1, source_target_pairs={{24,0},{16,8},{8,16},{0,24},{25,1},{17,9},{9,17},{1,25},{26,2},{18... | collective-permute-start | bytes 208904 | tf_op jit(solution)/shard_map/ppermute | solution.py:546
  11.9 3.9 %collective-permute-start.2 = (f32[272,128]{1,0:T(8,128)S(1)}, f32[272,128]{1,0:T(8,128)S(1)}, u32[]{:S(2)}, u32[]{:S(2)}) collective-permute-start(f32[272,128]{1,0:T(8,128)S(1)} %collective-permute-done.refs_2_), channel_id=1, source_target_pairs={{1,0},{0,1},{3,2},{2,3},{5,4},{4,5},{7,6},{6,7},{9,8},{8,9},{11,10... | collective-permute-start | bytes 417800 | tf_op jit(solution)/shard_map/ppermute | solution.py:546
  11.9 3.9 %collective-permute-start.1 = (f32[272,128]{1,0:T(8,128)S(1)}, f32[272,128]{1,0:T(8,128)S(1)}, u32[]{:S(2)}, u32[]{:S(2)}) collective-permute-start(f32[272,128]{1,0:T(8,128)S(1)} %pack.1.refs_0_), channel_id=1, source_target_pairs={{1,0},{0,1},{3,2},{2,3},{5,4},{4,5},{7,6},{6,7},{9,8},{8,9},{11,10... | collective-permute-start | bytes 417800 | tf_op jit(solution)/shard_map/ppermute | solution.py:546
  13.2 2.6 %collective-permute-start.4 = (f32[272,128]{1,0:T(8,128)S(1)}, f32[272,128]{1,0:T(8,128)S(1)}, u32[]{:S(2)}, u32[]{:S(2)}) collective-permute-start(f32[272,128]{1,0:T(8,128)S(1)} %collective-permute-done.3.refs_4_), channel_id=1, source_target_pairs={{1,0},{0,1},{3,2},{2,3},{5,4},{4,5},{7,6},{6,7},{9,8},{8,9},{11,10... | collective-permute-start | bytes 417800 | tf_op jit(solution)/shard_map/ppermute | solution.py:546
  13.3 2.6 %collective-permute-start.6 = (f32[272,128]{1,0:T(8,128)S(1)}, f32[272,128]{1,0:T(8,128)S(1)}, u32[]{:S(2)}, u32[]{:S(2)}) collective-permute-start(f32[272,128]{1,0:T(8,128)S(1)} %collective-permute-done.5.refs_6_), channel_id=1, source_target_pairs={{1,0},{0,1},{3,2},{2,3},{5,4},{4,5},{7,6},{6,7},{9,8},{8,9},{11,10... | collective-permute-start | bytes 417800 | tf_op jit(solution)/shard_map/ppermute | solution.py:546
  15.8 8.0 %collective-permute-start.9 = (f32[136,128]{1,0:T(8,128)S(1)}, f32[136,128]{1,0:T(8,128)S(1)}, u32[]{:S(2)}, u32[]{:S(2)}) collective-permute-start(f32[136,128]{1,0:T(8,128)S(1)} %collective-permute-done.7.refs_1_), channel_id=1, source_target_pairs={{1,0},{0,1},{3,2},{2,3},{5,4},{4,5},{7,6},{6,7},{9,8},{8,9},{11,10... | collective-permute-start | bytes 208904 | tf_op jit(solution)/shard_map/ppermute | solution.py:546

commit v28 on v27

--- a/solution.py
+++ b/solution.py
@@ -498,15 +498,17 @@
 
 
 def gram_kernel(points, scalars, *refs):
-    tiles = refs[:points]
-    highs, lows, applied, out_b, out_a, limits = refs[points:]
+    tile, mixed, far, other_mixed, other_far = refs[: points + 1]
+    highs, lows, applied, out_b, out_a, limits = refs[points + 1 :]
     planes, count, _ = applied.shape
     groups = count // SUB
     size = BASIS * count
     here = lax.axis_index("point")
     core = jnp.bitwise_and(lax.axis_index("dom"), CORES - 1)
-    for far, tile in zip((0, 1 + core, 3, 2 - core), tiles):
-        limits[jnp.bitwise_xor(here, far)] = tile[:SUB, :]
+    limits[here] = tile[:SUB, :]
+    limits[jnp.bitwise_xor(here, 1 + core)] = mixed[:SUB, :]
+    limits[jnp.bitwise_xor(here, 2 - core)] = other_mixed[:SUB, :]
+    limits[jnp.bitwise_xor(here, 3)] = jnp.where(core == 0, far[:SUB, :], other_far[:SUB, :])
 
     bounds = [jnp.concatenate([limits[j]] * groups, axis=0) for j in range(points)]
     alphas = [scalars[i] for i in range(ITERS)]
@@ -558,9 +560,14 @@
         for point in range(points)
         for part in range(parts)
     ]
-    tiles = [lax.ppermute(tile, ("point", "dom"), mixed), swapped(tile, "point", points, 3)]
+    far = [
+        ((point ^ 3) * parts + part, point * parts + part)
+        for point in range(points)
+        for part in range(0, parts, CORES)
+    ]
+    tiles = [lax.ppermute(tile, ("point", "dom"), pairs) for pairs in (mixed, far)]
     tiles = list(lax.optimization_barrier(tuple(tiles)))
-    tiles.append(swapped(tiles[0], "dom", parts, 1))
+    tiles += [swapped(value, "dom", parts, 1) for value in tiles]
     own, even[1] = lax.optimization_barrier((block, even[1]))
     odd = [swapped(value, "dom", parts, 1) for value in [own] + even[1:]]
     blocks = [value for pair in zip(even, odd) for value in pair]
@@ -593,7 +600,7 @@
     return pl.pallas_call(
         functools.partial(gram_kernel, points),
         out_shape=(out, out),
-        in_specs=[vmem] * (4 + points),
+        in_specs=[vmem] * (5 + points),
         out_specs=(vmem, vmem),
         scratch_shapes=[pltpu.VMEM((points, SUB, LANES), jnp.float32)],
         compiler_params=pltpu.CompilerParams(vmem_limit_bytes=16 * 2**20),

time: 27.9 us -> 30.2 us (1.082)
  starting transfers between devices: 10.1 us -> 13.5 us
  waiting for transfers between devices: 2.87 us -> 1.77 us
    ppermute x1 -> x2, starting transfers between devices: 2.1 us -> 7.76 us  [whole_grid(): lax.ppermute(tile, ('point', 'dom'), pairs)]
    ppermute x9, waiting for transfers between devices: 2.87 us -> 0.02 us  [swapped(): lax.ppermute(values, axis, [(index ^ mask, index) for index in range(size)])]
    ppermute x9, starting transfers between devices: 8.04 us -> 5.7 us  [swapped(): lax.ppermute(values, axis, [(index ^ mask, index) for index in range(size)])]
    ppermute x1 -> x2, waiting for transfers between devices: 0.01 us -> 1.74 us  [whole_grid(): lax.ppermute(tile, ('point', 'dom'), pairs)]
  transfers between devices with their start and end apart: 10 -> 11, of which waited for: 2 -> 1; matrix products, arithmetic and copies ran while one was open for 0% -> 0% of each run, Pallas kernels for 29% -> 27%
where the time goes in v28:
time: 30.2 us; the launch traced here: 29.9 us
  starting transfers between devices  13.5 us (45%)
  Pallas kernels  12.4 us (41%)
  waiting for transfers between devices  1.77 us (6%)
  between operations  1.34 us (4%)
  other arithmetic  0.93 us (3%)
    pallas_call x1, Pallas kernels, whole_grid(): pl.pallas_call(functools.partial(krylov_kernel, parts, count), out_shape=...  7.95 us
    ppermute x2, starting transfers between devices, whole_grid(): lax.ppermute(tile, ('point', 'dom'), pairs)  7.76 us
    ppermute x9, starting transfers between devices, swapped(): lax.ppermute(values, axis, [(index ^ mask, index) for index in range(size)])  5.7 us
    pallas_call x1, Pallas kernels, whole_grid(): pl.pallas_call(functools.partial(gram_kernel, points), out_shape=(out, ou...  3.88 us
    ppermute x2, waiting for transfers between devices, whole_grid(): lax.ppermute(tile, ('point', 'dom'), pairs)  1.74 us
    concatenate x1, other arithmetic, packed_block(): jnp.concatenate([rows, levels], axis=0)  0.93 us
  transfers between devices with their start and end apart: 11, of which 1 were waited for; matrix products, arithmetic and copies ran while one was open for 0% of the time, Pallas kernels for 27%

profile of v28, /device:TPU:0, one launch (start us, length us, event | category | flops | bytes accessed | tf_op | source)
XLA Modules:
  0.0 29.9 jit_solution(15477917772740921006)
XLA Ops:
  0.6 0.9 %pad_maximum_fusion.rows = f32[272,128]{1,0:T(8,128)S(1)} fusion(f32[16,128]{1,0:T(8,128)} %bitcast.12, f32[256,128]{1,0:T(8,128)} %bitcast.11), kind=kLoop, calls=%fused_computation | loop fusion | flops 34816 | bytes 278528 | tf_op jit(solution)/shard_map/concatenate | solution.py:231
  1.6 0.6 %pack.1.refs_0_ = f32[272,128]{1,0:T(8,128)S(1)} custom-call(f32[272,128]{1,0:T(8,128)S(1)} %pad_maximum_fusion.rows), custom_call_target="tpu_custom_call" | custom-call | tf_op jit(solution)/shard_map/pack/pallas_call | solution.py:224
  2.1 3.0 %collective-permute-start = (f32[272,128]{1,0:T(8,128)S(1)}, f32[272,128]{1,0:T(8,128)S(1)}, u32[]{:S(2)}, u32[]{:S(2)}) collective-permute-start(f32[272,128]{1,0:T(8,128)S(1)} %pack.1.refs_0_), channel_id=1, source_target_pairs={{2,0},{3,1},{0,2},{1,3},{6,4},{7,5},{4,6},{5,7},{10,8},{11,9},{8,1... | collective-permute-start | bytes 417800 | tf_op jit(solution)/shard_map/ppermute | solution.py:548
  5.1 1.5 %collective-permute-start.3 = (f32[272,128]{1,0:T(8,128)S(1)}, f32[272,128]{1,0:T(8,128)S(1)}, u32[]{:S(2)}, u32[]{:S(2)}) collective-permute-start(f32[272,128]{1,0:T(8,128)S(1)} %pack.1.refs_0_), channel_id=1, source_target_pairs={{4,0},{5,1},{6,2},{7,3},{0,4},{1,5},{2,6},{3,7},{12,8},{13,9},{14,... | collective-permute-start | bytes 417800 | tf_op jit(solution)/shard_map/ppermute | solution.py:548
  6.7 0.0 collective-permute-start.5
  7.3 2.1 %collective-permute-start.7 = (f32[136,128]{1,0:T(8,128)S(1)}, f32[136,128]{1,0:T(8,128)S(1)}, u32[]{:S(2)}, u32[]{:S(2)}) collective-permute-start(f32[136,128]{1,0:T(8,128)S(1)} %broadcast_in_dim.2.refs_0_), channel_id=1, source_target_pairs={{8,0},{17,1},{10,2},{19,3},{12,4},{21,5},{14,6},{23,7},{0,8},{25,9... | collective-permute-start | bytes 208904 | tf_op jit(solution)/shard_map/ppermute | solution.py:568
  9.4 0.0 collective-permute-done.refs_2_
  9.4 0.0 collective-permute-start.2
  9.4 5.7 %collective-permute-start.8 = (f32[136,128]{1,0:T(8,128)S(1)}, f32[136,128]{1,0:T(8,128)S(1)}, u32[]{:S(2)}, u32[]{:S(2)}) collective-permute-start(f32[136,128]{1,0:T(8,128)S(1)} %broadcast_in_dim.2.refs_0_), channel_id=1, source_target_pairs={{24,0},{26,2},{28,4},{30,6},{16,8},{18,10},{20,12},{22,14},{8,16},... | collective-permute-start | bytes 208904 | tf_op jit(solution)/shard_map/ppermute | solution.py:568
  15.1 0.0 collective-permute-done.7.refs_1_
  15.1 0.1 collective-permute-start.1
  15.2 0.0 collective-permute-done.3.refs_4_
  15.2 0.5 %collective-permute-start.4 = (f32[272,128]{1,0:T(8,128)S(1)}, f32[272,128]{1,0:T(8,128)S(1)}, u32[]{:S(2)}, u32[]{:S(2)}) collective-permute-start(f32[272,128]{1,0:T(8,128)S(1)} %collective-permute-done.3.refs_4_), channel_id=1, source_target_pairs={{1,0},{0,1},{3,2},{2,3},{5,4},{4,5},{7,6},{6,7},{9,8},{8,9},{11,10... | collective-permute-start | bytes 417800 | tf_op jit(solution)/shard_map/ppermute | solution.py:548
  15.7 0.0 collective-permute-done.5.refs_6_
  15.7 0.1 collective-permute-start.6
  15.8 1.7 %collective-permute-done.8.refs_2_ = f32[136,128]{1,0:T(8,128)S(1)} collective-permute-done((f32[136,128]{1,0:T(8,128)S(1)}, f32[136,128]{1,0:T(8,128)S(1)}, u32[]{:S(2)}, u32[]{:S(2)}) %collective-permute-start.8) | collective-permute-done | bytes 69664 | tf_op jit(solution)/shard_map/ppermute | solution.py:568
  17.5 0.0 collective-permute-start.10
  17.5 0.0 collective-permute-done.2.refs_3_
  17.5 0.5 %collective-permute-start.9 = (f32[136,128]{1,0:T(8,128)S(1)}, f32[136,128]{1,0:T(8,128)S(1)}, u32[]{:S(2)}, u32[]{:S(2)}) collective-permute-start(f32[136,128]{1,0:T(8,128)S(1)} %collective-permute-done.7.refs_1_), channel_id=1, source_target_pairs={{1,0},{0,1},{3,2},{2,3},{5,4},{4,5},{7,6},{6,7},{9,8},{8,9},{11,10... | collective-permute-start | bytes 208904 | tf_op jit(solution)/shard_map/ppermute | solution.py:548
  18.1 0.0 collective-permute-done.1.refs_1_
  18.1 0.0 collective-permute-done.4.refs_5_
  18.1 0.0 collective-permute-done.6.refs_7_
  18.1 8.0 %krylov.1 = (bf16[6,16,16,1024]{3,2,1,0:T(8,128)(2,1)S(1)}, bf16[6,16,16,1024]{3,2,1,0:T(8,128)(2,1)S(1)}, f32[16,16,1024]{2,1,0:T(8,128)S(1)}, f32[13,16,128]{2,1,0:T(8,128)S(1)}) custom-call(f32[272,128]{1,0:T(8,128)S(1)} %pack.1.refs_0_, f32[272,128]{1,0:T(8,128)S(1)} %collective-permute-done.1.refs_1_, f32[272,128]{1,0:T(8,128)S(1)} %collective-permute-done.refs_2_, ...), custom_call_target="tpu_custom_call" | custom-call | tf_op jit(solution)/shard_map/krylov/pallas_call | solution.py:577
  26.0 0.0 collective-permute-done.10.refs_4_
  26.0 0.0 collective-permute-done.9.refs_3_
  26.0 3.9 %gram.1 = (f32[2,64,64]{2,1,0:T(8,128)}, f32[2,64,64]{2,1,0:T(8,128)}) custom-call(f32[13,16,128]{2,1,0:T(8,128)S(1)} %get-tuple-element.12.scalars, f32[136,128]{1,0:T(8,128)S(1)} %broadcast_in_dim.2.refs_0_, f32[136,128]{1,0:T(8,128)S(1)} %collective-permute-done.7.refs_1_, f32[136,128]{1,0:T(8,128)S(1)} %collective-permute-done.8.refs_2_, ...), custom_call_target="tpu_custom_call" | custom-call | tf_op jit(solution)/shard_map/gram/pallas_call | solution.py:600
  (1 shorter events, 0.0 us)
Async XLA Ops:
  2.1 7.3 %collective-permute-start = (f32[272,128]{1,0:T(8,128)S(1)}, f32[272,128]{1,0:T(8,128)S(1)}, u32[]{:S(2)}, u32[]{:S(2)}) collective-permute-start(f32[272,128]{1,0:T(8,128)S(1)} %pack.1.refs_0_), channel_id=1, source_target_pairs={{2,0},{3,1},{0,2},{1,3},{6,4},{7,5},{4,6},{5,7},{10,8},{11,9},{8,1... | collective-permute-start | bytes 417800 | tf_op jit(solution)/shard_map/ppermute | solution.py:548
  5.1 10.1 %collective-permute-start.3 = (f32[272,128]{1,0:T(8,128)S(1)}, f32[272,128]{1,0:T(8,128)S(1)}, u32[]{:S(2)}, u32[]{:S(2)}) collective-permute-start(f32[272,128]{1,0:T(8,128)S(1)} %pack.1.refs_0_), channel_id=1, source_target_pairs={{4,0},{5,1},{6,2},{7,3},{0,4},{1,5},{2,6},{3,7},{12,8},{13,9},{14,... | collective-permute-start | bytes 417800 | tf_op jit(solution)/shard_map/ppermute | solution.py:548
  6.7 9.1 %collective-permute-start.5 = (f32[272,128]{1,0:T(8,128)S(1)}, f32[272,128]{1,0:T(8,128)S(1)}, u32[]{:S(2)}, u32[]{:S(2)}) collective-permute-start(f32[272,128]{1,0:T(8,128)S(1)} %pack.1.refs_0_), channel_id=1, source_target_pairs={{6,0},{7,1},{4,2},{5,3},{2,4},{3,5},{0,6},{1,7},{14,8},{15,9},{12,... | collective-permute-start | bytes 417800 | tf_op jit(solution)/shard_map/ppermute | solution.py:548
  7.3 7.8 %collective-permute-start.7 = (f32[136,128]{1,0:T(8,128)S(1)}, f32[136,128]{1,0:T(8,128)S(1)}, u32[]{:S(2)}, u32[]{:S(2)}) collective-permute-start(f32[136,128]{1,0:T(8,128)S(1)} %broadcast_in_dim.2.refs_0_), channel_id=1, source_target_pairs={{8,0},{17,1},{10,2},{19,3},{12,4},{21,5},{14,6},{23,7},{0,8},{25,9... | collective-permute-start | bytes 208904 | tf_op jit(solution)/shard_map/ppermute | solution.py:568
  9.4 8.1 %collective-permute-start.2 = (f32[272,128]{1,0:T(8,128)S(1)}, f32[272,128]{1,0:T(8,128)S(1)}, u32[]{:S(2)}, u32[]{:S(2)}) collective-permute-start(f32[272,128]{1,0:T(8,128)S(1)} %collective-permute-done.refs_2_), channel_id=1, source_target_pairs={{1,0},{0,1},{3,2},{2,3},{5,4},{4,5},{7,6},{6,7},{9,8},{8,9},{11,10... | collective-permute-start | bytes 417800 | tf_op jit(solution)/shard_map/ppermute | solution.py:548
  9.4 8.1 %collective-permute-start.8 = (f32[136,128]{1,0:T(8,128)S(1)}, f32[136,128]{1,0:T(8,128)S(1)}, u32[]{:S(2)}, u32[]{:S(2)}) collective-permute-start(f32[136,128]{1,0:T(8,128)S(1)} %broadcast_in_dim.2.refs_0_), channel_id=1, source_target_pairs={{24,0},{26,2},{28,4},{30,6},{16,8},{18,10},{20,12},{22,14},{8,16},... | collective-permute-start | bytes 208904 | tf_op jit(solution)/shard_map/ppermute | solution.py:568
  15.1 2.9 %collective-permute-start.1 = (f32[272,128]{1,0:T(8,128)S(1)}, f32[272,128]{1,0:T(8,128)S(1)}, u32[]{:S(2)}, u32[]{:S(2)}) collective-permute-start(f32[272,128]{1,0:T(8,128)S(1)} %pack.1.refs_0_), channel_id=1, source_target_pairs={{1,0},{0,1},{3,2},{2,3},{5,4},{4,5},{7,6},{6,7},{9,8},{8,9},{11,10... | collective-permute-start | bytes 417800 | tf_op jit(solution)/shard_map/ppermute | solution.py:548
  15.2 2.8 %collective-permute-start.4 = (f32[272,128]{1,0:T(8,128)S(1)}, f32[272,128]{1,0:T(8,128)S(1)}, u32[]{:S(2)}, u32[]{:S(2)}) collective-permute-start(f32[272,128]{1,0:T(8,128)S(1)} %collective-permute-done.3.refs_4_), channel_id=1, source_target_pairs={{1,0},{0,1},{3,2},{2,3},{5,4},{4,5},{7,6},{6,7},{9,8},{8,9},{11,10... | collective-permute-start | bytes 417800 | tf_op jit(solution)/shard_map/ppermute | solution.py:548
  15.7 2.4 %collective-permute-start.6 = (f32[272,128]{1,0:T(8,128)S(1)}, f32[272,128]{1,0:T(8,128)S(1)}, u32[]{:S(2)}, u32[]{:S(2)}) collective-permute-start(f32[272,128]{1,0:T(8,128)S(1)} %collective-permute-done.5.refs_6_), channel_id=1, source_target_pairs={{1,0},{0,1},{3,2},{2,3},{5,4},{4,5},{7,6},{6,7},{9,8},{8,9},{11,10... | collective-permute-start | bytes 417800 | tf_op jit(solution)/shard_map/ppermute | solution.py:548
  17.5 8.5 %collective-permute-start.10 = (f32[136,128]{1,0:T(8,128)S(1)}, f32[136,128]{1,0:T(8,128)S(1)}, u32[]{:S(2)}, u32[]{:S(2)}) collective-permute-start(f32[136,128]{1,0:T(8,128)S(1)} %collective-permute-done.8.refs_2_), channel_id=1, source_target_pairs={{1,0},{0,1},{3,2},{2,3},{5,4},{4,5},{7,6},{6,7},{9,8},{8,9},{11,10... | collective-permute-start | bytes 208904 | tf_op jit(solution)/shard_map/ppermute | solution.py:548
  17.5 8.5 %collective-permute-start.9 = (f32[136,128]{1,0:T(8,128)S(1)}, f32[136,128]{1,0:T(8,128)S(1)}, u32[]{:S(2)}, u32[]{:S(2)}) collective-permute-start(f32[136,128]{1,0:T(8,128)S(1)} %collective-permute-done.7.refs_1_), channel_id=1, source_target_pairs={{1,0},{0,1},{3,2},{2,3},{5,4},{4,5},{7,6},{6,7},{9,8},{8,9},{11,10... | collective-permute-start | bytes 208904 | tf_op jit(solution)/shard_map/ppermute | solution.py:548

commit v29 on v27

--- a/solution.py
+++ b/solution.py
@@ -511,11 +511,12 @@
     bounds = [jnp.concatenate([limits[j]] * groups, axis=0) for j in range(points)]
     alphas = [scalars[i] for i in range(ITERS)]
     norms = [scalars[ITERS + 1 + i] for i in range(ITERS)]
-    weights = weights_of(alphas, norms, bounds)
-    real = jnp.concatenate([pair[0] for pair in weights], axis=0)
-    imag = jnp.concatenate([pair[1] for pair in weights], axis=0)
     gram = None
     for plane in range(planes):
+        if plane == planes // 2:
+            weights = weights_of(alphas, norms, bounds)
+            real = jnp.concatenate([pair[0] for pair in weights], axis=0)
+            imag = jnp.concatenate([pair[1] for pair in weights], axis=0)
         last_high, last_low = split(applied[plane])
         high = jnp.concatenate([highs[i, plane] for i in range(ITERS)] + [last_high], axis=0)
         low = jnp.concatenate([lows[i, plane] for i in range(ITERS)] + [last_low], axis=0)

time: 27.9 us -> 27.9 us (level)
  no operation moved by 1% of the time
where the time goes in v29:
time: 27.9 us; the launch traced here: 27.7 us
  Pallas kernels  12.4 us (44%)
  starting transfers between devices  10.1 us (36%)
  waiting for transfers between devices  2.87 us (10%)
  between operations  1.33 us (5%)
  other arithmetic  0.93 us (3%)
    ppermute x9, starting transfers between devices, swapped(): lax.ppermute(values, axis, [(index ^ mask, index) for index in range(size)])  8.04 us
    pallas_call x1, Pallas kernels, whole_grid(): pl.pallas_call(functools.partial(krylov_kernel, parts, count), out_shape=...  7.95 us
    pallas_call x1, Pallas kernels, whole_grid(): pl.pallas_call(functools.partial(gram_kernel, points), out_shape=(out, ou...  3.88 us
    ppermute x9, waiting for transfers between devices, swapped(): lax.ppermute(values, axis, [(index ^ mask, index) for index in range(size)])  2.87 us
    ppermute x1, starting transfers between devices, whole_grid(): lax.ppermute(tile, ('point', 'dom'), mixed)  2.1 us
    concatenate x1, other arithmetic, packed_block(): jnp.concatenate([rows, levels], axis=0)  0.93 us
  transfers between devices with their start and end apart: 10, of which 2 were waited for; matrix products, arithmetic and copies ran while one was open for 0% of the time, Pallas kernels for 29%

profile of v29, /device:TPU:0, one launch (start us, length us, event | category | flops | bytes accessed | tf_op | source)
XLA Modules:
  0.0 27.7 jit_solution(13287895153362793050)
XLA Ops:
  0.6 0.9 %pad_maximum_fusion.rows = f32[272,128]{1,0:T(8,128)S(1)} fusion(f32[16,128]{1,0:T(8,128)} %bitcast.12, f32[256,128]{1,0:T(8,128)} %bitcast.11), kind=kLoop, calls=%fused_computation | loop fusion | flops 34816 | bytes 278528 | tf_op jit(solution)/shard_map/concatenate | solution.py:231
  1.6 0.6 %pack.1.refs_0_ = f32[272,128]{1,0:T(8,128)S(1)} custom-call(f32[272,128]{1,0:T(8,128)S(1)} %pad_maximum_fusion.rows), custom_call_target="tpu_custom_call" | custom-call | tf_op jit(solution)/shard_map/pack/pallas_call | solution.py:224
  2.1 3.0 %collective-permute-start = (f32[272,128]{1,0:T(8,128)S(1)}, f32[272,128]{1,0:T(8,128)S(1)}, u32[]{:S(2)}, u32[]{:S(2)}) collective-permute-start(f32[272,128]{1,0:T(8,128)S(1)} %pack.1.refs_0_), channel_id=1, source_target_pairs={{2,0},{3,1},{0,2},{1,3},{6,4},{7,5},{4,6},{5,7},{10,8},{11,9},{8,1... | collective-permute-start | bytes 417800 | tf_op jit(solution)/shard_map/ppermute | solution.py:547
  5.1 1.5 %collective-permute-start.3 = (f32[272,128]{1,0:T(8,128)S(1)}, f32[272,128]{1,0:T(8,128)S(1)}, u32[]{:S(2)}, u32[]{:S(2)}) collective-permute-start(f32[272,128]{1,0:T(8,128)S(1)} %pack.1.refs_0_), channel_id=1, source_target_pairs={{4,0},{5,1},{6,2},{7,3},{0,4},{1,5},{2,6},{3,7},{12,8},{13,9},{14,... | collective-permute-start | bytes 417800 | tf_op jit(solution)/shard_map/ppermute | solution.py:547
  6.7 0.0 collective-permute-start.5
  7.3 2.1 %collective-permute-start.7 = (f32[136,128]{1,0:T(8,128)S(1)}, f32[136,128]{1,0:T(8,128)S(1)}, u32[]{:S(2)}, u32[]{:S(2)}) collective-permute-start(f32[136,128]{1,0:T(8,128)S(1)} %broadcast_in_dim.2.refs_0_), channel_id=1, source_target_pairs={{8,0},{17,1},{10,2},{19,3},{12,4},{21,5},{14,6},{23,7},{0,8},{25,9... | collective-permute-start | bytes 208904 | tf_op jit(solution)/shard_map/ppermute | solution.py:562
  9.4 2.5 %collective-permute-start.8 = (f32[136,128]{1,0:T(8,128)S(1)}, f32[136,128]{1,0:T(8,128)S(1)}, u32[]{:S(2)}, u32[]{:S(2)}) collective-permute-start(f32[136,128]{1,0:T(8,128)S(1)} %broadcast_in_dim.2.refs_0_), channel_id=1, source_target_pairs={{24,0},{16,8},{8,16},{0,24},{25,1},{17,9},{9,17},{1,25},{26,2},{18... | collective-permute-start | bytes 208904 | tf_op jit(solution)/shard_map/ppermute | solution.py:547
  11.9 0.0 collective-permute-done.refs_2_
  11.9 0.0 collective-permute-start.2
  11.9 0.0 collective-permute-done.7.refs_1_
  11.9 0.5 %collective-permute-start.1 = (f32[272,128]{1,0:T(8,128)S(1)}, f32[272,128]{1,0:T(8,128)S(1)}, u32[]{:S(2)}, u32[]{:S(2)}) collective-permute-start(f32[272,128]{1,0:T(8,128)S(1)} %pack.1.refs_0_), channel_id=1, source_target_pairs={{1,0},{0,1},{3,2},{2,3},{5,4},{4,5},{7,6},{6,7},{9,8},{8,9},{11,10... | collective-permute-start | bytes 417800 | tf_op jit(solution)/shard_map/ppermute | solution.py:547
  12.4 0.8 %collective-permute-done.3.refs_4_ = f32[272,128]{1,0:T(8,128)S(1)} collective-permute-done((f32[272,128]{1,0:T(8,128)S(1)}, f32[272,128]{1,0:T(8,128)S(1)}, u32[]{:S(2)}, u32[]{:S(2)}) %collective-permute-start.3) | collective-permute-done | bytes 139296 | tf_op jit(solution)/shard_map/ppermute | solution.py:547
  13.2 0.0 collective-permute-start.4
  13.2 0.0 collective-permute-done.5.refs_6_
  13.3 0.5 %collective-permute-start.6 = (f32[272,128]{1,0:T(8,128)S(1)}, f32[272,128]{1,0:T(8,128)S(1)}, u32[]{:S(2)}, u32[]{:S(2)}) collective-permute-start(f32[272,128]{1,0:T(8,128)S(1)} %collective-permute-done.5.refs_6_), channel_id=1, source_target_pairs={{1,0},{0,1},{3,2},{2,3},{5,4},{4,5},{7,6},{6,7},{9,8},{8,9},{11,10... | collective-permute-start | bytes 417800 | tf_op jit(solution)/shard_map/ppermute | solution.py:547
  13.8 2.0 %collective-permute-done.8.refs_2_ = f32[136,128]{1,0:T(8,128)S(1)} collective-permute-done((f32[136,128]{1,0:T(8,128)S(1)}, f32[136,128]{1,0:T(8,128)S(1)}, u32[]{:S(2)}, u32[]{:S(2)}) %collective-permute-start.8) | collective-permute-done | bytes 69664 | tf_op jit(solution)/shard_map/ppermute | solution.py:547
  15.8 0.0 collective-permute-start.9
  15.8 0.0 collective-permute-done.2.refs_3_
  15.8 0.0 collective-permute-done.1.refs_1_
  15.8 0.0 collective-permute-done.4.refs_5_
  15.8 0.0 collective-permute-done.6.refs_7_
  15.8 8.0 %krylov.1 = (bf16[6,16,16,1024]{3,2,1,0:T(8,128)(2,1)S(1)}, bf16[6,16,16,1024]{3,2,1,0:T(8,128)(2,1)S(1)}, f32[16,16,1024]{2,1,0:T(8,128)S(1)}, f32[13,16,128]{2,1,0:T(8,128)S(1)}) custom-call(f32[272,128]{1,0:T(8,128)S(1)} %pack.1.refs_0_, f32[272,128]{1,0:T(8,128)S(1)} %collective-permute-done.1.refs_1_, f32[272,128]{1,0:T(8,128)S(1)} %collective-permute-done.refs_2_, ...), custom_call_target="tpu_custom_call" | custom-call | tf_op jit(solution)/shard_map/krylov/pallas_call | solution.py:571
  23.8 0.0 collective-permute-done.9.refs_3_
  23.8 3.9 %gram.1 = (f32[2,64,64]{2,1,0:T(8,128)}, f32[2,64,64]{2,1,0:T(8,128)}) custom-call(f32[13,16,128]{2,1,0:T(8,128)S(1)} %get-tuple-element.12.scalars, f32[136,128]{1,0:T(8,128)S(1)} %broadcast_in_dim.2.refs_0_, f32[136,128]{1,0:T(8,128)S(1)} %collective-permute-done.7.refs_1_, f32[136,128]{1,0:T(8,128)S(1)} %collective-permute-done.8.refs_2_, ...), custom_call_target="tpu_custom_call" | custom-call | tf_op jit(solution)/shard_map/gram/pallas_call | solution.py:594
  (1 shorter events, 0.0 us)
Async XLA Ops:
  2.1 9.8 %collective-permute-start = (f32[272,128]{1,0:T(8,128)S(1)}, f32[272,128]{1,0:T(8,128)S(1)}, u32[]{:S(2)}, u32[]{:S(2)}) collective-permute-start(f32[272,128]{1,0:T(8,128)S(1)} %pack.1.refs_0_), channel_id=1, source_target_pairs={{2,0},{3,1},{0,2},{1,3},{6,4},{7,5},{4,6},{5,7},{10,8},{11,9},{8,1... | collective-permute-start | bytes 417800 | tf_op jit(solution)/shard_map/ppermute | solution.py:547
  5.1 8.1 %collective-permute-start.3 = (f32[272,128]{1,0:T(8,128)S(1)}, f32[272,128]{1,0:T(8,128)S(1)}, u32[]{:S(2)}, u32[]{:S(2)}) collective-permute-start(f32[272,128]{1,0:T(8,128)S(1)} %pack.1.refs_0_), channel_id=1, source_target_pairs={{4,0},{5,1},{6,2},{7,3},{0,4},{1,5},{2,6},{3,7},{12,8},{13,9},{14,... | collective-permute-start | bytes 417800 | tf_op jit(solution)/shard_map/ppermute | solution.py:547
  6.7 6.6 %collective-permute-start.5 = (f32[272,128]{1,0:T(8,128)S(1)}, f32[272,128]{1,0:T(8,128)S(1)}, u32[]{:S(2)}, u32[]{:S(2)}) collective-permute-start(f32[272,128]{1,0:T(8,128)S(1)} %pack.1.refs_0_), channel_id=1, source_target_pairs={{6,0},{7,1},{4,2},{5,3},{2,4},{3,5},{0,6},{1,7},{14,8},{15,9},{12,... | collective-permute-start | bytes 417800 | tf_op jit(solution)/shard_map/ppermute | solution.py:547
  7.3 4.6 %collective-permute-start.7 = (f32[136,128]{1,0:T(8,128)S(1)}, f32[136,128]{1,0:T(8,128)S(1)}, u32[]{:S(2)}, u32[]{:S(2)}) collective-permute-start(f32[136,128]{1,0:T(8,128)S(1)} %broadcast_in_dim.2.refs_0_), channel_id=1, source_target_pairs={{8,0},{17,1},{10,2},{19,3},{12,4},{21,5},{14,6},{23,7},{0,8},{25,9... | collective-permute-start | bytes 208904 | tf_op jit(solution)/shard_map/ppermute | solution.py:562
  9.4 6.4 %collective-permute-start.8 = (f32[136,128]{1,0:T(8,128)S(1)}, f32[136,128]{1,0:T(8,128)S(1)}, u32[]{:S(2)}, u32[]{:S(2)}) collective-permute-start(f32[136,128]{1,0:T(8,128)S(1)} %broadcast_in_dim.2.refs_0_), channel_id=1, source_target_pairs={{24,0},{16,8},{8,16},{0,24},{25,1},{17,9},{9,17},{1,25},{26,2},{18... | collective-permute-start | bytes 208904 | tf_op jit(solution)/shard_map/ppermute | solution.py:547
  11.9 3.9 %collective-permute-start.2 = (f32[272,128]{1,0:T(8,128)S(1)}, f32[272,128]{1,0:T(8,128)S(1)}, u32[]{:S(2)}, u32[]{:S(2)}) collective-permute-start(f32[272,128]{1,0:T(8,128)S(1)} %collective-permute-done.refs_2_), channel_id=1, source_target_pairs={{1,0},{0,1},{3,2},{2,3},{5,4},{4,5},{7,6},{6,7},{9,8},{8,9},{11,10... | collective-permute-start | bytes 417800 | tf_op jit(solution)/shard_map/ppermute | solution.py:547
  11.9 3.9 %collective-permute-start.1 = (f32[272,128]{1,0:T(8,128)S(1)}, f32[272,128]{1,0:T(8,128)S(1)}, u32[]{:S(2)}, u32[]{:S(2)}) collective-permute-start(f32[272,128]{1,0:T(8,128)S(1)} %pack.1.refs_0_), channel_id=1, source_target_pairs={{1,0},{0,1},{3,2},{2,3},{5,4},{4,5},{7,6},{6,7},{9,8},{8,9},{11,10... | collective-permute-start | bytes 417800 | tf_op jit(solution)/shard_map/ppermute | solution.py:547
  13.2 2.6 %collective-permute-start.4 = (f32[272,128]{1,0:T(8,128)S(1)}, f32[272,128]{1,0:T(8,128)S(1)}, u32[]{:S(2)}, u32[]{:S(2)}) collective-permute-start(f32[272,128]{1,0:T(8,128)S(1)} %collective-permute-done.3.refs_4_), channel_id=1, source_target_pairs={{1,0},{0,1},{3,2},{2,3},{5,4},{4,5},{7,6},{6,7},{9,8},{8,9},{11,10... | collective-permute-start | bytes 417800 | tf_op jit(solution)/shard_map/ppermute | solution.py:547
  13.3 2.6 %collective-permute-start.6 = (f32[272,128]{1,0:T(8,128)S(1)}, f32[272,128]{1,0:T(8,128)S(1)}, u32[]{:S(2)}, u32[]{:S(2)}) collective-permute-start(f32[272,128]{1,0:T(8,128)S(1)} %collective-permute-done.5.refs_6_), channel_id=1, source_target_pairs={{1,0},{0,1},{3,2},{2,3},{5,4},{4,5},{7,6},{6,7},{9,8},{8,9},{11,10... | collective-permute-start | bytes 417800 | tf_op jit(solution)/shard_map/ppermute | solution.py:547
  15.8 8.0 %collective-permute-start.9 = (f32[136,128]{1,0:T(8,128)S(1)}, f32[136,128]{1,0:T(8,128)S(1)}, u32[]{:S(2)}, u32[]{:S(2)}) collective-permute-start(f32[136,128]{1,0:T(8,128)S(1)} %collective-permute-done.7.refs_1_), channel_id=1, source_target_pairs={{1,0},{0,1},{3,2},{2,3},{5,4},{4,5},{7,6},{6,7},{9,8},{8,9},{11,10... | collective-permute-start | bytes 208904 | tf_op jit(solution)/shard_map/ppermute | solution.py:547
